TPU v7x, 32 devices: a whole 2x2x4 slice. The times are simulated.
32 devices in a mesh: groups: 2 (over x), blk: 16 (over z, y, core).
Axes of the slice: x: 2, y: 2, z: 4, core: 2. Of those that a mesh axis runs over, the one named last changes fastest.
Arguments:
- embeddings: bfloat16 [8192, 768], P(('groups', 'blk')), parts along dimension 0, may hold values from -0.21875 to 0.21875
- pos_ids: int32 [8192, 32], P(('groups', 'blk')), parts along dimension 0, may hold values from 0 to 4095, all different within a row
- pos_count: int32 [8192], P(('groups', 'blk')), parts along dimension 0, may hold values from 1 to 32
- label_slot: int32 [4096], replicated, may hold values from 0 to 4095, each once
- weights: float32 [4096, 768], P('blk'), may hold values from -6 to 6
- first_moment: float32 [4096, 768], P('blk'), may hold values from -6 to 6
- second_moment: float32 [4096, 768], P('blk'), may hold values from 0.5 to 5
Outputs:
- new_weights: float32 [8192, 768], P(('groups', 'blk')), parts along dimension 0
- new_first: float32 [8192, 768], P(('groups', 'blk')), parts along dimension 0
- new_second: float32 [8192, 768], P(('groups', 'blk')), parts along dimension 0
There are 2 independent parts, one for each index of `groups`. A program takes and returns all parts, laid end to end along the dimension named above; an argument that names none is the same for every part. Nothing has to cross between parts.
Inputs may be any that keep to these rules, and one draw needn't show every extreme that they name: `pos_ids`: the 32 ids of one document are distinct. Only the first pos_count entries of a document's list are positives. `label_slot`: a permutation of the label rows.
All inputs are finite; a program needn't handle non-finite values.
Results may differ from a plain program's by a relative error of at most 0.00032.
Values may be sent and summed in bfloat16 or wider, within the bound.
No kernel may reach another device: no remote copies, remote signals or barrier semaphores. Data moves between devices by JAX's collectives and lax.ppermute only.
A program may use at most 128 MiB of HBM per device.

v0:
```python
import jax
import jax.numpy as jnp
from jax import lax
from jax.sharding import PartitionSpec as P

learn_rate = 0.01
beta_one = 0.9
beta_two = 0.95
adam_eps = 1e-08
decay_rate = 0.1
correct_one = 1.0 - 0.9**10
correct_two = 1.0 - 0.95**10


def live_mask(count_block, slots):
    return jnp.arange(slots, dtype=jnp.int32)[None, :] < count_block[:, None]


def lookup_rows(label_slot, pos_ids):
    table = label_slot.reshape(-1, 128).astype(jnp.float32)
    flat_ids = pos_ids.reshape(-1)
    high_part = flat_ids // 128
    low_part = flat_ids % 128
    picker = (high_part[:, None] == jnp.arange(table.shape[0], dtype=jnp.int32)[None, :]).astype(
        jnp.float32
    )
    chosen = jnp.dot(
        picker, table, precision=lax.Precision.HIGHEST, preferred_element_type=jnp.float32
    )
    within = low_part[:, None] == jnp.arange(128, dtype=jnp.int32)[None, :]
    values = jnp.sum(jnp.where(within, chosen, 0.0), axis=1)
    return values.astype(jnp.int32).reshape(pos_ids.shape)


def block_signal(weight_rows, offset, doc_block, slot_rows, is_live):
    height = weight_rows.shape[0]
    logits = lax.dot_general(
        weight_rows, doc_block, (((1,), (1,)), ((), ())), preferred_element_type=jnp.float32
    )
    local_row = jnp.where(is_live, slot_rows - offset, -1)
    row_index = jnp.arange(height, dtype=jnp.int32)[:, None, None]
    target = jnp.any(local_row[None, :, :] == row_index, axis=2).astype(jnp.float32)
    return (jax.nn.sigmoid(logits) - target).astype(jnp.bfloat16)


def adam_step(weights, first_moment, second_moment, gradient):
    new_first = beta_one * first_moment + (1.0 - beta_one) * gradient
    new_second = beta_two * second_moment + (1.0 - beta_two) * gradient * gradient
    update = new_first / correct_one / (jnp.sqrt(new_second / correct_two) + adam_eps)
    new_weights = weights - learn_rate * (update + decay_rate * weights)
    return (new_weights, new_first, new_second)


def per_device(embeddings, pos_ids, pos_count, label_slot, weights, first_moment, second_moment):
    owned = weights.shape[0]
    slot_rows = lookup_rows(label_slot, pos_ids)
    cast_weights = weights.astype(jnp.bfloat16)
    first_row = lax.axis_index("blk") * owned
    doc_piece = lax.all_gather(embeddings, "blk", axis=0, tiled=True)
    row_piece = lax.all_gather(slot_rows, "blk", axis=0, tiled=True)
    count_piece = lax.all_gather(pos_count, "blk", axis=0, tiled=True)
    signal = block_signal(
        cast_weights, first_row, doc_piece, row_piece, live_mask(count_piece, row_piece.shape[1])
    )
    gradient = jnp.dot(signal, doc_piece, preferred_element_type=jnp.float32)
    new_weights, new_first, new_second = adam_step(weights, first_moment, second_moment, gradient)
    return (new_weights, new_first, new_second)


def solution(mesh):
    in_specs = (
        P(("groups", "blk"), None),
        P(("groups", "blk"), None),
        P(("groups", "blk")),
        P(),
        P("blk", None),
        P("blk", None),
        P("blk", None),
    )
    out_specs = (P(("groups", "blk"), None), P(("groups", "blk"), None), P(("groups", "blk"), None))
    return jax.shard_map(
        per_device, mesh=mesh, in_specs=in_specs, out_specs=out_specs, check_vma=False
    )
```

profile of v0, /device:TPU:0, one launch (start us, length us, event | category | flops | bytes accessed | tf_op | source)
XLA Modules:
  0.0 121.8 jit_solution(5868569387432173062)
XLA Ops:
  7.2 0.0 copy-start
  7.2 0.0 all-gather.3.cloned.1.call-start
  7.2 0.7 all-gather.3.cloned.1.call-update
  7.9 0.9 copy.14
  8.8 0.1 reshape.65
  8.9 2.9 %fusion.6 = f32[8192]{0:T(1024)S(1)} fusion(s32[8192]{0:T(1024)S(1)} %get-tuple-element.7, s32[8192]{0:T(1024)S(1)} %get-tuple-element.6, s32[4096]{0:T(1024)} %param.10), kind=kOutput, calls=%fused_computation.12 | convolution fusion | flops 406056960 | bytes 114688 | tf_op jit(solution)/shard_map/dot_general | solution.py:27
  11.9 0.1 convert_element_type.27
  11.9 0.0 copy-done
  12.0 23.3 %all-gather = s32[16,1,256]{2,1,0:T(1,128)S(1)} all-gather(s32[1,1,256]{2,1,0:T(1,128)S(1)} %bitcast.8), channel_id=1, replica_groups=mesh['groups'=2,'blk'=16] {'blk'}, dimensions={0}, use_global_device_ids=true | all-gather | bytes 17408 | tf_op jit(solution)/shard_map/all_gather | solution.py:61
  35.2 38.4 %all_gather.11 = s32[4096,32]{1,0:T(8,128)S(1)} all-gather(s32[256,32]{1,0:T(8,128)S(1)} %convert_element_type.27), channel_id=1, replica_groups=mesh['groups'=2,'blk'=16] {'blk'}, dimensions={0}, use_global_device_ids=true | all-gather | bytes 557056 | tf_op jit(solution)/shard_map/all_gather | solution.py:60
  73.7 0.0 copy-start.1
  73.7 1.8 %subtract_select_fusion = s32[4096,32]{1,0:T(8,128)S(1)} fusion(s32[4096,32]{1,0:T(8,128)S(1)} %all_gather.11, s32[]{:T(128)S(6)} %mul.38, s32[4096]{0:T(1024)S(1)} %bitcast.7), kind=kLoop, calls=%fused_computation.10 | loop fusion | flops 393216 | bytes 1064964 | tf_op jit(solution)/shard_map/jit(_where)/select_n | solution.py:40
  75.5 0.6 copy.15
  76.1 28.4 %fusion = pred[256,4096]{1,0:T(8,128)(4,1)S(1)} fusion(s32[4096,32]{0,1:T(8,128)S(1)} %copy.15), kind=kLoop, calls=%fused_computation.1 | loop fusion | flops 66060288 | bytes 1572864 | tf_op jit(solution)/shard_map/reduce_or | solution.py:42
  104.5 0.0 all-gather.3.cloned.1.call-done
  104.5 0.0 copy-done.1
  104.5 10.4 %multiply_subtract_fusion = (f32[256,768]{1,0:T(8,128)}, f32[256,768]{1,0:T(8,128)}, f32[256,768]{1,0:T(8,128)}) fusion(f32[256,768]{1,0:T(8,128)S(1)} %copy-done.1, f32[256,768]{1,0:T(8,128)} %param.12, f32[256,768]{1,0:T(8,128)} %param.13, bf16[4096,768]{1,0:T(8,128)(2,1)} %all-gather.3.cloned.1.call-done, pred[256,4096]{1,0:T(8,128)(4,1)S(1)} %fusion), kind=kOutput, calls=%fused_computation.17 | convolution fusion | flops 3230662656 | bytes 12058624 | tf_op jit(solution)/shard_map/dot_general | solution.py:65
  (2 shorter events, 0.0 us)
Async XLA Ops:
  7.2 4.8 %copy-start = (s32[256]{0:T(256)S(1)}, s32[256]{0:T(256)}, u32[]{:S(2)}) copy-start(s32[256]{0:T(256)} %param.9) | copy-start | bytes 3076
  7.2 97.3 %all-gather.3.cloned.1.call-start = ((), (), s32[]{:S(2)}) async-start(), calls=%async_computation | async-start | bytes 6684672 | tf_op jit(solution)/shard_map/all_gather | solution.py:59
  73.7 30.8 %copy-start.1 = (f32[256,768]{1,0:T(8,128)S(1)}, f32[256,768]{1,0:T(8,128)}, u32[]{:S(2)}) copy-start(f32[256,768]{1,0:T(8,128)} %param.11) | copy-start | bytes 2359300
Sparse Core Ops, SparseCore 0:
  10.3 75.9 all-gather.2
where the time goes:
time: 123 us; the launch traced here: 122 us
  blocking collectives  61.7 us (50%)
  other arithmetic  30.2 us (25%)
  between operations  14.1 us (11%)
  matrix products  13.3 us (11%)
  local copies, waits for them, and re-layouts  1.6 us (1%)
    all_gather x1, blocking collectives, per_device(): row_piece = lax.all_gather(slot_rows, 'blk', axis=0, tiled=True)  38.4 us
    reduce_or x1, other arithmetic, block_signal(): jnp.any(local_row[None, :, :] == row_index, axis=2).astype(jnp.float32)  28.4 us
    all_gather x1, blocking collectives, per_device(): count_piece = lax.all_gather(pos_count, 'blk', axis=0, tiled=True)  23.3 us
    dot_general x1, matrix products, per_device(): gradient = jnp.dot(signal, doc_piece, preferred_element_type=jnp.float32)  10.4 us
    dot_general x1, matrix products, lookup_rows(): jnp.dot(picker, table, precision=lax.Precision.HIGHEST, preferred_element...  2.93 us
  transfers between devices with their start and end apart: 1, of which 0 were waited for; matrix products, arithmetic and copies ran while one was open for 29% of the time, Pallas kernels for 0%

commit v1 on v0

v1 whole, which is shorter than its diff:
```python
import functools

import jax
import jax.numpy as jnp
from jax import lax
from jax.experimental import pallas as pl
from jax.experimental.pallas import tpu as pltpu
from jax.sharding import PartitionSpec as P

learn_rate = 0.01
beta_one = 0.9
beta_two = 0.95
adam_eps = 1e-08
decay_rate = 0.1
correct_one = 1.0 - 0.9**10
correct_two = 1.0 - 0.95**10

WORD = 32
VMEM_LIMIT = 48 * 1024 * 1024


def lookup_kernel(ids_ref, count_ref, table_ref, rows_ref):
    slots, docs = ids_ref.shape
    table_rows = table_ref.shape[0]
    for start in range(0, docs, 128):
        ids = ids_ref[:, start : start + 128]
        high_part = ids >> 7
        low_part = ids & 127

        def pick(t, found):
            line = jnp.broadcast_to(table_ref[pl.ds(t, 1), :], (slots, 128))
            here = jnp.take_along_axis(line, low_part, axis=1)
            return jnp.where(high_part == t, here, found)

        found = lax.fori_loop(0, table_rows, pick, jnp.full((slots, 128), -1, jnp.int32), unroll=8)
        place = lax.broadcasted_iota(jnp.int32, (slots, 128), 0)
        live = place < count_ref[:, start : start + 128]
        rows_ref[:, start : start + 128] = jnp.where(live, found, -1)


def lookup_rows(label_slot, pos_ids, pos_count):
    docs, slots = pos_ids.shape
    return pl.pallas_call(
        lookup_kernel,
        out_shape=jax.ShapeDtypeStruct((slots, docs), jnp.int32),
        name="lookup",
    )(pos_ids.T, pos_count.reshape(1, docs), label_slot.reshape(-1, 128))


def target_of(rows, base, height):
    slots, docs = rows.shape
    local = rows - base
    word = local >> 5
    bit = jnp.left_shift(jnp.ones_like(local), local & (WORD - 1))
    words = [
        jnp.sum(jnp.where(word == w, bit, 0), axis=0, keepdims=True) for w in range(height // WORD)
    ]
    shift = lax.broadcasted_iota(jnp.int32, (WORD, docs), 0)
    spread = [(jnp.broadcast_to(line, (WORD, docs)) >> shift) & 1 for line in words]
    return jnp.concatenate(spread, axis=0).astype(jnp.float32)


def gradient_kernel(base_ref, mine_ref, other_ref, docs_ref, rows_ref, mine_out, other_out):
    height = mine_ref.shape[0]

    @pl.when(pl.program_id(0) == 0)
    def _():
        mine_out[...] = jnp.zeros_like(mine_out)
        other_out[...] = jnp.zeros_like(other_out)

    docs = docs_ref[...]
    rows = rows_ref[...].astype(jnp.int32)
    for half, (w_ref, out_ref) in enumerate(((mine_ref, mine_out), (other_ref, other_out))):
        logits = lax.dot_general(
            w_ref[...], docs, (((1,), (1,)), ((), ())), preferred_element_type=jnp.float32
        )
        target = target_of(rows, base_ref[half], height)
        signal = (jax.nn.sigmoid(logits) - target).astype(jnp.bfloat16)
        out_ref[...] += jnp.dot(signal, docs, preferred_element_type=jnp.float32)


def gradient_parts(bases, mine, other, docs, rows, tile):
    height, width = mine.shape
    slots = rows.shape[1]
    steps = docs.shape[0] // tile
    whole = pl.BlockSpec((height, width), lambda i: (0, 0))
    shape = jax.ShapeDtypeStruct((height, width), jnp.float32)
    return pl.pallas_call(
        gradient_kernel,
        grid=(steps,),
        in_specs=[
            pl.BlockSpec(memory_space=pltpu.SMEM),
            whole,
            whole,
            pl.BlockSpec((tile, width), lambda i: (i, 0)),
            pl.BlockSpec((None, slots, tile), lambda i: (i, 0, 0)),
        ],
        out_specs=[whole, whole],
        out_shape=[shape, shape],
        compiler_params=pltpu.CompilerParams(vmem_limit_bytes=VMEM_LIMIT),
        name="gradient",
    )(bases, mine, other, docs, rows)


def adam_step(weights, first_moment, second_moment, gradient):
    new_first = beta_one * first_moment + (1.0 - beta_one) * gradient
    new_second = beta_two * second_moment + (1.0 - beta_two) * gradient * gradient
    update = new_first / correct_one / (jnp.sqrt(new_second / correct_two) + adam_eps)
    new_weights = weights - learn_rate * (update + decay_rate * weights)
    return (new_weights, new_first, new_second)


def per_device(
    blocks, embeddings, pos_ids, pos_count, label_slot, weights, first_moment, second_moment
):
    owned = weights.shape[0]
    me = lax.axis_index("blk")
    swap = [(i, i ^ 1) for i in range(blocks)]
    columns = [list(range(core, blocks, 2)) for core in range(2)]
    mine = weights.astype(jnp.bfloat16)
    other = lax.ppermute(mine, "blk", swap)
    docs = lax.all_gather(embeddings, "blk", axis=0, tiled=True, axis_index_groups=columns)
    rows = lookup_rows(label_slot, pos_ids, pos_count)
    rows = lax.all_gather(rows, "blk", axis=0, axis_index_groups=columns)
    bases = jnp.stack([me * owned, (me ^ 1) * owned]).astype(jnp.int32)
    mine_part, other_part = gradient_parts(bases, mine, other, docs, rows, embeddings.shape[0])
    gradient = mine_part + lax.ppermute(other_part, "blk", swap)
    return adam_step(weights, first_moment, second_moment, gradient)


def solution(mesh):
    in_specs = (
        P(("groups", "blk"), None),
        P(("groups", "blk"), None),
        P(("groups", "blk")),
        P(),
        P("blk", None),
        P("blk", None),
        P("blk", None),
    )
    out_specs = (P(("groups", "blk"), None), P(("groups", "blk"), None), P(("groups", "blk"), None))
    return jax.shard_map(
        functools.partial(per_device, mesh.shape["blk"]),
        mesh=mesh,
        in_specs=in_specs,
        out_specs=out_specs,
        check_vma=False,
    )
```

time: 123 us -> 97.4 us (0.79)
  waiting for transfers between devices: 0.7 us -> 32.4 us
  blocking collectives: 61.7 us -> 32.9 us
  other arithmetic: 30.2 us -> 3.07 us
  matrix products: 13.3 us -> 0 us
  Pallas kernels: 0 us -> 12.2 us
    all_gather x1, waiting for transfers between devices: 0.02 us -> 29.4 us  [per_device(): lax.all_gather(embeddings, 'blk', axis=0, tiled=True, axis_index_groups=c...]
    all_gather x2 -> x1, blocking collectives: 61.7 us -> 32.9 us  [per_device(): rows = lax.all_gather(rows, 'blk', axis=0, axis_index_groups=columns)]
    reduce_or x1 -> x0, other arithmetic: 28.4 us -> none  [block_signal(): jnp.any(local_row[None, :, :] == row_index, axis=2).astype(jnp.float32)]
    dot_general x2 -> x0, matrix products: 13.3 us -> none  [the longest x1 10.4 us: per_device(): gradient = jnp.dot(signal, doc_piece, preferred_element_type=jnp.float32)]
    pallas_call x0 -> x2, Pallas kernels: none -> 12.2 us  [the longest x1 9.62 us: gradient_parts(): pl.pallas_call(gradient_kernel, grid=(steps,), in_specs=[pl.BlockSpec(mem...]
    ppermute x0 -> x2, waiting for transfers between devices: none -> 2.27 us  [the longest x1 2.27 us: per_device(): gradient = mine_part + lax.ppermute(other_part, 'blk', swap)]
    select_n x2 -> x0, other arithmetic: 1.87 us -> none  [the longest x1 1.83 us: block_signal(): local_row = jnp.where(is_live, slot_rows - offset, -1)]
    sub x0 -> x1, other arithmetic: none -> 1.82 us  [adam_step(): new_weights = weights - learn_rate * (update + decay_rate * weights)]
  transfers between devices with their start and end apart: 1 -> 3, of which waited for: 0 -> 2; matrix products, arithmetic and copies ran while one was open for 29% -> 1% of each run, Pallas kernels for 0% -> 3%
where the time goes in v1:
time: 97.4 us; the launch traced here: 97.1 us
  blocking collectives  32.9 us (34%)
  waiting for transfers between devices  32.4 us (33%)
  between operations  14.1 us (14%)
  Pallas kernels  12.2 us (13%)
  other arithmetic  3.07 us (3%)
  local copies, waits for them, and re-layouts  1.9 us (2%)
    all_gather x1, blocking collectives, per_device(): rows = lax.all_gather(rows, 'blk', axis=0, axis_index_groups=columns)  32.9 us
    all_gather x1, waiting for transfers between devices, per_device(): lax.all_gather(embeddings, 'blk', axis=0, tiled=True, axis_index_groups=c...  29.4 us
    pallas_call x1, Pallas kernels, gradient_parts(): pl.pallas_call(gradient_kernel, grid=(steps,), in_specs=[pl.BlockSpec(mem...  9.62 us
    pallas_call x1, Pallas kernels, lookup_rows(): pl.pallas_call(lookup_kernel, out_shape=jax.ShapeDtypeStruct((slots, docs...  2.61 us
    ppermute x1, waiting for transfers between devices, per_device(): gradient = mine_part + lax.ppermute(other_part, 'blk', swap)  2.27 us
  transfers between devices with their start and end apart: 3, of which 2 were waited for; matrix products, arithmetic and copies ran while one was open for 1% of the time, Pallas kernels for 3%

profile of v1, /device:TPU:0, one launch (start us, length us, event | category | flops | bytes accessed | tf_op | source)
XLA Modules:
  0.0 97.1 jit_solution(4403832514502494473)
XLA Ops:
  7.2 0.0 copy-start.1
  7.2 0.0 copy-start.2
  7.2 0.0 all-gather.3.cloned.1.call-start
  7.2 0.7 all-gather.3.cloned.1.call-update
  7.9 1.2 %convert_element_type.3.mine_ref = bf16[256,768]{1,0:T(8,128)(2,1)S(1)} convert(f32[256,768]{1,0:T(8,128)} %param.11) | non-fusion elementwise | flops 196608 | bytes 1179648 | tf_op jit(solution)/shard_map/convert_element_type | solution.py:120
  9.1 0.5 collective-permute-start
  9.6 2.6 %lookup.1 = s32[32,256]{1,0:T(8,128)} custom-call(s32[32,256]{1,0:T(8,128)} %bitcast.7, s32[1,256]{1,0:T(1,128)} %bitcast.9, s32[32,128]{1,0:T(8,128)} %bitcast.8), custom_call_target="tpu_custom_call" | custom-call | tf_op jit(solution)/shard_map/lookup/pallas_call | solution.py:43
  12.2 0.1 pad_add_fusion.base_ref
  12.3 32.9 %all-gather = s32[256,256]{1,0:T(8,128)S(1)} all-gather(s32[32,256]{1,0:T(8,128)} %lookup.1), channel_id=2, replica_groups={{0,2,4,6,8,10,12,14},{1,3,5,7,9,11,13,15},{16,18,20,22,24,26,28,30},{17..., dimensions={0}, use_global_device_ids=true | all-gather | bytes 294912 | tf_op jit(solution)/shard_map/all_gather | solution.py:124
  45.2 0.0 collective-permute-done.other_ref
  45.2 29.4 %all-gather.3.cloned.1.call-done.docs_ref = bf16[2048,768]{1,0:T(8,128)(2,1)} async-done(((bf16[256,768]{1,0:T(8,128)(2,1)}), bf16[2048,768]{1,0:T(8,128)(2,1)}) %all-gather.3.cloned.1.call-update) | async-done | bytes 3145744 | tf_op jit(solution)/shard_map/all_gather | solution.py:122
  74.6 0.0 copy-start
  74.6 1.9 %copy-done = bf16[2048,768]{1,0:T(8,128)(2,1)S(1)} copy-done((bf16[2048,768]{1,0:T(8,128)(2,1)S(1)}, bf16[2048,768]{1,0:T(8,128)(2,1)}, u32[]{:S(2)}) %copy-start) | copy-done | bytes 3145752
  76.5 0.0 copy-start.3
  76.5 9.6 %gradient.1 = (f32[256,768]{1,0:T(8,128)S(1)}, f32[256,768]{1,0:T(8,128)S(1)}) custom-call(s32[2]{0:T(128)S(1)} %pad_add_fusion.base_ref, bf16[256,768]{1,0:T(8,128)(2,1)S(1)} %convert_element_type.3.mine_ref, bf16[256,768]{1,0:T(8,128)(2,1)S(1)} %collective-permute-done.other_ref, bf16[2048,768]{1,0:T(8,128)(2,1)S(1)} %copy-done, s32[8,32,256]{2,1,0:T(8,128)S(1)} %bitcast.6), custom_call_target="tpu_custom_call" | custom-call | tf_op jit(solution)/shard_map/gradient/pallas_call | solution.py:88
  86.1 0.1 collective-permute-start.1
  86.2 2.3 %collective-permute-done.1 = f32[256,768]{1,0:T(8,128)S(1)} collective-permute-done((f32[256,768]{1,0:T(8,128)S(1)}, f32[256,768]{1,0:T(8,128)S(1)}, u32[]{:S(2)}, u32[]{:S(2)}) %collective-permute-start.1) | collective-permute-done | bytes 786464 | tf_op jit(solution)/shard_map/ppermute | solution.py:127
  88.5 0.0 copy-done.1
  88.5 0.0 copy-done.2
  88.5 0.0 copy-done.3
  88.5 1.8 %multiply_subtract_fusion = (f32[256,768]{1,0:T(8,128)}, f32[256,768]{1,0:T(8,128)}, f32[256,768]{1,0:T(8,128)}) fusion(f32[256,768]{1,0:T(8,128)S(1)} %copy-done.1, f32[256,768]{1,0:T(8,128)S(1)} %get-tuple-element.5, f32[256,768]{1,0:T(8,128)S(1)} %collective-permute-done.1, f32[256,768]{1,0:T(8,128)S(1)} %copy-done.2, f32[256,768]{1,0:T(8,128)S(1)} %copy-done.3), kind=kLoop, calls=%fused_computation.2 | loop fusion | flops 3145728 | bytes 6291456 | tf_op jit(solution)/shard_map/sub | solution.py:109
Async XLA Ops:
  7.2 81.3 %copy-start.1 = (f32[256,768]{1,0:T(8,128)S(1)}, f32[256,768]{1,0:T(8,128)}, u32[]{:S(2)}) copy-start(f32[256,768]{1,0:T(8,128)} %param.11) | copy-start | bytes 2359300
  7.2 81.3 %copy-start.2 = (f32[256,768]{1,0:T(8,128)S(1)}, f32[256,768]{1,0:T(8,128)}, u32[]{:S(2)}) copy-start(f32[256,768]{1,0:T(8,128)} %param.12) | copy-start | bytes 2359300
  7.2 67.4 %all-gather.3.cloned.1.call-start = ((), (), s32[]{:S(2)}) async-start(), calls=%async_computation | async-start | bytes 3538944 | tf_op jit(solution)/shard_map/all_gather | solution.py:122
  9.1 36.1 %collective-permute-start = (bf16[256,768]{1,0:T(8,128)(2,1)S(1)}, bf16[256,768]{1,0:T(8,128)(2,1)S(1)}, u32[]{:S(2)}, u32[]{:S(2)}) collective-permute-start(bf16[256,768]{1,0:T(8,128)(2,1)S(1)} %convert_element_type.3.mine_ref), channel_id=1, source_target_pairs={{0,1},{1,0},{2,3},{3,2},{4,5},{5,4},{6,7},{7,6},{8,9},{9,8},{10,11... | collective-permute-start | bytes 1179656 | tf_op jit(solution)/shard_map/ppermute | solution.py:121
  74.6 1.9 %copy-start = (bf16[2048,768]{1,0:T(8,128)(2,1)S(1)}, bf16[2048,768]{1,0:T(8,128)(2,1)}, u32[]{:S(2)}) copy-start(bf16[2048,768]{1,0:T(8,128)(2,1)} %all-gather.3.cloned.1.call-done.docs_ref) | copy-start | bytes 9437188
  76.5 12.0 %copy-start.3 = (f32[256,768]{1,0:T(8,128)S(1)}, f32[256,768]{1,0:T(8,128)}, u32[]{:S(2)}) copy-start(f32[256,768]{1,0:T(8,128)} %param.13) | copy-start | bytes 2359300
  86.1 2.4 %collective-permute-start.1 = (f32[256,768]{1,0:T(8,128)S(1)}, f32[256,768]{1,0:T(8,128)S(1)}, u32[]{:S(2)}, u32[]{:S(2)}) collective-permute-start(f32[256,768]{1,0:T(8,128)S(1)} %get-tuple-element.6), channel_id=1, source_target_pairs={{0,1},{1,0},{2,3},{3,2},{4,5},{5,4},{6,7},{7,6},{8,9},{9,8},{10,11... | collective-permute-start | bytes 2359304 | tf_op jit(solution)/shard_map/ppermute | solution.py:127
Sparse Core Ops, SparseCore 0:
  10.2 64.3 all-gather.2

commit v2 on v1

v2 whole, which is shorter than its diff:
```python
import functools

import jax
import jax.numpy as jnp
import numpy as np
from jax import lax
from jax.experimental import pallas as pl
from jax.experimental.pallas import tpu as pltpu
from jax.sharding import PartitionSpec as P

learn_rate = 0.01
beta_one = 0.9
beta_two = 0.95
adam_eps = 1e-08
decay_rate = 0.1
correct_one = 1.0 - 0.9**10
correct_two = 1.0 - 0.95**10

WORD = 32
VMEM_LIMIT = 32 * 1024 * 1024


def lookup_kernel(ids_ref, count_ref, table_ref, rows_ref):
    slots, docs = ids_ref.shape
    table_rows = table_ref.shape[0]
    for start in range(0, docs, 128):
        ids = ids_ref[:, start : start + 128]
        high_part = ids >> 7
        low_part = ids & 127

        def pick(t, found):
            line = jnp.broadcast_to(table_ref[pl.ds(t, 1), :], (slots, 128))
            here = jnp.take_along_axis(line, low_part, axis=1)
            return jnp.where(high_part == t, here, found)

        found = lax.fori_loop(0, table_rows, pick, jnp.full((slots, 128), -1, jnp.int32), unroll=8)
        place = lax.broadcasted_iota(jnp.int32, (slots, 128), 0)
        live = place < count_ref[:, start : start + 128]
        rows_ref[:, start : start + 128] = jnp.where(live, found, -1).astype(jnp.int16)


def lookup_rows(label_slot, pos_ids, pos_count):
    docs, slots = pos_ids.shape
    return pl.pallas_call(
        lookup_kernel,
        out_shape=jax.ShapeDtypeStruct((slots, docs), jnp.int16),
        name="lookup",
    )(pos_ids.T, pos_count.reshape(1, docs), label_slot.reshape(-1, 128))


def target_of(rows, base, height):
    slots, docs = rows.shape
    local = rows - base
    word = local >> 5
    bit = jnp.left_shift(jnp.ones_like(local), local & (WORD - 1))
    words = [
        jnp.sum(jnp.where(word == w, bit, 0), axis=0, keepdims=True) for w in range(height // WORD)
    ]
    shift = lax.broadcasted_iota(jnp.int32, (WORD, docs), 0)
    spread = [(jnp.broadcast_to(line, (WORD, docs)) >> shift) & 1 for line in words]
    return jnp.concatenate(spread, axis=0).astype(jnp.float32)


def gradient_kernel(bases, slots, fresh, info_ref, *refs):
    halves = len(bases)
    w_refs, refs = refs[:halves], refs[halves:]
    up_ref, down_ref, rows_ref = refs[:3]
    old_refs, new_refs = refs[3:-halves], refs[-halves:]
    split = up_ref.shape[0]
    docs = jnp.concatenate([up_ref[...], down_ref[...]], axis=0)
    rows = jnp.concatenate(
        [rows_ref[info_ref[slots[0]], :, :split], rows_ref[info_ref[slots[1]], :, split:]], axis=1
    ).astype(jnp.int32)
    for half in range(halves):
        weights = w_refs[half][...]
        logits = lax.dot_general(
            weights, docs, (((1,), (1,)), ((), ())), preferred_element_type=jnp.float32
        )
        target = target_of(rows, info_ref[bases[half]], weights.shape[0])
        signal = (jax.nn.sigmoid(logits) - target).astype(jnp.bfloat16)
        part = jnp.dot(signal, docs, preferred_element_type=jnp.float32)
        new_refs[half][...] = part if fresh else old_refs[half][...] + part


def add_gradient(info, bases, slots, weights, up, down, rows, sums):
    halves = len(weights)
    height, width = weights[0].shape
    docs = up.shape[0] + down.shape[0]
    vmem = pl.BlockSpec(memory_space=pltpu.VMEM)
    sums = list(sums or [])
    first_sum = 1 + halves + 3
    return pl.pallas_call(
        functools.partial(gradient_kernel, bases, slots, not sums),
        in_specs=[pl.BlockSpec(memory_space=pltpu.SMEM)] + [vmem] * (halves + 3 + len(sums)),
        out_specs=[vmem] * halves,
        out_shape=[jax.ShapeDtypeStruct((height, width), jnp.float32)] * halves,
        input_output_aliases={first_sum + i: i for i in range(len(sums))},
        compiler_params=pltpu.CompilerParams(vmem_limit_bytes=VMEM_LIMIT),
        cost_estimate=pl.CostEstimate(
            flops=4 * halves * height * width * docs,
            bytes_accessed=halves * height * width * 10,
            transcendentals=halves * height * docs,
        ),
        name="gradient",
    )(info, *weights, up, down, rows, *sums)


def adam_step(weights, first_moment, second_moment, gradient):
    new_first = beta_one * first_moment + (1.0 - beta_one) * gradient
    new_second = beta_two * second_moment + (1.0 - beta_two) * gradient * gradient
    update = new_first / correct_one / (jnp.sqrt(new_second / correct_two) + adam_eps)
    new_weights = weights - learn_rate * (update + decay_rate * weights)
    return (new_weights, new_first, new_second)


def closed_path(chips):
    return list(range(0, chips, 2)) + list(range(1, chips, 2))[::-1]


def over_cores(pairs):
    return [(2 * a + core, 2 * b + core) for a, b in pairs for core in range(2)]


def constants_of(blocks, owned, path, slot_of):
    chips = blocks // 2
    table = np.zeros((blocks, 2 + 2 * chips), np.int32)
    for me in range(blocks):
        chip = me // 2
        place = path.index(chip)
        table[me, :2] = me * owned, (me ^ 1) * owned
        for step in range(chips):
            table[me, 2 + 2 * step] = slot_of.index(path[(place - step) % chips] ^ chip)
            table[me, 3 + 2 * step] = slot_of.index(path[(place + step) % chips] ^ chip)
    return table


def after(values, first):
    return lax.optimization_barrier((values, first))[0]


def per_device(
    blocks, embeddings, pos_ids, pos_count, label_slot, weights, first_moment, second_moment
):
    owned = weights.shape[0]
    chips = blocks // 2
    path = closed_path(chips)
    upward = over_cores([(path[i], path[(i + 1) % chips]) for i in range(chips)])
    downward = [(b, a) for a, b in upward]
    swap = [(i, i ^ 1) for i in range(blocks)]
    distances = [chips >> (i + 1) for i in range(chips.bit_length() - 1)]
    slot_of = [0]
    for distance in distances:
        slot_of = slot_of + [s ^ distance for s in slot_of]
    table = jnp.asarray(constants_of(blocks, owned, path, slot_of))
    info = lax.dynamic_index_in_dim(table, lax.axis_index("blk"), keepdims=False)

    split = embeddings.shape[0] // 2
    halves = [(embeddings[:split], embeddings[split:])]
    rows = mine = other = sums = None
    worked = 0
    for step in range(1, chips):
        up, down = halves[-1]
        arriving = (lax.ppermute(up, "blk", upward), lax.ppermute(down, "blk", downward))
        if step == 1:
            rows = lookup_rows(label_slot, pos_ids, pos_count)[None]
            mine = weights.astype(jnp.bfloat16)
            other = lax.ppermute(mine, "blk", swap)
            done = (rows, mine)
        elif step - 2 < len(distances):
            exchange = over_cores([(c, c ^ distances[step - 2]) for c in range(chips)])
            rows = jnp.concatenate([rows, lax.ppermute(rows, "blk", exchange)], axis=0)
            done = (rows, other)
        else:
            for _ in range(2 if step < chips - 1 else chips):
                if worked < step and worked < chips - 1:
                    slots = (2 + 2 * worked, 3 + 2 * worked)
                    sums = add_gradient(info, (0, 1), slots, [mine, other], *halves[worked], rows, sums)
                    worked += 1
            done = sums
        halves.append(after(arriving, done))
    for late in range(worked, chips - 1):
        slots = (2 + 2 * late, 3 + 2 * late)
        sums = add_gradient(info, (0, 1), slots, [mine, other], *halves[late], rows, sums)
    slots = (2 * chips, 2 * chips + 1)
    (other_sum,) = add_gradient(info, (1,), slots, [other], *halves[-1], rows, sums[1:])
    got = lax.ppermute(other_sum, "blk", swap)
    (mine_sum,) = add_gradient(info, (0,), slots, [mine], *halves[-1], rows, sums[:1])
    return adam_step(weights, first_moment, second_moment, mine_sum + got)


def solution(mesh):
    in_specs = (
        P(("groups", "blk"), None),
        P(("groups", "blk"), None),
        P(("groups", "blk")),
        P(),
        P("blk", None),
        P("blk", None),
        P("blk", None),
    )
    out_specs = (P(("groups", "blk"), None), P(("groups", "blk"), None), P(("groups", "blk"), None))
    return jax.shard_map(
        functools.partial(per_device, mesh.shape["blk"]),
        mesh=mesh,
        in_specs=in_specs,
        out_specs=out_specs,
        check_vma=False,
    )
```

time: 97.4 us -> 63.9 us (0.66)
  blocking collectives: 32.9 us -> 0 us
  starting transfers between devices: 0.63 us -> 19.7 us
  between operations: 14.1 us -> 0.85 us
  waiting for transfers between devices: 32.4 us -> 21.9 us
  Pallas kernels: 12.2 us -> 16.6 us
    all_gather x1 -> x0, blocking collectives: 32.9 us -> none  [per_device(): rows = lax.all_gather(rows, 'blk', axis=0, axis_index_groups=columns)]
    all_gather x1 -> x0, waiting for transfers between devices: 29.4 us -> none  [per_device(): lax.all_gather(embeddings, 'blk', axis=0, tiled=True, axis_index_groups=c...]
    ppermute x1 -> x18, waiting for transfers between devices: 2.27 us -> 21.9 us  [the longest x3 15.1 us: per_device(): rows = jnp.concatenate([rows, lax.ppermute(rows, 'blk', exchange)], axis=0)]
    ppermute x1 -> x18, starting transfers between devices: 0.07 us -> 19.6 us  [the longest x7 10 us: per_device(): lax.ppermute(up, 'blk', upward)]
    pallas_call x1 -> x9, Pallas kernels: 9.62 us -> 14 us  [add_gradient(): pl.pallas_call(functools.partial(gradient_kernel, bases, slots, not sums)...]
    unnamed x8 -> x10, local copies, waits for them, and re-layouts: 1.9 us -> 0.03 us
    convert_element_type x1, other arithmetic: 1.17 us -> 0.04 us  [per_device(): mine = weights.astype(jnp.bfloat16)]
    slice x0 -> x1, local copies, waits for them, and re-layouts: none -> 1.12 us  [per_device(): halves = [(embeddings[:split], embeddings[split:])]]
  transfers between devices with their start and end apart: 3 -> 19, of which waited for: 2 -> 9; matrix products, arithmetic and copies ran while one was open for 1% -> 2% of each run, Pallas kernels for 3% -> 24%
where the time goes in v2:
time: 63.9 us; the launch traced here: 63.6 us
  waiting for transfers between devices  21.9 us (34%)
  starting transfers between devices  19.7 us (31%)
  Pallas kernels  16.6 us (26%)
  other arithmetic  2.57 us (4%)
  local copies, waits for them, and re-layouts  1.84 us (3%)
  between operations  0.85 us (1%)
    ppermute x3, waiting for transfers between devices, per_device(): rows = jnp.concatenate([rows, lax.ppermute(rows, 'blk', exchange)], axis=0)  15.1 us
    pallas_call x9, Pallas kernels, add_gradient(): pl.pallas_call(functools.partial(gradient_kernel, bases, slots, not sums)...  14 us
    ppermute x7, starting transfers between devices, per_device(): lax.ppermute(up, 'blk', upward)  10 us
    ppermute x7, starting transfers between devices, per_device(): lax.ppermute(down, 'blk', downward)  5.37 us
    ppermute x3, starting transfers between devices, per_device(): rows = jnp.concatenate([rows, lax.ppermute(rows, 'blk', exchange)], axis=0)  4.19 us
    ppermute x7, waiting for transfers between devices, per_device(): lax.ppermute(down, 'blk', downward)  3.41 us
    pallas_call x1, Pallas kernels, lookup_rows(): pl.pallas_call(lookup_kernel, out_shape=jax.ShapeDtypeStruct((slots, docs...  2.61 us
    ppermute x7, waiting for transfers between devices, per_device(): lax.ppermute(up, 'blk', upward)  2.42 us
  transfers between devices with their start and end apart: 19, of which 9 were waited for; matrix products, arithmetic and copies ran while one was open for 2% of the time, Pallas kernels for 24%

profile of v2, /device:TPU:0, one launch (start us, length us, event | category | flops | bytes accessed | tf_op | source)
XLA Modules:
  0.0 63.6 jit_solution(8248703857699894637)
XLA Ops:
  0.6 1.1 %fusion.2 = (bf16[128,768]{1,0:T(8,128)(2,1)S(1)}, bf16[128,768]{1,0:T(8,128)(2,1)S(1)}) fusion(bf16[256,768]{1,0:T(8,128)(2,1)} %param.8), kind=kLoop, calls=%fused_computation.8 | loop fusion | bytes 786432 | tf_op jit(solution)/shard_map/slice | solution.py:158
  1.8 3.1 %collective-permute-start = (bf16[128,768]{1,0:T(8,128)(2,1)S(1)}, bf16[128,768]{1,0:T(8,128)(2,1)S(1)}, u32[]{:S(2)}, u32[]{:S(2)}) collective-permute-start(bf16[128,768]{1,0:T(8,128)(2,1)S(1)} %get-tuple-element.63.refs_2_), channel_id=1, source_target_pairs={{0,4},{1,5},{4,8},{5,9},{8,12},{9,13},{12,14},{13,15},{14,10},{15,... | collective-permute-start | bytes 589832 | tf_op jit(solution)/shard_map/ppermute | solution.py:163
  5.0 2.6 %lookup.1 = s16[32,256]{1,0:T(8,128)(2,1)} custom-call(s32[32,256]{1,0:T(8,128)} %bitcast.10, s32[1,256]{1,0:T(1,128)} %bitcast.12, s32[32,128]{1,0:T(8,128)} %bitcast.11), custom_call_target="tpu_custom_call" | custom-call | tf_op jit(solution)/shard_map/lookup/pallas_call | solution.py:44
  7.6 2.1 %collective-permute-done.refs_2_ = bf16[128,768]{1,0:T(8,128)(2,1)S(1)} collective-permute-done((bf16[128,768]{1,0:T(8,128)(2,1)S(1)}, bf16[128,768]{1,0:T(8,128)(2,1)S(1)}, u32[]{:S(2)}, u32[]{:S(2)}) %collective-permute-start) | collective-permute-done | bytes 196640 | tf_op jit(solution)/shard_map/ppermute | solution.py:163
  9.7 1.5 %collective-permute-done.1.refs_3_ = bf16[128,768]{1,0:T(8,128)(2,1)S(1)} collective-permute-done((bf16[128,768]{1,0:T(8,128)(2,1)S(1)}, bf16[128,768]{1,0:T(8,128)(2,1)S(1)}, u32[]{:S(2)}, u32[]{:S(2)}) %collective-permute-start.1) | collective-permute-done | bytes 196640 | tf_op jit(solution)/shard_map/ppermute | solution.py:163
  11.2 1.6 %collective-permute-start.2 = (bf16[128,768]{1,0:T(8,128)(2,1)S(1)}, bf16[128,768]{1,0:T(8,128)(2,1)S(1)}, u32[]{:S(2)}, u32[]{:S(2)}) collective-permute-start(bf16[128,768]{1,0:T(8,128)(2,1)S(1)} %collective-permute-done.refs_2_), channel_id=1, source_target_pairs={{0,4},{1,5},{4,8},{5,9},{8,12},{9,13},{12,14},{13,15},{14,10},{15,... | collective-permute-start | bytes 589832 | tf_op jit(solution)/shard_map/ppermute | solution.py:163
  13.2 2.6 %collective-permute-start.4 = (s16[1,32,256]{2,1,0:T(8,128)(2,1)}, s16[1,32,256]{2,1,0:T(8,128)(2,1)S(1)}, u32[]{:S(2)}, u32[]{:S(2)}) collective-permute-start(s16[1,32,256]{2,1,0:T(8,128)(2,1)} %bitcast.6), channel_id=1, source_target_pairs={{0,8},{1,9},{2,10},{3,11},{4,12},{5,13},{6,14},{7,15},{8,0},{9,1},... | collective-permute-start | bytes 49160 | tf_op jit(solution)/shard_map/ppermute | solution.py:171
  15.8 4.0 %collective-permute-done.4 = s16[1,32,256]{2,1,0:T(8,128)(2,1)S(1)} collective-permute-done((s16[1,32,256]{2,1,0:T(8,128)(2,1)}, s16[1,32,256]{2,1,0:T(8,128)(2,1)S(1)}, u32[]{:S(2)}, u32[]{:S(2)}) %collective-permute-start.4) | collective-permute-done | bytes 16416 | tf_op jit(solution)/shard_map/ppermute | solution.py:171
  19.8 0.7 %pad_add_fusion.2 = s16[2,32,256]{2,1,0:T(8,128)(2,1)S(1)} fusion(s16[1,32,256]{2,1,0:T(8,128)(2,1)S(1)} %collective-permute-done.4, s16[1,32,256]{2,1,0:T(8,128)(2,1)} %bitcast.7), kind=kLoop, calls=%fused_computation.6 | loop fusion | flops 16384 | bytes 65536 | tf_op jit(solution)/shard_map/concatenate | solution.py:171
  20.6 1.4 %collective-permute-start.6 = (bf16[128,768]{1,0:T(8,128)(2,1)S(1)}, bf16[128,768]{1,0:T(8,128)(2,1)S(1)}, u32[]{:S(2)}, u32[]{:S(2)}) collective-permute-start(bf16[128,768]{1,0:T(8,128)(2,1)S(1)} %collective-permute-done.2.refs_2_), channel_id=1, source_target_pairs={{0,4},{1,5},{4,8},{5,9},{8,12},{9,13},{12,14},{13,15},{14,10},{15,... | collective-permute-start | bytes 589832 | tf_op jit(solution)/shard_map/ppermute | solution.py:163
  22.0 0.7 %collective-permute-start.7 = (bf16[128,768]{1,0:T(8,128)(2,1)S(1)}, bf16[128,768]{1,0:T(8,128)(2,1)S(1)}, u32[]{:S(2)}, u32[]{:S(2)}) collective-permute-start(bf16[128,768]{1,0:T(8,128)(2,1)S(1)} %collective-permute-done.3.refs_3_), channel_id=1, source_target_pairs={{4,0},{5,1},{8,4},{9,5},{12,8},{13,9},{14,12},{15,13},{10,14},{11,... | collective-permute-start | bytes 589832 | tf_op jit(solution)/shard_map/ppermute | solution.py:163
  22.6 1.3 %collective-permute-start.8 = (s16[2,32,256]{2,1,0:T(8,128)(2,1)S(1)}, s16[2,32,256]{2,1,0:T(8,128)(2,1)S(1)}, u32[]{:S(2)}, u32[]{:S(2)}) collective-permute-start(s16[2,32,256]{2,1,0:T(8,128)(2,1)S(1)} %pad_add_fusion.2), channel_id=1, source_target_pairs={{0,4},{1,5},{2,6},{3,7},{4,0},{5,1},{6,2},{7,3},{8,12},{9,13},{10,... | collective-permute-start | bytes 98312 | tf_op jit(solution)/shard_map/ppermute | solution.py:171
  24.0 5.4 %collective-permute-done.8 = s16[2,32,256]{2,1,0:T(8,128)(2,1)S(1)} collective-permute-done((s16[2,32,256]{2,1,0:T(8,128)(2,1)S(1)}, s16[2,32,256]{2,1,0:T(8,128)(2,1)S(1)}, u32[]{:S(2)}, u32[]{:S(2)}) %collective-permute-start.8) | collective-permute-done | bytes 32800 | tf_op jit(solution)/shard_map/ppermute | solution.py:171
  29.7 1.8 %collective-permute-start.9 = (bf16[128,768]{1,0:T(8,128)(2,1)S(1)}, bf16[128,768]{1,0:T(8,128)(2,1)S(1)}, u32[]{:S(2)}, u32[]{:S(2)}) collective-permute-start(bf16[128,768]{1,0:T(8,128)(2,1)S(1)} %collective-permute-done.6.refs_2_), channel_id=1, source_target_pairs={{0,4},{1,5},{4,8},{5,9},{8,12},{9,13},{12,14},{13,15},{14,10},{15,... | collective-permute-start | bytes 589832 | tf_op jit(solution)/shard_map/ppermute | solution.py:163
  31.8 5.6 %collective-permute-done.11 = s16[4,32,256]{2,1,0:T(8,128)(2,1)S(1)} collective-permute-done((s16[4,32,256]{2,1,0:T(8,128)(2,1)S(1)}, s16[4,32,256]{2,1,0:T(8,128)(2,1)S(1)}, u32[]{:S(2)}, u32[]{:S(2)}) %collective-permute-start.11) | collective-permute-done | bytes 65568 | tf_op jit(solution)/shard_map/ppermute | solution.py:171
  37.5 2.0 %collective-permute-start.13 = (bf16[128,768]{1,0:T(8,128)(2,1)S(1)}, bf16[128,768]{1,0:T(8,128)(2,1)S(1)}, u32[]{:S(2)}, u32[]{:S(2)}) collective-permute-start(bf16[128,768]{1,0:T(8,128)(2,1)S(1)} %collective-permute-done.10.refs_3_), channel_id=1, source_target_pairs={{4,0},{5,1},{8,4},{9,5},{12,8},{13,9},{14,12},{15,13},{10,14},{11,... | collective-permute-start | bytes 589832 | tf_op jit(solution)/shard_map/ppermute | solution.py:163
  39.5 0.7 %dynamic-slice_bitcast_fusion.info_ref = s32[18]{0:T(128)S(1)} fusion(s32[16,18]{1,0:T(8,128)} %constant.30.clone, s32[]{:T(128)S(6)} %select_n.4), kind=kLoop, calls=%fused_computation.7 | loop fusion | bytes 148 | tf_op jit(solution)/shard_map/jit(dynamic_index_in_dim)/squeeze | solution.py:155
  40.2 1.6 %gradient.9 = (f32[256,768]{1,0:T(8,128)S(1)}, f32[256,768]{1,0:T(8,128)S(1)}) custom-call(s32[18]{0:T(128)S(1)} %dynamic-slice_bitcast_fusion.info_ref, bf16[256,768]{1,0:T(8,128)(2,1)S(1)} %convert_element_type.3.refs_0_, bf16[256,768]{1,0:T(8,128)(2,1)S(1)} %collective-permute-done.5.refs_1_.refs_0_, bf16[128,768]{1,0:T(8,128)(2,1)S(1)} %get-tuple-element.63.refs_2_, ...), custom_call_target="tpu_custom_call" | custom-call | flops 402653184 | bytes 3932160 | tf_op jit(solution)/shard_map/gradient/pallas_call | solution.py:92
  41.9 1.7 %gradient.10 = (f32[256,768]{1,0:T(8,128)S(1)}, f32[256,768]{1,0:T(8,128)S(1)}) custom-call(s32[18]{0:T(128)S(1)} %dynamic-slice_bitcast_fusion.info_ref, bf16[256,768]{1,0:T(8,128)(2,1)S(1)} %convert_element_type.3.refs_0_, bf16[256,768]{1,0:T(8,128)(2,1)S(1)} %collective-permute-done.5.refs_1_.refs_0_, ...), custom_call_target="tpu_custom_call", output_to_operand_aliasing={{0}: (6, {}), {1}: (7, {})} | custom-call | flops 402653184 | bytes 3932160 | tf_op jit(solution)/shard_map/gradient/pallas_call | solution.py:92
  43.8 1.6 %collective-permute-start.14 = (bf16[128,768]{1,0:T(8,128)(2,1)S(1)}, bf16[128,768]{1,0:T(8,128)(2,1)S(1)}, u32[]{:S(2)}, u32[]{:S(2)}) collective-permute-start(bf16[128,768]{1,0:T(8,128)(2,1)S(1)} %collective-permute-done.12.refs_2_), channel_id=1, source_target_pairs={{0,4},{1,5},{4,8},{5,9},{8,12},{9,13},{12,14},{13,15},{14,10},{15,... | collective-permute-start | bytes 589832 | tf_op jit(solution)/shard_map/ppermute | solution.py:163
  45.8 1.7 %gradient.11 = (f32[256,768]{1,0:T(8,128)S(1)}, f32[256,768]{1,0:T(8,128)S(1)}) custom-call(s32[18]{0:T(128)S(1)} %dynamic-slice_bitcast_fusion.info_ref, bf16[256,768]{1,0:T(8,128)(2,1)S(1)} %convert_element_type.3.refs_0_, bf16[256,768]{1,0:T(8,128)(2,1)S(1)} %collective-permute-done.5.refs_1_.refs_0_, ...), custom_call_target="tpu_custom_call", output_to_operand_aliasing={{0}: (6, {}), {1}: (7, {})} | custom-call | flops 402653184 | bytes 3932160 | tf_op jit(solution)/shard_map/gradient/pallas_call | solution.py:92
  47.5 1.7 %gradient.12 = (f32[256,768]{1,0:T(8,128)S(1)}, f32[256,768]{1,0:T(8,128)S(1)}) custom-call(s32[18]{0:T(128)S(1)} %dynamic-slice_bitcast_fusion.info_ref, bf16[256,768]{1,0:T(8,128)(2,1)S(1)} %convert_element_type.3.refs_0_, bf16[256,768]{1,0:T(8,128)(2,1)S(1)} %collective-permute-done.5.refs_1_.refs_0_, ...), custom_call_target="tpu_custom_call", output_to_operand_aliasing={{0}: (6, {}), {1}: (7, {})} | custom-call | flops 402653184 | bytes 3932160 | tf_op jit(solution)/shard_map/gradient/pallas_call | solution.py:92
  49.5 1.6 %collective-permute-done.15.refs_3_ = bf16[128,768]{1,0:T(8,128)(2,1)S(1)} collective-permute-done((bf16[128,768]{1,0:T(8,128)(2,1)S(1)}, bf16[128,768]{1,0:T(8,128)(2,1)S(1)}, u32[]{:S(2)}, u32[]{:S(2)}) %collective-permute-start.15) | collective-permute-done | bytes 196640 | tf_op jit(solution)/shard_map/ppermute | solution.py:163
  51.1 0.5 collective-permute-start.16
  51.6 1.5 %collective-permute-start.17 = (bf16[128,768]{1,0:T(8,128)(2,1)S(1)}, bf16[128,768]{1,0:T(8,128)(2,1)S(1)}, u32[]{:S(2)}, u32[]{:S(2)}) collective-permute-start(bf16[128,768]{1,0:T(8,128)(2,1)S(1)} %collective-permute-done.15.refs_3_), channel_id=1, source_target_pairs={{4,0},{5,1},{8,4},{9,5},{12,8},{13,9},{14,12},{15,13},{10,14},{11,... | collective-permute-start | bytes 589832 | tf_op jit(solution)/shard_map/ppermute | solution.py:163
  53.1 1.7 %gradient.13 = (f32[256,768]{1,0:T(8,128)S(1)}, f32[256,768]{1,0:T(8,128)S(1)}) custom-call(s32[18]{0:T(128)S(1)} %dynamic-slice_bitcast_fusion.info_ref, bf16[256,768]{1,0:T(8,128)(2,1)S(1)} %convert_element_type.3.refs_0_, bf16[256,768]{1,0:T(8,128)(2,1)S(1)} %collective-permute-done.5.refs_1_.refs_0_, ...), custom_call_target="tpu_custom_call", output_to_operand_aliasing={{0}: (6, {}), {1}: (7, {})} | custom-call | flops 402653184 | bytes 3932160 | tf_op jit(solution)/shard_map/gradient/pallas_call | solution.py:92
  54.8 1.7 %gradient.14 = (f32[256,768]{1,0:T(8,128)S(1)}, f32[256,768]{1,0:T(8,128)S(1)}) custom-call(s32[18]{0:T(128)S(1)} %dynamic-slice_bitcast_fusion.info_ref, bf16[256,768]{1,0:T(8,128)(2,1)S(1)} %convert_element_type.3.refs_0_, bf16[256,768]{1,0:T(8,128)(2,1)S(1)} %collective-permute-done.5.refs_1_.refs_0_, ...), custom_call_target="tpu_custom_call", output_to_operand_aliasing={{0}: (6, {}), {1}: (7, {})} | custom-call | flops 402653184 | bytes 3932160 | tf_op jit(solution)/shard_map/gradient/pallas_call | solution.py:92
  56.5 1.7 %gradient.15 = (f32[256,768]{1,0:T(8,128)S(1)}, f32[256,768]{1,0:T(8,128)S(1)}) custom-call(s32[18]{0:T(128)S(1)} %dynamic-slice_bitcast_fusion.info_ref, bf16[256,768]{1,0:T(8,128)(2,1)S(1)} %convert_element_type.3.refs_0_, bf16[256,768]{1,0:T(8,128)(2,1)S(1)} %collective-permute-done.5.refs_1_.refs_0_, ...), custom_call_target="tpu_custom_call", output_to_operand_aliasing={{0}: (6, {}), {1}: (7, {})} | custom-call | flops 402653184 | bytes 3932160 | tf_op jit(solution)/shard_map/gradient/pallas_call | solution.py:92
  58.2 1.2 %gradient.17 = f32[256,768]{1,0:T(8,128)S(1)} custom-call(s32[18]{0:T(128)S(1)} %dynamic-slice_bitcast_fusion.info_ref, bf16[256,768]{1,0:T(8,128)(2,1)S(1)} %collective-permute-done.5.refs_1_.refs_0_, bf16[128,768]{1,0:T(8,128)(2,1)S(1)} %collective-permute-done.16.refs_1_, ...), custom_call_target="tpu_custom_call", output_to_operand_aliasing={{}: (5, {})} | custom-call | flops 201326592 | bytes 1966080 | tf_op jit(solution)/shard_map/gradient/pallas_call | solution.py:92
  59.5 1.2 %gradient.16 = f32[256,768]{1,0:T(8,128)S(1)} custom-call(s32[18]{0:T(128)S(1)} %dynamic-slice_bitcast_fusion.info_ref, bf16[256,768]{1,0:T(8,128)(2,1)S(1)} %convert_element_type.3.refs_0_, bf16[128,768]{1,0:T(8,128)(2,1)S(1)} %collective-permute-done.16.refs_1_, ...), custom_call_target="tpu_custom_call", output_to_operand_aliasing={{}: (5, {})} | custom-call | flops 201326592 | bytes 1966080 | tf_op jit(solution)/shard_map/gradient/pallas_call | solution.py:92
  60.7 1.1 %collective-permute-done.18 = f32[256,768]{1,0:T(8,128)S(1)} collective-permute-done((f32[256,768]{1,0:T(8,128)S(1)}, f32[256,768]{1,0:T(8,128)S(1)}, u32[]{:S(2)}, u32[]{:S(2)}) %collective-permute-start.18) | collective-permute-done | bytes 786464 | tf_op jit(solution)/shard_map/ppermute | solution.py:186
  61.8 1.8 %multiply_subtract_fusion = (f32[256,768]{1,0:T(8,128)}, f32[256,768]{1,0:T(8,128)}, f32[256,768]{1,0:T(8,128)}) fusion(f32[256,768]{1,0:T(8,128)S(1)} %copy-done.1, f32[256,768]{1,0:T(8,128)S(1)} %gradient.16, f32[256,768]{1,0:T(8,128)S(1)} %collective-permute-done.18, f32[256,768]{1,0:T(8,128)S(1)} %copy-done.2, f32[256,768]{1,0:T(8,128)S(1)} %copy-done.3), kind=kLoop, calls=%fused_computation.2 | loop fusion | flops 3145728 | bytes 6291456 | tf_op jit(solution)/shard_map/sub | solution.py:112
  (33 shorter events, 2.3 us)
Async XLA Ops:
  0.6 4.2 %copy-start = (f32[256,768]{1,0:T(8,128)S(1)}, f32[256,768]{1,0:T(8,128)}, u32[]{:S(2)}) copy-start(f32[256,768]{1,0:T(8,128)} %param.12) | copy-start | bytes 2359300
  1.8 7.9 %collective-permute-start = (bf16[128,768]{1,0:T(8,128)(2,1)S(1)}, bf16[128,768]{1,0:T(8,128)(2,1)S(1)}, u32[]{:S(2)}, u32[]{:S(2)}) collective-permute-start(bf16[128,768]{1,0:T(8,128)(2,1)S(1)} %get-tuple-element.63.refs_2_), channel_id=1, source_target_pairs={{0,4},{1,5},{4,8},{5,9},{8,12},{9,13},{12,14},{13,15},{14,10},{15,... | collective-permute-start | bytes 589832 | tf_op jit(solution)/shard_map/ppermute | solution.py:163
  4.8 6.4 %collective-permute-start.1 = (bf16[128,768]{1,0:T(8,128)(2,1)S(1)}, bf16[128,768]{1,0:T(8,128)(2,1)S(1)}, u32[]{:S(2)}, u32[]{:S(2)}) collective-permute-start(bf16[128,768]{1,0:T(8,128)(2,1)S(1)} %get-tuple-element.62.refs_3_), channel_id=1, source_target_pairs={{4,0},{5,1},{8,4},{9,5},{12,8},{13,9},{14,12},{15,13},{10,14},{11,... | collective-permute-start | bytes 589832 | tf_op jit(solution)/shard_map/ppermute | solution.py:163
  4.9 15.6 %collective-permute-start.5 = (bf16[256,768]{1,0:T(8,128)(2,1)S(1)}, bf16[256,768]{1,0:T(8,128)(2,1)S(1)}, u32[]{:S(2)}, u32[]{:S(2)}) collective-permute-start(bf16[256,768]{1,0:T(8,128)(2,1)S(1)} %convert_element_type.3.refs_0_), channel_id=1, source_target_pairs={{0,1},{1,0},{2,3},{3,2},{4,5},{5,4},{6,7},{7,6},{8,9},{9,8},{10,11... | collective-permute-start | bytes 1179656 | tf_op jit(solution)/shard_map/ppermute | solution.py:167
  11.2 18.2 %copy-start.4 = (s16[32,256]{1,0:T(8,128)(2,1)S(1)}, s16[32,256]{1,0:T(8,128)(2,1)}, u32[]{:S(2)}) copy-start(s16[32,256]{1,0:T(8,128)(2,1)} %lookup.1) | copy-start | bytes 49156
  11.2 9.3 %collective-permute-start.2 = (bf16[128,768]{1,0:T(8,128)(2,1)S(1)}, bf16[128,768]{1,0:T(8,128)(2,1)S(1)}, u32[]{:S(2)}, u32[]{:S(2)}) collective-permute-start(bf16[128,768]{1,0:T(8,128)(2,1)S(1)} %collective-permute-done.refs_2_), channel_id=1, source_target_pairs={{0,4},{1,5},{4,8},{5,9},{8,12},{9,13},{12,14},{13,15},{14,10},{15,... | collective-permute-start | bytes 589832 | tf_op jit(solution)/shard_map/ppermute | solution.py:163
  12.8 7.8 %collective-permute-start.3 = (bf16[128,768]{1,0:T(8,128)(2,1)S(1)}, bf16[128,768]{1,0:T(8,128)(2,1)S(1)}, u32[]{:S(2)}, u32[]{:S(2)}) collective-permute-start(bf16[128,768]{1,0:T(8,128)(2,1)S(1)} %collective-permute-done.1.refs_3_), channel_id=1, source_target_pairs={{4,0},{5,1},{8,4},{9,5},{12,8},{13,9},{14,12},{15,13},{10,14},{11,... | collective-permute-start | bytes 589832 | tf_op jit(solution)/shard_map/ppermute | solution.py:163
  13.2 6.6 %collective-permute-start.4 = (s16[1,32,256]{2,1,0:T(8,128)(2,1)}, s16[1,32,256]{2,1,0:T(8,128)(2,1)S(1)}, u32[]{:S(2)}, u32[]{:S(2)}) collective-permute-start(s16[1,32,256]{2,1,0:T(8,128)(2,1)} %bitcast.6), channel_id=1, source_target_pairs={{0,8},{1,9},{2,10},{3,11},{4,12},{5,13},{6,14},{7,15},{8,0},{9,1},... | collective-permute-start | bytes 49160 | tf_op jit(solution)/shard_map/ppermute | solution.py:171
  20.6 8.9 %collective-permute-start.6 = (bf16[128,768]{1,0:T(8,128)(2,1)S(1)}, bf16[128,768]{1,0:T(8,128)(2,1)S(1)}, u32[]{:S(2)}, u32[]{:S(2)}) collective-permute-start(bf16[128,768]{1,0:T(8,128)(2,1)S(1)} %collective-permute-done.2.refs_2_), channel_id=1, source_target_pairs={{0,4},{1,5},{4,8},{5,9},{8,12},{9,13},{12,14},{13,15},{14,10},{15,... | collective-permute-start | bytes 589832 | tf_op jit(solution)/shard_map/ppermute | solution.py:163
  22.0 7.5 %collective-permute-start.7 = (bf16[128,768]{1,0:T(8,128)(2,1)S(1)}, bf16[128,768]{1,0:T(8,128)(2,1)S(1)}, u32[]{:S(2)}, u32[]{:S(2)}) collective-permute-start(bf16[128,768]{1,0:T(8,128)(2,1)S(1)} %collective-permute-done.3.refs_3_), channel_id=1, source_target_pairs={{4,0},{5,1},{8,4},{9,5},{12,8},{13,9},{14,12},{15,13},{10,14},{11,... | collective-permute-start | bytes 589832 | tf_op jit(solution)/shard_map/ppermute | solution.py:163
  22.6 6.8 %collective-permute-start.8 = (s16[2,32,256]{2,1,0:T(8,128)(2,1)S(1)}, s16[2,32,256]{2,1,0:T(8,128)(2,1)S(1)}, u32[]{:S(2)}, u32[]{:S(2)}) collective-permute-start(s16[2,32,256]{2,1,0:T(8,128)(2,1)S(1)} %pad_add_fusion.2), channel_id=1, source_target_pairs={{0,4},{1,5},{2,6},{3,7},{4,0},{5,1},{6,2},{7,3},{8,12},{9,13},{10,... | collective-permute-start | bytes 98312 | tf_op jit(solution)/shard_map/ppermute | solution.py:171
  29.4 8.0 %collective-permute-start.10 = (bf16[128,768]{1,0:T(8,128)(2,1)S(1)}, bf16[128,768]{1,0:T(8,128)(2,1)S(1)}, u32[]{:S(2)}, u32[]{:S(2)}) collective-permute-start(bf16[128,768]{1,0:T(8,128)(2,1)S(1)} %collective-permute-done.7.refs_3_), channel_id=1, source_target_pairs={{4,0},{5,1},{8,4},{9,5},{12,8},{13,9},{14,12},{15,13},{10,14},{11,... | collective-permute-start | bytes 589832 | tf_op jit(solution)/shard_map/ppermute | solution.py:163
  29.7 7.7 %collective-permute-start.9 = (bf16[128,768]{1,0:T(8,128)(2,1)S(1)}, bf16[128,768]{1,0:T(8,128)(2,1)S(1)}, u32[]{:S(2)}, u32[]{:S(2)}) collective-permute-start(bf16[128,768]{1,0:T(8,128)(2,1)S(1)} %collective-permute-done.6.refs_2_), channel_id=1, source_target_pairs={{0,4},{1,5},{4,8},{5,9},{8,12},{9,13},{12,14},{13,15},{14,10},{15,... | collective-permute-start | bytes 589832 | tf_op jit(solution)/shard_map/ppermute | solution.py:163
  31.5 5.9 %collective-permute-start.11 = (s16[4,32,256]{2,1,0:T(8,128)(2,1)S(1)}, s16[4,32,256]{2,1,0:T(8,128)(2,1)S(1)}, u32[]{:S(2)}, u32[]{:S(2)}) collective-permute-start(s16[4,32,256]{2,1,0:T(8,128)(2,1)S(1)} %pad_add_fusion.1), channel_id=1, source_target_pairs={{0,2},{1,3},{2,0},{3,1},{4,6},{5,7},{6,4},{7,5},{8,10},{9,11},{10,... | collective-permute-start | bytes 196616 | tf_op jit(solution)/shard_map/ppermute | solution.py:171
  37.5 6.1 %collective-permute-start.12 = (bf16[128,768]{1,0:T(8,128)(2,1)S(1)}, bf16[128,768]{1,0:T(8,128)(2,1)S(1)}, u32[]{:S(2)}, u32[]{:S(2)}) collective-permute-start(bf16[128,768]{1,0:T(8,128)(2,1)S(1)} %collective-permute-done.9.refs_2_), channel_id=1, source_target_pairs={{0,4},{1,5},{4,8},{5,9},{8,12},{9,13},{12,14},{13,15},{14,10},{15,... | collective-permute-start | bytes 589832 | tf_op jit(solution)/shard_map/ppermute | solution.py:163
  37.5 6.3 %collective-permute-start.13 = (bf16[128,768]{1,0:T(8,128)(2,1)S(1)}, bf16[128,768]{1,0:T(8,128)(2,1)S(1)}, u32[]{:S(2)}, u32[]{:S(2)}) collective-permute-start(bf16[128,768]{1,0:T(8,128)(2,1)S(1)} %collective-permute-done.10.refs_3_), channel_id=1, source_target_pairs={{4,0},{5,1},{8,4},{9,5},{12,8},{13,9},{14,12},{15,13},{10,14},{11,... | collective-permute-start | bytes 589832 | tf_op jit(solution)/shard_map/ppermute | solution.py:163
  43.8 5.7 %collective-permute-start.14 = (bf16[128,768]{1,0:T(8,128)(2,1)S(1)}, bf16[128,768]{1,0:T(8,128)(2,1)S(1)}, u32[]{:S(2)}, u32[]{:S(2)}) collective-permute-start(bf16[128,768]{1,0:T(8,128)(2,1)S(1)} %collective-permute-done.12.refs_2_), channel_id=1, source_target_pairs={{0,4},{1,5},{4,8},{5,9},{8,12},{9,13},{12,14},{13,15},{14,10},{15,... | collective-permute-start | bytes 589832 | tf_op jit(solution)/shard_map/ppermute | solution.py:163
  45.4 5.7 %collective-permute-start.15 = (bf16[128,768]{1,0:T(8,128)(2,1)S(1)}, bf16[128,768]{1,0:T(8,128)(2,1)S(1)}, u32[]{:S(2)}, u32[]{:S(2)}) collective-permute-start(bf16[128,768]{1,0:T(8,128)(2,1)S(1)} %collective-permute-done.13.refs_3_), channel_id=1, source_target_pairs={{4,0},{5,1},{8,4},{9,5},{12,8},{13,9},{14,12},{15,13},{10,14},{11,... | collective-permute-start | bytes 589832 | tf_op jit(solution)/shard_map/ppermute | solution.py:163
  51.1 7.0 %collective-permute-start.16 = (bf16[128,768]{1,0:T(8,128)(2,1)S(1)}, bf16[128,768]{1,0:T(8,128)(2,1)S(1)}, u32[]{:S(2)}, u32[]{:S(2)}) collective-permute-start(bf16[128,768]{1,0:T(8,128)(2,1)S(1)} %collective-permute-done.14.refs_2_), channel_id=1, source_target_pairs={{0,4},{1,5},{4,8},{5,9},{8,12},{9,13},{12,14},{13,15},{14,10},{15,... | collective-permute-start | bytes 589832 | tf_op jit(solution)/shard_map/ppermute | solution.py:163
  51.6 6.5 %collective-permute-start.17 = (bf16[128,768]{1,0:T(8,128)(2,1)S(1)}, bf16[128,768]{1,0:T(8,128)(2,1)S(1)}, u32[]{:S(2)}, u32[]{:S(2)}) collective-permute-start(bf16[128,768]{1,0:T(8,128)(2,1)S(1)} %collective-permute-done.15.refs_3_), channel_id=1, source_target_pairs={{4,0},{5,1},{8,4},{9,5},{12,8},{13,9},{14,12},{15,13},{10,14},{11,... | collective-permute-start | bytes 589832 | tf_op jit(solution)/shard_map/ppermute | solution.py:163
  59.4 2.4 %copy-start.1 = (f32[256,768]{1,0:T(8,128)S(1)}, f32[256,768]{1,0:T(8,128)}, u32[]{:S(2)}) copy-start(f32[256,768]{1,0:T(8,128)} %param.12) | copy-start | bytes 2359300
  59.4 2.4 %copy-start.2 = (f32[256,768]{1,0:T(8,128)S(1)}, f32[256,768]{1,0:T(8,128)}, u32[]{:S(2)}) copy-start(f32[256,768]{1,0:T(8,128)} %param.13) | copy-start | bytes 2359300
  59.4 2.4 %copy-start.3 = (f32[256,768]{1,0:T(8,128)S(1)}, f32[256,768]{1,0:T(8,128)}, u32[]{:S(2)}) copy-start(f32[256,768]{1,0:T(8,128)} %param.14) | copy-start | bytes 2359300
  59.4 2.4 %collective-permute-start.18 = (f32[256,768]{1,0:T(8,128)S(1)}, f32[256,768]{1,0:T(8,128)S(1)}, u32[]{:S(2)}, u32[]{:S(2)}) collective-permute-start(f32[256,768]{1,0:T(8,128)S(1)} %gradient.17), channel_id=1, source_target_pairs={{0,1},{1,0},{2,3},{3,2},{4,5},{5,4},{6,7},{7,6},{8,9},{9,8},{10,11... | collective-permute-start | bytes 2359304 | tf_op jit(solution)/shard_map/ppermute | solution.py:186

commit v3 on v1

v3 whole, which is shorter than its diff:
```python
import functools

import jax
import jax.numpy as jnp
import numpy as np
from jax import lax
from jax.experimental import pallas as pl
from jax.experimental.pallas import tpu as pltpu
from jax.sharding import PartitionSpec as P

learn_rate = 0.01
beta_one = 0.9
beta_two = 0.95
adam_eps = 1e-08
decay_rate = 0.1
correct_one = 1.0 - 0.9**10
correct_two = 1.0 - 0.95**10

WORD = 32
VMEM_LIMIT = 32 * 1024 * 1024


def lookup_kernel(ids_ref, count_ref, table_ref, rows_ref):
    slots, docs = ids_ref.shape
    table_rows = table_ref.shape[0]
    for start in range(0, docs, 128):
        ids = ids_ref[:, start : start + 128]
        high_part = ids >> 7
        low_part = ids & 127

        def pick(t, found):
            line = jnp.broadcast_to(table_ref[pl.ds(t, 1), :], (slots, 128))
            here = jnp.take_along_axis(line, low_part, axis=1)
            return jnp.where(high_part == t, here, found)

        found = lax.fori_loop(0, table_rows, pick, jnp.full((slots, 128), -1, jnp.int32), unroll=8)
        place = lax.broadcasted_iota(jnp.int32, (slots, 128), 0)
        live = place < count_ref[:, start : start + 128]
        rows_ref[:, start : start + 128] = jnp.where(live, found, -1).astype(jnp.int16)


def lookup_rows(label_slot, pos_ids, pos_count):
    docs, slots = pos_ids.shape
    return pl.pallas_call(
        lookup_kernel,
        out_shape=jax.ShapeDtypeStruct((slots, docs), jnp.int16),
        name="lookup",
    )(pos_ids.T, pos_count.reshape(1, docs), label_slot.reshape(-1, 128))


def signs_of(rows, base, height):
    slots, docs = rows.shape
    local = rows - base
    word = local >> 5
    bit = jnp.left_shift(jnp.ones_like(local), local & (WORD - 1))
    words = [
        jnp.sum(jnp.where(word == w, bit, 0), axis=0, keepdims=True) for w in range(height // WORD)
    ]
    place = jnp.left_shift(
        jnp.ones((WORD, docs), jnp.int32), lax.broadcasted_iota(jnp.int32, (WORD, docs), 0)
    )
    spread = [
        jnp.where((jnp.broadcast_to(line, (WORD, docs)) & place) != 0, -1.0, 1.0) for line in words
    ]
    return jnp.concatenate(spread, axis=0)


def gradient_kernel(bases, pieces, fresh, info_ref, rows_ref, *refs):
    blocks = len(bases)
    w_refs, refs = refs[:blocks], refs[blocks:]
    doc_refs, refs = refs[: len(pieces)], refs[len(pieces) :]
    old_refs, new_refs = refs[:-blocks], refs[-blocks:]
    height = w_refs[0].shape[0]
    docs = jnp.concatenate([ref[...] for ref in doc_refs], axis=0)
    weights = jnp.concatenate([ref[...] for ref in w_refs], axis=0)
    rows = jnp.concatenate(
        [rows_ref[info_ref[column], :, start:end] for column, start, end in pieces], axis=1
    ).astype(jnp.int32)
    halved = lax.dot_general(
        weights, docs, (((1,), (1,)), ((), ())), preferred_element_type=jnp.float32
    )
    signs = jnp.concatenate([signs_of(rows, info_ref[base], height) for base in bases], axis=0)
    signal = (jnp.tanh(halved) + signs).astype(jnp.bfloat16)
    part = jnp.dot(signal, docs, preferred_element_type=jnp.float32)
    for block in range(blocks):
        piece = part[block * height : (block + 1) * height]
        new_refs[block][...] = piece if fresh else old_refs[block][...] + piece


def add_gradient(info, bases, pieces, rows, weights, docs, sums):
    blocks = len(weights)
    height, width = weights[0].shape
    number = sum(doc.shape[0] for doc in docs)
    vmem = pl.BlockSpec(memory_space=pltpu.VMEM)
    sums = list(sums or [])
    inputs = [rows, *weights, *docs, *sums]
    first_sum = 1 + len(inputs) - len(sums)
    return pl.pallas_call(
        functools.partial(gradient_kernel, bases, pieces, not sums),
        in_specs=[pl.BlockSpec(memory_space=pltpu.SMEM)] + [vmem] * len(inputs),
        out_specs=[vmem] * blocks,
        out_shape=[jax.ShapeDtypeStruct((height, width), jnp.float32)] * blocks,
        input_output_aliases={first_sum + i: i for i in range(len(sums))},
        compiler_params=pltpu.CompilerParams(vmem_limit_bytes=VMEM_LIMIT),
        cost_estimate=pl.CostEstimate(
            flops=4 * blocks * height * width * number,
            bytes_accessed=blocks * height * width * 10,
            transcendentals=blocks * height * number,
        ),
        name="gradient",
    )(info, *inputs)


def adam_step(weights, first_moment, second_moment, gradient):
    new_first = beta_one * first_moment + (1.0 - beta_one) * gradient
    new_second = beta_two * second_moment + (1.0 - beta_two) * gradient * gradient
    update = new_first / correct_one / (jnp.sqrt(new_second / correct_two) + adam_eps)
    new_weights = weights - learn_rate * (update + decay_rate * weights)
    return (new_weights, new_first, new_second)


def over_cores(pairs):
    return [(2 * a + core, 2 * b + core) for a, b in pairs for core in range(2)]


def constants_of(blocks, owned, across, distances):
    chips = blocks // 2
    along = chips // across
    slot_of = [0]
    for distance in distances:
        slot_of = slot_of + [s ^ distance for s in slot_of]
    table = np.zeros((blocks, 2 + 4 * along), np.int32)
    for me in range(blocks):
        chip = me // 2
        z, y = divmod(chip, across)
        table[me, :2] = me * owned, (me ^ 1) * owned
        for step in range(along):
            sources = [((z + sign * step) % along, other) for other in (0, 1) for sign in (-1, 1)]
            for i, (from_z, other) in enumerate(sources):
                from_chip = from_z * across + (y + other) % across
                table[me, 2 + 4 * step + i] = slot_of.index(from_chip ^ chip)
    return table


def after(values, first):
    return lax.optimization_barrier((values, first))[0]


def per_device(
    blocks,
    across,
    embeddings,
    pos_ids,
    pos_count,
    label_slot,
    weights,
    first_moment,
    second_moment,
):
    owned = weights.shape[0]
    chips = blocks // 2
    along = chips // across
    upward = over_cores([(c, (c + across) % chips) for c in range(chips)])
    downward = [(b, a) for a, b in upward]
    beside = over_cores([(c, c ^ 1) for c in range(chips)])
    swap = [(i, i ^ 1) for i in range(blocks)]
    distances = [1] * (across - 1)
    distances += [chips >> (i + 1) for i in range(along.bit_length() - 1)]
    table = jnp.asarray(constants_of(blocks, owned, across, distances))
    info = lax.dynamic_index_in_dim(table, lax.axis_index("blk"), keepdims=False)
    number = embeddings.shape[0]
    split = number // 2

    def send(value, pairs):
        return lax.ppermute(value, "blk", pairs)

    def pieces_of(step, other):
        column = 2 + 4 * step + 2 * other
        return ((column, 0, split), (column + 1, split, number))

    own = ((2, 0, number),)
    neighbour = ((4, 0, number),)
    if across == 2:
        beside_own = send(embeddings, beside)
    a_half, b_half = embeddings[:split], embeddings[split:]
    a_next, b_next = send(a_half, upward), send(b_half, downward)
    mine = weights.astype(jnp.bfloat16) * 0.5
    other = send(mine, swap)
    rows = lookup_rows(label_slot, pos_ids, pos_count)[None]
    row_parts = [rows]
    row_next = send(rows, over_cores([(c, c ^ distances[0]) for c in range(chips)]))
    sums = add_gradient(info, (0, 1), own, rows, [mine, other], [embeddings], None)
    waiting = []
    late = []
    if across == 2:
        waiting.append((1, neighbour, [beside_own]))
        late_b = None
    stage = 0

    def advance(tie):
        nonlocal rows, row_next, stage
        if stage == len(distances):
            return
        got = after(row_next, tie)
        rows = jnp.concatenate([rows, got], axis=0)
        stage += 1
        if stage < len(distances):
            row_next = send(rows, over_cores([(c, c ^ distances[stage]) for c in range(chips)]))

    def work(limit):
        nonlocal sums
        while waiting and limit and (waiting[0][0] <= stage):
            _, pieces, docs = waiting.pop(0)
            sums = add_gradient(info, (0, 1), pieces, rows, [mine, other], docs, sums)
            limit -= 1

    for step in range(1, along):
        last = step == along - 1
        a_half = after(a_next, sums)
        if not last:
            a_next = send(a_half, upward)
        if across == 2:
            a_beside = send(a_half, beside)
        b_half = after(b_next, sums)
        if not last:
            b_next = send(b_half, downward)
        if across == 2 and not last:
            b_beside = send(b_half, beside)
        if across == 2 and step == 1:
            late_b = send(after(beside_own, sums)[split:], upward)
        advance(sums)
        work(1)
        advance(sums)
        waiting.append((len(distances), pieces_of(step, 0), [a_half, b_half]))
        if across == 2:
            waiting.append((len(distances), pieces_of(step, 1), [a_beside, late_b if last else b_beside]))
        if step > 1:
            work(1 if not last else len(waiting) - 1)
    while stage < len(distances):
        advance(sums)
    work(len(waiting) - 1)
    _, pieces, docs = waiting.pop()
    (other_sum,) = add_gradient(info, (1,), pieces, rows, [other], docs, sums[1:])
    got = send(other_sum, swap)
    (mine_sum,) = add_gradient(info, (0,), pieces, rows, [mine], docs, sums[:1])
    return adam_step(weights, first_moment, second_moment, 0.5 * (mine_sum + got))


def solution(mesh):
    in_specs = (
        P(("groups", "blk"), None),
        P(("groups", "blk"), None),
        P(("groups", "blk")),
        P(),
        P("blk", None),
        P("blk", None),
        P("blk", None),
    )
    out_specs = (P(("groups", "blk"), None), P(("groups", "blk"), None), P(("groups", "blk"), None))
    return jax.shard_map(
        functools.partial(per_device, mesh.shape["blk"], 4 // mesh.shape["groups"]),
        mesh=mesh,
        in_specs=in_specs,
        out_specs=out_specs,
        check_vma=False,
    )
```

time: 97.4 us -> 55.5 us (0.57)
  blocking collectives: 32.9 us -> 0 us
  starting transfers between devices: 0.63 us -> 25.5 us
  waiting for transfers between devices: 32.4 us -> 8.44 us
  between operations: 14.1 us -> 0.85 us
  Pallas kernels: 12.2 us -> 15.8 us
    all_gather x1 -> x0, blocking collectives: 32.9 us -> none  [per_device(): rows = lax.all_gather(rows, 'blk', axis=0, axis_index_groups=columns)]
    all_gather x1 -> x0, waiting for transfers between devices: 29.4 us -> none  [per_device(): lax.all_gather(embeddings, 'blk', axis=0, tiled=True, axis_index_groups=c...]
    ppermute x2 -> x18, starting transfers between devices: 0.59 us -> 25.5 us  [send(): return lax.ppermute(value, 'blk', pairs)]
    ppermute x2 -> x18, waiting for transfers between devices: 2.27 us -> 8.44 us  [send(): return lax.ppermute(value, 'blk', pairs)]
    pallas_call x1 -> x9, Pallas kernels: 9.62 us -> 13.2 us  [add_gradient(): pl.pallas_call(functools.partial(gradient_kernel, bases, pieces, not sums...]
    mul x0 -> x1, other arithmetic: none -> 1.23 us  [per_device(): mine = weights.astype(jnp.bfloat16) * 0.5]
    convert_element_type x1 -> x0, other arithmetic: 1.17 us -> none  [per_device(): mine = weights.astype(jnp.bfloat16)]
    unnamed x8 -> x12, local copies, waits for them, and re-layouts: 1.9 us -> 0.74 us
  transfers between devices with their start and end apart: 3 -> 18, of which waited for: 2 -> 4; matrix products, arithmetic and copies ran while one was open for 1% -> 1% of each run, Pallas kernels for 3% -> 27%
where the time goes in v3:
time: 55.5 us; the launch traced here: 55.1 us
  starting transfers between devices  25.5 us (46%)
  Pallas kernels  15.8 us (28%)
  waiting for transfers between devices  8.44 us (15%)
  other arithmetic  3.07 us (6%)
  local copies, waits for them, and re-layouts  1.48 us (3%)
  between operations  0.85 us (2%)
    ppermute x18, starting transfers between devices, send(): return lax.ppermute(value, 'blk', pairs)  25.5 us
    pallas_call x9, Pallas kernels, add_gradient(): pl.pallas_call(functools.partial(gradient_kernel, bases, pieces, not sums...  13.2 us
    ppermute x18, waiting for transfers between devices, send(): return lax.ppermute(value, 'blk', pairs)  8.44 us
    pallas_call x1, Pallas kernels, lookup_rows(): pl.pallas_call(lookup_kernel, out_shape=jax.ShapeDtypeStruct((slots, docs...  2.6 us
    sub x1, other arithmetic, adam_step(): new_weights = weights - learn_rate * (update + decay_rate * weights)  1.82 us
    mul x1, other arithmetic, per_device(): mine = weights.astype(jnp.bfloat16) * 0.5  1.23 us
  transfers between devices with their start and end apart: 18, of which 4 were waited for; matrix products, arithmetic and copies ran while one was open for 1% of the time, Pallas kernels for 27%

profile of v3, /device:TPU:0, one launch (start us, length us, event | category | flops | bytes accessed | tf_op | source)
XLA Modules:
  0.0 55.1 jit_solution(11439748620762526012)
XLA Ops:
  0.6 1.2 %convert_multiply_fusion.refs_0_ = bf16[256,768]{1,0:T(8,128)(2,1)S(1)} fusion(f32[256,768]{1,0:T(8,128)} %param.12), kind=kLoop, calls=%fused_computation.3 | loop fusion | flops 393216 | bytes 1179648 | tf_op jit(solution)/shard_map/mul | solution.py:187
  1.9 0.5 collective-permute-start.1
  2.4 2.6 %collective-permute-start.3 = (bf16[256,768]{1,0:T(8,128)(2,1)S(1)}, bf16[256,768]{1,0:T(8,128)(2,1)S(1)}, u32[]{:S(2)}, u32[]{:S(2)}) collective-permute-start(bf16[256,768]{1,0:T(8,128)(2,1)S(1)} %copy-done), channel_id=1, source_target_pairs={{0,2},{1,3},{2,0},{3,1},{4,6},{5,7},{6,4},{7,5},{8,10},{9,11},{10,... | collective-permute-start | bytes 1179656 | tf_op jit(solution)/shard_map/ppermute | solution.py:175
  5.0 1.6 %collective-permute-start.5 = (bf16[128,768]{1,0:T(8,128)(2,1)S(1)}, bf16[128,768]{1,0:T(8,128)(2,1)S(1)}, u32[]{:S(2)}, u32[]{:S(2)}) collective-permute-start(bf16[128,768]{1,0:T(8,128)(2,1)S(1)} %get-tuple-element.55), channel_id=1, source_target_pairs={{0,4},{1,5},{2,6},{3,7},{4,8},{5,9},{6,10},{7,11},{8,12},{9,13},{1... | collective-permute-start | bytes 589832 | tf_op jit(solution)/shard_map/ppermute | solution.py:175
  6.7 2.2 %collective-permute-start.9 = (bf16[128,768]{1,0:T(8,128)(2,1)S(1)}, bf16[128,768]{1,0:T(8,128)(2,1)S(1)}, u32[]{:S(2)}, u32[]{:S(2)}) collective-permute-start(bf16[128,768]{1,0:T(8,128)(2,1)S(1)} %get-tuple-element.54), channel_id=1, source_target_pairs={{4,0},{5,1},{6,2},{7,3},{8,4},{9,5},{10,6},{11,7},{12,8},{13,9},{1... | collective-permute-start | bytes 589832 | tf_op jit(solution)/shard_map/ppermute | solution.py:175
  8.9 2.6 %lookup.1 = s16[32,256]{1,0:T(8,128)(2,1)} custom-call(s32[32,256]{1,0:T(8,128)} %bitcast.11, s32[1,256]{1,0:T(1,128)} %bitcast.13, s32[32,128]{1,0:T(8,128)} %bitcast.12), custom_call_target="tpu_custom_call" | custom-call | tf_op jit(solution)/shard_map/lookup/pallas_call | solution.py:44
  11.5 0.3 collective-permute-start
  11.9 0.7 %dynamic-slice_bitcast_fusion.info_ref = s32[18]{0:T(128)S(1)} fusion(s32[16,18]{1,0:T(8,128)} %constant.37.clone, s32[]{:T(128)S(6)} %select_n.4), kind=kLoop, calls=%fused_computation.7 | loop fusion | bytes 148 | tf_op jit(solution)/shard_map/jit(dynamic_index_in_dim)/squeeze | solution.py:170
  12.6 0.7 %copy-done.1 = s16[32,256]{1,0:T(8,128)(2,1)S(1)} copy-done((s16[32,256]{1,0:T(8,128)(2,1)S(1)}, s16[32,256]{1,0:T(8,128)(2,1)}, u32[]{:S(2)}) %copy-start.1) | copy-done | bytes 16408
  13.3 1.5 %gradient.9 = (f32[256,768]{1,0:T(8,128)S(1)}, f32[256,768]{1,0:T(8,128)S(1)}) custom-call(s32[18]{0:T(128)S(1)} %dynamic-slice_bitcast_fusion.info_ref, s16[1,32,256]{2,1,0:T(8,128)(2,1)S(1)} %bitcast.7, bf16[256,768]{1,0:T(8,128)(2,1)S(1)} %convert_multiply_fusion.refs_0_, bf16[256,768]{1,0:T(8,128)(2,1)S(1)} %collective-permute-done.1.refs_1_.refs_0_, ...), custom_call_target="tpu_custom_call" | custom-call | flops 402653184 | bytes 3932160 | tf_op jit(solution)/shard_map/gradient/pallas_call | solution.py:98
  14.9 1.7 %collective-permute-start.8 = (bf16[128,768]{1,0:T(8,128)(2,1)S(1)}, bf16[128,768]{1,0:T(8,128)(2,1)S(1)}, u32[]{:S(2)}, u32[]{:S(2)}) collective-permute-start(bf16[128,768]{1,0:T(8,128)(2,1)S(1)} %collective-permute-done.5.refs_2_), channel_id=1, source_target_pairs={{0,2},{1,3},{2,0},{3,1},{4,6},{5,7},{6,4},{7,5},{8,10},{9,11},{10,... | collective-permute-start | bytes 589832 | tf_op jit(solution)/shard_map/ppermute | solution.py:175
  16.6 0.9 %collective-permute-done.9.refs_3_ = bf16[128,768]{1,0:T(8,128)(2,1)S(1)} collective-permute-done((bf16[128,768]{1,0:T(8,128)(2,1)S(1)}, bf16[128,768]{1,0:T(8,128)(2,1)S(1)}, u32[]{:S(2)}, u32[]{:S(2)}) %collective-permute-start.9) | collective-permute-done | bytes 196640 | tf_op jit(solution)/shard_map/ppermute | solution.py:175
  17.6 2.9 %collective-permute-start.13 = (bf16[128,768]{1,0:T(8,128)(2,1)S(1)}, bf16[128,768]{1,0:T(8,128)(2,1)S(1)}, u32[]{:S(2)}, u32[]{:S(2)}) collective-permute-start(bf16[128,768]{1,0:T(8,128)(2,1)S(1)} %collective-permute-done.9.refs_3_), channel_id=1, source_target_pairs={{4,0},{5,1},{6,2},{7,3},{8,4},{9,5},{10,6},{11,7},{12,8},{13,9},{1... | collective-permute-start | bytes 589832 | tf_op jit(solution)/shard_map/ppermute | solution.py:175
  20.5 1.0 %collective-permute-start.2 = (s16[2,32,256]{2,1,0:T(8,128)(2,1)S(1)}, s16[2,32,256]{2,1,0:T(8,128)(2,1)S(1)}, u32[]{:S(2)}, u32[]{:S(2)}) collective-permute-start(s16[2,32,256]{2,1,0:T(8,128)(2,1)S(1)} %pad_add_fusion.2.rows_ref), channel_id=1, source_target_pairs={{0,8},{1,9},{2,10},{3,11},{4,12},{5,13},{6,14},{7,15},{8,0},{9,1},... | collective-permute-start | bytes 98312 | tf_op jit(solution)/shard_map/ppermute | solution.py:175
  21.5 1.6 %gradient.10 = (f32[256,768]{1,0:T(8,128)S(1)}, f32[256,768]{1,0:T(8,128)S(1)}) custom-call(s32[18]{0:T(128)S(1)} %dynamic-slice_bitcast_fusion.info_ref, s16[2,32,256]{2,1,0:T(8,128)(2,1)S(1)} %pad_add_fusion.2.rows_ref, bf16[256,768]{1,0:T(8,128)(2,1)S(1)} %convert_multiply_fusion.refs_0_, ...), custom_call_target="tpu_custom_call", output_to_operand_aliasing={{0}: (5, {}), {1}: (6, {})} | custom-call | flops 402653184 | bytes 3932160 | tf_op jit(solution)/shard_map/gradient/pallas_call | solution.py:98
  23.0 5.6 %collective-permute-done.2 = s16[2,32,256]{2,1,0:T(8,128)(2,1)S(1)} collective-permute-done((s16[2,32,256]{2,1,0:T(8,128)(2,1)S(1)}, s16[2,32,256]{2,1,0:T(8,128)(2,1)S(1)}, u32[]{:S(2)}, u32[]{:S(2)}) %collective-permute-start.2) | collective-permute-done | bytes 32800 | tf_op jit(solution)/shard_map/ppermute | solution.py:175
  28.8 1.6 %collective-permute-start.10 = (bf16[128,768]{1,0:T(8,128)(2,1)S(1)}, bf16[128,768]{1,0:T(8,128)(2,1)S(1)}, u32[]{:S(2)}, u32[]{:S(2)}) collective-permute-start(bf16[128,768]{1,0:T(8,128)(2,1)S(1)} %collective-permute-done.9.refs_3_), channel_id=1, source_target_pairs={{0,2},{1,3},{2,0},{3,1},{4,6},{5,7},{6,4},{7,5},{8,10},{9,11},{10,... | collective-permute-start | bytes 589832 | tf_op jit(solution)/shard_map/ppermute | solution.py:175
  30.4 1.9 %collective-permute-start.7 = (bf16[128,768]{1,0:T(8,128)(2,1)S(1)}, bf16[128,768]{1,0:T(8,128)(2,1)S(1)}, u32[]{:S(2)}, u32[]{:S(2)}) collective-permute-start(bf16[128,768]{1,0:T(8,128)(2,1)S(1)} %collective-permute-done.6.refs_2_), channel_id=1, source_target_pairs={{0,4},{1,5},{2,6},{3,7},{4,8},{5,9},{6,10},{7,11},{8,12},{9,13},{1... | collective-permute-start | bytes 589832 | tf_op jit(solution)/shard_map/ppermute | solution.py:175
  32.3 0.8 %collective-permute-done.4 = s16[4,32,256]{2,1,0:T(8,128)(2,1)S(1)} collective-permute-done((s16[4,32,256]{2,1,0:T(8,128)(2,1)S(1)}, s16[4,32,256]{2,1,0:T(8,128)(2,1)S(1)}, u32[]{:S(2)}, u32[]{:S(2)}) %collective-permute-start.4) | collective-permute-done | bytes 65568 | tf_op jit(solution)/shard_map/ppermute | solution.py:175
  33.1 2.1 %collective-permute-start.14 = (bf16[128,768]{1,0:T(8,128)(2,1)S(1)}, bf16[128,768]{1,0:T(8,128)(2,1)S(1)}, u32[]{:S(2)}, u32[]{:S(2)}) collective-permute-start(bf16[128,768]{1,0:T(8,128)(2,1)S(1)} %collective-permute-done.13.refs_3_), channel_id=1, source_target_pairs={{4,0},{5,1},{6,2},{7,3},{8,4},{9,5},{10,6},{11,7},{12,8},{13,9},{1... | collective-permute-start | bytes 589832 | tf_op jit(solution)/shard_map/ppermute | solution.py:175
  35.2 2.4 %collective-permute-start.16 = (bf16[128,768]{1,0:T(8,128)(2,1)S(1)}, bf16[128,768]{1,0:T(8,128)(2,1)S(1)}, u32[]{:S(2)}, u32[]{:S(2)}) collective-permute-start(bf16[128,768]{1,0:T(8,128)(2,1)S(1)} %collective-permute-done.13.refs_3_), channel_id=1, source_target_pairs={{0,2},{1,3},{2,0},{3,1},{4,6},{5,7},{6,4},{7,5},{8,10},{9,11},{10,... | collective-permute-start | bytes 589832 | tf_op jit(solution)/shard_map/ppermute | solution.py:175
  37.8 1.6 %gradient.11 = (f32[256,768]{1,0:T(8,128)S(1)}, f32[256,768]{1,0:T(8,128)S(1)}) custom-call(s32[18]{0:T(128)S(1)} %dynamic-slice_bitcast_fusion.info_ref, s16[8,32,256]{2,1,0:T(8,128)(2,1)S(1)} %pad_add_fusion.rows_ref, bf16[256,768]{1,0:T(8,128)(2,1)S(1)} %convert_multiply_fusion.refs_0_, ...), custom_call_target="tpu_custom_call", output_to_operand_aliasing={{0}: (6, {}), {1}: (7, {})} | custom-call | flops 402653184 | bytes 3932160 | tf_op jit(solution)/shard_map/gradient/pallas_call | solution.py:98
  39.4 2.1 %collective-permute-start.12 = (bf16[128,768]{1,0:T(8,128)(2,1)S(1)}, bf16[128,768]{1,0:T(8,128)(2,1)S(1)}, u32[]{:S(2)}, u32[]{:S(2)}) collective-permute-start(bf16[128,768]{1,0:T(8,128)(2,1)S(1)} %slice.11), channel_id=1, source_target_pairs={{0,4},{1,5},{2,6},{3,7},{4,8},{5,9},{6,10},{7,11},{8,12},{9,13},{1... | collective-permute-start | bytes 589832 | tf_op jit(solution)/shard_map/ppermute | solution.py:175
  41.4 1.6 %gradient.12 = (f32[256,768]{1,0:T(8,128)S(1)}, f32[256,768]{1,0:T(8,128)S(1)}) custom-call(s32[18]{0:T(128)S(1)} %dynamic-slice_bitcast_fusion.info_ref, s16[8,32,256]{2,1,0:T(8,128)(2,1)S(1)} %pad_add_fusion.rows_ref, bf16[256,768]{1,0:T(8,128)(2,1)S(1)} %convert_multiply_fusion.refs_0_, ...), custom_call_target="tpu_custom_call", output_to_operand_aliasing={{0}: (6, {}), {1}: (7, {})} | custom-call | flops 402653184 | bytes 3932160 | tf_op jit(solution)/shard_map/gradient/pallas_call | solution.py:98
  43.0 2.0 %collective-permute-start.11 = (bf16[128,768]{1,0:T(8,128)(2,1)S(1)}, bf16[128,768]{1,0:T(8,128)(2,1)S(1)}, u32[]{:S(2)}, u32[]{:S(2)}) collective-permute-start(bf16[128,768]{1,0:T(8,128)(2,1)S(1)} %collective-permute-done.7.refs_2_), channel_id=1, source_target_pairs={{0,2},{1,3},{2,0},{3,1},{4,6},{5,7},{6,4},{7,5},{8,10},{9,11},{10,... | collective-permute-start | bytes 589832 | tf_op jit(solution)/shard_map/ppermute | solution.py:175
  45.0 1.6 %gradient.13 = (f32[256,768]{1,0:T(8,128)S(1)}, f32[256,768]{1,0:T(8,128)S(1)}) custom-call(s32[18]{0:T(128)S(1)} %dynamic-slice_bitcast_fusion.info_ref, s16[8,32,256]{2,1,0:T(8,128)(2,1)S(1)} %pad_add_fusion.rows_ref, bf16[256,768]{1,0:T(8,128)(2,1)S(1)} %convert_multiply_fusion.refs_0_, ...), custom_call_target="tpu_custom_call", output_to_operand_aliasing={{0}: (6, {}), {1}: (7, {})} | custom-call | flops 402653184 | bytes 3932160 | tf_op jit(solution)/shard_map/gradient/pallas_call | solution.py:98
  46.6 1.6 %gradient.14 = (f32[256,768]{1,0:T(8,128)S(1)}, f32[256,768]{1,0:T(8,128)S(1)}) custom-call(s32[18]{0:T(128)S(1)} %dynamic-slice_bitcast_fusion.info_ref, s16[8,32,256]{2,1,0:T(8,128)(2,1)S(1)} %pad_add_fusion.rows_ref, bf16[256,768]{1,0:T(8,128)(2,1)S(1)} %convert_multiply_fusion.refs_0_, ...), custom_call_target="tpu_custom_call", output_to_operand_aliasing={{0}: (6, {}), {1}: (7, {})} | custom-call | flops 402653184 | bytes 3932160 | tf_op jit(solution)/shard_map/gradient/pallas_call | solution.py:98
  48.2 1.6 %gradient.15 = (f32[256,768]{1,0:T(8,128)S(1)}, f32[256,768]{1,0:T(8,128)S(1)}) custom-call(s32[18]{0:T(128)S(1)} %dynamic-slice_bitcast_fusion.info_ref, s16[8,32,256]{2,1,0:T(8,128)(2,1)S(1)} %pad_add_fusion.rows_ref, bf16[256,768]{1,0:T(8,128)(2,1)S(1)} %convert_multiply_fusion.refs_0_, ...), custom_call_target="tpu_custom_call", output_to_operand_aliasing={{0}: (6, {}), {1}: (7, {})} | custom-call | flops 402653184 | bytes 3932160 | tf_op jit(solution)/shard_map/gradient/pallas_call | solution.py:98
  49.7 1.2 %gradient.17 = f32[256,768]{1,0:T(8,128)S(1)} custom-call(s32[18]{0:T(128)S(1)} %dynamic-slice_bitcast_fusion.info_ref, s16[8,32,256]{2,1,0:T(8,128)(2,1)S(1)} %pad_add_fusion.rows_ref, bf16[256,768]{1,0:T(8,128)(2,1)S(1)} %collective-permute-done.1.refs_1_.refs_0_, ...), custom_call_target="tpu_custom_call", output_to_operand_aliasing={{}: (5, {})} | custom-call | flops 201326592 | bytes 1966080 | tf_op jit(solution)/shard_map/gradient/pallas_call | solution.py:98
  51.1 1.2 %gradient.16 = f32[256,768]{1,0:T(8,128)S(1)} custom-call(s32[18]{0:T(128)S(1)} %dynamic-slice_bitcast_fusion.info_ref, s16[8,32,256]{2,1,0:T(8,128)(2,1)S(1)} %pad_add_fusion.rows_ref, bf16[256,768]{1,0:T(8,128)(2,1)S(1)} %convert_multiply_fusion.refs_0_, bf16[128,768]{1,0:T(8,128)(2,1)S(1)} %collective-permute-done.11.refs_1_, ...), custom_call_target="tpu_custom_call", output_to_operand_aliasing={{}: (5, {})} | custom-call | flops 201326592 | bytes 1966080 | tf_op jit(solution)/shard_map/gradient/pallas_call | solution.py:98
  52.3 1.0 %collective-permute-done.17 = f32[256,768]{1,0:T(8,128)S(1)} collective-permute-done((f32[256,768]{1,0:T(8,128)S(1)}, f32[256,768]{1,0:T(8,128)S(1)}, u32[]{:S(2)}, u32[]{:S(2)}) %collective-permute-start.17) | collective-permute-done | bytes 786464 | tf_op jit(solution)/shard_map/ppermute | solution.py:175
  53.3 1.8 %multiply_subtract_fusion = (f32[256,768]{1,0:T(8,128)}, f32[256,768]{1,0:T(8,128)}, f32[256,768]{1,0:T(8,128)}) fusion(f32[256,768]{1,0:T(8,128)S(1)} %copy-done.3, f32[256,768]{1,0:T(8,128)S(1)} %gradient.16, f32[256,768]{1,0:T(8,128)S(1)} %collective-permute-done.17, f32[256,768]{1,0:T(8,128)S(1)} %copy-done.4, f32[256,768]{1,0:T(8,128)S(1)} %copy-done.5), kind=kLoop, calls=%fused_computation | loop fusion | flops 3342336 | bytes 6291456 | tf_op jit(solution)/shard_map/sub | solution.py:118
  (34 shorter events, 0.4 us)
Async XLA Ops:
  0.6 1.8 %copy-start = (bf16[256,768]{1,0:T(8,128)(2,1)S(1)}, bf16[256,768]{1,0:T(8,128)(2,1)}, u32[]{:S(2)}) copy-start(bf16[256,768]{1,0:T(8,128)(2,1)} %refs_2_.1) | copy-start | bytes 1179652
  1.9 10.7 %collective-permute-start.1 = (bf16[256,768]{1,0:T(8,128)(2,1)S(1)}, bf16[256,768]{1,0:T(8,128)(2,1)S(1)}, u32[]{:S(2)}, u32[]{:S(2)}) collective-permute-start(bf16[256,768]{1,0:T(8,128)(2,1)S(1)} %convert_multiply_fusion.refs_0_), channel_id=1, source_target_pairs={{0,1},{1,0},{2,3},{3,2},{4,5},{5,4},{6,7},{7,6},{8,9},{9,8},{10,11... | collective-permute-start | bytes 1179656 | tf_op jit(solution)/shard_map/ppermute | solution.py:175
  2.4 15.2 %collective-permute-start.3 = (bf16[256,768]{1,0:T(8,128)(2,1)S(1)}, bf16[256,768]{1,0:T(8,128)(2,1)S(1)}, u32[]{:S(2)}, u32[]{:S(2)}) collective-permute-start(bf16[256,768]{1,0:T(8,128)(2,1)S(1)} %copy-done), channel_id=1, source_target_pairs={{0,2},{1,3},{2,0},{3,1},{4,6},{5,7},{6,4},{7,5},{8,10},{9,11},{10,... | collective-permute-start | bytes 1179656 | tf_op jit(solution)/shard_map/ppermute | solution.py:175
  5.0 9.8 %collective-permute-start.5 = (bf16[128,768]{1,0:T(8,128)(2,1)S(1)}, bf16[128,768]{1,0:T(8,128)(2,1)S(1)}, u32[]{:S(2)}, u32[]{:S(2)}) collective-permute-start(bf16[128,768]{1,0:T(8,128)(2,1)S(1)} %get-tuple-element.55), channel_id=1, source_target_pairs={{0,4},{1,5},{2,6},{3,7},{4,8},{5,9},{6,10},{7,11},{8,12},{9,13},{1... | collective-permute-start | bytes 589832 | tf_op jit(solution)/shard_map/ppermute | solution.py:175
  6.7 10.9 %collective-permute-start.9 = (bf16[128,768]{1,0:T(8,128)(2,1)S(1)}, bf16[128,768]{1,0:T(8,128)(2,1)S(1)}, u32[]{:S(2)}, u32[]{:S(2)}) collective-permute-start(bf16[128,768]{1,0:T(8,128)(2,1)S(1)} %get-tuple-element.54), channel_id=1, source_target_pairs={{4,0},{5,1},{6,2},{7,3},{8,4},{9,5},{10,6},{11,7},{12,8},{13,9},{1... | collective-permute-start | bytes 589832 | tf_op jit(solution)/shard_map/ppermute | solution.py:175
  11.5 5.1 %collective-permute-start = (s16[1,32,256]{2,1,0:T(8,128)(2,1)}, s16[1,32,256]{2,1,0:T(8,128)(2,1)S(1)}, u32[]{:S(2)}, u32[]{:S(2)}) collective-permute-start(s16[1,32,256]{2,1,0:T(8,128)(2,1)} %bitcast.6), channel_id=1, source_target_pairs={{0,2},{1,3},{2,0},{3,1},{4,6},{5,7},{6,4},{7,5},{8,10},{9,11},{10,... | collective-permute-start | bytes 49160 | tf_op jit(solution)/shard_map/ppermute | solution.py:175
  12.5 0.7 %copy-start.1 = (s16[32,256]{1,0:T(8,128)(2,1)S(1)}, s16[32,256]{1,0:T(8,128)(2,1)}, u32[]{:S(2)}) copy-start(s16[32,256]{1,0:T(8,128)(2,1)} %lookup.1) | copy-start | bytes 49156
  14.8 15.6 %collective-permute-start.6 = (bf16[128,768]{1,0:T(8,128)(2,1)S(1)}, bf16[128,768]{1,0:T(8,128)(2,1)S(1)}, u32[]{:S(2)}, u32[]{:S(2)}) collective-permute-start(bf16[128,768]{1,0:T(8,128)(2,1)S(1)} %collective-permute-done.5.refs_2_), channel_id=1, source_target_pairs={{0,4},{1,5},{2,6},{3,7},{4,8},{5,9},{6,10},{7,11},{8,12},{9,13},{1... | collective-permute-start | bytes 589832 | tf_op jit(solution)/shard_map/ppermute | solution.py:175
  14.9 22.8 %collective-permute-start.8 = (bf16[128,768]{1,0:T(8,128)(2,1)S(1)}, bf16[128,768]{1,0:T(8,128)(2,1)S(1)}, u32[]{:S(2)}, u32[]{:S(2)}) collective-permute-start(bf16[128,768]{1,0:T(8,128)(2,1)S(1)} %collective-permute-done.5.refs_2_), channel_id=1, source_target_pairs={{0,2},{1,3},{2,0},{3,1},{4,6},{5,7},{6,4},{7,5},{8,10},{9,11},{10,... | collective-permute-start | bytes 589832 | tf_op jit(solution)/shard_map/ppermute | solution.py:175
  17.6 11.1 %copy-start.2 = (s16[32,256]{1,0:T(8,128)(2,1)S(1)}, s16[32,256]{1,0:T(8,128)(2,1)}, u32[]{:S(2)}) copy-start(s16[32,256]{1,0:T(8,128)(2,1)} %lookup.1) | copy-start | bytes 49156
  17.6 15.5 %collective-permute-start.13 = (bf16[128,768]{1,0:T(8,128)(2,1)S(1)}, bf16[128,768]{1,0:T(8,128)(2,1)S(1)}, u32[]{:S(2)}, u32[]{:S(2)}) collective-permute-start(bf16[128,768]{1,0:T(8,128)(2,1)S(1)} %collective-permute-done.9.refs_3_), channel_id=1, source_target_pairs={{4,0},{5,1},{6,2},{7,3},{8,4},{9,5},{10,6},{11,7},{12,8},{13,9},{1... | collective-permute-start | bytes 589832 | tf_op jit(solution)/shard_map/ppermute | solution.py:175
  20.5 8.2 %collective-permute-start.2 = (s16[2,32,256]{2,1,0:T(8,128)(2,1)S(1)}, s16[2,32,256]{2,1,0:T(8,128)(2,1)S(1)}, u32[]{:S(2)}, u32[]{:S(2)}) collective-permute-start(s16[2,32,256]{2,1,0:T(8,128)(2,1)S(1)} %pad_add_fusion.2.rows_ref), channel_id=1, source_target_pairs={{0,8},{1,9},{2,10},{3,11},{4,12},{5,13},{6,14},{7,15},{8,0},{9,1},... | collective-permute-start | bytes 98312 | tf_op jit(solution)/shard_map/ppermute | solution.py:175
  28.7 4.4 %collective-permute-start.4 = (s16[4,32,256]{2,1,0:T(8,128)(2,1)S(1)}, s16[4,32,256]{2,1,0:T(8,128)(2,1)S(1)}, u32[]{:S(2)}, u32[]{:S(2)}) collective-permute-start(s16[4,32,256]{2,1,0:T(8,128)(2,1)S(1)} %pad_add_fusion.1), channel_id=1, source_target_pairs={{0,4},{1,5},{2,6},{3,7},{4,0},{5,1},{6,2},{7,3},{8,12},{9,13},{10,... | collective-permute-start | bytes 196616 | tf_op jit(solution)/shard_map/ppermute | solution.py:175
  28.8 10.6 %collective-permute-start.10 = (bf16[128,768]{1,0:T(8,128)(2,1)S(1)}, bf16[128,768]{1,0:T(8,128)(2,1)S(1)}, u32[]{:S(2)}, u32[]{:S(2)}) collective-permute-start(bf16[128,768]{1,0:T(8,128)(2,1)S(1)} %collective-permute-done.9.refs_3_), channel_id=1, source_target_pairs={{0,2},{1,3},{2,0},{3,1},{4,6},{5,7},{6,4},{7,5},{8,10},{9,11},{10,... | collective-permute-start | bytes 589832 | tf_op jit(solution)/shard_map/ppermute | solution.py:175
  30.4 12.6 %collective-permute-start.7 = (bf16[128,768]{1,0:T(8,128)(2,1)S(1)}, bf16[128,768]{1,0:T(8,128)(2,1)S(1)}, u32[]{:S(2)}, u32[]{:S(2)}) collective-permute-start(bf16[128,768]{1,0:T(8,128)(2,1)S(1)} %collective-permute-done.6.refs_2_), channel_id=1, source_target_pairs={{0,4},{1,5},{2,6},{3,7},{4,8},{5,9},{6,10},{7,11},{8,12},{9,13},{1... | collective-permute-start | bytes 589832 | tf_op jit(solution)/shard_map/ppermute | solution.py:175
  33.1 11.9 %collective-permute-start.14 = (bf16[128,768]{1,0:T(8,128)(2,1)S(1)}, bf16[128,768]{1,0:T(8,128)(2,1)S(1)}, u32[]{:S(2)}, u32[]{:S(2)}) collective-permute-start(bf16[128,768]{1,0:T(8,128)(2,1)S(1)} %collective-permute-done.13.refs_3_), channel_id=1, source_target_pairs={{4,0},{5,1},{6,2},{7,3},{8,4},{9,5},{10,6},{11,7},{12,8},{13,9},{1... | collective-permute-start | bytes 589832 | tf_op jit(solution)/shard_map/ppermute | solution.py:175
  35.2 11.3 %collective-permute-start.16 = (bf16[128,768]{1,0:T(8,128)(2,1)S(1)}, bf16[128,768]{1,0:T(8,128)(2,1)S(1)}, u32[]{:S(2)}, u32[]{:S(2)}) collective-permute-start(bf16[128,768]{1,0:T(8,128)(2,1)S(1)} %collective-permute-done.13.refs_3_), channel_id=1, source_target_pairs={{0,2},{1,3},{2,0},{3,1},{4,6},{5,7},{6,4},{7,5},{8,10},{9,11},{10,... | collective-permute-start | bytes 589832 | tf_op jit(solution)/shard_map/ppermute | solution.py:175
  37.7 8.9 %collective-permute-start.15 = (bf16[128,768]{1,0:T(8,128)(2,1)S(1)}, bf16[128,768]{1,0:T(8,128)(2,1)S(1)}, u32[]{:S(2)}, u32[]{:S(2)}) collective-permute-start(bf16[128,768]{1,0:T(8,128)(2,1)S(1)} %collective-permute-done.6.refs_2_), channel_id=1, source_target_pairs={{0,2},{1,3},{2,0},{3,1},{4,6},{5,7},{6,4},{7,5},{8,10},{9,11},{10,... | collective-permute-start | bytes 589832 | tf_op jit(solution)/shard_map/ppermute | solution.py:175
  39.4 10.4 %collective-permute-start.12 = (bf16[128,768]{1,0:T(8,128)(2,1)S(1)}, bf16[128,768]{1,0:T(8,128)(2,1)S(1)}, u32[]{:S(2)}, u32[]{:S(2)}) collective-permute-start(bf16[128,768]{1,0:T(8,128)(2,1)S(1)} %slice.11), channel_id=1, source_target_pairs={{0,4},{1,5},{2,6},{3,7},{4,8},{5,9},{6,10},{7,11},{8,12},{9,13},{1... | collective-permute-start | bytes 589832 | tf_op jit(solution)/shard_map/ppermute | solution.py:175
  43.0 6.7 %collective-permute-start.11 = (bf16[128,768]{1,0:T(8,128)(2,1)S(1)}, bf16[128,768]{1,0:T(8,128)(2,1)S(1)}, u32[]{:S(2)}, u32[]{:S(2)}) collective-permute-start(bf16[128,768]{1,0:T(8,128)(2,1)S(1)} %collective-permute-done.7.refs_2_), channel_id=1, source_target_pairs={{0,2},{1,3},{2,0},{3,1},{4,6},{5,7},{6,4},{7,5},{8,10},{9,11},{10,... | collective-permute-start | bytes 589832 | tf_op jit(solution)/shard_map/ppermute | solution.py:175
  50.9 2.4 %collective-permute-start.17 = (f32[256,768]{1,0:T(8,128)S(1)}, f32[256,768]{1,0:T(8,128)S(1)}, u32[]{:S(2)}, u32[]{:S(2)}) collective-permute-start(f32[256,768]{1,0:T(8,128)S(1)} %gradient.17), channel_id=1, source_target_pairs={{0,1},{1,0},{2,3},{3,2},{4,5},{5,4},{6,7},{7,6},{8,9},{9,8},{10,11... | collective-permute-start | bytes 2359304 | tf_op jit(solution)/shard_map/ppermute | solution.py:175
  51.0 2.3 %copy-start.3 = (f32[256,768]{1,0:T(8,128)S(1)}, f32[256,768]{1,0:T(8,128)}, u32[]{:S(2)}) copy-start(f32[256,768]{1,0:T(8,128)} %param.12) | copy-start | bytes 2359300
  51.0 2.3 %copy-start.4 = (f32[256,768]{1,0:T(8,128)S(1)}, f32[256,768]{1,0:T(8,128)}, u32[]{:S(2)}) copy-start(f32[256,768]{1,0:T(8,128)} %param.13) | copy-start | bytes 2359300
  51.0 2.3 %copy-start.5 = (f32[256,768]{1,0:T(8,128)S(1)}, f32[256,768]{1,0:T(8,128)}, u32[]{:S(2)}) copy-start(f32[256,768]{1,0:T(8,128)} %param.14) | copy-start | bytes 2359300

commit v4 on v3

v4 whole, which is shorter than its diff:
```python
import functools

import jax
import jax.numpy as jnp
from jax import lax
from jax.experimental import pallas as pl
from jax.experimental.pallas import tpu as pltpu
from jax.sharding import PartitionSpec as P

learn_rate = 0.01
beta_one = 0.9
beta_two = 0.95
adam_eps = 1e-08
decay_rate = 0.1
correct_one = 1.0 - 0.9**10
correct_two = 1.0 - 0.95**10

WORD = 32
VMEM_LIMIT = 32 * 1024 * 1024
SMALL = pl.CostEstimate(flops=1, bytes_accessed=1, transcendentals=0)


def lookup_kernel(ids_ref, count_ref, table_ref, rows_ref):
    slots, docs = ids_ref.shape
    pairs = table_ref.shape[0] // 2
    starts = range(0, docs, 128)
    ids = [ids_ref[:, start : start + 128] for start in starts]
    line_of = [(chunk >> 7) & (pairs - 1) for chunk in ids]
    lane_of = [chunk & 127 for chunk in ids]

    def pick(t, found):
        both = table_ref[pl.ds(t, 1), :] | (table_ref[pl.ds(t + pairs, 1), :] << 16)
        line = jnp.broadcast_to(both, (slots, 128))
        return tuple(
            jnp.where(line_of[i] == t, jnp.take_along_axis(line, lane_of[i], axis=1), found[i])
            for i in range(len(ids))
        )

    found = tuple(jnp.zeros((slots, 128), jnp.int32) for _ in ids)
    if pairs <= 16:
        for t in range(pairs):
            found = pick(t, found)
    else:
        found = lax.fori_loop(0, pairs, pick, found, unroll=8)
    place = lax.broadcasted_iota(jnp.int32, (slots, 128), 0)
    for i, start in enumerate(starts):
        row = jnp.where((ids[i] >> 7) < pairs, found[i], found[i] >> 16) & 0xFFFF
        live = place < count_ref[:, start : start + 128]
        rows_ref[:, start : start + 128] = jnp.where(live, row, -1).astype(jnp.int16)


def lookup_rows(label_slot, pos_ids, pos_count):
    docs, slots = pos_ids.shape
    return pl.pallas_call(
        lookup_kernel,
        out_shape=jax.ShapeDtypeStruct((slots, docs), jnp.int16),
        cost_estimate=SMALL,
        name="lookup",
    )(pos_ids.T, pos_count.reshape(1, docs), label_slot.reshape(-1, 128))


def signs_of(rows, base, height):
    slots, docs = rows.shape
    local = rows - base
    word = local >> 5
    bit = jnp.left_shift(jnp.ones_like(local), local & (WORD - 1))
    words = [
        jnp.sum(jnp.where(word == w, bit, 0), axis=0, keepdims=True) for w in range(height // WORD)
    ]
    place = jnp.left_shift(
        jnp.ones((WORD, docs), jnp.int32), lax.broadcasted_iota(jnp.int32, (WORD, docs), 0)
    )
    spread = [
        jnp.where((jnp.broadcast_to(line, (WORD, docs)) & place) != 0, -1.0, 1.0) for line in words
    ]
    return jnp.concatenate(spread, axis=0)


def row_slot(layout, step, other):
    across, along, distances = layout
    me = lax.axis_index("blk")
    core, chip = me & 1, me >> 1
    shift = across.bit_length() - 1
    from_z = ((chip >> shift) - step * (1 - 2 * core)) & (along - 1)
    from_chip = (from_z << shift) | ((chip & (across - 1)) ^ other)
    apart = chip ^ from_chip
    slot = 0
    for place, distance in enumerate(distances):
        slot = slot | (((apart >> (distance.bit_length() - 1)) & 1) << place)
    return slot


def gradient_kernel(layout, owners, sources, fresh, rows_ref, *refs):
    blocks = len(owners)
    w_refs, refs = refs[:blocks], refs[blocks:]
    doc_refs, refs = refs[: len(sources)], refs[len(sources) :]
    old_refs, new_refs = refs[:-blocks], refs[-blocks:]
    height = w_refs[0].shape[0]
    me = lax.axis_index("blk")
    docs = jnp.concatenate([ref[...] for ref in doc_refs], axis=0)
    weights = jnp.concatenate([ref[...] for ref in w_refs], axis=0)
    rows = jnp.concatenate(
        [rows_ref[row_slot(layout, *source)] for source in sources], axis=1
    ).astype(jnp.int32)
    halved = lax.dot_general(
        weights, docs, (((1,), (1,)), ((), ())), preferred_element_type=jnp.float32
    )
    signs = jnp.concatenate(
        [signs_of(rows, (me ^ owner) * height, height) for owner in owners], axis=0
    )
    signal = (jnp.tanh(halved) + signs).astype(jnp.bfloat16)
    part = jnp.dot(signal, docs, preferred_element_type=jnp.float32)
    for block in range(blocks):
        piece = part[block * height : (block + 1) * height]
        new_refs[block][...] = piece if fresh else old_refs[block][...] + piece


def add_gradient(layout, owners, sources, rows, weights, docs, sums):
    blocks = len(weights)
    height, width = weights[0].shape
    vmem = pl.BlockSpec(memory_space=pltpu.VMEM)
    sums = list(sums)
    inputs = [rows, *weights, *docs, *sums]
    first_sum = len(inputs) - len(sums)
    return pl.pallas_call(
        functools.partial(gradient_kernel, layout, owners, sources, not sums),
        in_specs=[vmem] * len(inputs),
        out_specs=[vmem] * blocks,
        out_shape=[jax.ShapeDtypeStruct((height, width), jnp.float32)] * blocks,
        input_output_aliases={first_sum + i: i for i in range(len(sums))},
        compiler_params=pltpu.CompilerParams(vmem_limit_bytes=VMEM_LIMIT),
        cost_estimate=SMALL,
        name="gradient",
    )(*inputs)


def adam_step(weights, first_moment, second_moment, gradient):
    new_first = beta_one * first_moment + (1.0 - beta_one) * gradient
    new_second = beta_two * second_moment + (1.0 - beta_two) * gradient * gradient
    update = new_first / correct_one / (jnp.sqrt(new_second / correct_two) + adam_eps)
    new_weights = weights - learn_rate * (update + decay_rate * weights)
    return (new_weights, new_first, new_second)


def over_cores(pairs):
    return [(2 * a + core, 2 * b + core) for a, b in pairs for core in range(2)]


together = lax.optimization_barrier


def per_device(
    blocks,
    across,
    embeddings,
    pos_ids,
    pos_count,
    label_slot,
    weights,
    first_moment,
    second_moment,
):
    chips = blocks // 2
    along = chips // across
    distances = [1] * (across - 1)
    distances += [chips >> (i + 1) for i in range(along.bit_length() - 1)]
    layout = (across, along, tuple(distances))

    def send(value, pairs):
        return lax.ppermute(value, "blk", pairs)

    ring = [(i, (i + (2 - 4 * (i & 1)) * across) % blocks) for i in range(blocks)]
    back = [(b, a) for a, b in ring]
    beside = over_cores([(c, c ^ 1) for c in range(chips)])
    swap = [(i, i ^ 1) for i in range(blocks)]
    stages = [over_cores([(c, c ^ distance) for c in range(chips)]) for distance in distances]

    coming = send(embeddings, ring)
    if across == 2:
        neighbour = send(embeddings, beside)
    rows = lookup_rows(label_slot, pos_ids, pos_count)[None]
    coming_rows = [send(rows, stages[0])]
    mine = weights.astype(jnp.bfloat16) * 0.5
    other = send(mine, swap)
    sums = ()

    def work(source, docs):
        nonlocal sums
        sums = add_gradient(layout, (0, 1), [source], rows, [mine, other], [docs], sums)

    def gather_rows():
        nonlocal rows, sums
        stage = len(coming_rows)
        if coming_rows[-1] is not None:
            got, sums = together((coming_rows[-1], sums))
            rows = jnp.concatenate([rows, got], axis=0)
            coming_rows.append(send(rows, stages[stage]) if stage < len(stages) else None)

    gather_rows()
    waiting = [((0, 0), embeddings)]
    arrived = [coming, sums, rows]
    if across == 2:
        arrived.append(neighbour)
    for step in range(1, along):
        arrived = together(tuple(arrived))
        block, sums, rows = arrived[:3]
        if across == 2:
            waiting.append(((step - 1, 1), arrived[3]))
        if step == along - 1:
            break
        coming = send(block, ring)
        arrived = [coming, None, None]
        if across == 2:
            arrived.append(send(block, beside))
            if step == 1:
                far = ((along - 1, 1), send(waiting[-1][1], back))
        for source, docs in waiting:
            work(source, docs)
            gather_rows()
        waiting = [((step, 0), block)]
        if across == 2 and step == 2:
            waiting.append(far)
        arrived[1:3] = sums, rows
    waiting.append(((along - 1, 0), block))
    while coming_rows[-1] is not None:
        gather_rows()
    while len(waiting) > 1:
        work(*waiting.pop(0))
    source, docs = waiting.pop()
    (other_sum,) = add_gradient(layout, (1,), [source], rows, [other], [docs], sums[1:])
    got = send(other_sum, swap)
    (mine_sum,) = add_gradient(layout, (0,), [source], rows, [mine], [docs], sums[:1])
    return adam_step(weights, first_moment, second_moment, 0.5 * (mine_sum + got))


def solution(mesh):
    in_specs = (
        P(("groups", "blk"), None),
        P(("groups", "blk"), None),
        P(("groups", "blk")),
        P(),
        P("blk", None),
        P("blk", None),
        P("blk", None),
    )
    out_specs = (P(("groups", "blk"), None), P(("groups", "blk"), None), P(("groups", "blk"), None))
    return jax.shard_map(
        functools.partial(per_device, mesh.shape["blk"], 4 // mesh.shape["groups"]),
        mesh=mesh,
        in_specs=in_specs,
        out_specs=out_specs,
        check_vma=False,
    )
```

time: 55.5 us -> 56 us (level)
  waiting for transfers between devices: 8.44 us -> 24.5 us
  starting transfers between devices: 25.5 us -> 16.6 us
  Pallas kernels: 15.8 us -> 10.2 us
  local copies, waits for them, and re-layouts: 1.48 us -> 0.03 us
  other arithmetic: 3.07 us -> 3.71 us
    ppermute x18 -> x12, waiting for transfers between devices: 8.44 us -> 24.5 us  [send(): return lax.ppermute(value, 'blk', pairs)]
    ppermute x18 -> x12, starting transfers between devices: 25.5 us -> 16.6 us  [send(): return lax.ppermute(value, 'blk', pairs)]
    pallas_call x9, Pallas kernels: 13.2 us -> 8.37 us  [add_gradient(): pl.pallas_call(functools.partial(gradient_kernel, layout, owners, sources...]
    pallas_call x1, Pallas kernels: 2.6 us -> 1.81 us  [lookup_rows(): pl.pallas_call(lookup_kernel, out_shape=jax.ShapeDtypeStruct((slots, docs...]
    unnamed x12 -> x9, local copies, waits for them, and re-layouts: 0.74 us -> 0.03 us
    concatenate x3 -> x2, other arithmetic: 0.02 us -> 0.73 us  [gather_rows(): rows = jnp.concatenate([rows, got], axis=0)]
    squeeze x1 -> x0, local copies, waits for them, and re-layouts: 0.69 us -> none  [per_device(): lax.dynamic_index_in_dim(table, lax.axis_index('blk'), keepdims=False)]
  transfers between devices with their start and end apart: 18 -> 12, of which waited for: 4 -> 7; matrix products, arithmetic and copies ran while one was open for 1% -> 3% of each run, Pallas kernels for 27% -> 13%
where the time goes in v4:
time: 56 us; the launch traced here: 55.7 us
  waiting for transfers between devices  24.5 us (44%)
  starting transfers between devices  16.6 us (30%)
  Pallas kernels  10.2 us (18%)
  other arithmetic  3.71 us (7%)
  between operations  0.76 us (1%)
    ppermute x12, waiting for transfers between devices, send(): return lax.ppermute(value, 'blk', pairs)  24.5 us
    ppermute x12, starting transfers between devices, send(): return lax.ppermute(value, 'blk', pairs)  16.6 us
    pallas_call x9, Pallas kernels, add_gradient(): pl.pallas_call(functools.partial(gradient_kernel, layout, owners, sources...  8.37 us
    pallas_call x1, Pallas kernels, lookup_rows(): pl.pallas_call(lookup_kernel, out_shape=jax.ShapeDtypeStruct((slots, docs...  1.81 us
    sub x1, other arithmetic, adam_step(): new_weights = weights - learn_rate * (update + decay_rate * weights)  1.81 us
    mul x1, other arithmetic, per_device(): mine = weights.astype(jnp.bfloat16) * 0.5  1.18 us
  transfers between devices with their start and end apart: 12, of which 7 were waited for; matrix products, arithmetic and copies ran while one was open for 3% of the time, Pallas kernels for 13%

profile of v4, /device:TPU:0, one launch (start us, length us, event | category | flops | bytes accessed | tf_op | source)
XLA Modules:
  0.0 55.7 jit_solution(15256131476235294046)
XLA Ops:
  0.6 3.1 %collective-permute-start = (bf16[256,768]{1,0:T(8,128)(2,1)}, bf16[256,768]{1,0:T(8,128)(2,1)S(1)}, u32[]{:S(2)}, u32[]{:S(2)}) collective-permute-start(bf16[256,768]{1,0:T(8,128)(2,1)} %refs_2_.1), channel_id=1, source_target_pairs={{0,4},{1,13},{2,6},{3,15},{4,8},{5,1},{6,10},{7,3},{8,12},{9,5},{1... | collective-permute-start | bytes 1179656 | tf_op jit(solution)/shard_map/ppermute | solution.py:170
  3.7 1.5 %collective-permute-start.2 = (bf16[256,768]{1,0:T(8,128)(2,1)}, bf16[256,768]{1,0:T(8,128)(2,1)S(1)}, u32[]{:S(2)}, u32[]{:S(2)}) collective-permute-start(bf16[256,768]{1,0:T(8,128)(2,1)} %refs_2_.1), channel_id=1, source_target_pairs={{0,2},{1,3},{2,0},{3,1},{4,6},{5,7},{6,4},{7,5},{8,10},{9,11},{10,... | collective-permute-start | bytes 1179656 | tf_op jit(solution)/shard_map/ppermute | solution.py:170
  5.2 1.2 %convert_multiply_fusion.refs_0_ = bf16[256,768]{1,0:T(8,128)(2,1)S(1)} fusion(f32[256,768]{1,0:T(8,128)} %param.11), kind=kLoop, calls=%fused_computation.3 | loop fusion | flops 393216 | bytes 1179648 | tf_op jit(solution)/shard_map/mul | solution.py:183
  6.4 1.4 %collective-permute-start.5 = (bf16[256,768]{1,0:T(8,128)(2,1)S(1)}, bf16[256,768]{1,0:T(8,128)(2,1)S(1)}, u32[]{:S(2)}, u32[]{:S(2)}) collective-permute-start(bf16[256,768]{1,0:T(8,128)(2,1)S(1)} %convert_multiply_fusion.refs_0_), channel_id=1, source_target_pairs={{0,1},{1,0},{2,3},{3,2},{4,5},{5,4},{6,7},{7,6},{8,9},{9,8},{10,11... | collective-permute-start | bytes 1179656 | tf_op jit(solution)/shard_map/ppermute | solution.py:170
  7.8 1.8 %lookup.1 = s16[32,256]{1,0:T(8,128)(2,1)} custom-call(s32[32,256]{1,0:T(8,128)} %bitcast.6, s32[1,256]{1,0:T(1,128)} %bitcast.8, s32[32,128]{1,0:T(8,128)} %bitcast.7), custom_call_target="tpu_custom_call" | custom-call | flops 1 | bytes 1 | tf_op jit(solution)/shard_map/lookup/pallas_call | solution.py:54
  9.6 0.5 collective-permute-start.1
  10.1 5.6 %collective-permute-done.1 = s16[1,32,256]{2,1,0:T(8,128)(2,1)S(1)} collective-permute-done((s16[1,32,256]{2,1,0:T(8,128)(2,1)}, s16[1,32,256]{2,1,0:T(8,128)(2,1)S(1)}, u32[]{:S(2)}, u32[]{:S(2)}) %collective-permute-start.1) | collective-permute-done | bytes 16416 | tf_op jit(solution)/shard_map/ppermute | solution.py:170
  15.7 0.7 %pad_add_fusion.1.rows_ref = s16[2,32,256]{2,1,0:T(8,128)(2,1)S(1)} fusion(s16[1,32,256]{2,1,0:T(8,128)(2,1)S(1)} %collective-permute-done.1, s16[1,32,256]{2,1,0:T(8,128)(2,1)} %bitcast.5), kind=kLoop, calls=%fused_computation.5 | loop fusion | flops 16384 | bytes 65536 | tf_op jit(solution)/shard_map/concatenate | solution.py:196
  16.4 0.6 %collective-permute-start.4 = (s16[2,32,256]{2,1,0:T(8,128)(2,1)S(1)}, s16[2,32,256]{2,1,0:T(8,128)(2,1)S(1)}, u32[]{:S(2)}, u32[]{:S(2)}) collective-permute-start(s16[2,32,256]{2,1,0:T(8,128)(2,1)S(1)} %pad_add_fusion.1.rows_ref), channel_id=1, source_target_pairs={{0,8},{1,9},{2,10},{3,11},{4,12},{5,13},{6,14},{7,15},{8,0},{9,1},... | collective-permute-start | bytes 98312 | tf_op jit(solution)/shard_map/ppermute | solution.py:170
  17.0 1.6 %collective-permute-start.3 = (bf16[256,768]{1,0:T(8,128)(2,1)S(1)}, bf16[256,768]{1,0:T(8,128)(2,1)S(1)}, u32[]{:S(2)}, u32[]{:S(2)}) collective-permute-start(bf16[256,768]{1,0:T(8,128)(2,1)S(1)} %collective-permute-done.refs_2_), channel_id=1, source_target_pairs={{0,4},{1,13},{2,6},{3,15},{4,8},{5,1},{6,10},{7,3},{8,12},{9,5},{1... | collective-permute-start | bytes 1179656 | tf_op jit(solution)/shard_map/ppermute | solution.py:170
  18.6 1.5 %collective-permute-start.7 = (bf16[256,768]{1,0:T(8,128)(2,1)S(1)}, bf16[256,768]{1,0:T(8,128)(2,1)S(1)}, u32[]{:S(2)}, u32[]{:S(2)}) collective-permute-start(bf16[256,768]{1,0:T(8,128)(2,1)S(1)} %collective-permute-done.refs_2_), channel_id=1, source_target_pairs={{0,2},{1,3},{2,0},{3,1},{4,6},{5,7},{6,4},{7,5},{8,10},{9,11},{10,... | collective-permute-start | bytes 1179656 | tf_op jit(solution)/shard_map/ppermute | solution.py:170
  20.1 1.0 %gradient.9 = (f32[256,768]{1,0:T(8,128)S(1)}, f32[256,768]{1,0:T(8,128)S(1)}) custom-call(s16[2,32,256]{2,1,0:T(8,128)(2,1)S(1)} %pad_add_fusion.1.rows_ref, bf16[256,768]{1,0:T(8,128)(2,1)S(1)} %convert_multiply_fusion.refs_0_, bf16[256,768]{1,0:T(8,128)(2,1)S(1)} %collective-permute-done.5.refs_1_.refs_0_, bf16[256,768]{1,0:T(8,128)(2,1)S(1)} %copy-done), custom_call_target="tpu_custom_call" | custom-call | flops 1 | bytes 1 | tf_op jit(solution)/shard_map/gradient/pallas_call | solution.py:125
  21.1 0.4 collective-permute-done.4
  21.6 1.0 %collective-permute-start.6 = (s16[4,32,256]{2,1,0:T(8,128)(2,1)S(1)}, s16[4,32,256]{2,1,0:T(8,128)(2,1)S(1)}, u32[]{:S(2)}, u32[]{:S(2)}) collective-permute-start(s16[4,32,256]{2,1,0:T(8,128)(2,1)S(1)} %constant_dynamic-update-slice_fusion.rows_ref), channel_id=1, source_target_pairs={{0,4},{1,5},{2,6},{3,7},{4,0},{5,1},{6,2},{7,3},{8,12},{9,13},{10,... | collective-permute-start | bytes 196616 | tf_op jit(solution)/shard_map/ppermute | solution.py:170
  22.6 1.0 %gradient.10 = (f32[256,768]{1,0:T(8,128)S(1)}, f32[256,768]{1,0:T(8,128)S(1)}) custom-call(s16[4,32,256]{2,1,0:T(8,128)(2,1)S(1)} %constant_dynamic-update-slice_fusion.rows_ref, bf16[256,768]{1,0:T(8,128)(2,1)S(1)} %convert_multiply_fusion.refs_0_, ...), custom_call_target="tpu_custom_call", output_to_operand_aliasing={{0}: (4, {}), {1}: (5, {})} | custom-call | flops 1 | bytes 1 | tf_op jit(solution)/shard_map/gradient/pallas_call | solution.py:125
  23.6 4.5 %collective-permute-done.6 = s16[4,32,256]{2,1,0:T(8,128)(2,1)S(1)} collective-permute-done((s16[4,32,256]{2,1,0:T(8,128)(2,1)S(1)}, s16[4,32,256]{2,1,0:T(8,128)(2,1)S(1)}, u32[]{:S(2)}, u32[]{:S(2)}) %collective-permute-start.6) | collective-permute-done | bytes 65568 | tf_op jit(solution)/shard_map/ppermute | solution.py:170
  28.1 2.5 %collective-permute-done.3.refs_2_ = bf16[256,768]{1,0:T(8,128)(2,1)S(1)} collective-permute-done((bf16[256,768]{1,0:T(8,128)(2,1)S(1)}, bf16[256,768]{1,0:T(8,128)(2,1)S(1)}, u32[]{:S(2)}, u32[]{:S(2)}) %collective-permute-start.3) | collective-permute-done | bytes 393248 | tf_op jit(solution)/shard_map/ppermute | solution.py:170
  30.6 1.5 %collective-permute-start.9 = (bf16[256,768]{1,0:T(8,128)(2,1)S(1)}, bf16[256,768]{1,0:T(8,128)(2,1)S(1)}, u32[]{:S(2)}, u32[]{:S(2)}) collective-permute-start(bf16[256,768]{1,0:T(8,128)(2,1)S(1)} %collective-permute-done.3.refs_2_), channel_id=1, source_target_pairs={{0,2},{1,3},{2,0},{3,1},{4,6},{5,7},{6,4},{7,5},{8,10},{9,11},{10,... | collective-permute-start | bytes 1179656 | tf_op jit(solution)/shard_map/ppermute | solution.py:170
  32.1 3.8 %collective-permute-start.10 = (bf16[256,768]{1,0:T(8,128)(2,1)S(1)}, bf16[256,768]{1,0:T(8,128)(2,1)S(1)}, u32[]{:S(2)}, u32[]{:S(2)}) collective-permute-start(bf16[256,768]{1,0:T(8,128)(2,1)S(1)} %collective-permute-done.2.refs_2_), channel_id=1, source_target_pairs={{4,0},{13,1},{6,2},{15,3},{8,4},{1,5},{10,6},{3,7},{12,8},{5,9},{1... | collective-permute-start | bytes 1179656 | tf_op jit(solution)/shard_map/ppermute | solution.py:170
  36.0 1.0 %gradient.11 = (f32[256,768]{1,0:T(8,128)S(1)}, f32[256,768]{1,0:T(8,128)S(1)}) custom-call(s16[8,32,256]{2,1,0:T(8,128)(2,1)S(1)} %pad_add_fusion.rows_ref, bf16[256,768]{1,0:T(8,128)(2,1)S(1)} %convert_multiply_fusion.refs_0_, bf16[256,768]{1,0:T(8,128)(2,1)S(1)} %collective-permute-done.5.refs_1_.refs_0_, ...), custom_call_target="tpu_custom_call", output_to_operand_aliasing={{0}: (4, {}), {1}: (5, {})} | custom-call | flops 1 | bytes 1 | tf_op jit(solution)/shard_map/gradient/pallas_call | solution.py:125
  37.0 1.0 %gradient.12 = (f32[256,768]{1,0:T(8,128)S(1)}, f32[256,768]{1,0:T(8,128)S(1)}) custom-call(s16[8,32,256]{2,1,0:T(8,128)(2,1)S(1)} %pad_add_fusion.rows_ref, bf16[256,768]{1,0:T(8,128)(2,1)S(1)} %convert_multiply_fusion.refs_0_, bf16[256,768]{1,0:T(8,128)(2,1)S(1)} %collective-permute-done.5.refs_1_.refs_0_, ...), custom_call_target="tpu_custom_call", output_to_operand_aliasing={{0}: (4, {}), {1}: (5, {})} | custom-call | flops 1 | bytes 1 | tf_op jit(solution)/shard_map/gradient/pallas_call | solution.py:125
  38.0 6.6 %collective-permute-done.8.refs_1_ = bf16[256,768]{1,0:T(8,128)(2,1)S(1)} collective-permute-done((bf16[256,768]{1,0:T(8,128)(2,1)S(1)}, bf16[256,768]{1,0:T(8,128)(2,1)S(1)}, u32[]{:S(2)}, u32[]{:S(2)}) %collective-permute-start.8) | collective-permute-done | bytes 393248 | tf_op jit(solution)/shard_map/ppermute | solution.py:170
  44.6 1.0 %gradient.13 = (f32[256,768]{1,0:T(8,128)S(1)}, f32[256,768]{1,0:T(8,128)S(1)}) custom-call(s16[8,32,256]{2,1,0:T(8,128)(2,1)S(1)} %pad_add_fusion.rows_ref, bf16[256,768]{1,0:T(8,128)(2,1)S(1)} %convert_multiply_fusion.refs_0_, bf16[256,768]{1,0:T(8,128)(2,1)S(1)} %collective-permute-done.5.refs_1_.refs_0_, ...), custom_call_target="tpu_custom_call", output_to_operand_aliasing={{0}: (4, {}), {1}: (5, {})} | custom-call | flops 1 | bytes 1 | tf_op jit(solution)/shard_map/gradient/pallas_call | solution.py:125
  45.7 3.2 %collective-permute-done.10.refs_2_ = bf16[256,768]{1,0:T(8,128)(2,1)S(1)} collective-permute-done((bf16[256,768]{1,0:T(8,128)(2,1)S(1)}, bf16[256,768]{1,0:T(8,128)(2,1)S(1)}, u32[]{:S(2)}, u32[]{:S(2)}) %collective-permute-start.10) | collective-permute-done | bytes 393248 | tf_op jit(solution)/shard_map/ppermute | solution.py:170
  48.8 1.0 %gradient.14 = (f32[256,768]{1,0:T(8,128)S(1)}, f32[256,768]{1,0:T(8,128)S(1)}) custom-call(s16[8,32,256]{2,1,0:T(8,128)(2,1)S(1)} %pad_add_fusion.rows_ref, bf16[256,768]{1,0:T(8,128)(2,1)S(1)} %convert_multiply_fusion.refs_0_, bf16[256,768]{1,0:T(8,128)(2,1)S(1)} %collective-permute-done.5.refs_1_.refs_0_, ...), custom_call_target="tpu_custom_call", output_to_operand_aliasing={{0}: (4, {}), {1}: (5, {})} | custom-call | flops 1 | bytes 1 | tf_op jit(solution)/shard_map/gradient/pallas_call | solution.py:125
  49.9 1.0 %gradient.15 = (f32[256,768]{1,0:T(8,128)S(1)}, f32[256,768]{1,0:T(8,128)S(1)}) custom-call(s16[8,32,256]{2,1,0:T(8,128)(2,1)S(1)} %pad_add_fusion.rows_ref, bf16[256,768]{1,0:T(8,128)(2,1)S(1)} %convert_multiply_fusion.refs_0_, bf16[256,768]{1,0:T(8,128)(2,1)S(1)} %collective-permute-done.5.refs_1_.refs_0_, ...), custom_call_target="tpu_custom_call", output_to_operand_aliasing={{0}: (4, {}), {1}: (5, {})} | custom-call | flops 1 | bytes 1 | tf_op jit(solution)/shard_map/gradient/pallas_call | solution.py:125
  50.9 0.7 %gradient.17 = f32[256,768]{1,0:T(8,128)S(1)} custom-call(s16[8,32,256]{2,1,0:T(8,128)(2,1)S(1)} %pad_add_fusion.rows_ref, bf16[256,768]{1,0:T(8,128)(2,1)S(1)} %collective-permute-done.5.refs_1_.refs_0_, bf16[256,768]{1,0:T(8,128)(2,1)S(1)} %collective-permute-done.8.refs_1_, f32[256,768]{1,0:T(8,128)S(1)} %get-tuple-element.68.refs_2_), custom_call_target="tpu_custom_call", output_to_operand_aliasing={{}: (3, {})} | custom-call | flops 1 | bytes 1 | tf_op jit(solution)/shard_map/gradient/pallas_call | solution.py:125
  51.6 0.1 collective-permute-start.11
  51.6 0.0 copy-start.2
  51.7 0.7 %gradient.16 = f32[256,768]{1,0:T(8,128)S(1)} custom-call(s16[8,32,256]{2,1,0:T(8,128)(2,1)S(1)} %pad_add_fusion.rows_ref, bf16[256,768]{1,0:T(8,128)(2,1)S(1)} %convert_multiply_fusion.refs_0_, bf16[256,768]{1,0:T(8,128)(2,1)S(1)} %collective-permute-done.8.refs_1_, f32[256,768]{1,0:T(8,128)S(1)} %get-tuple-element.67.refs_2_), custom_call_target="tpu_custom_call", output_to_operand_aliasing={{}: (3, {})} | custom-call | flops 1 | bytes 1 | tf_op jit(solution)/shard_map/gradient/pallas_call | solution.py:125
  52.3 1.6 %collective-permute-done.11 = f32[256,768]{1,0:T(8,128)S(1)} collective-permute-done((f32[256,768]{1,0:T(8,128)S(1)}, f32[256,768]{1,0:T(8,128)S(1)}, u32[]{:S(2)}, u32[]{:S(2)}) %collective-permute-start.11) | collective-permute-done | bytes 786464 | tf_op jit(solution)/shard_map/ppermute | solution.py:170
  53.9 1.8 %multiply_subtract_fusion = (f32[256,768]{1,0:T(8,128)}, f32[256,768]{1,0:T(8,128)}, f32[256,768]{1,0:T(8,128)}) fusion(f32[256,768]{1,0:T(8,128)S(1)} %copy-done.1, f32[256,768]{1,0:T(8,128)S(1)} %gradient.16, f32[256,768]{1,0:T(8,128)S(1)} %collective-permute-done.11, f32[256,768]{1,0:T(8,128)S(1)} %copy-done.2, f32[256,768]{1,0:T(8,128)S(1)} %copy-done.3), kind=kLoop, calls=%fused_computation | loop fusion | flops 3342336 | bytes 6291456 | tf_op jit(solution)/shard_map/sub | solution.py:141
  (16 shorter events, 0.1 us)
Async XLA Ops:
  0.6 19.5 %copy-start = (bf16[256,768]{1,0:T(8,128)(2,1)S(1)}, bf16[256,768]{1,0:T(8,128)(2,1)}, u32[]{:S(2)}) copy-start(bf16[256,768]{1,0:T(8,128)(2,1)} %refs_2_.1) | copy-start | bytes 1179652
  0.6 16.4 %collective-permute-start = (bf16[256,768]{1,0:T(8,128)(2,1)}, bf16[256,768]{1,0:T(8,128)(2,1)S(1)}, u32[]{:S(2)}, u32[]{:S(2)}) collective-permute-start(bf16[256,768]{1,0:T(8,128)(2,1)} %refs_2_.1), channel_id=1, source_target_pairs={{0,4},{1,13},{2,6},{3,15},{4,8},{5,1},{6,10},{7,3},{8,12},{9,5},{1... | collective-permute-start | bytes 1179656 | tf_op jit(solution)/shard_map/ppermute | solution.py:170
  3.7 13.3 %collective-permute-start.2 = (bf16[256,768]{1,0:T(8,128)(2,1)}, bf16[256,768]{1,0:T(8,128)(2,1)S(1)}, u32[]{:S(2)}, u32[]{:S(2)}) collective-permute-start(bf16[256,768]{1,0:T(8,128)(2,1)} %refs_2_.1), channel_id=1, source_target_pairs={{0,2},{1,3},{2,0},{3,1},{4,6},{5,7},{6,4},{7,5},{8,10},{9,11},{10,... | collective-permute-start | bytes 1179656 | tf_op jit(solution)/shard_map/ppermute | solution.py:170
  6.4 13.7 %collective-permute-start.5 = (bf16[256,768]{1,0:T(8,128)(2,1)S(1)}, bf16[256,768]{1,0:T(8,128)(2,1)S(1)}, u32[]{:S(2)}, u32[]{:S(2)}) collective-permute-start(bf16[256,768]{1,0:T(8,128)(2,1)S(1)} %convert_multiply_fusion.refs_0_), channel_id=1, source_target_pairs={{0,1},{1,0},{2,3},{3,2},{4,5},{5,4},{6,7},{7,6},{8,9},{9,8},{10,11... | collective-permute-start | bytes 1179656 | tf_op jit(solution)/shard_map/ppermute | solution.py:170
  9.6 6.1 %collective-permute-start.1 = (s16[1,32,256]{2,1,0:T(8,128)(2,1)}, s16[1,32,256]{2,1,0:T(8,128)(2,1)S(1)}, u32[]{:S(2)}, u32[]{:S(2)}) collective-permute-start(s16[1,32,256]{2,1,0:T(8,128)(2,1)} %bitcast.4), channel_id=1, source_target_pairs={{0,2},{1,3},{2,0},{3,1},{4,6},{5,7},{6,4},{7,5},{8,10},{9,11},{10,... | collective-permute-start | bytes 49160 | tf_op jit(solution)/shard_map/ppermute | solution.py:170
  16.4 5.1 %collective-permute-start.4 = (s16[2,32,256]{2,1,0:T(8,128)(2,1)S(1)}, s16[2,32,256]{2,1,0:T(8,128)(2,1)S(1)}, u32[]{:S(2)}, u32[]{:S(2)}) collective-permute-start(s16[2,32,256]{2,1,0:T(8,128)(2,1)S(1)} %pad_add_fusion.1.rows_ref), channel_id=1, source_target_pairs={{0,8},{1,9},{2,10},{3,11},{4,12},{5,13},{6,14},{7,15},{8,0},{9,1},... | collective-permute-start | bytes 98312 | tf_op jit(solution)/shard_map/ppermute | solution.py:170
  17.0 13.6 %collective-permute-start.3 = (bf16[256,768]{1,0:T(8,128)(2,1)S(1)}, bf16[256,768]{1,0:T(8,128)(2,1)S(1)}, u32[]{:S(2)}, u32[]{:S(2)}) collective-permute-start(bf16[256,768]{1,0:T(8,128)(2,1)S(1)} %collective-permute-done.refs_2_), channel_id=1, source_target_pairs={{0,4},{1,13},{2,6},{3,15},{4,8},{5,1},{6,10},{7,3},{8,12},{9,5},{1... | collective-permute-start | bytes 1179656 | tf_op jit(solution)/shard_map/ppermute | solution.py:170
  18.6 12.0 %collective-permute-start.7 = (bf16[256,768]{1,0:T(8,128)(2,1)S(1)}, bf16[256,768]{1,0:T(8,128)(2,1)S(1)}, u32[]{:S(2)}, u32[]{:S(2)}) collective-permute-start(bf16[256,768]{1,0:T(8,128)(2,1)S(1)} %collective-permute-done.refs_2_), channel_id=1, source_target_pairs={{0,2},{1,3},{2,0},{3,1},{4,6},{5,7},{6,4},{7,5},{8,10},{9,11},{10,... | collective-permute-start | bytes 1179656 | tf_op jit(solution)/shard_map/ppermute | solution.py:170
  21.6 6.6 %collective-permute-start.6 = (s16[4,32,256]{2,1,0:T(8,128)(2,1)S(1)}, s16[4,32,256]{2,1,0:T(8,128)(2,1)S(1)}, u32[]{:S(2)}, u32[]{:S(2)}) collective-permute-start(s16[4,32,256]{2,1,0:T(8,128)(2,1)S(1)} %constant_dynamic-update-slice_fusion.rows_ref), channel_id=1, source_target_pairs={{0,4},{1,5},{2,6},{3,7},{4,0},{5,1},{6,2},{7,3},{8,12},{9,13},{10,... | collective-permute-start | bytes 196616 | tf_op jit(solution)/shard_map/ppermute | solution.py:170
  30.6 14.0 %collective-permute-start.8 = (bf16[256,768]{1,0:T(8,128)(2,1)S(1)}, bf16[256,768]{1,0:T(8,128)(2,1)S(1)}, u32[]{:S(2)}, u32[]{:S(2)}) collective-permute-start(bf16[256,768]{1,0:T(8,128)(2,1)S(1)} %collective-permute-done.3.refs_2_), channel_id=1, source_target_pairs={{0,4},{1,13},{2,6},{3,15},{4,8},{5,1},{6,10},{7,3},{8,12},{9,5},{1... | collective-permute-start | bytes 1179656 | tf_op jit(solution)/shard_map/ppermute | solution.py:170
  30.6 14.0 %collective-permute-start.9 = (bf16[256,768]{1,0:T(8,128)(2,1)S(1)}, bf16[256,768]{1,0:T(8,128)(2,1)S(1)}, u32[]{:S(2)}, u32[]{:S(2)}) collective-permute-start(bf16[256,768]{1,0:T(8,128)(2,1)S(1)} %collective-permute-done.3.refs_2_), channel_id=1, source_target_pairs={{0,2},{1,3},{2,0},{3,1},{4,6},{5,7},{6,4},{7,5},{8,10},{9,11},{10,... | collective-permute-start | bytes 1179656 | tf_op jit(solution)/shard_map/ppermute | solution.py:170
  32.1 16.7 %collective-permute-start.10 = (bf16[256,768]{1,0:T(8,128)(2,1)S(1)}, bf16[256,768]{1,0:T(8,128)(2,1)S(1)}, u32[]{:S(2)}, u32[]{:S(2)}) collective-permute-start(bf16[256,768]{1,0:T(8,128)(2,1)S(1)} %collective-permute-done.2.refs_2_), channel_id=1, source_target_pairs={{4,0},{13,1},{6,2},{15,3},{8,4},{1,5},{10,6},{3,7},{12,8},{5,9},{1... | collective-permute-start | bytes 1179656 | tf_op jit(solution)/shard_map/ppermute | solution.py:170
  51.6 2.4 %collective-permute-start.11 = (f32[256,768]{1,0:T(8,128)S(1)}, f32[256,768]{1,0:T(8,128)S(1)}, u32[]{:S(2)}, u32[]{:S(2)}) collective-permute-start(f32[256,768]{1,0:T(8,128)S(1)} %gradient.17), channel_id=1, source_target_pairs={{0,1},{1,0},{2,3},{3,2},{4,5},{5,4},{6,7},{7,6},{8,9},{9,8},{10,11... | collective-permute-start | bytes 2359304 | tf_op jit(solution)/shard_map/ppermute | solution.py:170
  51.6 2.3 %copy-start.1 = (f32[256,768]{1,0:T(8,128)S(1)}, f32[256,768]{1,0:T(8,128)}, u32[]{:S(2)}) copy-start(f32[256,768]{1,0:T(8,128)} %param.11) | copy-start | bytes 2359300
  51.6 2.3 %copy-start.2 = (f32[256,768]{1,0:T(8,128)S(1)}, f32[256,768]{1,0:T(8,128)}, u32[]{:S(2)}) copy-start(f32[256,768]{1,0:T(8,128)} %param.12) | copy-start | bytes 2359300
  51.7 2.3 %copy-start.3 = (f32[256,768]{1,0:T(8,128)S(1)}, f32[256,768]{1,0:T(8,128)}, u32[]{:S(2)}) copy-start(f32[256,768]{1,0:T(8,128)} %param.13) | copy-start | bytes 2359300

commit v5 on v4

v5 whole, which is shorter than its diff:
```python
import functools

import jax
import jax.numpy as jnp
from jax import lax
from jax.experimental import pallas as pl
from jax.experimental.pallas import tpu as pltpu
from jax.sharding import PartitionSpec as P

learn_rate = 0.01
beta_one = 0.9
beta_two = 0.95
adam_eps = 1e-08
decay_rate = 0.1
correct_one = 1.0 - 0.9**10
correct_two = 1.0 - 0.95**10

WORD = 32
LANES = 128
VMEM_LIMIT = 32 * 1024 * 1024
LONG = pl.CostEstimate(flops=10**10, bytes_accessed=10**6, transcendentals=0)


def power_of_two(exponent, bits, start, sign):
    value = start
    for bit in range(bits):
        factor = 2.0 ** (sign * (1 << bit))
        value = value * jnp.where(((exponent >> bit) & 1) == 1, factor, 1.0)
    return value


def lookup_kernel(bits, ids_ref, count_ref, table_ref, docs_ref, out_ref):
    slots, docs = ids_ref.shape
    pairs = table_ref.shape[0] // 2
    starts = range(0, docs, LANES)
    ids = [ids_ref[:, start : start + LANES] for start in starts]
    line_of = [(chunk >> 7) & (pairs - 1) for chunk in ids]
    lane_of = [chunk & (LANES - 1) for chunk in ids]

    def pick(t, found):
        both = table_ref[pl.ds(t, 1), :] | (table_ref[pl.ds(t + pairs, 1), :] << 16)
        line = jnp.broadcast_to(both, (slots, LANES))
        return tuple(
            jnp.where(line_of[i] == t, jnp.take_along_axis(line, lane_of[i], axis=1), found[i])
            for i in range(len(ids))
        )

    found = tuple(jnp.zeros((slots, LANES), jnp.int32) for _ in ids)
    if pairs <= 16:
        for t in range(pairs):
            found = pick(t, found)
    else:
        found = lax.fori_loop(0, pairs, pick, found, unroll=8)
    place = lax.broadcasted_iota(jnp.int32, (slots, LANES), 0)
    head = out_ref.shape[0] - slots // 2
    out_ref[:head, :] = docs_ref[:head, :]
    out_ref[head:, :] = jnp.zeros((slots // 2, out_ref.shape[1]), jnp.bfloat16)
    for i, start in enumerate(starts):
        row = jnp.where((ids[i] >> 7) < pairs, found[i], found[i] >> 16) & 0xFFFF
        low = (LANES + (row & (LANES - 1))).astype(jnp.float32)
        code = power_of_two(row >> 7, bits, low * 2.0**-64, 1)
        code = jnp.where(place < count_ref[:, start : start + LANES], code, 0.0)
        code = code.astype(jnp.bfloat16)
        out_ref[head:, start : start + LANES] = code[: slots // 2]
        out_ref[head:, docs + start : docs + start + LANES] = code[slots // 2 :]


def lookup_rows(label_slot, pos_ids, pos_count, embeddings, head):
    docs, slots = pos_ids.shape
    lines = label_slot.shape[0] // LANES
    return pl.pallas_call(
        functools.partial(lookup_kernel, (lines - 1).bit_length()),
        out_shape=jax.ShapeDtypeStruct((head + slots // 2, embeddings.shape[1]), jnp.bfloat16),
        name="lookup",
    )(pos_ids.T, pos_count.reshape(1, docs), label_slot.reshape(lines, LANES), embeddings)


def signs_of(codes, owner, bits, height):
    docs = codes.shape[1]
    scale = power_of_two(owner * (height // LANES), bits, jnp.float32(2.0**64), -1)
    scaled = codes * scale
    place = jnp.left_shift(
        jnp.ones((WORD, docs), jnp.int32), lax.broadcasted_iota(jnp.int32, (WORD, docs), 0)
    )
    spread = []
    for part in range(height // LANES):
        row = jnp.minimum(scaled * 2.0**-part, 512.0).astype(jnp.int32) - LANES
        word = row >> 5
        bit = jnp.left_shift(jnp.ones_like(row), row & (WORD - 1))
        for w in range(LANES // WORD):
            line = jnp.sum(jnp.where(word == w, bit, 0), axis=0, keepdims=True)
            line = jnp.broadcast_to(line, (WORD, docs))
            spread.append(jnp.where((line & place) != 0, -1.0, 1.0))
    return jnp.concatenate(spread, axis=0)


def gradient_kernel(bits, owners, fresh, a_ref, b_ref, *refs):
    blocks = len(owners)
    w_refs, refs = refs[:blocks], refs[blocks:]
    old_refs, new_refs = refs[:-blocks], refs[-blocks:]
    height = w_refs[0].shape[0]
    me = lax.axis_index("blk")
    after = b_ref.shape[0]
    head = a_ref.shape[0]
    slots = 32
    head = head - slots // 2
    docs = jnp.concatenate([a_ref[:head, :], b_ref[...]], axis=0)
    number = head + after
    codes = jnp.concatenate(
        [a_ref[head:, :number], a_ref[head:, number : 2 * number]], axis=0
    ).astype(jnp.float32)
    weights = jnp.concatenate([ref[...] for ref in w_refs], axis=0)
    halved = lax.dot_general(
        weights, docs, (((1,), (1,)), ((), ())), preferred_element_type=jnp.float32
    )
    signs = jnp.concatenate([signs_of(codes, me ^ owner, bits, height) for owner in owners], axis=0)
    signal = (jnp.tanh(halved) + signs).astype(jnp.bfloat16)
    part = jnp.dot(signal, docs, preferred_element_type=jnp.float32)
    for block in range(blocks):
        piece = part[block * height : (block + 1) * height]
        new_refs[block][...] = piece if fresh else old_refs[block][...] + piece


def add_gradient(bits, owners, a, b, weights, sums):
    blocks = len(weights)
    height, width = weights[0].shape
    vmem = pl.BlockSpec(memory_space=pltpu.VMEM)
    sums = list(sums)
    inputs = [a, b, *weights, *sums]
    first_sum = len(inputs) - len(sums)
    return pl.pallas_call(
        functools.partial(gradient_kernel, bits, owners, not sums),
        in_specs=[vmem] * len(inputs),
        out_specs=[vmem] * blocks,
        out_shape=[jax.ShapeDtypeStruct((height, width), jnp.float32)] * blocks,
        input_output_aliases={first_sum + i: i for i in range(len(sums))},
        compiler_params=pltpu.CompilerParams(vmem_limit_bytes=VMEM_LIMIT),
        cost_estimate=LONG,
        name="gradient",
    )(*inputs)


def adam_step(weights, first_moment, second_moment, gradient):
    new_first = beta_one * first_moment + (1.0 - beta_one) * gradient
    new_second = beta_two * second_moment + (1.0 - beta_two) * gradient * gradient
    update = new_first / correct_one / (jnp.sqrt(new_second / correct_two) + adam_eps)
    new_weights = weights - learn_rate * (update + decay_rate * weights)
    return (new_weights, new_first, new_second)


def ring_of(blocks, across):
    path = list(range(0, blocks // 2, across))
    if across == 2:
        path += list(range(1, blocks // 2, 2))[::-1]
    pairs = []
    for here, there in zip(path, path[1:] + path[:1]):
        pairs += [(2 * here, 2 * there), (2 * there + 1, 2 * here + 1)]
    return pairs


together = lax.optimization_barrier


def per_device(
    blocks,
    across,
    embeddings,
    pos_ids,
    pos_count,
    label_slot,
    weights,
    first_moment,
    second_moment,
):
    chips = blocks // 2
    ring = ring_of(blocks, across)
    swap = [(i, i ^ 1) for i in range(blocks)]
    bits = (label_slot.shape[0] // LANES - 1).bit_length()
    head = embeddings.shape[0] // 2

    def send(value, pairs):
        return lax.ppermute(value, "blk", pairs)

    def add(owner, docs, total):
        (total,) = add_gradient(bits, (owner,), *docs, [(mine, other)[owner]], total)
        return (total,)

    b = embeddings[head:]
    next_b = send(b, ring)
    a = lookup_rows(label_slot, pos_ids, pos_count, embeddings, head)
    next_a = send(a, ring)
    mine = weights.astype(jnp.bfloat16) * 0.5
    other = send(mine, swap)
    mine_sum, other_sum = (), ()
    for step in range(1, chips):
        before = (a, b)
        b, before, other_sum = together((next_b, before, other_sum))
        if step < chips - 1:
            next_b = send(b, ring)
        mine_sum = add(0, before, mine_sum)
        a, before, mine_sum = together((next_a, before, mine_sum))
        if step < chips - 1:
            next_a = send(a, ring)
        other_sum = add(1, before, other_sum)
    other_sum = add(1, (a, b), other_sum)
    got = send(other_sum[0], swap)
    mine_sum = add(0, (a, b), mine_sum)
    return adam_step(weights, first_moment, second_moment, 0.5 * (mine_sum[0] + got))


def solution(mesh):
    in_specs = (
        P(("groups", "blk"), None),
        P(("groups", "blk"), None),
        P(("groups", "blk")),
        P(),
        P("blk", None),
        P("blk", None),
        P("blk", None),
    )
    out_specs = (P(("groups", "blk"), None), P(("groups", "blk"), None), P(("groups", "blk"), None))
    return jax.shard_map(
        functools.partial(per_device, mesh.shape["blk"], 4 // mesh.shape["groups"]),
        mesh=mesh,
        in_specs=in_specs,
        out_specs=out_specs,
        check_vma=False,
    )
```

time: 56 us -> 54.4 us (0.971)
  waiting for transfers between devices: 24.5 us -> 13.6 us
  starting transfers between devices: 16.6 us -> 24.2 us
  Pallas kernels: 10.2 us -> 12.7 us
  other arithmetic: 3.71 us -> 1.85 us
  local copies, waits for them, and re-layouts: 0.03 us -> 1.04 us
    ppermute x12 -> x16, waiting for transfers between devices: 24.5 us -> 13.6 us  [send(): return lax.ppermute(value, 'blk', pairs)]
    ppermute x12 -> x16, starting transfers between devices: 16.6 us -> 24.2 us  [send(): return lax.ppermute(value, 'blk', pairs)]
    pallas_call x10 -> x17, Pallas kernels: 10.2 us -> 12.7 us  [the longest x16 10.5 us: add_gradient(): pl.pallas_call(functools.partial(gradient_kernel, bits, owners, not sums)...]
    mul x1, other arithmetic: 1.18 us -> 0.05 us  [per_device(): mine = weights.astype(jnp.bfloat16) * 0.5]
    slice x0 -> x1, local copies, waits for them, and re-layouts: none -> 1.02 us  [per_device(): b = embeddings[head:]]
    concatenate x2 -> x0, other arithmetic: 0.73 us -> none  [gather_rows(): rows = jnp.concatenate([rows, got], axis=0)]
  transfers between devices with their start and end apart: 12 -> 16, of which waited for: 7 -> 8; matrix products, arithmetic and copies ran while one was open for 3% -> 0% of each run, Pallas kernels for 13% -> 21%
where the time goes in v5:
time: 54.4 us; the launch traced here: 54.2 us
  starting transfers between devices  24.2 us (44%)
  waiting for transfers between devices  13.6 us (25%)
  Pallas kernels  12.7 us (23%)
  other arithmetic  1.85 us (3%)
  local copies, waits for them, and re-layouts  1.04 us (2%)
  between operations  0.87 us (2%)
    ppermute x16, starting transfers between devices, send(): return lax.ppermute(value, 'blk', pairs)  24.2 us
    ppermute x16, waiting for transfers between devices, send(): return lax.ppermute(value, 'blk', pairs)  13.6 us
    pallas_call x16, Pallas kernels, add_gradient(): pl.pallas_call(functools.partial(gradient_kernel, bits, owners, not sums)...  10.5 us
    pallas_call x1, Pallas kernels, lookup_rows(): pl.pallas_call(functools.partial(lookup_kernel, (lines - 1).bit_length())...  2.18 us
    sub x1, other arithmetic, adam_step(): new_weights = weights - learn_rate * (update + decay_rate * weights)  1.81 us
  transfers between devices with their start and end apart: 16, of which 8 were waited for; matrix products, arithmetic and copies ran while one was open for 0% of the time, Pallas kernels for 21%

profile of v5, /device:TPU:0, one launch (start us, length us, event | category | flops | bytes accessed | tf_op | source)
XLA Modules:
  0.0 54.2 jit_solution(7678354324739234477)
XLA Ops:
  0.6 1.0 %slice.3.b_ref = bf16[128,768]{1,0:T(8,128)(2,1)S(1)} slice(bf16[256,768]{1,0:T(8,128)(2,1)} %docs_ref.1), slice={[128:256], [0:768]} | slice | bytes 393216 | tf_op jit(solution)/shard_map/slice | solution.py:188
  1.7 3.1 %collective-permute-start.1 = (bf16[128,768]{1,0:T(8,128)(2,1)S(1)}, bf16[128,768]{1,0:T(8,128)(2,1)S(1)}, u32[]{:S(2)}, u32[]{:S(2)}) collective-permute-start(bf16[128,768]{1,0:T(8,128)(2,1)S(1)} %slice.3.b_ref), channel_id=1, source_target_pairs={{0,4},{5,1},{4,8},{9,5},{8,12},{13,9},{12,14},{15,13},{14,10},{11,... | collective-permute-start | bytes 589832 | tf_op jit(solution)/shard_map/ppermute | solution.py:182
  4.7 2.2 %lookup.1.a_ref = bf16[144,768]{1,0:T(8,128)(2,1)} custom-call(s32[32,256]{1,0:T(8,128)} %bitcast.3, s32[1,256]{1,0:T(1,128)} %bitcast.5, s32[32,128]{1,0:T(8,128)} %bitcast.4, bf16[256,768]{1,0:T(8,128)(2,1)} %docs_ref.1), custom_call_target="tpu_custom_call" | custom-call | tf_op jit(solution)/shard_map/lookup/pallas_call | solution.py:71
  6.9 1.6 %collective-permute-start = (bf16[144,768]{1,0:T(8,128)(2,1)}, bf16[144,768]{1,0:T(8,128)(2,1)S(1)}, u32[]{:S(2)}, u32[]{:S(2)}) collective-permute-start(bf16[144,768]{1,0:T(8,128)(2,1)} %lookup.1.a_ref), channel_id=1, source_target_pairs={{0,4},{5,1},{4,8},{9,5},{8,12},{13,9},{12,14},{15,13},{14,10},{11,... | collective-permute-start | bytes 663560 | tf_op jit(solution)/shard_map/ppermute | solution.py:182
  8.6 1.8 %collective-permute-start.3 = (bf16[128,768]{1,0:T(8,128)(2,1)S(1)}, bf16[128,768]{1,0:T(8,128)(2,1)S(1)}, u32[]{:S(2)}, u32[]{:S(2)}) collective-permute-start(bf16[128,768]{1,0:T(8,128)(2,1)S(1)} %collective-permute-done.1.b_ref), channel_id=1, source_target_pairs={{0,4},{5,1},{4,8},{9,5},{8,12},{13,9},{12,14},{15,13},{14,10},{11,... | collective-permute-start | bytes 589832 | tf_op jit(solution)/shard_map/ppermute | solution.py:182
  11.1 2.0 %collective-permute-done.a_ref = bf16[144,768]{1,0:T(8,128)(2,1)S(1)} collective-permute-done((bf16[144,768]{1,0:T(8,128)(2,1)}, bf16[144,768]{1,0:T(8,128)(2,1)S(1)}, u32[]{:S(2)}, u32[]{:S(2)}) %collective-permute-start) | collective-permute-done | bytes 221216 | tf_op jit(solution)/shard_map/ppermute | solution.py:182
  13.1 1.6 %collective-permute-start.2 = (bf16[144,768]{1,0:T(8,128)(2,1)S(1)}, bf16[144,768]{1,0:T(8,128)(2,1)S(1)}, u32[]{:S(2)}, u32[]{:S(2)}) collective-permute-start(bf16[144,768]{1,0:T(8,128)(2,1)S(1)} %collective-permute-done.a_ref), channel_id=1, source_target_pairs={{0,4},{5,1},{4,8},{9,5},{8,12},{13,9},{12,14},{15,13},{14,10},{11,... | collective-permute-start | bytes 663560 | tf_op jit(solution)/shard_map/ppermute | solution.py:182
  15.3 1.6 %collective-permute-start.6 = (bf16[128,768]{1,0:T(8,128)(2,1)S(1)}, bf16[128,768]{1,0:T(8,128)(2,1)S(1)}, u32[]{:S(2)}, u32[]{:S(2)}) collective-permute-start(bf16[128,768]{1,0:T(8,128)(2,1)S(1)} %collective-permute-done.3.b_ref), channel_id=1, source_target_pairs={{0,4},{5,1},{4,8},{9,5},{8,12},{13,9},{12,14},{15,13},{14,10},{11,... | collective-permute-start | bytes 589832 | tf_op jit(solution)/shard_map/ppermute | solution.py:182
  16.9 0.7 %gradient.18.refs_1_ = f32[256,768]{1,0:T(8,128)S(1)} custom-call(bf16[144,768]{1,0:T(8,128)(2,1)S(1)} %collective-permute-done.a_ref, bf16[128,768]{1,0:T(8,128)(2,1)S(1)} %collective-permute-done.1.b_ref, bf16[256,768]{1,0:T(8,128)(2,1)S(1)} %convert_multiply_fusion.refs_0_, f32[256,768]{1,0:T(8,128)S(1)} %gradient.16.refs_1_), custom_call_target="tpu_custom_call", output_to_operand_aliasing={{}: (3, {})} | custom-call | flops 10000000000 | bytes 1000000 | tf_op jit(solution)/shard_map/gradient/pallas_call | solution.py:131
  17.6 1.4 %collective-permute-done.2.a_ref = bf16[144,768]{1,0:T(8,128)(2,1)S(1)} collective-permute-done((bf16[144,768]{1,0:T(8,128)(2,1)S(1)}, bf16[144,768]{1,0:T(8,128)(2,1)S(1)}, u32[]{:S(2)}, u32[]{:S(2)}) %collective-permute-start.2) | collective-permute-done | bytes 221216 | tf_op jit(solution)/shard_map/ppermute | solution.py:182
  19.0 1.6 %collective-permute-start.5 = (bf16[144,768]{1,0:T(8,128)(2,1)S(1)}, bf16[144,768]{1,0:T(8,128)(2,1)S(1)}, u32[]{:S(2)}, u32[]{:S(2)}) collective-permute-start(bf16[144,768]{1,0:T(8,128)(2,1)S(1)} %collective-permute-done.2.a_ref), channel_id=1, source_target_pairs={{0,4},{5,1},{4,8},{9,5},{8,12},{13,9},{12,14},{15,13},{14,10},{11,... | collective-permute-start | bytes 663560 | tf_op jit(solution)/shard_map/ppermute | solution.py:182
  20.6 0.7 %gradient.19.refs_1_ = f32[256,768]{1,0:T(8,128)S(1)} custom-call(bf16[144,768]{1,0:T(8,128)(2,1)S(1)} %collective-permute-done.a_ref, bf16[128,768]{1,0:T(8,128)(2,1)S(1)} %collective-permute-done.1.b_ref, bf16[256,768]{1,0:T(8,128)(2,1)S(1)} %collective-permute-done.4.refs_0_, f32[256,768]{1,0:T(8,128)S(1)} %gradient.17.refs_1_), custom_call_target="tpu_custom_call", output_to_operand_aliasing={{}: (3, {})} | custom-call | flops 10000000000 | bytes 1000000 | tf_op jit(solution)/shard_map/gradient/pallas_call | solution.py:131
  21.2 1.6 %collective-permute-start.8 = (bf16[128,768]{1,0:T(8,128)(2,1)S(1)}, bf16[128,768]{1,0:T(8,128)(2,1)S(1)}, u32[]{:S(2)}, u32[]{:S(2)}) collective-permute-start(bf16[128,768]{1,0:T(8,128)(2,1)S(1)} %collective-permute-done.6.b_ref), channel_id=1, source_target_pairs={{0,4},{5,1},{4,8},{9,5},{8,12},{13,9},{12,14},{15,13},{14,10},{11,... | collective-permute-start | bytes 589832 | tf_op jit(solution)/shard_map/ppermute | solution.py:182
  23.5 1.4 %collective-permute-done.5.a_ref = bf16[144,768]{1,0:T(8,128)(2,1)S(1)} collective-permute-done((bf16[144,768]{1,0:T(8,128)(2,1)S(1)}, bf16[144,768]{1,0:T(8,128)(2,1)S(1)}, u32[]{:S(2)}, u32[]{:S(2)}) %collective-permute-start.5) | collective-permute-done | bytes 221216 | tf_op jit(solution)/shard_map/ppermute | solution.py:182
  24.9 1.6 %collective-permute-start.7 = (bf16[144,768]{1,0:T(8,128)(2,1)S(1)}, bf16[144,768]{1,0:T(8,128)(2,1)S(1)}, u32[]{:S(2)}, u32[]{:S(2)}) collective-permute-start(bf16[144,768]{1,0:T(8,128)(2,1)S(1)} %collective-permute-done.5.a_ref), channel_id=1, source_target_pairs={{0,4},{5,1},{4,8},{9,5},{8,12},{13,9},{12,14},{15,13},{14,10},{11,... | collective-permute-start | bytes 663560 | tf_op jit(solution)/shard_map/ppermute | solution.py:182
  27.2 1.6 %collective-permute-start.10 = (bf16[128,768]{1,0:T(8,128)(2,1)S(1)}, bf16[128,768]{1,0:T(8,128)(2,1)S(1)}, u32[]{:S(2)}, u32[]{:S(2)}) collective-permute-start(bf16[128,768]{1,0:T(8,128)(2,1)S(1)} %collective-permute-done.8.b_ref), channel_id=1, source_target_pairs={{0,4},{5,1},{4,8},{9,5},{8,12},{13,9},{12,14},{15,13},{14,10},{11,... | collective-permute-start | bytes 589832 | tf_op jit(solution)/shard_map/ppermute | solution.py:182
  28.8 0.7 %gradient.22.refs_1_ = f32[256,768]{1,0:T(8,128)S(1)} custom-call(bf16[144,768]{1,0:T(8,128)(2,1)S(1)} %collective-permute-done.5.a_ref, bf16[128,768]{1,0:T(8,128)(2,1)S(1)} %collective-permute-done.6.b_ref, bf16[256,768]{1,0:T(8,128)(2,1)S(1)} %convert_multiply_fusion.refs_0_, f32[256,768]{1,0:T(8,128)S(1)} %gradient.20.refs_1_), custom_call_target="tpu_custom_call", output_to_operand_aliasing={{}: (3, {})} | custom-call | flops 10000000000 | bytes 1000000 | tf_op jit(solution)/shard_map/gradient/pallas_call | solution.py:131
  29.5 1.4 %collective-permute-done.7.a_ref = bf16[144,768]{1,0:T(8,128)(2,1)S(1)} collective-permute-done((bf16[144,768]{1,0:T(8,128)(2,1)S(1)}, bf16[144,768]{1,0:T(8,128)(2,1)S(1)}, u32[]{:S(2)}, u32[]{:S(2)}) %collective-permute-start.7) | collective-permute-done | bytes 221216 | tf_op jit(solution)/shard_map/ppermute | solution.py:182
  30.9 1.6 %collective-permute-start.9 = (bf16[144,768]{1,0:T(8,128)(2,1)S(1)}, bf16[144,768]{1,0:T(8,128)(2,1)S(1)}, u32[]{:S(2)}, u32[]{:S(2)}) collective-permute-start(bf16[144,768]{1,0:T(8,128)(2,1)S(1)} %collective-permute-done.7.a_ref), channel_id=1, source_target_pairs={{0,4},{5,1},{4,8},{9,5},{8,12},{13,9},{12,14},{15,13},{14,10},{11,... | collective-permute-start | bytes 663560 | tf_op jit(solution)/shard_map/ppermute | solution.py:182
  32.4 0.7 %gradient.23.refs_1_ = f32[256,768]{1,0:T(8,128)S(1)} custom-call(bf16[144,768]{1,0:T(8,128)(2,1)S(1)} %collective-permute-done.5.a_ref, bf16[128,768]{1,0:T(8,128)(2,1)S(1)} %collective-permute-done.6.b_ref, bf16[256,768]{1,0:T(8,128)(2,1)S(1)} %collective-permute-done.4.refs_0_, f32[256,768]{1,0:T(8,128)S(1)} %gradient.21.refs_1_), custom_call_target="tpu_custom_call", output_to_operand_aliasing={{}: (3, {})} | custom-call | flops 10000000000 | bytes 1000000 | tf_op jit(solution)/shard_map/gradient/pallas_call | solution.py:131
  33.1 1.6 %collective-permute-start.12 = (bf16[128,768]{1,0:T(8,128)(2,1)S(1)}, bf16[128,768]{1,0:T(8,128)(2,1)S(1)}, u32[]{:S(2)}, u32[]{:S(2)}) collective-permute-start(bf16[128,768]{1,0:T(8,128)(2,1)S(1)} %collective-permute-done.10.b_ref), channel_id=1, source_target_pairs={{0,4},{5,1},{4,8},{9,5},{8,12},{13,9},{12,14},{15,13},{14,10},{11,... | collective-permute-start | bytes 589832 | tf_op jit(solution)/shard_map/ppermute | solution.py:182
  35.4 1.4 %collective-permute-done.9.a_ref = bf16[144,768]{1,0:T(8,128)(2,1)S(1)} collective-permute-done((bf16[144,768]{1,0:T(8,128)(2,1)S(1)}, bf16[144,768]{1,0:T(8,128)(2,1)S(1)}, u32[]{:S(2)}, u32[]{:S(2)}) %collective-permute-start.9) | collective-permute-done | bytes 221216 | tf_op jit(solution)/shard_map/ppermute | solution.py:182
  36.8 1.6 %collective-permute-start.11 = (bf16[144,768]{1,0:T(8,128)(2,1)S(1)}, bf16[144,768]{1,0:T(8,128)(2,1)S(1)}, u32[]{:S(2)}, u32[]{:S(2)}) collective-permute-start(bf16[144,768]{1,0:T(8,128)(2,1)S(1)} %collective-permute-done.9.a_ref), channel_id=1, source_target_pairs={{0,4},{5,1},{4,8},{9,5},{8,12},{13,9},{12,14},{15,13},{14,10},{11,... | collective-permute-start | bytes 663560 | tf_op jit(solution)/shard_map/ppermute | solution.py:182
  39.0 1.6 %collective-permute-start.14 = (bf16[128,768]{1,0:T(8,128)(2,1)S(1)}, bf16[128,768]{1,0:T(8,128)(2,1)S(1)}, u32[]{:S(2)}, u32[]{:S(2)}) collective-permute-start(bf16[128,768]{1,0:T(8,128)(2,1)S(1)} %collective-permute-done.12.b_ref), channel_id=1, source_target_pairs={{0,4},{5,1},{4,8},{9,5},{8,12},{13,9},{12,14},{15,13},{14,10},{11,... | collective-permute-start | bytes 589832 | tf_op jit(solution)/shard_map/ppermute | solution.py:182
  41.3 1.4 %collective-permute-done.11.a_ref = bf16[144,768]{1,0:T(8,128)(2,1)S(1)} collective-permute-done((bf16[144,768]{1,0:T(8,128)(2,1)S(1)}, bf16[144,768]{1,0:T(8,128)(2,1)S(1)}, u32[]{:S(2)}, u32[]{:S(2)}) %collective-permute-start.11) | collective-permute-done | bytes 221216 | tf_op jit(solution)/shard_map/ppermute | solution.py:182
  42.7 1.6 %collective-permute-start.13 = (bf16[144,768]{1,0:T(8,128)(2,1)S(1)}, bf16[144,768]{1,0:T(8,128)(2,1)S(1)}, u32[]{:S(2)}, u32[]{:S(2)}) collective-permute-start(bf16[144,768]{1,0:T(8,128)(2,1)S(1)} %collective-permute-done.11.a_ref), channel_id=1, source_target_pairs={{0,4},{5,1},{4,8},{9,5},{8,12},{13,9},{12,14},{15,13},{14,10},{11,... | collective-permute-start | bytes 663560 | tf_op jit(solution)/shard_map/ppermute | solution.py:182
  45.0 0.7 %gradient.28.refs_1_ = f32[256,768]{1,0:T(8,128)S(1)} custom-call(bf16[144,768]{1,0:T(8,128)(2,1)S(1)} %collective-permute-done.11.a_ref, bf16[128,768]{1,0:T(8,128)(2,1)S(1)} %collective-permute-done.12.b_ref, bf16[256,768]{1,0:T(8,128)(2,1)S(1)} %convert_multiply_fusion.refs_0_, f32[256,768]{1,0:T(8,128)S(1)} %gradient.26.refs_1_), custom_call_target="tpu_custom_call", output_to_operand_aliasing={{}: (3, {})} | custom-call | flops 10000000000 | bytes 1000000 | tf_op jit(solution)/shard_map/gradient/pallas_call | solution.py:131
  45.6 3.0 %collective-permute-done.13.a_ref = bf16[144,768]{1,0:T(8,128)(2,1)S(1)} collective-permute-done((bf16[144,768]{1,0:T(8,128)(2,1)S(1)}, bf16[144,768]{1,0:T(8,128)(2,1)S(1)}, u32[]{:S(2)}, u32[]{:S(2)}) %collective-permute-start.13) | collective-permute-done | bytes 221216 | tf_op jit(solution)/shard_map/ppermute | solution.py:182
  49.3 0.7 %gradient.31 = f32[256,768]{1,0:T(8,128)S(1)} custom-call(bf16[144,768]{1,0:T(8,128)(2,1)S(1)} %collective-permute-done.13.a_ref, bf16[128,768]{1,0:T(8,128)(2,1)S(1)} %collective-permute-done.14.b_ref, bf16[256,768]{1,0:T(8,128)(2,1)S(1)} %collective-permute-done.4.refs_0_, f32[256,768]{1,0:T(8,128)S(1)} %gradient.30.refs_1_), custom_call_target="tpu_custom_call", output_to_operand_aliasing={{}: (3, {})} | custom-call | flops 10000000000 | bytes 1000000 | tf_op jit(solution)/shard_map/gradient/pallas_call | solution.py:131
  50.1 0.7 %gradient.29 = f32[256,768]{1,0:T(8,128)S(1)} custom-call(bf16[144,768]{1,0:T(8,128)(2,1)S(1)} %collective-permute-done.13.a_ref, bf16[128,768]{1,0:T(8,128)(2,1)S(1)} %collective-permute-done.14.b_ref, bf16[256,768]{1,0:T(8,128)(2,1)S(1)} %convert_multiply_fusion.refs_0_, f32[256,768]{1,0:T(8,128)S(1)} %gradient.28.refs_1_), custom_call_target="tpu_custom_call", output_to_operand_aliasing={{}: (3, {})} | custom-call | flops 10000000000 | bytes 1000000 | tf_op jit(solution)/shard_map/gradient/pallas_call | solution.py:131
  50.8 1.6 %collective-permute-done.15 = f32[256,768]{1,0:T(8,128)S(1)} collective-permute-done((f32[256,768]{1,0:T(8,128)S(1)}, f32[256,768]{1,0:T(8,128)S(1)}, u32[]{:S(2)}, u32[]{:S(2)}) %collective-permute-start.15) | collective-permute-done | bytes 786464 | tf_op jit(solution)/shard_map/ppermute | solution.py:182
  52.4 1.8 %multiply_subtract_fusion = (f32[256,768]{1,0:T(8,128)}, f32[256,768]{1,0:T(8,128)}, f32[256,768]{1,0:T(8,128)}) fusion(f32[256,768]{1,0:T(8,128)S(1)} %copy-done.2, f32[256,768]{1,0:T(8,128)S(1)} %gradient.29, f32[256,768]{1,0:T(8,128)S(1)} %collective-permute-done.15, f32[256,768]{1,0:T(8,128)S(1)} %copy-done.3, f32[256,768]{1,0:T(8,128)S(1)} %copy-done.4), kind=kLoop, calls=%fused_computation | loop fusion | flops 3342336 | bytes 6291456 | tf_op jit(solution)/shard_map/sub | solution.py:147
  (30 shorter events, 6.1 us)
Async XLA Ops:
  0.6 7.9 %copy-start.1 = (f32[256,768]{1,0:T(8,128)S(1)}, f32[256,768]{1,0:T(8,128)}, u32[]{:S(2)}) copy-start(f32[256,768]{1,0:T(8,128)} %param.11) | copy-start | bytes 2359300
  1.7 7.0 %collective-permute-start.1 = (bf16[128,768]{1,0:T(8,128)(2,1)S(1)}, bf16[128,768]{1,0:T(8,128)(2,1)S(1)}, u32[]{:S(2)}, u32[]{:S(2)}) collective-permute-start(bf16[128,768]{1,0:T(8,128)(2,1)S(1)} %slice.3.b_ref), channel_id=1, source_target_pairs={{0,4},{5,1},{4,8},{9,5},{8,12},{13,9},{12,14},{15,13},{14,10},{11,... | collective-permute-start | bytes 589832 | tf_op jit(solution)/shard_map/ppermute | solution.py:182
  6.9 3.5 %copy-start = (bf16[144,768]{1,0:T(8,128)(2,1)S(1)}, bf16[144,768]{1,0:T(8,128)(2,1)}, u32[]{:S(2)}) copy-start(bf16[144,768]{1,0:T(8,128)(2,1)} %lookup.1.a_ref) | copy-start | bytes 663556
  6.9 6.1 %collective-permute-start = (bf16[144,768]{1,0:T(8,128)(2,1)}, bf16[144,768]{1,0:T(8,128)(2,1)S(1)}, u32[]{:S(2)}, u32[]{:S(2)}) collective-permute-start(bf16[144,768]{1,0:T(8,128)(2,1)} %lookup.1.a_ref), channel_id=1, source_target_pairs={{0,4},{5,1},{4,8},{9,5},{8,12},{13,9},{12,14},{15,13},{14,10},{11,... | collective-permute-start | bytes 663560 | tf_op jit(solution)/shard_map/ppermute | solution.py:182
  8.5 6.1 %collective-permute-start.4 = (bf16[256,768]{1,0:T(8,128)(2,1)S(1)}, bf16[256,768]{1,0:T(8,128)(2,1)S(1)}, u32[]{:S(2)}, u32[]{:S(2)}) collective-permute-start(bf16[256,768]{1,0:T(8,128)(2,1)S(1)} %convert_multiply_fusion.refs_0_), channel_id=1, source_target_pairs={{0,1},{1,0},{2,3},{3,2},{4,5},{5,4},{6,7},{7,6},{8,9},{9,8},{10,11... | collective-permute-start | bytes 1179656 | tf_op jit(solution)/shard_map/ppermute | solution.py:182
  8.6 6.7 %collective-permute-start.3 = (bf16[128,768]{1,0:T(8,128)(2,1)S(1)}, bf16[128,768]{1,0:T(8,128)(2,1)S(1)}, u32[]{:S(2)}, u32[]{:S(2)}) collective-permute-start(bf16[128,768]{1,0:T(8,128)(2,1)S(1)} %collective-permute-done.1.b_ref), channel_id=1, source_target_pairs={{0,4},{5,1},{4,8},{9,5},{8,12},{13,9},{12,14},{15,13},{14,10},{11,... | collective-permute-start | bytes 589832 | tf_op jit(solution)/shard_map/ppermute | solution.py:182
  13.1 5.9 %collective-permute-start.2 = (bf16[144,768]{1,0:T(8,128)(2,1)S(1)}, bf16[144,768]{1,0:T(8,128)(2,1)S(1)}, u32[]{:S(2)}, u32[]{:S(2)}) collective-permute-start(bf16[144,768]{1,0:T(8,128)(2,1)S(1)} %collective-permute-done.a_ref), channel_id=1, source_target_pairs={{0,4},{5,1},{4,8},{9,5},{8,12},{13,9},{12,14},{15,13},{14,10},{11,... | collective-permute-start | bytes 663560 | tf_op jit(solution)/shard_map/ppermute | solution.py:182
  15.3 5.9 %collective-permute-start.6 = (bf16[128,768]{1,0:T(8,128)(2,1)S(1)}, bf16[128,768]{1,0:T(8,128)(2,1)S(1)}, u32[]{:S(2)}, u32[]{:S(2)}) collective-permute-start(bf16[128,768]{1,0:T(8,128)(2,1)S(1)} %collective-permute-done.3.b_ref), channel_id=1, source_target_pairs={{0,4},{5,1},{4,8},{9,5},{8,12},{13,9},{12,14},{15,13},{14,10},{11,... | collective-permute-start | bytes 589832 | tf_op jit(solution)/shard_map/ppermute | solution.py:182
  19.0 5.9 %collective-permute-start.5 = (bf16[144,768]{1,0:T(8,128)(2,1)S(1)}, bf16[144,768]{1,0:T(8,128)(2,1)S(1)}, u32[]{:S(2)}, u32[]{:S(2)}) collective-permute-start(bf16[144,768]{1,0:T(8,128)(2,1)S(1)} %collective-permute-done.2.a_ref), channel_id=1, source_target_pairs={{0,4},{5,1},{4,8},{9,5},{8,12},{13,9},{12,14},{15,13},{14,10},{11,... | collective-permute-start | bytes 663560 | tf_op jit(solution)/shard_map/ppermute | solution.py:182
  21.2 5.9 %collective-permute-start.8 = (bf16[128,768]{1,0:T(8,128)(2,1)S(1)}, bf16[128,768]{1,0:T(8,128)(2,1)S(1)}, u32[]{:S(2)}, u32[]{:S(2)}) collective-permute-start(bf16[128,768]{1,0:T(8,128)(2,1)S(1)} %collective-permute-done.6.b_ref), channel_id=1, source_target_pairs={{0,4},{5,1},{4,8},{9,5},{8,12},{13,9},{12,14},{15,13},{14,10},{11,... | collective-permute-start | bytes 589832 | tf_op jit(solution)/shard_map/ppermute | solution.py:182
  24.9 5.9 %collective-permute-start.7 = (bf16[144,768]{1,0:T(8,128)(2,1)S(1)}, bf16[144,768]{1,0:T(8,128)(2,1)S(1)}, u32[]{:S(2)}, u32[]{:S(2)}) collective-permute-start(bf16[144,768]{1,0:T(8,128)(2,1)S(1)} %collective-permute-done.5.a_ref), channel_id=1, source_target_pairs={{0,4},{5,1},{4,8},{9,5},{8,12},{13,9},{12,14},{15,13},{14,10},{11,... | collective-permute-start | bytes 663560 | tf_op jit(solution)/shard_map/ppermute | solution.py:182
  27.2 5.9 %collective-permute-start.10 = (bf16[128,768]{1,0:T(8,128)(2,1)S(1)}, bf16[128,768]{1,0:T(8,128)(2,1)S(1)}, u32[]{:S(2)}, u32[]{:S(2)}) collective-permute-start(bf16[128,768]{1,0:T(8,128)(2,1)S(1)} %collective-permute-done.8.b_ref), channel_id=1, source_target_pairs={{0,4},{5,1},{4,8},{9,5},{8,12},{13,9},{12,14},{15,13},{14,10},{11,... | collective-permute-start | bytes 589832 | tf_op jit(solution)/shard_map/ppermute | solution.py:182
  30.9 5.9 %collective-permute-start.9 = (bf16[144,768]{1,0:T(8,128)(2,1)S(1)}, bf16[144,768]{1,0:T(8,128)(2,1)S(1)}, u32[]{:S(2)}, u32[]{:S(2)}) collective-permute-start(bf16[144,768]{1,0:T(8,128)(2,1)S(1)} %collective-permute-done.7.a_ref), channel_id=1, source_target_pairs={{0,4},{5,1},{4,8},{9,5},{8,12},{13,9},{12,14},{15,13},{14,10},{11,... | collective-permute-start | bytes 663560 | tf_op jit(solution)/shard_map/ppermute | solution.py:182
  33.1 5.9 %collective-permute-start.12 = (bf16[128,768]{1,0:T(8,128)(2,1)S(1)}, bf16[128,768]{1,0:T(8,128)(2,1)S(1)}, u32[]{:S(2)}, u32[]{:S(2)}) collective-permute-start(bf16[128,768]{1,0:T(8,128)(2,1)S(1)} %collective-permute-done.10.b_ref), channel_id=1, source_target_pairs={{0,4},{5,1},{4,8},{9,5},{8,12},{13,9},{12,14},{15,13},{14,10},{11,... | collective-permute-start | bytes 589832 | tf_op jit(solution)/shard_map/ppermute | solution.py:182
  36.8 5.9 %collective-permute-start.11 = (bf16[144,768]{1,0:T(8,128)(2,1)S(1)}, bf16[144,768]{1,0:T(8,128)(2,1)S(1)}, u32[]{:S(2)}, u32[]{:S(2)}) collective-permute-start(bf16[144,768]{1,0:T(8,128)(2,1)S(1)} %collective-permute-done.9.a_ref), channel_id=1, source_target_pairs={{0,4},{5,1},{4,8},{9,5},{8,12},{13,9},{12,14},{15,13},{14,10},{11,... | collective-permute-start | bytes 663560 | tf_op jit(solution)/shard_map/ppermute | solution.py:182
  39.0 5.9 %collective-permute-start.14 = (bf16[128,768]{1,0:T(8,128)(2,1)S(1)}, bf16[128,768]{1,0:T(8,128)(2,1)S(1)}, u32[]{:S(2)}, u32[]{:S(2)}) collective-permute-start(bf16[128,768]{1,0:T(8,128)(2,1)S(1)} %collective-permute-done.12.b_ref), channel_id=1, source_target_pairs={{0,4},{5,1},{4,8},{9,5},{8,12},{13,9},{12,14},{15,13},{14,10},{11,... | collective-permute-start | bytes 589832 | tf_op jit(solution)/shard_map/ppermute | solution.py:182
  42.7 5.9 %collective-permute-start.13 = (bf16[144,768]{1,0:T(8,128)(2,1)S(1)}, bf16[144,768]{1,0:T(8,128)(2,1)S(1)}, u32[]{:S(2)}, u32[]{:S(2)}) collective-permute-start(bf16[144,768]{1,0:T(8,128)(2,1)S(1)} %collective-permute-done.11.a_ref), channel_id=1, source_target_pairs={{0,4},{5,1},{4,8},{9,5},{8,12},{13,9},{12,14},{15,13},{14,10},{11,... | collective-permute-start | bytes 663560 | tf_op jit(solution)/shard_map/ppermute | solution.py:182
  50.0 2.4 %copy-start.2 = (f32[256,768]{1,0:T(8,128)S(1)}, f32[256,768]{1,0:T(8,128)}, u32[]{:S(2)}) copy-start(f32[256,768]{1,0:T(8,128)} %param.11) | copy-start | bytes 2359300
  50.0 2.4 %copy-start.3 = (f32[256,768]{1,0:T(8,128)S(1)}, f32[256,768]{1,0:T(8,128)}, u32[]{:S(2)}) copy-start(f32[256,768]{1,0:T(8,128)} %param.12) | copy-start | bytes 2359300
  50.0 2.4 %copy-start.4 = (f32[256,768]{1,0:T(8,128)S(1)}, f32[256,768]{1,0:T(8,128)}, u32[]{:S(2)}) copy-start(f32[256,768]{1,0:T(8,128)} %param.13) | copy-start | bytes 2359300
  50.0 2.4 %collective-permute-start.15 = (f32[256,768]{1,0:T(8,128)S(1)}, f32[256,768]{1,0:T(8,128)S(1)}, u32[]{:S(2)}, u32[]{:S(2)}) collective-permute-start(f32[256,768]{1,0:T(8,128)S(1)} %gradient.31), channel_id=1, source_target_pairs={{0,1},{1,0},{2,3},{3,2},{4,5},{5,4},{6,7},{7,6},{8,9},{9,8},{10,11... | collective-permute-start | bytes 2359304 | tf_op jit(solution)/shard_map/ppermute | solution.py:182

commit v6 on v5

--- a/solution.py
+++ b/solution.py
@@ -18,7 +18,6 @@
 WORD = 32
 LANES = 128
 VMEM_LIMIT = 32 * 1024 * 1024
-LONG = pl.CostEstimate(flops=10**10, bytes_accessed=10**6, transcendentals=0)
 
 
 def power_of_two(exponent, bits, start, sign):
@@ -121,7 +120,7 @@
         new_refs[block][...] = piece if fresh else old_refs[block][...] + piece
 
 
-def add_gradient(bits, owners, a, b, weights, sums):
+def add_gradient(bits, owners, a, b, weights, sums, flops):
     blocks = len(weights)
     height, width = weights[0].shape
     vmem = pl.BlockSpec(memory_space=pltpu.VMEM)
@@ -135,7 +134,7 @@
         out_shape=[jax.ShapeDtypeStruct((height, width), jnp.float32)] * blocks,
         input_output_aliases={first_sum + i: i for i in range(len(sums))},
         compiler_params=pltpu.CompilerParams(vmem_limit_bytes=VMEM_LIMIT),
-        cost_estimate=LONG,
+        cost_estimate=pl.CostEstimate(flops=flops, bytes_accessed=10**6, transcendentals=0),
         name="gradient",
     )(*inputs)
 
@@ -152,10 +151,8 @@
     path = list(range(0, blocks // 2, across))
     if across == 2:
         path += list(range(1, blocks // 2, 2))[::-1]
-    pairs = []
-    for here, there in zip(path, path[1:] + path[:1]):
-        pairs += [(2 * here, 2 * there), (2 * there + 1, 2 * here + 1)]
-    return pairs
+    steps = zip(path, path[1:] + path[:1])
+    return [(2 * here + core, 2 * there + core) for here, there in steps for core in range(2)]
 
 
 together = lax.optimization_barrier
@@ -172,8 +169,9 @@
     first_moment,
     second_moment,
 ):
-    chips = blocks // 2
-    ring = ring_of(blocks, across)
+    half_way = blocks // 4
+    up = ring_of(blocks, across)
+    down = [(there, here) for here, there in up]
     swap = [(i, i ^ 1) for i in range(blocks)]
     bits = (label_slot.shape[0] // LANES - 1).bit_length()
     head = embeddings.shape[0] // 2
@@ -181,31 +179,41 @@
     def send(value, pairs):
         return lax.ppermute(value, "blk", pairs)
 
-    def add(owner, docs, total):
-        (total,) = add_gradient(bits, (owner,), *docs, [(mine, other)[owner]], total)
-        return (total,)
-
     b = embeddings[head:]
-    next_b = send(b, ring)
+    coming = {"up_b": send(b, up), "down_b": send(b, down)}
     a = lookup_rows(label_slot, pos_ids, pos_count, embeddings, head)
-    next_a = send(a, ring)
+    coming |= {"up_a": send(a, up), "down_a": send(a, down)}
     mine = weights.astype(jnp.bfloat16) * 0.5
     other = send(mine, swap)
-    mine_sum, other_sum = (), ()
-    for step in range(1, chips):
-        before = (a, b)
-        b, before, other_sum = together((next_b, before, other_sum))
-        if step < chips - 1:
-            next_b = send(b, ring)
-        mine_sum = add(0, before, mine_sum)
-        a, before, mine_sum = together((next_a, before, mine_sum))
-        if step < chips - 1:
-            next_a = send(a, ring)
-        other_sum = add(1, before, other_sum)
-    other_sum = add(1, (a, b), other_sum)
-    got = send(other_sum[0], swap)
-    mine_sum = add(0, (a, b), mine_sum)
-    return adam_step(weights, first_moment, second_moment, 0.5 * (mine_sum[0] + got))
+    sums = [(), ()]
+
+    def work(owner, docs, flops):
+        weights_of = [(mine, other)[owner]]
+        sums[owner] = add_gradient(bits, (owner,), *docs, weights_of, sums[owner], flops)
+
+    waiting = [(0, ()), (0, ()), (0, ()), (0, (a, b)), (1, (a, b))]
+    for step in range(1, half_way + 1):
+        messages = ["up_b", "down_b", "up_a", "down_a"] if step < half_way else ["down_b", "up_a"]
+        passed_on = messages if step < half_way - 1 else ["down_b", "up_a"]
+        while step == half_way and len(waiting) > len(messages):
+            work(*waiting.pop(0), 3 * 10**8)
+        flops = 6 * 10**8 if step < half_way - 1 else 5 * 10**8
+        came = {}
+        for message in messages:
+            owner, docs = waiting.pop(0)
+            came[message], docs, sums = together((coming[message], docs, sums))
+            if step < half_way and message in passed_on:
+                coming[message] = send(came[message], up if message in ("up_a", "up_b") else down)
+            if docs:
+                work(owner, docs, flops)
+        if step < half_way:
+            for docs in ((came["up_a"], came["up_b"]), (came["down_a"], came["down_b"])):
+                waiting += [(0, docs), (1, docs)]
+    docs = (came["up_a"], came["down_b"])
+    work(1, docs, 3 * 10**8)
+    got = send(sums[1][0], swap)
+    work(0, docs, 3 * 10**8)
+    return adam_step(weights, first_moment, second_moment, 0.5 * (sums[0][0] + got))
 
 
 def solution(mesh):

time: 54.4 us -> 46.8 us (0.86)
  starting transfers between devices: 24.2 us -> 16.3 us
  waiting for transfers between devices: 13.6 us -> 11.9 us
  other arithmetic: 1.85 us -> 3.01 us
  local copies, waits for them, and re-layouts: 1.04 us -> 1.9 us
    ppermute x16, starting transfers between devices: 24.2 us -> 16.3 us  [send(): return lax.ppermute(value, 'blk', pairs)]
    ppermute x16, waiting for transfers between devices: 13.6 us -> 11.9 us  [send(): return lax.ppermute(value, 'blk', pairs)]
    mul x1, other arithmetic: 0.05 us -> 1.18 us  [per_device(): mine = weights.astype(jnp.bfloat16) * 0.5]
    unnamed x10, local copies, waits for them, and re-layouts: 0.03 us -> 0.96 us
  transfers between devices with their start and end apart: 16 -> 16, of which waited for: 8 -> 11; matrix products, arithmetic and copies ran while one was open for 0% -> 3% of each run, Pallas kernels for 21% -> 24%
where the time goes in v6:
time: 46.8 us; the launch traced here: 46.6 us
  starting transfers between devices  16.3 us (35%)
  Pallas kernels  12.7 us (27%)
  waiting for transfers between devices  11.9 us (25%)
  other arithmetic  3.01 us (6%)
  local copies, waits for them, and re-layouts  1.9 us (4%)
  between operations  0.85 us (2%)
    ppermute x16, starting transfers between devices, send(): return lax.ppermute(value, 'blk', pairs)  16.3 us
    ppermute x16, waiting for transfers between devices, send(): return lax.ppermute(value, 'blk', pairs)  11.9 us
    pallas_call x16, Pallas kernels, add_gradient(): pl.pallas_call(functools.partial(gradient_kernel, bits, owners, not sums)...  10.5 us
    pallas_call x1, Pallas kernels, lookup_rows(): pl.pallas_call(functools.partial(lookup_kernel, (lines - 1).bit_length())...  2.18 us
    sub x1, other arithmetic, adam_step(): new_weights = weights - learn_rate * (update + decay_rate * weights)  1.83 us
    mul x1, other arithmetic, per_device(): mine = weights.astype(jnp.bfloat16) * 0.5  1.18 us
    unnamed x10, local copies, waits for them, and re-layouts  0.96 us
    slice x1, local copies, waits for them, and re-layouts, per_device(): b = embeddings[head:]  0.94 us
  transfers between devices with their start and end apart: 16, of which 11 were waited for; matrix products, arithmetic and copies ran while one was open for 3% of the time, Pallas kernels for 24%

profile of v6, /device:TPU:0, one launch (start us, length us, event | category | flops | bytes accessed | tf_op | source)
XLA Modules:
  0.0 46.6 jit_solution(7233753775491070616)
XLA Ops:
  0.6 0.9 %slice.3.b_ref = bf16[128,768]{1,0:T(8,128)(2,1)S(1)} slice(bf16[256,768]{1,0:T(8,128)(2,1)} %docs_ref.1), slice={[128:256], [0:768]} | slice | bytes 393216 | tf_op jit(solution)/shard_map/slice | solution.py:182
  1.6 3.1 %collective-permute-start.2 = (bf16[128,768]{1,0:T(8,128)(2,1)S(1)}, bf16[128,768]{1,0:T(8,128)(2,1)S(1)}, u32[]{:S(2)}, u32[]{:S(2)}) collective-permute-start(bf16[128,768]{1,0:T(8,128)(2,1)S(1)} %slice.3.b_ref), channel_id=1, source_target_pairs={{0,4},{1,5},{4,8},{5,9},{8,12},{9,13},{12,14},{13,15},{14,10},{15,... | collective-permute-start | bytes 589832 | tf_op jit(solution)/shard_map/ppermute | solution.py:180
  4.7 1.2 %convert_multiply_fusion.refs_0_ = bf16[256,768]{1,0:T(8,128)(2,1)S(1)} fusion(f32[256,768]{1,0:T(8,128)} %param.11), kind=kLoop, calls=%fused_computation.3 | loop fusion | flops 393216 | bytes 1179648 | tf_op jit(solution)/shard_map/mul | solution.py:186
  6.0 2.2 %lookup.1.a_ref = bf16[144,768]{1,0:T(8,128)(2,1)} custom-call(s32[32,256]{1,0:T(8,128)} %bitcast.3, s32[1,256]{1,0:T(1,128)} %bitcast.5, s32[32,128]{1,0:T(8,128)} %bitcast.4, bf16[256,768]{1,0:T(8,128)(2,1)} %docs_ref.1), custom_call_target="tpu_custom_call" | custom-call | tf_op jit(solution)/shard_map/lookup/pallas_call | solution.py:70
  8.2 2.0 %collective-permute-start = (bf16[144,768]{1,0:T(8,128)(2,1)}, bf16[144,768]{1,0:T(8,128)(2,1)S(1)}, u32[]{:S(2)}, u32[]{:S(2)}) collective-permute-start(bf16[144,768]{1,0:T(8,128)(2,1)} %lookup.1.a_ref), channel_id=1, source_target_pairs={{0,4},{1,5},{4,8},{5,9},{8,12},{9,13},{12,14},{13,15},{14,10},{15,... | collective-permute-start | bytes 663560 | tf_op jit(solution)/shard_map/ppermute | solution.py:180
  10.2 2.0 %collective-permute-start.5 = (bf16[128,768]{1,0:T(8,128)(2,1)S(1)}, bf16[128,768]{1,0:T(8,128)(2,1)S(1)}, u32[]{:S(2)}, u32[]{:S(2)}) collective-permute-start(bf16[128,768]{1,0:T(8,128)(2,1)S(1)} %collective-permute-done.2.b_ref), channel_id=1, source_target_pairs={{0,4},{1,5},{4,8},{5,9},{8,12},{9,13},{12,14},{13,15},{14,10},{15,... | collective-permute-start | bytes 589832 | tf_op jit(solution)/shard_map/ppermute | solution.py:180
  12.2 1.3 %collective-permute-done.3.b_ref = bf16[128,768]{1,0:T(8,128)(2,1)S(1)} collective-permute-done((bf16[128,768]{1,0:T(8,128)(2,1)S(1)}, bf16[128,768]{1,0:T(8,128)(2,1)S(1)}, u32[]{:S(2)}, u32[]{:S(2)}) %collective-permute-start.3) | collective-permute-done | bytes 196640 | tf_op jit(solution)/shard_map/ppermute | solution.py:180
  13.7 2.9 %collective-permute-done.a_ref = bf16[144,768]{1,0:T(8,128)(2,1)S(1)} collective-permute-done((bf16[144,768]{1,0:T(8,128)(2,1)}, bf16[144,768]{1,0:T(8,128)(2,1)S(1)}, u32[]{:S(2)}, u32[]{:S(2)}) %collective-permute-start) | collective-permute-done | bytes 221216 | tf_op jit(solution)/shard_map/ppermute | solution.py:180
  16.6 2.1 %collective-permute-start.1 = (bf16[144,768]{1,0:T(8,128)(2,1)S(1)}, bf16[144,768]{1,0:T(8,128)(2,1)S(1)}, u32[]{:S(2)}, u32[]{:S(2)}) collective-permute-start(bf16[144,768]{1,0:T(8,128)(2,1)S(1)} %collective-permute-done.a_ref), channel_id=1, source_target_pairs={{0,4},{1,5},{4,8},{5,9},{8,12},{9,13},{12,14},{13,15},{14,10},{15,... | collective-permute-start | bytes 663560 | tf_op jit(solution)/shard_map/ppermute | solution.py:180
  18.8 0.9 %copy-done = bf16[144,768]{1,0:T(8,128)(2,1)S(1)} copy-done((bf16[144,768]{1,0:T(8,128)(2,1)S(1)}, bf16[144,768]{1,0:T(8,128)(2,1)}, u32[]{:S(2)}) %copy-start) | copy-done | bytes 221208
  20.8 2.1 %collective-permute-start.10 = (bf16[128,768]{1,0:T(8,128)(2,1)S(1)}, bf16[128,768]{1,0:T(8,128)(2,1)S(1)}, u32[]{:S(2)}, u32[]{:S(2)}) collective-permute-start(bf16[128,768]{1,0:T(8,128)(2,1)S(1)} %collective-permute-done.5.b_ref), channel_id=1, source_target_pairs={{0,4},{1,5},{4,8},{5,9},{8,12},{9,13},{12,14},{13,15},{14,10},{15,... | collective-permute-start | bytes 589832 | tf_op jit(solution)/shard_map/ppermute | solution.py:180
  23.6 0.7 %gradient.18.refs_1_ = f32[256,768]{1,0:T(8,128)S(1)} custom-call(bf16[144,768]{1,0:T(8,128)(2,1)S(1)} %collective-permute-done.a_ref, bf16[128,768]{1,0:T(8,128)(2,1)S(1)} %collective-permute-done.2.b_ref, bf16[256,768]{1,0:T(8,128)(2,1)S(1)} %convert_multiply_fusion.refs_0_, f32[256,768]{1,0:T(8,128)S(1)} %gradient.16.refs_1_), custom_call_target="tpu_custom_call", output_to_operand_aliasing={{}: (3, {})} | custom-call | flops 600000000 | bytes 1000000 | tf_op jit(solution)/shard_map/gradient/pallas_call | solution.py:130
  24.3 1.3 %collective-permute-done.1.a_ref = bf16[144,768]{1,0:T(8,128)(2,1)S(1)} collective-permute-done((bf16[144,768]{1,0:T(8,128)(2,1)S(1)}, bf16[144,768]{1,0:T(8,128)(2,1)S(1)}, u32[]{:S(2)}, u32[]{:S(2)}) %collective-permute-start.1) | collective-permute-done | bytes 221216 | tf_op jit(solution)/shard_map/ppermute | solution.py:180
  25.6 2.1 %collective-permute-start.8 = (bf16[144,768]{1,0:T(8,128)(2,1)S(1)}, bf16[144,768]{1,0:T(8,128)(2,1)S(1)}, u32[]{:S(2)}, u32[]{:S(2)}) collective-permute-start(bf16[144,768]{1,0:T(8,128)(2,1)S(1)} %collective-permute-done.1.a_ref), channel_id=1, source_target_pairs={{0,4},{1,5},{4,8},{5,9},{8,12},{9,13},{12,14},{13,15},{14,10},{15,... | collective-permute-start | bytes 663560 | tf_op jit(solution)/shard_map/ppermute | solution.py:180
  27.6 0.7 %gradient.19.refs_1_ = f32[256,768]{1,0:T(8,128)S(1)} custom-call(bf16[144,768]{1,0:T(8,128)(2,1)S(1)} %collective-permute-done.a_ref, bf16[128,768]{1,0:T(8,128)(2,1)S(1)} %collective-permute-done.2.b_ref, bf16[256,768]{1,0:T(8,128)(2,1)S(1)} %collective-permute-done.7.refs_0_, f32[256,768]{1,0:T(8,128)S(1)} %gradient.17.refs_1_), custom_call_target="tpu_custom_call", output_to_operand_aliasing={{}: (3, {})} | custom-call | flops 600000000 | bytes 1000000 | tf_op jit(solution)/shard_map/gradient/pallas_call | solution.py:130
  28.3 0.7 %gradient.20.refs_1_ = f32[256,768]{1,0:T(8,128)S(1)} custom-call(bf16[144,768]{1,0:T(8,128)(2,1)S(1)} %collective-permute-done.6.a_ref, bf16[128,768]{1,0:T(8,128)(2,1)S(1)} %collective-permute-done.3.b_ref, bf16[256,768]{1,0:T(8,128)(2,1)S(1)} %convert_multiply_fusion.refs_0_, f32[256,768]{1,0:T(8,128)S(1)} %gradient.18.refs_1_), custom_call_target="tpu_custom_call", output_to_operand_aliasing={{}: (3, {})} | custom-call | flops 600000000 | bytes 1000000 | tf_op jit(solution)/shard_map/gradient/pallas_call | solution.py:130
  29.0 0.8 %collective-permute-done.10.b_ref = bf16[128,768]{1,0:T(8,128)(2,1)S(1)} collective-permute-done((bf16[128,768]{1,0:T(8,128)(2,1)S(1)}, bf16[128,768]{1,0:T(8,128)(2,1)S(1)}, u32[]{:S(2)}, u32[]{:S(2)}) %collective-permute-start.10) | collective-permute-done | bytes 196640 | tf_op jit(solution)/shard_map/ppermute | solution.py:180
  29.8 0.7 %gradient.21.refs_1_ = f32[256,768]{1,0:T(8,128)S(1)} custom-call(bf16[144,768]{1,0:T(8,128)(2,1)S(1)} %collective-permute-done.6.a_ref, bf16[128,768]{1,0:T(8,128)(2,1)S(1)} %collective-permute-done.3.b_ref, bf16[256,768]{1,0:T(8,128)(2,1)S(1)} %collective-permute-done.7.refs_0_, f32[256,768]{1,0:T(8,128)S(1)} %gradient.19.refs_1_), custom_call_target="tpu_custom_call", output_to_operand_aliasing={{}: (3, {})} | custom-call | flops 500000000 | bytes 1000000 | tf_op jit(solution)/shard_map/gradient/pallas_call | solution.py:130
  30.4 1.4 %collective-permute-done.9.b_ref = bf16[128,768]{1,0:T(8,128)(2,1)S(1)} collective-permute-done((bf16[128,768]{1,0:T(8,128)(2,1)S(1)}, bf16[128,768]{1,0:T(8,128)(2,1)S(1)}, u32[]{:S(2)}, u32[]{:S(2)}) %collective-permute-start.9) | collective-permute-done | bytes 196640 | tf_op jit(solution)/shard_map/ppermute | solution.py:180
  32.5 0.7 %gradient.22.refs_1_ = f32[256,768]{1,0:T(8,128)S(1)} custom-call(bf16[144,768]{1,0:T(8,128)(2,1)S(1)} %collective-permute-done.1.a_ref, bf16[128,768]{1,0:T(8,128)(2,1)S(1)} %collective-permute-done.5.b_ref, bf16[256,768]{1,0:T(8,128)(2,1)S(1)} %convert_multiply_fusion.refs_0_, f32[256,768]{1,0:T(8,128)S(1)} %gradient.20.refs_1_), custom_call_target="tpu_custom_call", output_to_operand_aliasing={{}: (3, {})} | custom-call | flops 500000000 | bytes 1000000 | tf_op jit(solution)/shard_map/gradient/pallas_call | solution.py:130
  33.2 0.9 %collective-permute-done.8.a_ref = bf16[144,768]{1,0:T(8,128)(2,1)S(1)} collective-permute-done((bf16[144,768]{1,0:T(8,128)(2,1)S(1)}, bf16[144,768]{1,0:T(8,128)(2,1)S(1)}, u32[]{:S(2)}, u32[]{:S(2)}) %collective-permute-start.8) | collective-permute-done | bytes 221216 | tf_op jit(solution)/shard_map/ppermute | solution.py:180
  34.1 1.7 %collective-permute-start.12 = (bf16[144,768]{1,0:T(8,128)(2,1)S(1)}, bf16[144,768]{1,0:T(8,128)(2,1)S(1)}, u32[]{:S(2)}, u32[]{:S(2)}) collective-permute-start(bf16[144,768]{1,0:T(8,128)(2,1)S(1)} %collective-permute-done.8.a_ref), channel_id=1, source_target_pairs={{0,4},{1,5},{4,8},{5,9},{8,12},{9,13},{12,14},{13,15},{14,10},{15,... | collective-permute-start | bytes 663560 | tf_op jit(solution)/shard_map/ppermute | solution.py:180
  36.7 0.7 %gradient.24.refs_1_ = f32[256,768]{1,0:T(8,128)S(1)} custom-call(bf16[144,768]{1,0:T(8,128)(2,1)S(1)} %collective-permute-done.11.a_ref, bf16[128,768]{1,0:T(8,128)(2,1)S(1)} %collective-permute-done.4.b_ref, bf16[256,768]{1,0:T(8,128)(2,1)S(1)} %convert_multiply_fusion.refs_0_, f32[256,768]{1,0:T(8,128)S(1)} %gradient.22.refs_1_), custom_call_target="tpu_custom_call", output_to_operand_aliasing={{}: (3, {})} | custom-call | flops 500000000 | bytes 1000000 | tf_op jit(solution)/shard_map/gradient/pallas_call | solution.py:130
  37.4 0.7 %gradient.25.refs_1_ = f32[256,768]{1,0:T(8,128)S(1)} custom-call(bf16[144,768]{1,0:T(8,128)(2,1)S(1)} %collective-permute-done.8.a_ref, bf16[128,768]{1,0:T(8,128)(2,1)S(1)} %collective-permute-done.10.b_ref, bf16[256,768]{1,0:T(8,128)(2,1)S(1)} %convert_multiply_fusion.refs_0_, f32[256,768]{1,0:T(8,128)S(1)} %gradient.24.refs_1_), custom_call_target="tpu_custom_call", output_to_operand_aliasing={{}: (3, {})} | custom-call | flops 300000000 | bytes 1000000 | tf_op jit(solution)/shard_map/gradient/pallas_call | solution.py:130
  38.0 0.7 %gradient.26.refs_1_ = f32[256,768]{1,0:T(8,128)S(1)} custom-call(bf16[144,768]{1,0:T(8,128)(2,1)S(1)} %collective-permute-done.11.a_ref, bf16[128,768]{1,0:T(8,128)(2,1)S(1)} %collective-permute-done.4.b_ref, bf16[256,768]{1,0:T(8,128)(2,1)S(1)} %collective-permute-done.7.refs_0_, f32[256,768]{1,0:T(8,128)S(1)} %gradient.23.refs_1_), custom_call_target="tpu_custom_call", output_to_operand_aliasing={{}: (3, {})} | custom-call | flops 300000000 | bytes 1000000 | tf_op jit(solution)/shard_map/gradient/pallas_call | solution.py:130
  38.7 0.7 %gradient.27.refs_1_ = f32[256,768]{1,0:T(8,128)S(1)} custom-call(bf16[144,768]{1,0:T(8,128)(2,1)S(1)} %collective-permute-done.8.a_ref, bf16[128,768]{1,0:T(8,128)(2,1)S(1)} %collective-permute-done.10.b_ref, bf16[256,768]{1,0:T(8,128)(2,1)S(1)} %collective-permute-done.7.refs_0_, f32[256,768]{1,0:T(8,128)S(1)} %gradient.26.refs_1_), custom_call_target="tpu_custom_call", output_to_operand_aliasing={{}: (3, {})} | custom-call | flops 300000000 | bytes 1000000 | tf_op jit(solution)/shard_map/gradient/pallas_call | solution.py:130
  39.4 0.7 %collective-permute-done.14.b_ref = bf16[128,768]{1,0:T(8,128)(2,1)S(1)} collective-permute-done((bf16[128,768]{1,0:T(8,128)(2,1)S(1)}, bf16[128,768]{1,0:T(8,128)(2,1)S(1)}, u32[]{:S(2)}, u32[]{:S(2)}) %collective-permute-start.14) | collective-permute-done | bytes 196640 | tf_op jit(solution)/shard_map/ppermute | solution.py:180
  40.1 0.7 %gradient.28.refs_1_ = f32[256,768]{1,0:T(8,128)S(1)} custom-call(bf16[144,768]{1,0:T(8,128)(2,1)S(1)} %collective-permute-done.13.a_ref, bf16[128,768]{1,0:T(8,128)(2,1)S(1)} %collective-permute-done.9.b_ref, bf16[256,768]{1,0:T(8,128)(2,1)S(1)} %convert_multiply_fusion.refs_0_, f32[256,768]{1,0:T(8,128)S(1)} %gradient.25.refs_1_), custom_call_target="tpu_custom_call", output_to_operand_aliasing={{}: (3, {})} | custom-call | flops 500000000 | bytes 1000000 | tf_op jit(solution)/shard_map/gradient/pallas_call | solution.py:130
  41.7 0.7 %gradient.31 = f32[256,768]{1,0:T(8,128)S(1)} custom-call(bf16[144,768]{1,0:T(8,128)(2,1)S(1)} %collective-permute-done.12.a_ref, bf16[128,768]{1,0:T(8,128)(2,1)S(1)} %collective-permute-done.14.b_ref, bf16[256,768]{1,0:T(8,128)(2,1)S(1)} %collective-permute-done.7.refs_0_, f32[256,768]{1,0:T(8,128)S(1)} %gradient.30.refs_1_), custom_call_target="tpu_custom_call", output_to_operand_aliasing={{}: (3, {})} | custom-call | flops 300000000 | bytes 1000000 | tf_op jit(solution)/shard_map/gradient/pallas_call | solution.py:130
  42.5 0.7 %gradient.29 = f32[256,768]{1,0:T(8,128)S(1)} custom-call(bf16[144,768]{1,0:T(8,128)(2,1)S(1)} %collective-permute-done.12.a_ref, bf16[128,768]{1,0:T(8,128)(2,1)S(1)} %collective-permute-done.14.b_ref, bf16[256,768]{1,0:T(8,128)(2,1)S(1)} %convert_multiply_fusion.refs_0_, f32[256,768]{1,0:T(8,128)S(1)} %gradient.28.refs_1_), custom_call_target="tpu_custom_call", output_to_operand_aliasing={{}: (3, {})} | custom-call | flops 300000000 | bytes 1000000 | tf_op jit(solution)/shard_map/gradient/pallas_call | solution.py:130
  43.2 1.6 %collective-permute-done.15 = f32[256,768]{1,0:T(8,128)S(1)} collective-permute-done((f32[256,768]{1,0:T(8,128)S(1)}, f32[256,768]{1,0:T(8,128)S(1)}, u32[]{:S(2)}, u32[]{:S(2)}) %collective-permute-start.15) | collective-permute-done | bytes 786464 | tf_op jit(solution)/shard_map/ppermute | solution.py:180
  44.8 1.8 %multiply_subtract_fusion = (f32[256,768]{1,0:T(8,128)}, f32[256,768]{1,0:T(8,128)}, f32[256,768]{1,0:T(8,128)}) fusion(f32[256,768]{1,0:T(8,128)S(1)} %copy-done.2, f32[256,768]{1,0:T(8,128)S(1)} %gradient.29, f32[256,768]{1,0:T(8,128)S(1)} %collective-permute-done.15, f32[256,768]{1,0:T(8,128)S(1)} %copy-done.3, f32[256,768]{1,0:T(8,128)S(1)} %copy-done.4), kind=kLoop, calls=%fused_computation | loop fusion | flops 3342336 | bytes 6291456 | tf_op jit(solution)/shard_map/sub | solution.py:146
  (30 shorter events, 5.0 us)
Async XLA Ops:
  1.6 8.6 %collective-permute-start.2 = (bf16[128,768]{1,0:T(8,128)(2,1)S(1)}, bf16[128,768]{1,0:T(8,128)(2,1)S(1)}, u32[]{:S(2)}, u32[]{:S(2)}) collective-permute-start(bf16[128,768]{1,0:T(8,128)(2,1)S(1)} %slice.3.b_ref), channel_id=1, source_target_pairs={{0,4},{1,5},{4,8},{5,9},{8,12},{9,13},{12,14},{13,15},{14,10},{15,... | collective-permute-start | bytes 589832 | tf_op jit(solution)/shard_map/ppermute | solution.py:180
  5.8 17.0 %collective-permute-start.7 = (bf16[256,768]{1,0:T(8,128)(2,1)S(1)}, bf16[256,768]{1,0:T(8,128)(2,1)S(1)}, u32[]{:S(2)}, u32[]{:S(2)}) collective-permute-start(bf16[256,768]{1,0:T(8,128)(2,1)S(1)} %convert_multiply_fusion.refs_0_), channel_id=1, source_target_pairs={{0,1},{1,0},{2,3},{3,2},{4,5},{5,4},{6,7},{7,6},{8,9},{9,8},{10,11... | collective-permute-start | bytes 1179656 | tf_op jit(solution)/shard_map/ppermute | solution.py:180
  5.9 7.6 %collective-permute-start.3 = (bf16[128,768]{1,0:T(8,128)(2,1)S(1)}, bf16[128,768]{1,0:T(8,128)(2,1)S(1)}, u32[]{:S(2)}, u32[]{:S(2)}) collective-permute-start(bf16[128,768]{1,0:T(8,128)(2,1)S(1)} %slice.3.b_ref), channel_id=1, source_target_pairs={{4,0},{5,1},{8,4},{9,5},{12,8},{13,9},{14,12},{15,13},{10,14},{11,... | collective-permute-start | bytes 589832 | tf_op jit(solution)/shard_map/ppermute | solution.py:180
  8.2 8.4 %collective-permute-start = (bf16[144,768]{1,0:T(8,128)(2,1)}, bf16[144,768]{1,0:T(8,128)(2,1)S(1)}, u32[]{:S(2)}, u32[]{:S(2)}) collective-permute-start(bf16[144,768]{1,0:T(8,128)(2,1)} %lookup.1.a_ref), channel_id=1, source_target_pairs={{0,4},{1,5},{4,8},{5,9},{8,12},{9,13},{12,14},{13,15},{14,10},{15,... | collective-permute-start | bytes 663560 | tf_op jit(solution)/shard_map/ppermute | solution.py:180
  10.2 8.5 %collective-permute-start.6 = (bf16[144,768]{1,0:T(8,128)(2,1)}, bf16[144,768]{1,0:T(8,128)(2,1)S(1)}, u32[]{:S(2)}, u32[]{:S(2)}) collective-permute-start(bf16[144,768]{1,0:T(8,128)(2,1)} %lookup.1.a_ref), channel_id=1, source_target_pairs={{4,0},{5,1},{8,4},{9,5},{12,8},{13,9},{14,12},{15,13},{10,14},{11,... | collective-permute-start | bytes 663560 | tf_op jit(solution)/shard_map/ppermute | solution.py:180
  10.2 10.6 %collective-permute-start.5 = (bf16[128,768]{1,0:T(8,128)(2,1)S(1)}, bf16[128,768]{1,0:T(8,128)(2,1)S(1)}, u32[]{:S(2)}, u32[]{:S(2)}) collective-permute-start(bf16[128,768]{1,0:T(8,128)(2,1)S(1)} %collective-permute-done.2.b_ref), channel_id=1, source_target_pairs={{0,4},{1,5},{4,8},{5,9},{8,12},{9,13},{12,14},{13,15},{14,10},{15,... | collective-permute-start | bytes 589832 | tf_op jit(solution)/shard_map/ppermute | solution.py:180
  13.5 10.0 %collective-permute-start.4 = (bf16[128,768]{1,0:T(8,128)(2,1)S(1)}, bf16[128,768]{1,0:T(8,128)(2,1)S(1)}, u32[]{:S(2)}, u32[]{:S(2)}) collective-permute-start(bf16[128,768]{1,0:T(8,128)(2,1)S(1)} %collective-permute-done.3.b_ref), channel_id=1, source_target_pairs={{4,0},{5,1},{8,4},{9,5},{12,8},{13,9},{14,12},{15,13},{10,14},{11,... | collective-permute-start | bytes 589832 | tf_op jit(solution)/shard_map/ppermute | solution.py:180
  16.6 9.0 %collective-permute-start.1 = (bf16[144,768]{1,0:T(8,128)(2,1)S(1)}, bf16[144,768]{1,0:T(8,128)(2,1)S(1)}, u32[]{:S(2)}, u32[]{:S(2)}) collective-permute-start(bf16[144,768]{1,0:T(8,128)(2,1)S(1)} %collective-permute-done.a_ref), channel_id=1, source_target_pairs={{0,4},{1,5},{4,8},{5,9},{8,12},{9,13},{12,14},{13,15},{14,10},{15,... | collective-permute-start | bytes 663560 | tf_op jit(solution)/shard_map/ppermute | solution.py:180
  18.7 9.6 %collective-permute-start.11 = (bf16[144,768]{1,0:T(8,128)(2,1)S(1)}, bf16[144,768]{1,0:T(8,128)(2,1)S(1)}, u32[]{:S(2)}, u32[]{:S(2)}) collective-permute-start(bf16[144,768]{1,0:T(8,128)(2,1)S(1)} %collective-permute-done.6.a_ref), channel_id=1, source_target_pairs={{4,0},{5,1},{8,4},{9,5},{12,8},{13,9},{14,12},{15,13},{10,14},{11,... | collective-permute-start | bytes 663560 | tf_op jit(solution)/shard_map/ppermute | solution.py:180
  18.8 0.9 %copy-start = (bf16[144,768]{1,0:T(8,128)(2,1)S(1)}, bf16[144,768]{1,0:T(8,128)(2,1)}, u32[]{:S(2)}) copy-start(bf16[144,768]{1,0:T(8,128)(2,1)} %lookup.1.a_ref) | copy-start | bytes 663556
  19.7 3.2 %copy-start.1 = (bf16[144,768]{1,0:T(8,128)(2,1)S(1)}, bf16[144,768]{1,0:T(8,128)(2,1)}, u32[]{:S(2)}) copy-start(bf16[144,768]{1,0:T(8,128)(2,1)} %lookup.1.a_ref) | copy-start | bytes 663556
  20.8 9.0 %collective-permute-start.10 = (bf16[128,768]{1,0:T(8,128)(2,1)S(1)}, bf16[128,768]{1,0:T(8,128)(2,1)S(1)}, u32[]{:S(2)}, u32[]{:S(2)}) collective-permute-start(bf16[128,768]{1,0:T(8,128)(2,1)S(1)} %collective-permute-done.5.b_ref), channel_id=1, source_target_pairs={{0,4},{1,5},{4,8},{5,9},{8,12},{9,13},{12,14},{13,15},{14,10},{15,... | collective-permute-start | bytes 589832 | tf_op jit(solution)/shard_map/ppermute | solution.py:180
  23.5 8.3 %collective-permute-start.9 = (bf16[128,768]{1,0:T(8,128)(2,1)S(1)}, bf16[128,768]{1,0:T(8,128)(2,1)S(1)}, u32[]{:S(2)}, u32[]{:S(2)}) collective-permute-start(bf16[128,768]{1,0:T(8,128)(2,1)S(1)} %collective-permute-done.4.b_ref), channel_id=1, source_target_pairs={{4,0},{5,1},{8,4},{9,5},{12,8},{13,9},{14,12},{15,13},{10,14},{11,... | collective-permute-start | bytes 589832 | tf_op jit(solution)/shard_map/ppermute | solution.py:180
  25.6 8.5 %collective-permute-start.8 = (bf16[144,768]{1,0:T(8,128)(2,1)S(1)}, bf16[144,768]{1,0:T(8,128)(2,1)S(1)}, u32[]{:S(2)}, u32[]{:S(2)}) collective-permute-start(bf16[144,768]{1,0:T(8,128)(2,1)S(1)} %collective-permute-done.1.a_ref), channel_id=1, source_target_pairs={{0,4},{1,5},{4,8},{5,9},{8,12},{9,13},{12,14},{13,15},{14,10},{15,... | collective-permute-start | bytes 663560 | tf_op jit(solution)/shard_map/ppermute | solution.py:180
  28.3 8.4 %collective-permute-start.13 = (bf16[144,768]{1,0:T(8,128)(2,1)S(1)}, bf16[144,768]{1,0:T(8,128)(2,1)S(1)}, u32[]{:S(2)}, u32[]{:S(2)}) collective-permute-start(bf16[144,768]{1,0:T(8,128)(2,1)S(1)} %collective-permute-done.11.a_ref), channel_id=1, source_target_pairs={{4,0},{5,1},{8,4},{9,5},{12,8},{13,9},{14,12},{15,13},{10,14},{11,... | collective-permute-start | bytes 663560 | tf_op jit(solution)/shard_map/ppermute | solution.py:180
  31.9 8.2 %collective-permute-start.14 = (bf16[128,768]{1,0:T(8,128)(2,1)S(1)}, bf16[128,768]{1,0:T(8,128)(2,1)S(1)}, u32[]{:S(2)}, u32[]{:S(2)}) collective-permute-start(bf16[128,768]{1,0:T(8,128)(2,1)S(1)} %collective-permute-done.9.b_ref), channel_id=1, source_target_pairs={{4,0},{5,1},{8,4},{9,5},{12,8},{13,9},{14,12},{15,13},{10,14},{11,... | collective-permute-start | bytes 589832 | tf_op jit(solution)/shard_map/ppermute | solution.py:180
  34.1 7.0 %collective-permute-start.12 = (bf16[144,768]{1,0:T(8,128)(2,1)S(1)}, bf16[144,768]{1,0:T(8,128)(2,1)S(1)}, u32[]{:S(2)}, u32[]{:S(2)}) collective-permute-start(bf16[144,768]{1,0:T(8,128)(2,1)S(1)} %collective-permute-done.8.a_ref), channel_id=1, source_target_pairs={{0,4},{1,5},{4,8},{5,9},{8,12},{9,13},{12,14},{13,15},{14,10},{15,... | collective-permute-start | bytes 663560 | tf_op jit(solution)/shard_map/ppermute | solution.py:180
  42.4 2.4 %copy-start.2 = (f32[256,768]{1,0:T(8,128)S(1)}, f32[256,768]{1,0:T(8,128)}, u32[]{:S(2)}) copy-start(f32[256,768]{1,0:T(8,128)} %param.11) | copy-start | bytes 2359300
  42.4 2.4 %copy-start.3 = (f32[256,768]{1,0:T(8,128)S(1)}, f32[256,768]{1,0:T(8,128)}, u32[]{:S(2)}) copy-start(f32[256,768]{1,0:T(8,128)} %param.12) | copy-start | bytes 2359300
  42.4 2.4 %copy-start.4 = (f32[256,768]{1,0:T(8,128)S(1)}, f32[256,768]{1,0:T(8,128)}, u32[]{:S(2)}) copy-start(f32[256,768]{1,0:T(8,128)} %param.13) | copy-start | bytes 2359300
  42.4 2.4 %collective-permute-start.15 = (f32[256,768]{1,0:T(8,128)S(1)}, f32[256,768]{1,0:T(8,128)S(1)}, u32[]{:S(2)}, u32[]{:S(2)}) collective-permute-start(f32[256,768]{1,0:T(8,128)S(1)} %gradient.31), channel_id=1, source_target_pairs={{0,1},{1,0},{2,3},{3,2},{4,5},{5,4},{6,7},{7,6},{8,9},{9,8},{10,11... | collective-permute-start | bytes 2359304 | tf_op jit(solution)/shard_map/ppermute | solution.py:180

commit v7 on v6

--- a/solution.py
+++ b/solution.py
@@ -18,6 +18,9 @@
 WORD = 32
 LANES = 128
 VMEM_LIMIT = 32 * 1024 * 1024
+FLOPS = 5 * 10**8
+LATE_FLOPS = 10 * 10**8
+END_FLOPS = 40 * 10**8
 
 
 def power_of_two(exponent, bits, start, sign):
@@ -28,7 +31,7 @@
     return value
 
 
-def lookup_kernel(bits, ids_ref, count_ref, table_ref, docs_ref, out_ref):
+def lookup_kernel(bits, ids_ref, count_ref, table_ref, docs_ref, weights_ref, out_ref, cast_ref):
     slots, docs = ids_ref.shape
     pairs = table_ref.shape[0] // 2
     starts = range(0, docs, LANES)
@@ -62,16 +65,21 @@
         code = code.astype(jnp.bfloat16)
         out_ref[head:, start : start + LANES] = code[: slots // 2]
         out_ref[head:, docs + start : docs + start + LANES] = code[slots // 2 :]
-
-
-def lookup_rows(label_slot, pos_ids, pos_count, embeddings, head):
+    cast_ref[...] = weights_ref[...].astype(jnp.bfloat16) * 0.5
+
+
+def lookup_rows(label_slot, pos_ids, pos_count, embeddings, weights, head):
     docs, slots = pos_ids.shape
     lines = label_slot.shape[0] // LANES
     return pl.pallas_call(
         functools.partial(lookup_kernel, (lines - 1).bit_length()),
-        out_shape=jax.ShapeDtypeStruct((head + slots // 2, embeddings.shape[1]), jnp.bfloat16),
+        out_shape=[
+            jax.ShapeDtypeStruct((head + slots // 2, embeddings.shape[1]), jnp.bfloat16),
+            jax.ShapeDtypeStruct(weights.shape, jnp.bfloat16),
+        ],
+        compiler_params=pltpu.CompilerParams(vmem_limit_bytes=VMEM_LIMIT),
         name="lookup",
-    )(pos_ids.T, pos_count.reshape(1, docs), label_slot.reshape(lines, LANES), embeddings)
+    )(pos_ids.T, pos_count.reshape(1, docs), label_slot.reshape(lines, LANES), embeddings, weights)
 
 
 def signs_of(codes, owner, bits, height):
@@ -181,39 +189,33 @@
 
     b = embeddings[head:]
     coming = {"up_b": send(b, up), "down_b": send(b, down)}
-    a = lookup_rows(label_slot, pos_ids, pos_count, embeddings, head)
+    a, mine = lookup_rows(label_slot, pos_ids, pos_count, embeddings, weights, head)
     coming |= {"up_a": send(a, up), "down_a": send(a, down)}
-    mine = weights.astype(jnp.bfloat16) * 0.5
-    other = send(mine, swap)
-    sums = [(), ()]
-
-    def work(owner, docs, flops):
-        weights_of = [(mine, other)[owner]]
-        sums[owner] = add_gradient(bits, (owner,), *docs, weights_of, sums[owner], flops)
-
-    waiting = [(0, ()), (0, ()), (0, ()), (0, (a, b)), (1, (a, b))]
-    for step in range(1, half_way + 1):
-        messages = ["up_b", "down_b", "up_a", "down_a"] if step < half_way else ["down_b", "up_a"]
-        passed_on = messages if step < half_way - 1 else ["down_b", "up_a"]
-        while step == half_way and len(waiting) > len(messages):
-            work(*waiting.pop(0), 3 * 10**8)
-        flops = 6 * 10**8 if step < half_way - 1 else 5 * 10**8
+    cast = [mine, send(mine, swap)]
+    sums = ()
+    waiting = [(a, b)]
+    for step in range(1, half_way):
         came = {}
-        for message in messages:
-            owner, docs = waiting.pop(0)
-            came[message], docs, sums = together((coming[message], docs, sums))
-            if step < half_way and message in passed_on:
+        for message in ("up_b", "down_b", "up_a", "down_a"):
+            came[message], waiting, sums = together((coming.pop(message), waiting, sums))
+            if step < half_way - 1 or message in ("down_b", "up_a"):
                 coming[message] = send(came[message], up if message in ("up_a", "up_b") else down)
-            if docs:
-                work(owner, docs, flops)
-        if step < half_way:
-            for docs in ((came["up_a"], came["up_b"]), (came["down_a"], came["down_b"])):
-                waiting += [(0, docs), (1, docs)]
-    docs = (came["up_a"], came["down_b"])
-    work(1, docs, 3 * 10**8)
-    got = send(sums[1][0], swap)
-    work(0, docs, 3 * 10**8)
-    return adam_step(weights, first_moment, second_moment, 0.5 * (sums[0][0] + got))
+            if (step > 1 and message in ("down_b", "up_a")) or (step == 2 and message == "down_a"):
+                flops = FLOPS if step < half_way - 1 else LATE_FLOPS
+                sums = add_gradient(bits, (0, 1), *waiting.pop(0), cast, sums, flops)
+        waiting += [(came["up_a"], came["up_b"]), (came["down_a"], came["down_b"])]
+    for docs in waiting:
+        sums = add_gradient(bits, (0, 1), *docs, cast, sums, FLOPS)
+    mine_sum, other_sum = sums
+    got = send(other_sum, swap)
+    last_b, mine_sum = together((coming["down_b"], mine_sum))
+    beside_b = send(last_b, swap)
+    last_a, mine_sum = together((coming["up_a"], mine_sum))
+    beside_a = send(last_a, swap)
+    mine_sum = add_gradient(bits, (0,), last_a, last_b, [mine], [mine_sum], END_FLOPS)
+    beside_a, beside_b, mine_sum = together((beside_a, beside_b, mine_sum))
+    (mine_sum,) = add_gradient(bits, (0,), beside_a, beside_b, [mine], mine_sum, END_FLOPS)
+    return adam_step(weights, first_moment, second_moment, 0.5 * (mine_sum + got))
 
 
 def solution(mesh):

time: 46.8 us -> 45.5 us (0.972)
  Pallas kernels: 12.7 us -> 8.86 us
  local copies, waits for them, and re-layouts: 1.9 us -> 4.65 us
  waiting for transfers between devices: 11.9 us -> 13.1 us
  other arithmetic: 3.01 us -> 1.83 us
    unnamed x10 -> x16, local copies, waits for them, and re-layouts: 0.96 us -> 3.65 us
    pallas_call x16 -> x9, Pallas kernels: 10.5 us -> 8.38 us  [add_gradient(): pl.pallas_call(functools.partial(gradient_kernel, bits, owners, not sums)...]
    pallas_call x1, Pallas kernels: 2.18 us -> 0.48 us  [lookup_rows(): pl.pallas_call(functools.partial(lookup_kernel, (lines - 1).bit_length())...]
    ppermute x16 -> x18, waiting for transfers between devices: 11.9 us -> 13.1 us  [send(): return lax.ppermute(value, 'blk', pairs)]
    mul x1 -> x0, other arithmetic: 1.18 us -> none  [per_device(): mine = weights.astype(jnp.bfloat16) * 0.5]
    ppermute x16 -> x18, starting transfers between devices: 16.3 us -> 15.9 us  [send(): return lax.ppermute(value, 'blk', pairs)]
  transfers between devices with their start and end apart: 16 -> 18, of which waited for: 11 -> 10; matrix products, arithmetic and copies ran while one was open for 3% -> 0% of each run, Pallas kernels for 24% -> 20%
where the time goes in v7:
time: 45.5 us; the launch traced here: 45.2 us
  starting transfers between devices  15.9 us (35%)
  waiting for transfers between devices  13.1 us (29%)
  Pallas kernels  8.86 us (19%)
  local copies, waits for them, and re-layouts  4.65 us (10%)
  other arithmetic  1.83 us (4%)
  between operations  0.79 us (2%)
    ppermute x18, starting transfers between devices, send(): return lax.ppermute(value, 'blk', pairs)  15.9 us
    ppermute x18, waiting for transfers between devices, send(): return lax.ppermute(value, 'blk', pairs)  13.1 us
    pallas_call x9, Pallas kernels, add_gradient(): pl.pallas_call(functools.partial(gradient_kernel, bits, owners, not sums)...  8.38 us
    unnamed x16, local copies, waits for them, and re-layouts  3.65 us
    sub x1, other arithmetic, adam_step(): new_weights = weights - learn_rate * (update + decay_rate * weights)  1.83 us
    slice x1, local copies, waits for them, and re-layouts, per_device(): b = embeddings[head:]  1 us
  transfers between devices with their start and end apart: 18, of which 10 were waited for; matrix products, arithmetic and copies ran while one was open for 0% of the time, Pallas kernels for 20%

profile of v7, /device:TPU:0, one launch (start us, length us, event | category | flops | bytes accessed | tf_op | source)
XLA Modules:
  0.0 45.2 jit_solution(5613888411816920219)
XLA Ops:
  0.6 1.0 %slice.3.b_ref = bf16[128,768]{1,0:T(8,128)(2,1)S(1)} slice(bf16[256,768]{1,0:T(8,128)(2,1)} %docs_ref.1), slice={[128:256], [0:768]} | slice | bytes 393216 | tf_op jit(solution)/shard_map/slice | solution.py:190
  1.6 3.1 %collective-permute-start.2 = (bf16[128,768]{1,0:T(8,128)(2,1)S(1)}, bf16[128,768]{1,0:T(8,128)(2,1)S(1)}, u32[]{:S(2)}, u32[]{:S(2)}) collective-permute-start(bf16[128,768]{1,0:T(8,128)(2,1)S(1)} %slice.3.b_ref), channel_id=1, source_target_pairs={{0,4},{1,5},{4,8},{5,9},{8,12},{9,13},{12,14},{13,15},{14,10},{15,... | collective-permute-start | bytes 589832 | tf_op jit(solution)/shard_map/ppermute | solution.py:188
  4.7 0.7 %copy-done.5 = s32[256]{0:T(256)S(1)} copy-done((s32[256]{0:T(256)S(1)}, s32[256]{0:T(256)}, u32[]{:S(2)}) %copy-start.5) | copy-done | bytes 1048
  5.4 1.1 %copy-done = f32[256,768]{1,0:T(8,128)S(1)} copy-done((f32[256,768]{1,0:T(8,128)S(1)}, f32[256,768]{1,0:T(8,128)}, u32[]{:S(2)}) %copy-start) | copy-done | bytes 786456
  6.5 0.8 %copy-done.3 = s32[256,32]{0,1:T(8,128)S(1)} copy-done((s32[256,32]{0,1:T(8,128)S(1)}, s32[256,32]{0,1:T(8,128)}, u32[]{:S(2)}) %copy-start.3) | copy-done | bytes 32792
  7.3 0.7 %copy-done.4 = s32[4096]{0:T(1024)S(1)} copy-done((s32[4096]{0:T(1024)S(1)}, s32[4096]{0:T(1024)}, u32[]{:S(2)}) %copy-start.4) | copy-done | bytes 16408
  8.0 0.5 %lookup.1 = (bf16[144,768]{1,0:T(8,128)(2,1)S(1)}, bf16[256,768]{1,0:T(8,128)(2,1)S(1)}) custom-call(s32[32,256]{1,0:T(8,128)S(1)} %bitcast.3, s32[1,256]{1,0:T(1,128)S(1)} %bitcast.5, s32[32,128]{1,0:T(8,128)S(1)} %bitcast.4, bf16[256,768]{1,0:T(8,128)(2,1)S(1)} %copy-done.2, f32[256,768]{1,0:T(8,128)S(1)} %copy-done), custom_call_target="tpu_custom_call" | custom-call | tf_op jit(solution)/shard_map/lookup/pallas_call | solution.py:74
  8.5 2.1 %collective-permute-start = (bf16[144,768]{1,0:T(8,128)(2,1)S(1)}, bf16[144,768]{1,0:T(8,128)(2,1)S(1)}, u32[]{:S(2)}, u32[]{:S(2)}) collective-permute-start(bf16[144,768]{1,0:T(8,128)(2,1)S(1)} %get-tuple-element.109.a_ref), channel_id=1, source_target_pairs={{0,4},{1,5},{4,8},{5,9},{8,12},{9,13},{12,14},{13,15},{14,10},{15,... | collective-permute-start | bytes 663560 | tf_op jit(solution)/shard_map/ppermute | solution.py:188
  10.7 1.9 %collective-permute-start.5 = (bf16[128,768]{1,0:T(8,128)(2,1)S(1)}, bf16[128,768]{1,0:T(8,128)(2,1)S(1)}, u32[]{:S(2)}, u32[]{:S(2)}) collective-permute-start(bf16[128,768]{1,0:T(8,128)(2,1)S(1)} %collective-permute-done.2.b_ref), channel_id=1, source_target_pairs={{0,4},{1,5},{4,8},{5,9},{8,12},{9,13},{12,14},{13,15},{14,10},{15,... | collective-permute-start | bytes 589832 | tf_op jit(solution)/shard_map/ppermute | solution.py:188
  12.7 4.2 %collective-permute-done.a_ref = bf16[144,768]{1,0:T(8,128)(2,1)S(1)} collective-permute-done((bf16[144,768]{1,0:T(8,128)(2,1)S(1)}, bf16[144,768]{1,0:T(8,128)(2,1)S(1)}, u32[]{:S(2)}, u32[]{:S(2)}) %collective-permute-start) | collective-permute-done | bytes 221216 | tf_op jit(solution)/shard_map/ppermute | solution.py:188
  16.9 2.0 %collective-permute-start.3 = (bf16[144,768]{1,0:T(8,128)(2,1)S(1)}, bf16[144,768]{1,0:T(8,128)(2,1)S(1)}, u32[]{:S(2)}, u32[]{:S(2)}) collective-permute-start(bf16[144,768]{1,0:T(8,128)(2,1)S(1)} %collective-permute-done.a_ref), channel_id=1, source_target_pairs={{0,4},{1,5},{4,8},{5,9},{8,12},{9,13},{12,14},{13,15},{14,10},{15,... | collective-permute-start | bytes 663560 | tf_op jit(solution)/shard_map/ppermute | solution.py:188
  19.0 2.2 %collective-permute-done.5.b_ref = bf16[128,768]{1,0:T(8,128)(2,1)S(1)} collective-permute-done((bf16[128,768]{1,0:T(8,128)(2,1)S(1)}, bf16[128,768]{1,0:T(8,128)(2,1)S(1)}, u32[]{:S(2)}, u32[]{:S(2)}) %collective-permute-start.5) | collective-permute-done | bytes 196640 | tf_op jit(solution)/shard_map/ppermute | solution.py:188
  21.1 2.0 %collective-permute-start.10 = (bf16[128,768]{1,0:T(8,128)(2,1)S(1)}, bf16[128,768]{1,0:T(8,128)(2,1)S(1)}, u32[]{:S(2)}, u32[]{:S(2)}) collective-permute-start(bf16[128,768]{1,0:T(8,128)(2,1)S(1)} %collective-permute-done.5.b_ref), channel_id=1, source_target_pairs={{0,4},{1,5},{4,8},{5,9},{8,12},{9,13},{12,14},{13,15},{14,10},{15,... | collective-permute-start | bytes 589832 | tf_op jit(solution)/shard_map/ppermute | solution.py:188
  23.2 1.0 %gradient.9 = (f32[256,768]{1,0:T(8,128)S(1)}, f32[256,768]{1,0:T(8,128)S(1)}) custom-call(bf16[144,768]{1,0:T(8,128)(2,1)S(1)} %get-tuple-element.109.a_ref, bf16[128,768]{1,0:T(8,128)(2,1)S(1)} %slice.3.b_ref, bf16[256,768]{1,0:T(8,128)(2,1)S(1)} %get-tuple-element.111.refs_0_, bf16[256,768]{1,0:T(8,128)(2,1)S(1)} %collective-permute-done.7.refs_1_), custom_call_target="tpu_custom_call" | custom-call | flops 500000000 | bytes 1000000 | tf_op jit(solution)/shard_map/gradient/pallas_call | solution.py:138
  24.2 1.7 %collective-permute-done.3.a_ref = bf16[144,768]{1,0:T(8,128)(2,1)S(1)} collective-permute-done((bf16[144,768]{1,0:T(8,128)(2,1)S(1)}, bf16[144,768]{1,0:T(8,128)(2,1)S(1)}, u32[]{:S(2)}, u32[]{:S(2)}) %collective-permute-start.3) | collective-permute-done | bytes 221216 | tf_op jit(solution)/shard_map/ppermute | solution.py:188
  25.9 2.0 %collective-permute-start.8 = (bf16[144,768]{1,0:T(8,128)(2,1)S(1)}, bf16[144,768]{1,0:T(8,128)(2,1)S(1)}, u32[]{:S(2)}, u32[]{:S(2)}) collective-permute-start(bf16[144,768]{1,0:T(8,128)(2,1)S(1)} %collective-permute-done.3.a_ref), channel_id=1, source_target_pairs={{0,4},{1,5},{4,8},{5,9},{8,12},{9,13},{12,14},{13,15},{14,10},{15,... | collective-permute-start | bytes 663560 | tf_op jit(solution)/shard_map/ppermute | solution.py:188
  27.9 1.0 %gradient.10 = (f32[256,768]{1,0:T(8,128)S(1)}, f32[256,768]{1,0:T(8,128)S(1)}) custom-call(bf16[144,768]{1,0:T(8,128)(2,1)S(1)} %collective-permute-done.a_ref, bf16[128,768]{1,0:T(8,128)(2,1)S(1)} %collective-permute-done.2.b_ref, bf16[256,768]{1,0:T(8,128)(2,1)S(1)} %get-tuple-element.111.refs_0_, ...), custom_call_target="tpu_custom_call", output_to_operand_aliasing={{0}: (4, {}), {1}: (5, {})} | custom-call | flops 500000000 | bytes 1000000 | tf_op jit(solution)/shard_map/gradient/pallas_call | solution.py:138
  29.0 1.0 %gradient.11 = (f32[256,768]{1,0:T(8,128)S(1)}, f32[256,768]{1,0:T(8,128)S(1)}) custom-call(bf16[144,768]{1,0:T(8,128)(2,1)S(1)} %collective-permute-done.6.a_ref, bf16[128,768]{1,0:T(8,128)(2,1)S(1)} %collective-permute-done.1.b_ref, bf16[256,768]{1,0:T(8,128)(2,1)S(1)} %get-tuple-element.111.refs_0_, ...), custom_call_target="tpu_custom_call", output_to_operand_aliasing={{0}: (4, {}), {1}: (5, {})} | custom-call | flops 500000000 | bytes 1000000 | tf_op jit(solution)/shard_map/gradient/pallas_call | solution.py:138
  30.1 1.9 %collective-permute-done.9.b_ref = bf16[128,768]{1,0:T(8,128)(2,1)S(1)} collective-permute-done((bf16[128,768]{1,0:T(8,128)(2,1)S(1)}, bf16[128,768]{1,0:T(8,128)(2,1)S(1)}, u32[]{:S(2)}, u32[]{:S(2)}) %collective-permute-start.9) | collective-permute-done | bytes 196640 | tf_op jit(solution)/shard_map/ppermute | solution.py:188
  32.1 1.0 %gradient.12 = (f32[256,768]{1,0:T(8,128)S(1)}, f32[256,768]{1,0:T(8,128)S(1)}) custom-call(bf16[144,768]{1,0:T(8,128)(2,1)S(1)} %collective-permute-done.3.a_ref, bf16[128,768]{1,0:T(8,128)(2,1)S(1)} %collective-permute-done.5.b_ref, bf16[256,768]{1,0:T(8,128)(2,1)S(1)} %get-tuple-element.111.refs_0_, ...), custom_call_target="tpu_custom_call", output_to_operand_aliasing={{0}: (4, {}), {1}: (5, {})} | custom-call | flops 1000000000 | bytes 1000000 | tf_op jit(solution)/shard_map/gradient/pallas_call | solution.py:138
  33.4 1.7 %collective-permute-start.12 = (bf16[144,768]{1,0:T(8,128)(2,1)S(1)}, bf16[144,768]{1,0:T(8,128)(2,1)S(1)}, u32[]{:S(2)}, u32[]{:S(2)}) collective-permute-start(bf16[144,768]{1,0:T(8,128)(2,1)S(1)} %collective-permute-done.8.a_ref), channel_id=1, source_target_pairs={{0,4},{1,5},{4,8},{5,9},{8,12},{9,13},{12,14},{13,15},{14,10},{15,... | collective-permute-start | bytes 663560 | tf_op jit(solution)/shard_map/ppermute | solution.py:188
  35.1 1.0 %gradient.13 = (f32[256,768]{1,0:T(8,128)S(1)}, f32[256,768]{1,0:T(8,128)S(1)}) custom-call(bf16[144,768]{1,0:T(8,128)(2,1)S(1)} %collective-permute-done.11.a_ref, bf16[128,768]{1,0:T(8,128)(2,1)S(1)} %collective-permute-done.4.b_ref, bf16[256,768]{1,0:T(8,128)(2,1)S(1)} %get-tuple-element.111.refs_0_, ...), custom_call_target="tpu_custom_call", output_to_operand_aliasing={{0}: (4, {}), {1}: (5, {})} | custom-call | flops 1000000000 | bytes 1000000 | tf_op jit(solution)/shard_map/gradient/pallas_call | solution.py:138
  36.1 1.2 %collective-permute-done.14.a_ref = bf16[144,768]{1,0:T(8,128)(2,1)S(1)} collective-permute-done((bf16[144,768]{1,0:T(8,128)(2,1)S(1)}, bf16[144,768]{1,0:T(8,128)(2,1)S(1)}, u32[]{:S(2)}, u32[]{:S(2)}) %collective-permute-start.14) | collective-permute-done | bytes 221216 | tf_op jit(solution)/shard_map/ppermute | solution.py:188
  37.3 1.0 %gradient.14 = (f32[256,768]{1,0:T(8,128)S(1)}, f32[256,768]{1,0:T(8,128)S(1)}) custom-call(bf16[144,768]{1,0:T(8,128)(2,1)S(1)} %collective-permute-done.8.a_ref, bf16[128,768]{1,0:T(8,128)(2,1)S(1)} %collective-permute-done.10.b_ref, bf16[256,768]{1,0:T(8,128)(2,1)S(1)} %get-tuple-element.111.refs_0_, ...), custom_call_target="tpu_custom_call", output_to_operand_aliasing={{0}: (4, {}), {1}: (5, {})} | custom-call | flops 500000000 | bytes 1000000 | tf_op jit(solution)/shard_map/gradient/pallas_call | solution.py:138
  38.3 1.0 %gradient.15 = (f32[256,768]{1,0:T(8,128)S(1)}, f32[256,768]{1,0:T(8,128)S(1)}) custom-call(bf16[144,768]{1,0:T(8,128)(2,1)S(1)} %collective-permute-done.14.a_ref, bf16[128,768]{1,0:T(8,128)(2,1)S(1)} %collective-permute-done.9.b_ref, bf16[256,768]{1,0:T(8,128)(2,1)S(1)} %get-tuple-element.111.refs_0_, ...), custom_call_target="tpu_custom_call", output_to_operand_aliasing={{0}: (4, {}), {1}: (5, {})} | custom-call | flops 500000000 | bytes 1000000 | tf_op jit(solution)/shard_map/gradient/pallas_call | solution.py:138
  39.4 1.1 %collective-permute-done.13.b_ref = bf16[128,768]{1,0:T(8,128)(2,1)S(1)} collective-permute-done((bf16[128,768]{1,0:T(8,128)(2,1)S(1)}, bf16[128,768]{1,0:T(8,128)(2,1)S(1)}, u32[]{:S(2)}, u32[]{:S(2)}) %collective-permute-start.13) | collective-permute-done | bytes 196640 | tf_op jit(solution)/shard_map/ppermute | solution.py:188
  40.5 0.5 %collective-permute-start.15 = (bf16[144,768]{1,0:T(8,128)(2,1)S(1)}, bf16[144,768]{1,0:T(8,128)(2,1)S(1)}, u32[]{:S(2)}, u32[]{:S(2)}) collective-permute-start(bf16[144,768]{1,0:T(8,128)(2,1)S(1)} %collective-permute-done.12.a_ref), channel_id=1, source_target_pairs={{0,1},{1,0},{2,3},{3,2},{4,5},{5,4},{6,7},{7,6},{8,9},{9,8},{10,11... | collective-permute-start | bytes 663560 | tf_op jit(solution)/shard_map/ppermute | solution.py:188
  41.1 0.7 %gradient.16.refs_1_ = f32[256,768]{1,0:T(8,128)S(1)} custom-call(bf16[144,768]{1,0:T(8,128)(2,1)S(1)} %collective-permute-done.12.a_ref, bf16[128,768]{1,0:T(8,128)(2,1)S(1)} %collective-permute-done.13.b_ref, bf16[256,768]{1,0:T(8,128)(2,1)S(1)} %get-tuple-element.111.refs_0_, ...), custom_call_target="tpu_custom_call", output_to_operand_aliasing={{}: (3, {})} | custom-call | flops 4000000000 | bytes 1000000 | tf_op jit(solution)/shard_map/gradient/pallas_call | solution.py:138
  42.0 0.3 collective-permute-done.15.a_ref
  42.3 0.7 %gradient.17 = f32[256,768]{1,0:T(8,128)S(1)} custom-call(bf16[144,768]{1,0:T(8,128)(2,1)S(1)} %collective-permute-done.15.a_ref, bf16[128,768]{1,0:T(8,128)(2,1)S(1)} %collective-permute-done.16.b_ref, bf16[256,768]{1,0:T(8,128)(2,1)S(1)} %get-tuple-element.111.refs_0_, f32[256,768]{1,0:T(8,128)S(1)} %gradient.16.refs_1_), custom_call_target="tpu_custom_call", output_to_operand_aliasing={{}: (3, {})} | custom-call | flops 4000000000 | bytes 1000000 | tf_op jit(solution)/shard_map/gradient/pallas_call | solution.py:138
  43.1 0.2 copy-done.7
  43.3 1.8 %multiply_subtract_fusion = (f32[256,768]{1,0:T(8,128)}, f32[256,768]{1,0:T(8,128)}, f32[256,768]{1,0:T(8,128)}) fusion(f32[256,768]{1,0:T(8,128)S(1)} %copy-done.1, f32[256,768]{1,0:T(8,128)S(1)} %gradient.17, f32[256,768]{1,0:T(8,128)S(1)} %collective-permute-done.17, f32[256,768]{1,0:T(8,128)S(1)} %copy-done.6, f32[256,768]{1,0:T(8,128)S(1)} %copy-done.7), kind=kLoop, calls=%fused_computation | loop fusion | flops 3342336 | bytes 6291456 | tf_op jit(solution)/shard_map/sub | solution.py:154
  (32 shorter events, 1.3 us)
Async XLA Ops:
  0.6 4.1 %copy-start.2 = (bf16[256,768]{1,0:T(8,128)(2,1)S(1)}, bf16[256,768]{1,0:T(8,128)(2,1)}, u32[]{:S(2)}) copy-start(bf16[256,768]{1,0:T(8,128)(2,1)} %docs_ref.1) | copy-start | bytes 1179652
  1.6 9.0 %collective-permute-start.2 = (bf16[128,768]{1,0:T(8,128)(2,1)S(1)}, bf16[128,768]{1,0:T(8,128)(2,1)S(1)}, u32[]{:S(2)}, u32[]{:S(2)}) collective-permute-start(bf16[128,768]{1,0:T(8,128)(2,1)S(1)} %slice.3.b_ref), channel_id=1, source_target_pairs={{0,4},{1,5},{4,8},{5,9},{8,12},{9,13},{12,14},{13,15},{14,10},{15,... | collective-permute-start | bytes 589832 | tf_op jit(solution)/shard_map/ppermute | solution.py:188
  4.7 7.9 %collective-permute-start.1 = (bf16[128,768]{1,0:T(8,128)(2,1)S(1)}, bf16[128,768]{1,0:T(8,128)(2,1)S(1)}, u32[]{:S(2)}, u32[]{:S(2)}) collective-permute-start(bf16[128,768]{1,0:T(8,128)(2,1)S(1)} %slice.3.b_ref), channel_id=1, source_target_pairs={{4,0},{5,1},{8,4},{9,5},{12,8},{13,9},{14,12},{15,13},{10,14},{11,... | collective-permute-start | bytes 589832 | tf_op jit(solution)/shard_map/ppermute | solution.py:188
  4.7 0.7 %copy-start.5 = (s32[256]{0:T(256)S(1)}, s32[256]{0:T(256)}, u32[]{:S(2)}) copy-start(s32[256]{0:T(256)} %param.9) | copy-start | bytes 3076
  5.4 1.1 %copy-start = (f32[256,768]{1,0:T(8,128)S(1)}, f32[256,768]{1,0:T(8,128)}, u32[]{:S(2)}) copy-start(f32[256,768]{1,0:T(8,128)} %weights_ref.1) | copy-start | bytes 2359300
  6.5 0.8 %copy-start.3 = (s32[256,32]{0,1:T(8,128)S(1)}, s32[256,32]{0,1:T(8,128)}, u32[]{:S(2)}) copy-start(s32[256,32]{0,1:T(8,128)} %param.8) | copy-start | bytes 98308
  7.3 0.7 %copy-start.4 = (s32[4096]{0:T(1024)S(1)}, s32[4096]{0:T(1024)}, u32[]{:S(2)}) copy-start(s32[4096]{0:T(1024)} %param.10) | copy-start | bytes 49156
  8.5 8.4 %collective-permute-start = (bf16[144,768]{1,0:T(8,128)(2,1)S(1)}, bf16[144,768]{1,0:T(8,128)(2,1)S(1)}, u32[]{:S(2)}, u32[]{:S(2)}) collective-permute-start(bf16[144,768]{1,0:T(8,128)(2,1)S(1)} %get-tuple-element.109.a_ref), channel_id=1, source_target_pairs={{0,4},{1,5},{4,8},{5,9},{8,12},{9,13},{12,14},{13,15},{14,10},{15,... | collective-permute-start | bytes 663560 | tf_op jit(solution)/shard_map/ppermute | solution.py:188
  10.6 12.6 %collective-permute-start.7 = (bf16[256,768]{1,0:T(8,128)(2,1)S(1)}, bf16[256,768]{1,0:T(8,128)(2,1)S(1)}, u32[]{:S(2)}, u32[]{:S(2)}) collective-permute-start(bf16[256,768]{1,0:T(8,128)(2,1)S(1)} %get-tuple-element.111.refs_0_), channel_id=1, source_target_pairs={{0,1},{1,0},{2,3},{3,2},{4,5},{5,4},{6,7},{7,6},{8,9},{9,8},{10,11... | collective-permute-start | bytes 1179656 | tf_op jit(solution)/shard_map/ppermute | solution.py:188
  10.6 8.3 %collective-permute-start.6 = (bf16[144,768]{1,0:T(8,128)(2,1)S(1)}, bf16[144,768]{1,0:T(8,128)(2,1)S(1)}, u32[]{:S(2)}, u32[]{:S(2)}) collective-permute-start(bf16[144,768]{1,0:T(8,128)(2,1)S(1)} %get-tuple-element.109.a_ref), channel_id=1, source_target_pairs={{4,0},{5,1},{8,4},{9,5},{12,8},{13,9},{14,12},{15,13},{10,14},{11,... | collective-permute-start | bytes 663560 | tf_op jit(solution)/shard_map/ppermute | solution.py:188
  10.7 10.5 %collective-permute-start.5 = (bf16[128,768]{1,0:T(8,128)(2,1)S(1)}, bf16[128,768]{1,0:T(8,128)(2,1)S(1)}, u32[]{:S(2)}, u32[]{:S(2)}) collective-permute-start(bf16[128,768]{1,0:T(8,128)(2,1)S(1)} %collective-permute-done.2.b_ref), channel_id=1, source_target_pairs={{0,4},{1,5},{4,8},{5,9},{8,12},{9,13},{12,14},{13,15},{14,10},{15,... | collective-permute-start | bytes 589832 | tf_op jit(solution)/shard_map/ppermute | solution.py:188
  12.6 10.5 %collective-permute-start.4 = (bf16[128,768]{1,0:T(8,128)(2,1)S(1)}, bf16[128,768]{1,0:T(8,128)(2,1)S(1)}, u32[]{:S(2)}, u32[]{:S(2)}) collective-permute-start(bf16[128,768]{1,0:T(8,128)(2,1)S(1)} %collective-permute-done.1.b_ref), channel_id=1, source_target_pairs={{4,0},{5,1},{8,4},{9,5},{12,8},{13,9},{14,12},{15,13},{10,14},{11,... | collective-permute-start | bytes 589832 | tf_op jit(solution)/shard_map/ppermute | solution.py:188
  16.9 9.0 %collective-permute-start.3 = (bf16[144,768]{1,0:T(8,128)(2,1)S(1)}, bf16[144,768]{1,0:T(8,128)(2,1)S(1)}, u32[]{:S(2)}, u32[]{:S(2)}) collective-permute-start(bf16[144,768]{1,0:T(8,128)(2,1)S(1)} %collective-permute-done.a_ref), channel_id=1, source_target_pairs={{0,4},{1,5},{4,8},{5,9},{8,12},{9,13},{12,14},{13,15},{14,10},{15,... | collective-permute-start | bytes 663560 | tf_op jit(solution)/shard_map/ppermute | solution.py:188
  18.9 10.0 %collective-permute-start.11 = (bf16[144,768]{1,0:T(8,128)(2,1)S(1)}, bf16[144,768]{1,0:T(8,128)(2,1)S(1)}, u32[]{:S(2)}, u32[]{:S(2)}) collective-permute-start(bf16[144,768]{1,0:T(8,128)(2,1)S(1)} %collective-permute-done.6.a_ref), channel_id=1, source_target_pairs={{4,0},{5,1},{8,4},{9,5},{12,8},{13,9},{14,12},{15,13},{10,14},{11,... | collective-permute-start | bytes 663560 | tf_op jit(solution)/shard_map/ppermute | solution.py:188
  21.1 9.0 %collective-permute-start.10 = (bf16[128,768]{1,0:T(8,128)(2,1)S(1)}, bf16[128,768]{1,0:T(8,128)(2,1)S(1)}, u32[]{:S(2)}, u32[]{:S(2)}) collective-permute-start(bf16[128,768]{1,0:T(8,128)(2,1)S(1)} %collective-permute-done.5.b_ref), channel_id=1, source_target_pairs={{0,4},{1,5},{4,8},{5,9},{8,12},{9,13},{12,14},{13,15},{14,10},{15,... | collective-permute-start | bytes 589832 | tf_op jit(solution)/shard_map/ppermute | solution.py:188
  23.1 8.9 %collective-permute-start.9 = (bf16[128,768]{1,0:T(8,128)(2,1)S(1)}, bf16[128,768]{1,0:T(8,128)(2,1)S(1)}, u32[]{:S(2)}, u32[]{:S(2)}) collective-permute-start(bf16[128,768]{1,0:T(8,128)(2,1)S(1)} %collective-permute-done.4.b_ref), channel_id=1, source_target_pairs={{4,0},{5,1},{8,4},{9,5},{12,8},{13,9},{14,12},{15,13},{10,14},{11,... | collective-permute-start | bytes 589832 | tf_op jit(solution)/shard_map/ppermute | solution.py:188
  25.9 7.5 %collective-permute-start.8 = (bf16[144,768]{1,0:T(8,128)(2,1)S(1)}, bf16[144,768]{1,0:T(8,128)(2,1)S(1)}, u32[]{:S(2)}, u32[]{:S(2)}) collective-permute-start(bf16[144,768]{1,0:T(8,128)(2,1)S(1)} %collective-permute-done.3.a_ref), channel_id=1, source_target_pairs={{0,4},{1,5},{4,8},{5,9},{8,12},{9,13},{12,14},{13,15},{14,10},{15,... | collective-permute-start | bytes 663560 | tf_op jit(solution)/shard_map/ppermute | solution.py:188
  28.9 8.4 %collective-permute-start.14 = (bf16[144,768]{1,0:T(8,128)(2,1)S(1)}, bf16[144,768]{1,0:T(8,128)(2,1)S(1)}, u32[]{:S(2)}, u32[]{:S(2)}) collective-permute-start(bf16[144,768]{1,0:T(8,128)(2,1)S(1)} %collective-permute-done.11.a_ref), channel_id=1, source_target_pairs={{4,0},{5,1},{8,4},{9,5},{12,8},{13,9},{14,12},{15,13},{10,14},{11,... | collective-permute-start | bytes 663560 | tf_op jit(solution)/shard_map/ppermute | solution.py:188
  32.0 8.6 %collective-permute-start.13 = (bf16[128,768]{1,0:T(8,128)(2,1)S(1)}, bf16[128,768]{1,0:T(8,128)(2,1)S(1)}, u32[]{:S(2)}, u32[]{:S(2)}) collective-permute-start(bf16[128,768]{1,0:T(8,128)(2,1)S(1)} %collective-permute-done.9.b_ref), channel_id=1, source_target_pairs={{4,0},{5,1},{8,4},{9,5},{12,8},{13,9},{14,12},{15,13},{10,14},{11,... | collective-permute-start | bytes 589832 | tf_op jit(solution)/shard_map/ppermute | solution.py:188
  33.4 7.2 %collective-permute-start.12 = (bf16[144,768]{1,0:T(8,128)(2,1)S(1)}, bf16[144,768]{1,0:T(8,128)(2,1)S(1)}, u32[]{:S(2)}, u32[]{:S(2)}) collective-permute-start(bf16[144,768]{1,0:T(8,128)(2,1)S(1)} %collective-permute-done.8.a_ref), channel_id=1, source_target_pairs={{0,4},{1,5},{4,8},{5,9},{8,12},{9,13},{12,14},{13,15},{14,10},{15,... | collective-permute-start | bytes 663560 | tf_op jit(solution)/shard_map/ppermute | solution.py:188
  39.3 3.6 %collective-permute-start.17 = (f32[256,768]{1,0:T(8,128)S(1)}, f32[256,768]{1,0:T(8,128)S(1)}, u32[]{:S(2)}, u32[]{:S(2)}) collective-permute-start(f32[256,768]{1,0:T(8,128)S(1)} %get-tuple-element.168), channel_id=1, source_target_pairs={{0,1},{1,0},{2,3},{3,2},{4,5},{5,4},{6,7},{7,6},{8,9},{9,8},{10,11... | collective-permute-start | bytes 2359304 | tf_op jit(solution)/shard_map/ppermute | solution.py:188
  40.5 1.4 %collective-permute-start.16 = (bf16[128,768]{1,0:T(8,128)(2,1)S(1)}, bf16[128,768]{1,0:T(8,128)(2,1)S(1)}, u32[]{:S(2)}, u32[]{:S(2)}) collective-permute-start(bf16[128,768]{1,0:T(8,128)(2,1)S(1)} %collective-permute-done.13.b_ref), channel_id=1, source_target_pairs={{0,1},{1,0},{2,3},{3,2},{4,5},{5,4},{6,7},{7,6},{8,9},{9,8},{10,11... | collective-permute-start | bytes 589832 | tf_op jit(solution)/shard_map/ppermute | solution.py:188
  40.5 1.8 %collective-permute-start.15 = (bf16[144,768]{1,0:T(8,128)(2,1)S(1)}, bf16[144,768]{1,0:T(8,128)(2,1)S(1)}, u32[]{:S(2)}, u32[]{:S(2)}) collective-permute-start(bf16[144,768]{1,0:T(8,128)(2,1)S(1)} %collective-permute-done.12.a_ref), channel_id=1, source_target_pairs={{0,1},{1,0},{2,3},{3,2},{4,5},{5,4},{6,7},{7,6},{8,9},{9,8},{10,11... | collective-permute-start | bytes 663560 | tf_op jit(solution)/shard_map/ppermute | solution.py:188
  41.7 1.3 %copy-start.1 = (f32[256,768]{1,0:T(8,128)S(1)}, f32[256,768]{1,0:T(8,128)}, u32[]{:S(2)}) copy-start(f32[256,768]{1,0:T(8,128)} %weights_ref.1) | copy-start | bytes 2359300
  41.7 1.4 %copy-start.6 = (f32[256,768]{1,0:T(8,128)S(1)}, f32[256,768]{1,0:T(8,128)}, u32[]{:S(2)}) copy-start(f32[256,768]{1,0:T(8,128)} %param.12) | copy-start | bytes 2359300
  41.7 1.6 %copy-start.7 = (f32[256,768]{1,0:T(8,128)S(1)}, f32[256,768]{1,0:T(8,128)}, u32[]{:S(2)}) copy-start(f32[256,768]{1,0:T(8,128)} %param.13) | copy-start | bytes 2359300

commit v8 on v7

--- a/solution.py
+++ b/solution.py
@@ -31,8 +31,41 @@
     return value
 
 
-def lookup_kernel(bits, ids_ref, count_ref, table_ref, docs_ref, weights_ref, out_ref, cast_ref):
+def prepare_kernel(
+    bits,
+    ids_hbm,
+    count_hbm,
+    table_hbm,
+    docs_hbm,
+    weights_hbm,
+    a_ref,
+    b_ref,
+    cast_ref,
+    ids_ref,
+    count_ref,
+    table_ref,
+    weights_ref,
+    done,
+):
     slots, docs = ids_ref.shape
+    head = docs - b_ref.shape[0]
+    fetches = [
+        pltpu.make_async_copy(source, target, done.at[i])
+        for i, (source, target) in enumerate(
+            (
+                (ids_hbm, ids_ref),
+                (table_hbm, table_ref),
+                (count_hbm, count_ref),
+                (docs_hbm.at[pl.ds(0, head)], a_ref.at[pl.ds(0, head)]),
+                (docs_hbm.at[pl.ds(head, docs - head)], b_ref),
+                (weights_hbm, weights_ref),
+            )
+        )
+    ]
+    for fetch in fetches:
+        fetch.start()
+    for fetch in fetches[:3]:
+        fetch.wait()
     pairs = table_ref.shape[0] // 2
     starts = range(0, docs, LANES)
     ids = [ids_ref[:, start : start + LANES] for start in starts]
@@ -54,32 +87,45 @@
     else:
         found = lax.fori_loop(0, pairs, pick, found, unroll=8)
     place = lax.broadcasted_iota(jnp.int32, (slots, LANES), 0)
-    head = out_ref.shape[0] - slots // 2
-    out_ref[:head, :] = docs_ref[:head, :]
-    out_ref[head:, :] = jnp.zeros((slots // 2, out_ref.shape[1]), jnp.bfloat16)
+    a_ref[head:, :] = jnp.zeros((slots // 2, a_ref.shape[1]), jnp.bfloat16)
     for i, start in enumerate(starts):
         row = jnp.where((ids[i] >> 7) < pairs, found[i], found[i] >> 16) & 0xFFFF
         low = (LANES + (row & (LANES - 1))).astype(jnp.float32)
         code = power_of_two(row >> 7, bits, low * 2.0**-64, 1)
         code = jnp.where(place < count_ref[:, start : start + LANES], code, 0.0)
         code = code.astype(jnp.bfloat16)
-        out_ref[head:, start : start + LANES] = code[: slots // 2]
-        out_ref[head:, docs + start : docs + start + LANES] = code[slots // 2 :]
+        a_ref[head:, start : start + LANES] = code[: slots // 2]
+        a_ref[head:, docs + start : docs + start + LANES] = code[slots // 2 :]
+    for fetch in fetches[3:]:
+        fetch.wait()
     cast_ref[...] = weights_ref[...].astype(jnp.bfloat16) * 0.5
 
 
-def lookup_rows(label_slot, pos_ids, pos_count, embeddings, weights, head):
+def prepare(label_slot, pos_ids, pos_count, embeddings, weights, head):
     docs, slots = pos_ids.shape
+    width = embeddings.shape[1]
     lines = label_slot.shape[0] // LANES
+    table = label_slot.reshape(lines, LANES)
+    inputs = (pos_ids.T, pos_count.reshape(1, docs), table, embeddings, weights)
     return pl.pallas_call(
-        functools.partial(lookup_kernel, (lines - 1).bit_length()),
+        functools.partial(prepare_kernel, (lines - 1).bit_length()),
+        in_specs=[pl.BlockSpec(memory_space=pltpu.HBM)] * 5,
+        out_specs=[pl.BlockSpec(memory_space=pltpu.VMEM)] * 3,
         out_shape=[
-            jax.ShapeDtypeStruct((head + slots // 2, embeddings.shape[1]), jnp.bfloat16),
+            jax.ShapeDtypeStruct((head + slots // 2, width), jnp.bfloat16),
+            jax.ShapeDtypeStruct((docs - head, width), jnp.bfloat16),
             jax.ShapeDtypeStruct(weights.shape, jnp.bfloat16),
         ],
+        scratch_shapes=[
+            pltpu.VMEM((slots, docs), jnp.int32),
+            pltpu.VMEM((1, docs), jnp.int32),
+            pltpu.VMEM((lines, LANES), jnp.int32),
+            pltpu.VMEM(weights.shape, jnp.float32),
+            pltpu.SemaphoreType.DMA((6,)),
+        ],
         compiler_params=pltpu.CompilerParams(vmem_limit_bytes=VMEM_LIMIT),
-        name="lookup",
-    )(pos_ids.T, pos_count.reshape(1, docs), label_slot.reshape(lines, LANES), embeddings, weights)
+        name="prepare",
+    )(*(pltpu.with_memory_space_constraint(x, pltpu.HBM) for x in inputs))
 
 
 def signs_of(codes, owner, bits, height):
@@ -187,9 +233,8 @@
     def send(value, pairs):
         return lax.ppermute(value, "blk", pairs)
 
-    b = embeddings[head:]
+    a, b, mine = prepare(label_slot, pos_ids, pos_count, embeddings, weights, head)
     coming = {"up_b": send(b, up), "down_b": send(b, down)}
-    a, mine = lookup_rows(label_slot, pos_ids, pos_count, embeddings, weights, head)
     coming |= {"up_a": send(a, up), "down_a": send(a, down)}
     cast = [mine, send(mine, swap)]
     sums = ()

time: 45.5 us -> 43.8 us (0.963)
  local copies, waits for them, and re-layouts: 4.65 us -> 0.02 us
  waiting for transfers between devices: 13.1 us -> 15 us
  Pallas kernels: 8.86 us -> 9.86 us
    unnamed x16 -> x6, local copies, waits for them, and re-layouts: 3.65 us -> 0.02 us
    ppermute x18, waiting for transfers between devices: 13.1 us -> 15 us  [send(): return lax.ppermute(value, 'blk', pairs)]
    pallas_call x1, Pallas kernels: 0.48 us -> 1.48 us  [prepare(): pl.pallas_call(functools.partial(prepare_kernel, (lines - 1).bit_length()...]
    slice x1 -> x0, local copies, waits for them, and re-layouts: 1 us -> none  [per_device(): b = embeddings[head:]]
  transfers between devices with their start and end apart: 18 -> 18, of which waited for: 10 -> 11; matrix products, arithmetic and copies ran while one was open for 0% -> 0% of each run, Pallas kernels for 20% -> 19%
where the time goes in v8:
time: 43.8 us; the launch traced here: 43.6 us
  starting transfers between devices  16.1 us (37%)
  waiting for transfers between devices  15 us (34%)
  Pallas kernels  9.86 us (23%)
  other arithmetic  1.81 us (4%)
  between operations  0.81 us (2%)
    ppermute x18, starting transfers between devices, send(): return lax.ppermute(value, 'blk', pairs)  16.1 us
    ppermute x18, waiting for transfers between devices, send(): return lax.ppermute(value, 'blk', pairs)  15 us
    pallas_call x9, Pallas kernels, add_gradient(): pl.pallas_call(functools.partial(gradient_kernel, bits, owners, not sums)...  8.38 us
    sub x1, other arithmetic, adam_step(): new_weights = weights - learn_rate * (update + decay_rate * weights)  1.81 us
    pallas_call x1, Pallas kernels, prepare(): pl.pallas_call(functools.partial(prepare_kernel, (lines - 1).bit_length()...  1.48 us
  transfers between devices with their start and end apart: 18, of which 11 were waited for; matrix products, arithmetic and copies ran while one was open for 0% of the time, Pallas kernels for 19%

profile of v8, /device:TPU:0, one launch (start us, length us, event | category | flops | bytes accessed | tf_op | source)
XLA Modules:
  0.0 43.6 jit_solution(13936814662161278831)
XLA Ops:
  0.6 1.5 %prepare.1 = (bf16[144,768]{1,0:T(8,128)(2,1)S(1)}, bf16[128,768]{1,0:T(8,128)(2,1)S(1)}, bf16[256,768]{1,0:T(8,128)(2,1)S(1)}) custom-call(s32[32,256]{1,0:T(8,128)} %bitcast.3, s32[1,256]{1,0:T(1,128)} %bitcast.5, s32[32,128]{1,0:T(8,128)} %bitcast.4, bf16[256,768]{1,0:T(8,128)(2,1)} %docs_hbm.1, f32[256,768]{1,0:T(8,128)} %weights_hbm.1), custom_call_target="tpu_custom_call" | custom-call | tf_op jit(solution)/shard_map/prepare/pallas_call | solution.py:110
  2.1 3.1 %collective-permute-start.2 = (bf16[128,768]{1,0:T(8,128)(2,1)S(1)}, bf16[128,768]{1,0:T(8,128)(2,1)S(1)}, u32[]{:S(2)}, u32[]{:S(2)}) collective-permute-start(bf16[128,768]{1,0:T(8,128)(2,1)S(1)} %get-tuple-element.112.b_ref), channel_id=1, source_target_pairs={{0,4},{1,5},{4,8},{5,9},{8,12},{9,13},{12,14},{13,15},{14,10},{15,... | collective-permute-start | bytes 589832 | tf_op jit(solution)/shard_map/ppermute | solution.py:234
  5.2 2.0 %collective-permute-start = (bf16[144,768]{1,0:T(8,128)(2,1)S(1)}, bf16[144,768]{1,0:T(8,128)(2,1)S(1)}, u32[]{:S(2)}, u32[]{:S(2)}) collective-permute-start(bf16[144,768]{1,0:T(8,128)(2,1)S(1)} %get-tuple-element.111.a_ref), channel_id=1, source_target_pairs={{0,4},{1,5},{4,8},{5,9},{8,12},{9,13},{12,14},{13,15},{14,10},{15,... | collective-permute-start | bytes 663560 | tf_op jit(solution)/shard_map/ppermute | solution.py:234
  7.2 3.6 %collective-permute-done.2.b_ref = bf16[128,768]{1,0:T(8,128)(2,1)S(1)} collective-permute-done((bf16[128,768]{1,0:T(8,128)(2,1)S(1)}, bf16[128,768]{1,0:T(8,128)(2,1)S(1)}, u32[]{:S(2)}, u32[]{:S(2)}) %collective-permute-start.2) | collective-permute-done | bytes 196640 | tf_op jit(solution)/shard_map/ppermute | solution.py:234
  10.9 2.1 %collective-permute-start.5 = (bf16[128,768]{1,0:T(8,128)(2,1)S(1)}, bf16[128,768]{1,0:T(8,128)(2,1)S(1)}, u32[]{:S(2)}, u32[]{:S(2)}) collective-permute-start(bf16[128,768]{1,0:T(8,128)(2,1)S(1)} %collective-permute-done.2.b_ref), channel_id=1, source_target_pairs={{0,4},{1,5},{4,8},{5,9},{8,12},{9,13},{12,14},{13,15},{14,10},{15,... | collective-permute-start | bytes 589832 | tf_op jit(solution)/shard_map/ppermute | solution.py:234
  13.0 2.6 %collective-permute-done.a_ref = bf16[144,768]{1,0:T(8,128)(2,1)S(1)} collective-permute-done((bf16[144,768]{1,0:T(8,128)(2,1)S(1)}, bf16[144,768]{1,0:T(8,128)(2,1)S(1)}, u32[]{:S(2)}, u32[]{:S(2)}) %collective-permute-start) | collective-permute-done | bytes 221216 | tf_op jit(solution)/shard_map/ppermute | solution.py:234
  15.6 2.1 %collective-permute-start.3 = (bf16[144,768]{1,0:T(8,128)(2,1)S(1)}, bf16[144,768]{1,0:T(8,128)(2,1)S(1)}, u32[]{:S(2)}, u32[]{:S(2)}) collective-permute-start(bf16[144,768]{1,0:T(8,128)(2,1)S(1)} %collective-permute-done.a_ref), channel_id=1, source_target_pairs={{0,4},{1,5},{4,8},{5,9},{8,12},{9,13},{12,14},{13,15},{14,10},{15,... | collective-permute-start | bytes 663560 | tf_op jit(solution)/shard_map/ppermute | solution.py:234
  17.7 2.1 %collective-permute-done.5.b_ref = bf16[128,768]{1,0:T(8,128)(2,1)S(1)} collective-permute-done((bf16[128,768]{1,0:T(8,128)(2,1)S(1)}, bf16[128,768]{1,0:T(8,128)(2,1)S(1)}, u32[]{:S(2)}, u32[]{:S(2)}) %collective-permute-start.5) | collective-permute-done | bytes 196640 | tf_op jit(solution)/shard_map/ppermute | solution.py:234
  19.8 2.1 %collective-permute-start.10 = (bf16[128,768]{1,0:T(8,128)(2,1)S(1)}, bf16[128,768]{1,0:T(8,128)(2,1)S(1)}, u32[]{:S(2)}, u32[]{:S(2)}) collective-permute-start(bf16[128,768]{1,0:T(8,128)(2,1)S(1)} %collective-permute-done.5.b_ref), channel_id=1, source_target_pairs={{0,4},{1,5},{4,8},{5,9},{8,12},{9,13},{12,14},{13,15},{14,10},{15,... | collective-permute-start | bytes 589832 | tf_op jit(solution)/shard_map/ppermute | solution.py:234
  22.0 1.0 %gradient.9 = (f32[256,768]{1,0:T(8,128)S(1)}, f32[256,768]{1,0:T(8,128)S(1)}) custom-call(bf16[144,768]{1,0:T(8,128)(2,1)S(1)} %get-tuple-element.111.a_ref, bf16[128,768]{1,0:T(8,128)(2,1)S(1)} %get-tuple-element.112.b_ref, bf16[256,768]{1,0:T(8,128)(2,1)S(1)} %get-tuple-element.113.refs_0_, bf16[256,768]{1,0:T(8,128)(2,1)S(1)} %collective-permute-done.7.refs_1_), custom_call_target="tpu_custom_call" | custom-call | flops 500000000 | bytes 1000000 | tf_op jit(solution)/shard_map/gradient/pallas_call | solution.py:184
  22.9 1.6 %collective-permute-done.3.a_ref = bf16[144,768]{1,0:T(8,128)(2,1)S(1)} collective-permute-done((bf16[144,768]{1,0:T(8,128)(2,1)S(1)}, bf16[144,768]{1,0:T(8,128)(2,1)S(1)}, u32[]{:S(2)}, u32[]{:S(2)}) %collective-permute-start.3) | collective-permute-done | bytes 221216 | tf_op jit(solution)/shard_map/ppermute | solution.py:234
  24.6 2.1 %collective-permute-start.8 = (bf16[144,768]{1,0:T(8,128)(2,1)S(1)}, bf16[144,768]{1,0:T(8,128)(2,1)S(1)}, u32[]{:S(2)}, u32[]{:S(2)}) collective-permute-start(bf16[144,768]{1,0:T(8,128)(2,1)S(1)} %collective-permute-done.3.a_ref), channel_id=1, source_target_pairs={{0,4},{1,5},{4,8},{5,9},{8,12},{9,13},{12,14},{13,15},{14,10},{15,... | collective-permute-start | bytes 663560 | tf_op jit(solution)/shard_map/ppermute | solution.py:234
  26.7 1.0 %gradient.10 = (f32[256,768]{1,0:T(8,128)S(1)}, f32[256,768]{1,0:T(8,128)S(1)}) custom-call(bf16[144,768]{1,0:T(8,128)(2,1)S(1)} %collective-permute-done.a_ref, bf16[128,768]{1,0:T(8,128)(2,1)S(1)} %collective-permute-done.2.b_ref, bf16[256,768]{1,0:T(8,128)(2,1)S(1)} %get-tuple-element.113.refs_0_, ...), custom_call_target="tpu_custom_call", output_to_operand_aliasing={{0}: (4, {}), {1}: (5, {})} | custom-call | flops 500000000 | bytes 1000000 | tf_op jit(solution)/shard_map/gradient/pallas_call | solution.py:184
  27.8 1.0 %gradient.11 = (f32[256,768]{1,0:T(8,128)S(1)}, f32[256,768]{1,0:T(8,128)S(1)}) custom-call(bf16[144,768]{1,0:T(8,128)(2,1)S(1)} %collective-permute-done.6.a_ref, bf16[128,768]{1,0:T(8,128)(2,1)S(1)} %collective-permute-done.1.b_ref, bf16[256,768]{1,0:T(8,128)(2,1)S(1)} %get-tuple-element.113.refs_0_, ...), custom_call_target="tpu_custom_call", output_to_operand_aliasing={{0}: (4, {}), {1}: (5, {})} | custom-call | flops 500000000 | bytes 1000000 | tf_op jit(solution)/shard_map/gradient/pallas_call | solution.py:184
  28.8 1.8 %collective-permute-done.9.b_ref = bf16[128,768]{1,0:T(8,128)(2,1)S(1)} collective-permute-done((bf16[128,768]{1,0:T(8,128)(2,1)S(1)}, bf16[128,768]{1,0:T(8,128)(2,1)S(1)}, u32[]{:S(2)}, u32[]{:S(2)}) %collective-permute-start.9) | collective-permute-done | bytes 196640 | tf_op jit(solution)/shard_map/ppermute | solution.py:234
  30.6 0.3 collective-permute-start.13
  30.9 1.0 %gradient.12 = (f32[256,768]{1,0:T(8,128)S(1)}, f32[256,768]{1,0:T(8,128)S(1)}) custom-call(bf16[144,768]{1,0:T(8,128)(2,1)S(1)} %collective-permute-done.3.a_ref, bf16[128,768]{1,0:T(8,128)(2,1)S(1)} %collective-permute-done.5.b_ref, bf16[256,768]{1,0:T(8,128)(2,1)S(1)} %get-tuple-element.113.refs_0_, ...), custom_call_target="tpu_custom_call", output_to_operand_aliasing={{0}: (4, {}), {1}: (5, {})} | custom-call | flops 1000000000 | bytes 1000000 | tf_op jit(solution)/shard_map/gradient/pallas_call | solution.py:184
  31.9 0.8 %collective-permute-done.8.a_ref = bf16[144,768]{1,0:T(8,128)(2,1)S(1)} collective-permute-done((bf16[144,768]{1,0:T(8,128)(2,1)S(1)}, bf16[144,768]{1,0:T(8,128)(2,1)S(1)}, u32[]{:S(2)}, u32[]{:S(2)}) %collective-permute-start.8) | collective-permute-done | bytes 221216 | tf_op jit(solution)/shard_map/ppermute | solution.py:234
  32.7 1.8 %collective-permute-start.12 = (bf16[144,768]{1,0:T(8,128)(2,1)S(1)}, bf16[144,768]{1,0:T(8,128)(2,1)S(1)}, u32[]{:S(2)}, u32[]{:S(2)}) collective-permute-start(bf16[144,768]{1,0:T(8,128)(2,1)S(1)} %collective-permute-done.8.a_ref), channel_id=1, source_target_pairs={{0,4},{1,5},{4,8},{5,9},{8,12},{9,13},{12,14},{13,15},{14,10},{15,... | collective-permute-start | bytes 663560 | tf_op jit(solution)/shard_map/ppermute | solution.py:234
  34.5 1.0 %gradient.13 = (f32[256,768]{1,0:T(8,128)S(1)}, f32[256,768]{1,0:T(8,128)S(1)}) custom-call(bf16[144,768]{1,0:T(8,128)(2,1)S(1)} %collective-permute-done.11.a_ref, bf16[128,768]{1,0:T(8,128)(2,1)S(1)} %collective-permute-done.4.b_ref, bf16[256,768]{1,0:T(8,128)(2,1)S(1)} %get-tuple-element.113.refs_0_, ...), custom_call_target="tpu_custom_call", output_to_operand_aliasing={{0}: (4, {}), {1}: (5, {})} | custom-call | flops 1000000000 | bytes 1000000 | tf_op jit(solution)/shard_map/gradient/pallas_call | solution.py:184
  35.5 0.6 %collective-permute-done.14.a_ref = bf16[144,768]{1,0:T(8,128)(2,1)S(1)} collective-permute-done((bf16[144,768]{1,0:T(8,128)(2,1)S(1)}, bf16[144,768]{1,0:T(8,128)(2,1)S(1)}, u32[]{:S(2)}, u32[]{:S(2)}) %collective-permute-start.14) | collective-permute-done | bytes 221216 | tf_op jit(solution)/shard_map/ppermute | solution.py:234
  36.1 1.0 %gradient.14 = (f32[256,768]{1,0:T(8,128)S(1)}, f32[256,768]{1,0:T(8,128)S(1)}) custom-call(bf16[144,768]{1,0:T(8,128)(2,1)S(1)} %collective-permute-done.8.a_ref, bf16[128,768]{1,0:T(8,128)(2,1)S(1)} %collective-permute-done.10.b_ref, bf16[256,768]{1,0:T(8,128)(2,1)S(1)} %get-tuple-element.113.refs_0_, ...), custom_call_target="tpu_custom_call", output_to_operand_aliasing={{0}: (4, {}), {1}: (5, {})} | custom-call | flops 500000000 | bytes 1000000 | tf_op jit(solution)/shard_map/gradient/pallas_call | solution.py:184
  37.1 1.0 %gradient.15 = (f32[256,768]{1,0:T(8,128)S(1)}, f32[256,768]{1,0:T(8,128)S(1)}) custom-call(bf16[144,768]{1,0:T(8,128)(2,1)S(1)} %collective-permute-done.14.a_ref, bf16[128,768]{1,0:T(8,128)(2,1)S(1)} %collective-permute-done.9.b_ref, bf16[256,768]{1,0:T(8,128)(2,1)S(1)} %get-tuple-element.113.refs_0_, ...), custom_call_target="tpu_custom_call", output_to_operand_aliasing={{0}: (4, {}), {1}: (5, {})} | custom-call | flops 500000000 | bytes 1000000 | tf_op jit(solution)/shard_map/gradient/pallas_call | solution.py:184
  38.2 0.1 collective-permute-start.17
  38.3 0.2 collective-permute-done.13.b_ref
  38.4 0.3 collective-permute-start.16
  38.8 0.5 %collective-permute-done.12.a_ref = bf16[144,768]{1,0:T(8,128)(2,1)S(1)} collective-permute-done((bf16[144,768]{1,0:T(8,128)(2,1)S(1)}, bf16[144,768]{1,0:T(8,128)(2,1)S(1)}, u32[]{:S(2)}, u32[]{:S(2)}) %collective-permute-start.12) | collective-permute-done | bytes 221216 | tf_op jit(solution)/shard_map/ppermute | solution.py:234
  39.3 0.7 %gradient.16.refs_1_ = f32[256,768]{1,0:T(8,128)S(1)} custom-call(bf16[144,768]{1,0:T(8,128)(2,1)S(1)} %collective-permute-done.12.a_ref, bf16[128,768]{1,0:T(8,128)(2,1)S(1)} %collective-permute-done.13.b_ref, bf16[256,768]{1,0:T(8,128)(2,1)S(1)} %get-tuple-element.113.refs_0_, ...), custom_call_target="tpu_custom_call", output_to_operand_aliasing={{}: (3, {})} | custom-call | flops 4000000000 | bytes 1000000 | tf_op jit(solution)/shard_map/gradient/pallas_call | solution.py:184
  40.0 0.8 %collective-permute-done.16.b_ref = bf16[128,768]{1,0:T(8,128)(2,1)S(1)} collective-permute-done((bf16[128,768]{1,0:T(8,128)(2,1)S(1)}, bf16[128,768]{1,0:T(8,128)(2,1)S(1)}, u32[]{:S(2)}, u32[]{:S(2)}) %collective-permute-start.16) | collective-permute-done | bytes 196640 | tf_op jit(solution)/shard_map/ppermute | solution.py:234
  40.8 0.3 collective-permute-done.15.a_ref
  41.1 0.7 %gradient.17 = f32[256,768]{1,0:T(8,128)S(1)} custom-call(bf16[144,768]{1,0:T(8,128)(2,1)S(1)} %collective-permute-done.15.a_ref, bf16[128,768]{1,0:T(8,128)(2,1)S(1)} %collective-permute-done.16.b_ref, bf16[256,768]{1,0:T(8,128)(2,1)S(1)} %get-tuple-element.113.refs_0_, f32[256,768]{1,0:T(8,128)S(1)} %gradient.16.refs_1_), custom_call_target="tpu_custom_call", output_to_operand_aliasing={{}: (3, {})} | custom-call | flops 4000000000 | bytes 1000000 | tf_op jit(solution)/shard_map/gradient/pallas_call | solution.py:184
  41.8 1.8 %multiply_subtract_fusion = (f32[256,768]{1,0:T(8,128)}, f32[256,768]{1,0:T(8,128)}, f32[256,768]{1,0:T(8,128)}) fusion(f32[256,768]{1,0:T(8,128)S(1)} %copy-done, f32[256,768]{1,0:T(8,128)S(1)} %gradient.17, f32[256,768]{1,0:T(8,128)S(1)} %collective-permute-done.17, f32[256,768]{1,0:T(8,128)S(1)} %copy-done.1, f32[256,768]{1,0:T(8,128)S(1)} %copy-done.2), kind=kLoop, calls=%fused_computation | loop fusion | flops 3342336 | bytes 6291456 | tf_op jit(solution)/shard_map/sub | solution.py:200
  (21 shorter events, 0.1 us)
Async XLA Ops:
  2.1 8.7 %collective-permute-start.2 = (bf16[128,768]{1,0:T(8,128)(2,1)S(1)}, bf16[128,768]{1,0:T(8,128)(2,1)S(1)}, u32[]{:S(2)}, u32[]{:S(2)}) collective-permute-start(bf16[128,768]{1,0:T(8,128)(2,1)S(1)} %get-tuple-element.112.b_ref), channel_id=1, source_target_pairs={{0,4},{1,5},{4,8},{5,9},{8,12},{9,13},{12,14},{13,15},{14,10},{15,... | collective-permute-start | bytes 589832 | tf_op jit(solution)/shard_map/ppermute | solution.py:234
  5.2 7.8 %collective-permute-start.1 = (bf16[128,768]{1,0:T(8,128)(2,1)S(1)}, bf16[128,768]{1,0:T(8,128)(2,1)S(1)}, u32[]{:S(2)}, u32[]{:S(2)}) collective-permute-start(bf16[128,768]{1,0:T(8,128)(2,1)S(1)} %get-tuple-element.112.b_ref), channel_id=1, source_target_pairs={{4,0},{5,1},{8,4},{9,5},{12,8},{13,9},{14,12},{15,13},{10,14},{11,... | collective-permute-start | bytes 589832 | tf_op jit(solution)/shard_map/ppermute | solution.py:234
  5.2 10.4 %collective-permute-start = (bf16[144,768]{1,0:T(8,128)(2,1)S(1)}, bf16[144,768]{1,0:T(8,128)(2,1)S(1)}, u32[]{:S(2)}, u32[]{:S(2)}) collective-permute-start(bf16[144,768]{1,0:T(8,128)(2,1)S(1)} %get-tuple-element.111.a_ref), channel_id=1, source_target_pairs={{0,4},{1,5},{4,8},{5,9},{8,12},{9,13},{12,14},{13,15},{14,10},{15,... | collective-permute-start | bytes 663560 | tf_op jit(solution)/shard_map/ppermute | solution.py:234
  7.2 14.7 %collective-permute-start.7 = (bf16[256,768]{1,0:T(8,128)(2,1)S(1)}, bf16[256,768]{1,0:T(8,128)(2,1)S(1)}, u32[]{:S(2)}, u32[]{:S(2)}) collective-permute-start(bf16[256,768]{1,0:T(8,128)(2,1)S(1)} %get-tuple-element.113.refs_0_), channel_id=1, source_target_pairs={{0,1},{1,0},{2,3},{3,2},{4,5},{5,4},{6,7},{7,6},{8,9},{9,8},{10,11... | collective-permute-start | bytes 1179656 | tf_op jit(solution)/shard_map/ppermute | solution.py:234
  7.2 10.5 %collective-permute-start.6 = (bf16[144,768]{1,0:T(8,128)(2,1)S(1)}, bf16[144,768]{1,0:T(8,128)(2,1)S(1)}, u32[]{:S(2)}, u32[]{:S(2)}) collective-permute-start(bf16[144,768]{1,0:T(8,128)(2,1)S(1)} %get-tuple-element.111.a_ref), channel_id=1, source_target_pairs={{4,0},{5,1},{8,4},{9,5},{12,8},{13,9},{14,12},{15,13},{10,14},{11,... | collective-permute-start | bytes 663560 | tf_op jit(solution)/shard_map/ppermute | solution.py:234
  10.9 9.0 %collective-permute-start.5 = (bf16[128,768]{1,0:T(8,128)(2,1)S(1)}, bf16[128,768]{1,0:T(8,128)(2,1)S(1)}, u32[]{:S(2)}, u32[]{:S(2)}) collective-permute-start(bf16[128,768]{1,0:T(8,128)(2,1)S(1)} %collective-permute-done.2.b_ref), channel_id=1, source_target_pairs={{0,4},{1,5},{4,8},{5,9},{8,12},{9,13},{12,14},{13,15},{14,10},{15,... | collective-permute-start | bytes 589832 | tf_op jit(solution)/shard_map/ppermute | solution.py:234
  13.0 9.0 %collective-permute-start.4 = (bf16[128,768]{1,0:T(8,128)(2,1)S(1)}, bf16[128,768]{1,0:T(8,128)(2,1)S(1)}, u32[]{:S(2)}, u32[]{:S(2)}) collective-permute-start(bf16[128,768]{1,0:T(8,128)(2,1)S(1)} %collective-permute-done.1.b_ref), channel_id=1, source_target_pairs={{4,0},{5,1},{8,4},{9,5},{12,8},{13,9},{14,12},{15,13},{10,14},{11,... | collective-permute-start | bytes 589832 | tf_op jit(solution)/shard_map/ppermute | solution.py:234
  15.6 9.0 %collective-permute-start.3 = (bf16[144,768]{1,0:T(8,128)(2,1)S(1)}, bf16[144,768]{1,0:T(8,128)(2,1)S(1)}, u32[]{:S(2)}, u32[]{:S(2)}) collective-permute-start(bf16[144,768]{1,0:T(8,128)(2,1)S(1)} %collective-permute-done.a_ref), channel_id=1, source_target_pairs={{0,4},{1,5},{4,8},{5,9},{8,12},{9,13},{12,14},{13,15},{14,10},{15,... | collective-permute-start | bytes 663560 | tf_op jit(solution)/shard_map/ppermute | solution.py:234
  17.7 10.0 %collective-permute-start.11 = (bf16[144,768]{1,0:T(8,128)(2,1)S(1)}, bf16[144,768]{1,0:T(8,128)(2,1)S(1)}, u32[]{:S(2)}, u32[]{:S(2)}) collective-permute-start(bf16[144,768]{1,0:T(8,128)(2,1)S(1)} %collective-permute-done.6.a_ref), channel_id=1, source_target_pairs={{4,0},{5,1},{8,4},{9,5},{12,8},{13,9},{14,12},{15,13},{10,14},{11,... | collective-permute-start | bytes 663560 | tf_op jit(solution)/shard_map/ppermute | solution.py:234
  19.8 9.0 %collective-permute-start.10 = (bf16[128,768]{1,0:T(8,128)(2,1)S(1)}, bf16[128,768]{1,0:T(8,128)(2,1)S(1)}, u32[]{:S(2)}, u32[]{:S(2)}) collective-permute-start(bf16[128,768]{1,0:T(8,128)(2,1)S(1)} %collective-permute-done.5.b_ref), channel_id=1, source_target_pairs={{0,4},{1,5},{4,8},{5,9},{8,12},{9,13},{12,14},{13,15},{14,10},{15,... | collective-permute-start | bytes 589832 | tf_op jit(solution)/shard_map/ppermute | solution.py:234
  21.9 8.7 %collective-permute-start.9 = (bf16[128,768]{1,0:T(8,128)(2,1)S(1)}, bf16[128,768]{1,0:T(8,128)(2,1)S(1)}, u32[]{:S(2)}, u32[]{:S(2)}) collective-permute-start(bf16[128,768]{1,0:T(8,128)(2,1)S(1)} %collective-permute-done.4.b_ref), channel_id=1, source_target_pairs={{4,0},{5,1},{8,4},{9,5},{12,8},{13,9},{14,12},{15,13},{10,14},{11,... | collective-permute-start | bytes 589832 | tf_op jit(solution)/shard_map/ppermute | solution.py:234
  24.6 8.1 %collective-permute-start.8 = (bf16[144,768]{1,0:T(8,128)(2,1)S(1)}, bf16[144,768]{1,0:T(8,128)(2,1)S(1)}, u32[]{:S(2)}, u32[]{:S(2)}) collective-permute-start(bf16[144,768]{1,0:T(8,128)(2,1)S(1)} %collective-permute-done.3.a_ref), channel_id=1, source_target_pairs={{0,4},{1,5},{4,8},{5,9},{8,12},{9,13},{12,14},{13,15},{14,10},{15,... | collective-permute-start | bytes 663560 | tf_op jit(solution)/shard_map/ppermute | solution.py:234
  27.7 8.4 %collective-permute-start.14 = (bf16[144,768]{1,0:T(8,128)(2,1)S(1)}, bf16[144,768]{1,0:T(8,128)(2,1)S(1)}, u32[]{:S(2)}, u32[]{:S(2)}) collective-permute-start(bf16[144,768]{1,0:T(8,128)(2,1)S(1)} %collective-permute-done.11.a_ref), channel_id=1, source_target_pairs={{4,0},{5,1},{8,4},{9,5},{12,8},{13,9},{14,12},{15,13},{10,14},{11,... | collective-permute-start | bytes 663560 | tf_op jit(solution)/shard_map/ppermute | solution.py:234
  30.6 7.8 %collective-permute-start.13 = (bf16[128,768]{1,0:T(8,128)(2,1)S(1)}, bf16[128,768]{1,0:T(8,128)(2,1)S(1)}, u32[]{:S(2)}, u32[]{:S(2)}) collective-permute-start(bf16[128,768]{1,0:T(8,128)(2,1)S(1)} %collective-permute-done.9.b_ref), channel_id=1, source_target_pairs={{4,0},{5,1},{8,4},{9,5},{12,8},{13,9},{14,12},{15,13},{10,14},{11,... | collective-permute-start | bytes 589832 | tf_op jit(solution)/shard_map/ppermute | solution.py:234
  32.7 6.6 %collective-permute-start.12 = (bf16[144,768]{1,0:T(8,128)(2,1)S(1)}, bf16[144,768]{1,0:T(8,128)(2,1)S(1)}, u32[]{:S(2)}, u32[]{:S(2)}) collective-permute-start(bf16[144,768]{1,0:T(8,128)(2,1)S(1)} %collective-permute-done.8.a_ref), channel_id=1, source_target_pairs={{0,4},{1,5},{4,8},{5,9},{8,12},{9,13},{12,14},{13,15},{14,10},{15,... | collective-permute-start | bytes 663560 | tf_op jit(solution)/shard_map/ppermute | solution.py:234
  38.2 3.6 %collective-permute-start.17 = (f32[256,768]{1,0:T(8,128)S(1)}, f32[256,768]{1,0:T(8,128)S(1)}, u32[]{:S(2)}, u32[]{:S(2)}) collective-permute-start(f32[256,768]{1,0:T(8,128)S(1)} %get-tuple-element.170), channel_id=1, source_target_pairs={{0,1},{1,0},{2,3},{3,2},{4,5},{5,4},{6,7},{7,6},{8,9},{9,8},{10,11... | collective-permute-start | bytes 2359304 | tf_op jit(solution)/shard_map/ppermute | solution.py:234
  38.4 2.4 %collective-permute-start.16 = (bf16[128,768]{1,0:T(8,128)(2,1)S(1)}, bf16[128,768]{1,0:T(8,128)(2,1)S(1)}, u32[]{:S(2)}, u32[]{:S(2)}) collective-permute-start(bf16[128,768]{1,0:T(8,128)(2,1)S(1)} %collective-permute-done.13.b_ref), channel_id=1, source_target_pairs={{0,1},{1,0},{2,3},{3,2},{4,5},{5,4},{6,7},{7,6},{8,9},{9,8},{10,11... | collective-permute-start | bytes 589832 | tf_op jit(solution)/shard_map/ppermute | solution.py:234
  39.3 1.8 %collective-permute-start.15 = (bf16[144,768]{1,0:T(8,128)(2,1)S(1)}, bf16[144,768]{1,0:T(8,128)(2,1)S(1)}, u32[]{:S(2)}, u32[]{:S(2)}) collective-permute-start(bf16[144,768]{1,0:T(8,128)(2,1)S(1)} %collective-permute-done.12.a_ref), channel_id=1, source_target_pairs={{0,1},{1,0},{2,3},{3,2},{4,5},{5,4},{6,7},{7,6},{8,9},{9,8},{10,11... | collective-permute-start | bytes 663560 | tf_op jit(solution)/shard_map/ppermute | solution.py:234
  40.0 1.8 %copy-start = (f32[256,768]{1,0:T(8,128)S(1)}, f32[256,768]{1,0:T(8,128)}, u32[]{:S(2)}) copy-start(f32[256,768]{1,0:T(8,128)} %weights_hbm.1) | copy-start | bytes 2359300
  40.0 1.8 %copy-start.1 = (f32[256,768]{1,0:T(8,128)S(1)}, f32[256,768]{1,0:T(8,128)}, u32[]{:S(2)}) copy-start(f32[256,768]{1,0:T(8,128)} %param.12) | copy-start | bytes 2359300
  40.0 1.8 %copy-start.2 = (f32[256,768]{1,0:T(8,128)S(1)}, f32[256,768]{1,0:T(8,128)}, u32[]{:S(2)}) copy-start(f32[256,768]{1,0:T(8,128)} %param.13) | copy-start | bytes 2359300

commit v9 on v8

--- a/solution.py
+++ b/solution.py
@@ -17,10 +17,11 @@
 
 WORD = 32
 LANES = 128
+PIECES = 4
 VMEM_LIMIT = 32 * 1024 * 1024
 FLOPS = 5 * 10**8
 LATE_FLOPS = 10 * 10**8
-END_FLOPS = 40 * 10**8
+END_FLOPS = 100 * 10**8
 
 
 def power_of_two(exponent, bits, start, sign):
@@ -147,28 +148,29 @@
     return jnp.concatenate(spread, axis=0)
 
 
+def doubled_gradient(bits, owners, a_ref, b_ref, w_refs):
+    height = w_refs[0].shape[0]
+    head = b_ref.shape[0]
+    number = 2 * head
+    docs = jnp.concatenate([a_ref[:head, :], b_ref[...]], axis=0)
+    codes = jnp.concatenate([a_ref[head:, :number], a_ref[head:, number : 2 * number]], axis=0)
+    codes = codes.astype(jnp.float32)
+    weights = jnp.concatenate([ref[...] for ref in w_refs], axis=0)
+    halved = lax.dot_general(
+        weights, docs, (((1,), (1,)), ((), ())), preferred_element_type=jnp.float32
+    )
+    me = lax.axis_index("blk")
+    signs = jnp.concatenate([signs_of(codes, me ^ owner, bits, height) for owner in owners], axis=0)
+    signal = (jnp.tanh(halved) + signs).astype(jnp.bfloat16)
+    return jnp.dot(signal, docs, preferred_element_type=jnp.float32)
+
+
 def gradient_kernel(bits, owners, fresh, a_ref, b_ref, *refs):
     blocks = len(owners)
     w_refs, refs = refs[:blocks], refs[blocks:]
     old_refs, new_refs = refs[:-blocks], refs[-blocks:]
     height = w_refs[0].shape[0]
-    me = lax.axis_index("blk")
-    after = b_ref.shape[0]
-    head = a_ref.shape[0]
-    slots = 32
-    head = head - slots // 2
-    docs = jnp.concatenate([a_ref[:head, :], b_ref[...]], axis=0)
-    number = head + after
-    codes = jnp.concatenate(
-        [a_ref[head:, :number], a_ref[head:, number : 2 * number]], axis=0
-    ).astype(jnp.float32)
-    weights = jnp.concatenate([ref[...] for ref in w_refs], axis=0)
-    halved = lax.dot_general(
-        weights, docs, (((1,), (1,)), ((), ())), preferred_element_type=jnp.float32
-    )
-    signs = jnp.concatenate([signs_of(codes, me ^ owner, bits, height) for owner in owners], axis=0)
-    signal = (jnp.tanh(halved) + signs).astype(jnp.bfloat16)
-    part = jnp.dot(signal, docs, preferred_element_type=jnp.float32)
+    part = doubled_gradient(bits, owners, a_ref, b_ref, w_refs)
     for block in range(blocks):
         piece = part[block * height : (block + 1) * height]
         new_refs[block][...] = piece if fresh else old_refs[block][...] + piece
@@ -193,6 +195,64 @@
     )(*inputs)
 
 
+def finish_kernel(
+    bits,
+    a_ref,
+    b_ref,
+    cast_ref,
+    sum_ref,
+    other_ref,
+    weights_ref,
+    first_ref,
+    second_ref,
+    weights_hbm,
+    first_hbm,
+    second_hbm,
+    weights_out,
+    first_out,
+    second_out,
+    done,
+):
+    part = doubled_gradient(bits, (0,), a_ref, b_ref, [cast_ref])
+    height = part.shape[0]
+    size = height // PIECES
+    writes = []
+    for i in range(PIECES):
+        here = pl.ds(i * size, size)
+        gradient = 0.5 * (sum_ref[here, :] + other_ref[here, :] + part[i * size : (i + 1) * size])
+        new_weights, new_first, new_second = adam_step(
+            weights_ref[here, :], first_ref[here, :], second_ref[here, :], gradient
+        )
+        for k, (value, out, hbm) in enumerate(
+            (
+                (new_first, first_out, first_hbm),
+                (new_second, second_out, second_hbm),
+                (new_weights, weights_out, weights_hbm),
+            )
+        ):
+            out[here, :] = value
+            write = pltpu.make_async_copy(out.at[here], hbm.at[here], done.at[i, k])
+            write.start()
+            writes.append(write)
+    for write in writes:
+        write.wait()
+
+
+def finish(bits, a, b, cast, mine_sum, other_sum, weights, first_moment, second_moment):
+    shape = jax.ShapeDtypeStruct(weights.shape, jnp.float32)
+    return pl.pallas_call(
+        functools.partial(finish_kernel, bits),
+        in_specs=[pl.BlockSpec(memory_space=pltpu.VMEM)] * 8,
+        out_specs=[pl.BlockSpec(memory_space=pltpu.HBM)] * 3,
+        out_shape=[shape] * 3,
+        scratch_shapes=[pltpu.VMEM(weights.shape, jnp.float32)] * 3
+        + [pltpu.SemaphoreType.DMA((PIECES, 3))],
+        compiler_params=pltpu.CompilerParams(vmem_limit_bytes=VMEM_LIMIT),
+        cost_estimate=pl.CostEstimate(flops=END_FLOPS, bytes_accessed=10**6, transcendentals=0),
+        name="finish",
+    )(a, b, cast, mine_sum, other_sum, weights, first_moment, second_moment)
+
+
 def adam_step(weights, first_moment, second_moment, gradient):
     new_first = beta_one * first_moment + (1.0 - beta_one) * gradient
     new_second = beta_two * second_moment + (1.0 - beta_two) * gradient * gradient
@@ -234,33 +294,38 @@
         return lax.ppermute(value, "blk", pairs)
 
     a, b, mine = prepare(label_slot, pos_ids, pos_count, embeddings, weights, head)
-    coming = {"up_b": send(b, up), "down_b": send(b, down)}
-    coming |= {"up_a": send(a, up), "down_a": send(a, down)}
+    coming = {"up_b": send(b, up), "down_a": send(a, down)}
+    coming |= {"up_a": send(a, up), "down_b": send(b, down)}
     cast = [mine, send(mine, swap)]
     sums = ()
     waiting = [(a, b)]
+
+    def work(flops):
+        return add_gradient(bits, (0, 1), *waiting.pop(0), cast, sums, flops)
+
     for step in range(1, half_way):
+        last = step == half_way - 1
         came = {}
-        for message in ("up_b", "down_b", "up_a", "down_a"):
+        for message in ("up_b", "down_a", "up_a", "down_b"):
             came[message], waiting, sums = together((coming.pop(message), waiting, sums))
-            if step < half_way - 1 or message in ("down_b", "up_a"):
+            if message in ("up_b", "down_a") or not last:
                 coming[message] = send(came[message], up if message in ("up_a", "up_b") else down)
-            if (step > 1 and message in ("down_b", "up_a")) or (step == 2 and message == "down_a"):
-                flops = FLOPS if step < half_way - 1 else LATE_FLOPS
-                sums = add_gradient(bits, (0, 1), *waiting.pop(0), cast, sums, flops)
-        waiting += [(came["up_a"], came["up_b"]), (came["down_a"], came["down_b"])]
-    for docs in waiting:
-        sums = add_gradient(bits, (0, 1), *docs, cast, sums, FLOPS)
+            if message in ("up_a", "down_b"):
+                side = message.split("_")[0]
+                waiting.append((came[side + "_a"], came[side + "_b"]))
+            if waiting and (last or (step > 1 and message != "down_b")):
+                sums = work(LATE_FLOPS if last else FLOPS)
+    while waiting:
+        sums = work(LATE_FLOPS)
     mine_sum, other_sum = sums
     got = send(other_sum, swap)
-    last_b, mine_sum = together((coming["down_b"], mine_sum))
+    last_b, mine_sum = together((coming["up_b"], mine_sum))
     beside_b = send(last_b, swap)
-    last_a, mine_sum = together((coming["up_a"], mine_sum))
+    last_a, mine_sum = together((coming["down_a"], mine_sum))
     beside_a = send(last_a, swap)
-    mine_sum = add_gradient(bits, (0,), last_a, last_b, [mine], [mine_sum], END_FLOPS)
-    beside_a, beside_b, mine_sum = together((beside_a, beside_b, mine_sum))
-    (mine_sum,) = add_gradient(bits, (0,), beside_a, beside_b, [mine], mine_sum, END_FLOPS)
-    return adam_step(weights, first_moment, second_moment, 0.5 * (mine_sum + got))
+    (mine_sum,) = add_gradient(bits, (0,), last_a, last_b, [mine], [mine_sum], END_FLOPS)
+    state = (weights, first_moment, second_moment)
+    return finish(bits, beside_a, beside_b, mine, mine_sum, got, *state)
 
 
 def solution(mesh):

time: 43.8 us -> 43.1 us (0.984)
  Pallas kernels: 9.86 us -> 11.7 us
  other arithmetic: 1.81 us -> 0 us
  waiting for transfers between devices: 15 us -> 14.1 us
    pallas_call x0 -> x1, Pallas kernels: none -> 2.51 us  [finish(): pl.pallas_call(functools.partial(finish_kernel, bits), in_specs=[pl.Block...]
    sub x1 -> x0, other arithmetic: 1.81 us -> none  [adam_step(): new_weights = weights - learn_rate * (update + decay_rate * weights)]
    ppermute x18, waiting for transfers between devices: 15 us -> 14.1 us  [send(): return lax.ppermute(value, 'blk', pairs)]
    pallas_call x9 -> x8, Pallas kernels: 8.38 us -> 7.72 us  [add_gradient(): pl.pallas_call(functools.partial(gradient_kernel, bits, owners, not sums)...]
  transfers between devices with their start and end apart: 18 -> 18, of which waited for: 11 -> 11; matrix products, arithmetic and copies ran while one was open for 0% -> 0% of each run, Pallas kernels for 19% -> 18%
where the time goes in v9:
time: 43.1 us; the launch traced here: 43 us
  starting transfers between devices  16.4 us (38%)
  waiting for transfers between devices  14.1 us (33%)
  Pallas kernels  11.7 us (27%)
  between operations  0.79 us (2%)
    ppermute x18, starting transfers between devices, send(): return lax.ppermute(value, 'blk', pairs)  16.4 us
    ppermute x18, waiting for transfers between devices, send(): return lax.ppermute(value, 'blk', pairs)  14.1 us
    pallas_call x8, Pallas kernels, add_gradient(): pl.pallas_call(functools.partial(gradient_kernel, bits, owners, not sums)...  7.72 us
    pallas_call x1, Pallas kernels, finish(): pl.pallas_call(functools.partial(finish_kernel, bits), in_specs=[pl.Block...  2.51 us
    pallas_call x1, Pallas kernels, prepare(): pl.pallas_call(functools.partial(prepare_kernel, (lines - 1).bit_length()...  1.48 us
  transfers between devices with their start and end apart: 18, of which 11 were waited for; matrix products, arithmetic and copies ran while one was open for 0% of the time, Pallas kernels for 18%

profile of v9, /device:TPU:0, one launch (start us, length us, event | category | flops | bytes accessed | tf_op | source)
XLA Modules:
  0.0 43.0 jit_solution(8531232076807235998)
XLA Ops:
  0.6 1.5 %prepare.1 = (bf16[144,768]{1,0:T(8,128)(2,1)S(1)}, bf16[128,768]{1,0:T(8,128)(2,1)S(1)}, bf16[256,768]{1,0:T(8,128)(2,1)S(1)}) custom-call(s32[32,256]{1,0:T(8,128)} %bitcast.3, s32[1,256]{1,0:T(1,128)} %bitcast.5, s32[32,128]{1,0:T(8,128)} %bitcast.4, bf16[256,768]{1,0:T(8,128)(2,1)} %docs_hbm.1, f32[256,768]{1,0:T(8,128)} %weights_ref.1), custom_call_target="tpu_custom_call" | custom-call | tf_op jit(solution)/shard_map/prepare/pallas_call | solution.py:111
  2.1 3.1 %collective-permute-start.1 = (bf16[128,768]{1,0:T(8,128)(2,1)S(1)}, bf16[128,768]{1,0:T(8,128)(2,1)S(1)}, u32[]{:S(2)}, u32[]{:S(2)}) collective-permute-start(bf16[128,768]{1,0:T(8,128)(2,1)S(1)} %get-tuple-element.101.b_ref), channel_id=1, source_target_pairs={{0,4},{1,5},{4,8},{5,9},{8,12},{9,13},{12,14},{13,15},{14,10},{15,... | collective-permute-start | bytes 589832 | tf_op jit(solution)/shard_map/ppermute | solution.py:294
  5.2 2.0 %collective-permute-start.5 = (bf16[144,768]{1,0:T(8,128)(2,1)S(1)}, bf16[144,768]{1,0:T(8,128)(2,1)S(1)}, u32[]{:S(2)}, u32[]{:S(2)}) collective-permute-start(bf16[144,768]{1,0:T(8,128)(2,1)S(1)} %get-tuple-element.100.a_ref), channel_id=1, source_target_pairs={{0,4},{1,5},{4,8},{5,9},{8,12},{9,13},{12,14},{13,15},{14,10},{15,... | collective-permute-start | bytes 663560 | tf_op jit(solution)/shard_map/ppermute | solution.py:294
  7.2 3.6 %collective-permute-done.1.b_ref = bf16[128,768]{1,0:T(8,128)(2,1)S(1)} collective-permute-done((bf16[128,768]{1,0:T(8,128)(2,1)S(1)}, bf16[128,768]{1,0:T(8,128)(2,1)S(1)}, u32[]{:S(2)}, u32[]{:S(2)}) %collective-permute-start.1) | collective-permute-done | bytes 196640 | tf_op jit(solution)/shard_map/ppermute | solution.py:294
  10.9 2.1 %collective-permute-start.3 = (bf16[128,768]{1,0:T(8,128)(2,1)S(1)}, bf16[128,768]{1,0:T(8,128)(2,1)S(1)}, u32[]{:S(2)}, u32[]{:S(2)}) collective-permute-start(bf16[128,768]{1,0:T(8,128)(2,1)S(1)} %collective-permute-done.1.b_ref), channel_id=1, source_target_pairs={{0,4},{1,5},{4,8},{5,9},{8,12},{9,13},{12,14},{13,15},{14,10},{15,... | collective-permute-start | bytes 589832 | tf_op jit(solution)/shard_map/ppermute | solution.py:294
  13.0 0.6 %collective-permute-done.a_ref = bf16[144,768]{1,0:T(8,128)(2,1)S(1)} collective-permute-done((bf16[144,768]{1,0:T(8,128)(2,1)S(1)}, bf16[144,768]{1,0:T(8,128)(2,1)S(1)}, u32[]{:S(2)}, u32[]{:S(2)}) %collective-permute-start) | collective-permute-done | bytes 221216 | tf_op jit(solution)/shard_map/ppermute | solution.py:294
  13.6 2.1 %collective-permute-done.5.a_ref = bf16[144,768]{1,0:T(8,128)(2,1)S(1)} collective-permute-done((bf16[144,768]{1,0:T(8,128)(2,1)S(1)}, bf16[144,768]{1,0:T(8,128)(2,1)S(1)}, u32[]{:S(2)}, u32[]{:S(2)}) %collective-permute-start.5) | collective-permute-done | bytes 221216 | tf_op jit(solution)/shard_map/ppermute | solution.py:294
  15.6 2.1 %collective-permute-start.10 = (bf16[144,768]{1,0:T(8,128)(2,1)S(1)}, bf16[144,768]{1,0:T(8,128)(2,1)S(1)}, u32[]{:S(2)}, u32[]{:S(2)}) collective-permute-start(bf16[144,768]{1,0:T(8,128)(2,1)S(1)} %collective-permute-done.5.a_ref), channel_id=1, source_target_pairs={{0,4},{1,5},{4,8},{5,9},{8,12},{9,13},{12,14},{13,15},{14,10},{15,... | collective-permute-start | bytes 663560 | tf_op jit(solution)/shard_map/ppermute | solution.py:294
  17.8 2.1 %collective-permute-done.3.b_ref = bf16[128,768]{1,0:T(8,128)(2,1)S(1)} collective-permute-done((bf16[128,768]{1,0:T(8,128)(2,1)S(1)}, bf16[128,768]{1,0:T(8,128)(2,1)S(1)}, u32[]{:S(2)}, u32[]{:S(2)}) %collective-permute-start.3) | collective-permute-done | bytes 196640 | tf_op jit(solution)/shard_map/ppermute | solution.py:294
  19.8 2.1 %collective-permute-start.8 = (bf16[128,768]{1,0:T(8,128)(2,1)S(1)}, bf16[128,768]{1,0:T(8,128)(2,1)S(1)}, u32[]{:S(2)}, u32[]{:S(2)}) collective-permute-start(bf16[128,768]{1,0:T(8,128)(2,1)S(1)} %collective-permute-done.3.b_ref), channel_id=1, source_target_pairs={{0,4},{1,5},{4,8},{5,9},{8,12},{9,13},{12,14},{13,15},{14,10},{15,... | collective-permute-start | bytes 589832 | tf_op jit(solution)/shard_map/ppermute | solution.py:294
  21.9 1.0 %gradient.8 = (f32[256,768]{1,0:T(8,128)S(1)}, f32[256,768]{1,0:T(8,128)S(1)}) custom-call(bf16[144,768]{1,0:T(8,128)(2,1)S(1)} %get-tuple-element.100.a_ref, bf16[128,768]{1,0:T(8,128)(2,1)S(1)} %get-tuple-element.101.b_ref, bf16[256,768]{1,0:T(8,128)(2,1)S(1)} %get-tuple-element.102.refs_0_.cast_ref, bf16[256,768]{1,0:T(8,128)(2,1)S(1)} %collective-permute-done.6.refs_1_), custom_call_target="tpu_custom_call" | custom-call | flops 500000000 | bytes 1000000 | tf_op jit(solution)/shard_map/gradient/pallas_call | solution.py:186
  22.9 0.1 collective-permute-start.7
  23.0 1.0 %gradient.9 = (f32[256,768]{1,0:T(8,128)S(1)}, f32[256,768]{1,0:T(8,128)S(1)}) custom-call(bf16[144,768]{1,0:T(8,128)(2,1)S(1)} %collective-permute-done.5.a_ref, bf16[128,768]{1,0:T(8,128)(2,1)S(1)} %collective-permute-done.1.b_ref, bf16[256,768]{1,0:T(8,128)(2,1)S(1)} %get-tuple-element.102.refs_0_.cast_ref, ...), custom_call_target="tpu_custom_call", output_to_operand_aliasing={{0}: (4, {}), {1}: (5, {})} | custom-call | flops 500000000 | bytes 1000000 | tf_op jit(solution)/shard_map/gradient/pallas_call | solution.py:186
  24.0 0.5 %collective-permute-done.10.a_ref = bf16[144,768]{1,0:T(8,128)(2,1)S(1)} collective-permute-done((bf16[144,768]{1,0:T(8,128)(2,1)S(1)}, bf16[144,768]{1,0:T(8,128)(2,1)S(1)}, u32[]{:S(2)}, u32[]{:S(2)}) %collective-permute-start.10) | collective-permute-done | bytes 221216 | tf_op jit(solution)/shard_map/ppermute | solution.py:294
  24.6 2.1 %collective-permute-start.14 = (bf16[144,768]{1,0:T(8,128)(2,1)S(1)}, bf16[144,768]{1,0:T(8,128)(2,1)S(1)}, u32[]{:S(2)}, u32[]{:S(2)}) collective-permute-start(bf16[144,768]{1,0:T(8,128)(2,1)S(1)} %collective-permute-done.10.a_ref), channel_id=1, source_target_pairs={{0,4},{1,5},{4,8},{5,9},{8,12},{9,13},{12,14},{13,15},{14,10},{15,... | collective-permute-start | bytes 663560 | tf_op jit(solution)/shard_map/ppermute | solution.py:294
  26.7 1.0 %gradient.10 = (f32[256,768]{1,0:T(8,128)S(1)}, f32[256,768]{1,0:T(8,128)S(1)}) custom-call(bf16[144,768]{1,0:T(8,128)(2,1)S(1)} %collective-permute-done.a_ref, bf16[128,768]{1,0:T(8,128)(2,1)S(1)} %collective-permute-done.4.b_ref, bf16[256,768]{1,0:T(8,128)(2,1)S(1)} %get-tuple-element.102.refs_0_.cast_ref, ...), custom_call_target="tpu_custom_call", output_to_operand_aliasing={{0}: (4, {}), {1}: (5, {})} | custom-call | flops 500000000 | bytes 1000000 | tf_op jit(solution)/shard_map/gradient/pallas_call | solution.py:186
  27.7 0.1 collective-permute-start.13
  27.8 1.0 %collective-permute-done.8.b_ref = bf16[128,768]{1,0:T(8,128)(2,1)S(1)} collective-permute-done((bf16[128,768]{1,0:T(8,128)(2,1)S(1)}, bf16[128,768]{1,0:T(8,128)(2,1)S(1)}, u32[]{:S(2)}, u32[]{:S(2)}) %collective-permute-start.8) | collective-permute-done | bytes 196640 | tf_op jit(solution)/shard_map/ppermute | solution.py:294
  28.8 2.1 %collective-permute-start.12 = (bf16[128,768]{1,0:T(8,128)(2,1)S(1)}, bf16[128,768]{1,0:T(8,128)(2,1)S(1)}, u32[]{:S(2)}, u32[]{:S(2)}) collective-permute-start(bf16[128,768]{1,0:T(8,128)(2,1)S(1)} %collective-permute-done.8.b_ref), channel_id=1, source_target_pairs={{0,4},{1,5},{4,8},{5,9},{8,12},{9,13},{12,14},{13,15},{14,10},{15,... | collective-permute-start | bytes 589832 | tf_op jit(solution)/shard_map/ppermute | solution.py:294
  30.9 1.0 %gradient.11 = (f32[256,768]{1,0:T(8,128)S(1)}, f32[256,768]{1,0:T(8,128)S(1)}) custom-call(bf16[144,768]{1,0:T(8,128)(2,1)S(1)} %collective-permute-done.10.a_ref, bf16[128,768]{1,0:T(8,128)(2,1)S(1)} %collective-permute-done.3.b_ref, bf16[256,768]{1,0:T(8,128)(2,1)S(1)} %get-tuple-element.102.refs_0_.cast_ref, ...), custom_call_target="tpu_custom_call", output_to_operand_aliasing={{0}: (4, {}), {1}: (5, {})} | custom-call | flops 1000000000 | bytes 1000000 | tf_op jit(solution)/shard_map/gradient/pallas_call | solution.py:186
  32.0 1.0 %gradient.12 = (f32[256,768]{1,0:T(8,128)S(1)}, f32[256,768]{1,0:T(8,128)S(1)}) custom-call(bf16[144,768]{1,0:T(8,128)(2,1)S(1)} %collective-permute-done.2.a_ref, bf16[128,768]{1,0:T(8,128)(2,1)S(1)} %collective-permute-done.9.b_ref, bf16[256,768]{1,0:T(8,128)(2,1)S(1)} %get-tuple-element.102.refs_0_.cast_ref, ...), custom_call_target="tpu_custom_call", output_to_operand_aliasing={{0}: (4, {}), {1}: (5, {})} | custom-call | flops 1000000000 | bytes 1000000 | tf_op jit(solution)/shard_map/gradient/pallas_call | solution.py:186
  33.0 0.5 %collective-permute-done.14.a_ref = bf16[144,768]{1,0:T(8,128)(2,1)S(1)} collective-permute-done((bf16[144,768]{1,0:T(8,128)(2,1)S(1)}, bf16[144,768]{1,0:T(8,128)(2,1)S(1)}, u32[]{:S(2)}, u32[]{:S(2)}) %collective-permute-start.14) | collective-permute-done | bytes 221216 | tf_op jit(solution)/shard_map/ppermute | solution.py:294
  33.5 1.0 %gradient.13 = (f32[256,768]{1,0:T(8,128)S(1)}, f32[256,768]{1,0:T(8,128)S(1)}) custom-call(bf16[144,768]{1,0:T(8,128)(2,1)S(1)} %collective-permute-done.14.a_ref, bf16[128,768]{1,0:T(8,128)(2,1)S(1)} %collective-permute-done.8.b_ref, bf16[256,768]{1,0:T(8,128)(2,1)S(1)} %get-tuple-element.102.refs_0_.cast_ref, ...), custom_call_target="tpu_custom_call", output_to_operand_aliasing={{0}: (4, {}), {1}: (5, {})} | custom-call | flops 1000000000 | bytes 1000000 | tf_op jit(solution)/shard_map/gradient/pallas_call | solution.py:186
  34.5 1.1 %collective-permute-done.13.b_ref = bf16[128,768]{1,0:T(8,128)(2,1)S(1)} collective-permute-done((bf16[128,768]{1,0:T(8,128)(2,1)S(1)}, bf16[128,768]{1,0:T(8,128)(2,1)S(1)}, u32[]{:S(2)}, u32[]{:S(2)}) %collective-permute-start.13) | collective-permute-done | bytes 196640 | tf_op jit(solution)/shard_map/ppermute | solution.py:294
  35.7 1.0 %gradient.14 = (f32[256,768]{1,0:T(8,128)S(1)}, f32[256,768]{1,0:T(8,128)S(1)}) custom-call(bf16[144,768]{1,0:T(8,128)(2,1)S(1)} %collective-permute-done.7.a_ref, bf16[128,768]{1,0:T(8,128)(2,1)S(1)} %collective-permute-done.13.b_ref, bf16[256,768]{1,0:T(8,128)(2,1)S(1)} %get-tuple-element.102.refs_0_.cast_ref, ...), custom_call_target="tpu_custom_call", output_to_operand_aliasing={{0}: (4, {}), {1}: (5, {})} | custom-call | flops 1000000000 | bytes 1000000 | tf_op jit(solution)/shard_map/gradient/pallas_call | solution.py:186
  36.7 0.1 collective-permute-start.17
  36.8 0.1 collective-permute-done.12.b_ref
  36.9 0.4 %collective-permute-start.16 = (bf16[128,768]{1,0:T(8,128)(2,1)S(1)}, bf16[128,768]{1,0:T(8,128)(2,1)S(1)}, u32[]{:S(2)}, u32[]{:S(2)}) collective-permute-start(bf16[128,768]{1,0:T(8,128)(2,1)S(1)} %collective-permute-done.12.b_ref), channel_id=1, source_target_pairs={{0,1},{1,0},{2,3},{3,2},{4,5},{5,4},{6,7},{7,6},{8,9},{9,8},{10,11... | collective-permute-start | bytes 589832 | tf_op jit(solution)/shard_map/ppermute | solution.py:294
  37.3 1.6 %collective-permute-done.11.a_ref = bf16[144,768]{1,0:T(8,128)(2,1)S(1)} collective-permute-done((bf16[144,768]{1,0:T(8,128)(2,1)S(1)}, bf16[144,768]{1,0:T(8,128)(2,1)S(1)}, u32[]{:S(2)}, u32[]{:S(2)}) %collective-permute-start.11) | collective-permute-done | bytes 221216 | tf_op jit(solution)/shard_map/ppermute | solution.py:294
  38.9 0.7 %gradient.15.sum_ref = f32[256,768]{1,0:T(8,128)S(1)} custom-call(bf16[144,768]{1,0:T(8,128)(2,1)S(1)} %collective-permute-done.11.a_ref, bf16[128,768]{1,0:T(8,128)(2,1)S(1)} %collective-permute-done.12.b_ref, bf16[256,768]{1,0:T(8,128)(2,1)S(1)} %get-tuple-element.102.refs_0_.cast_ref, ...), custom_call_target="tpu_custom_call", output_to_operand_aliasing={{}: (3, {})} | custom-call | flops 10000000000 | bytes 1000000 | tf_op jit(solution)/shard_map/gradient/pallas_call | solution.py:186
  39.6 0.8 %collective-permute-done.15.a_ref = bf16[144,768]{1,0:T(8,128)(2,1)S(1)} collective-permute-done((bf16[144,768]{1,0:T(8,128)(2,1)S(1)}, bf16[144,768]{1,0:T(8,128)(2,1)S(1)}, u32[]{:S(2)}, u32[]{:S(2)}) %collective-permute-start.15) | collective-permute-done | bytes 221216 | tf_op jit(solution)/shard_map/ppermute | solution.py:294
  40.4 2.5 %finish.1 = (f32[256,768]{1,0:T(8,128)}, f32[256,768]{1,0:T(8,128)}, f32[256,768]{1,0:T(8,128)}) custom-call(bf16[144,768]{1,0:T(8,128)(2,1)S(1)} %collective-permute-done.15.a_ref, bf16[128,768]{1,0:T(8,128)(2,1)S(1)} %collective-permute-done.16.b_ref, bf16[256,768]{1,0:T(8,128)(2,1)S(1)} %get-tuple-element.102.refs_0_.cast_ref, ...), custom_call_target="tpu_custom_call" | custom-call | flops 10000000000 | bytes 1000000 | tf_op jit(solution)/shard_map/finish/pallas_call | solution.py:243
  (20 shorter events, 0.1 us)
Async XLA Ops:
  2.1 8.7 %collective-permute-start.1 = (bf16[128,768]{1,0:T(8,128)(2,1)S(1)}, bf16[128,768]{1,0:T(8,128)(2,1)S(1)}, u32[]{:S(2)}, u32[]{:S(2)}) collective-permute-start(bf16[128,768]{1,0:T(8,128)(2,1)S(1)} %get-tuple-element.101.b_ref), channel_id=1, source_target_pairs={{0,4},{1,5},{4,8},{5,9},{8,12},{9,13},{12,14},{13,15},{14,10},{15,... | collective-permute-start | bytes 589832 | tf_op jit(solution)/shard_map/ppermute | solution.py:294
  5.2 8.4 %collective-permute-start = (bf16[144,768]{1,0:T(8,128)(2,1)S(1)}, bf16[144,768]{1,0:T(8,128)(2,1)S(1)}, u32[]{:S(2)}, u32[]{:S(2)}) collective-permute-start(bf16[144,768]{1,0:T(8,128)(2,1)S(1)} %get-tuple-element.100.a_ref), channel_id=1, source_target_pairs={{4,0},{5,1},{8,4},{9,5},{12,8},{13,9},{14,12},{15,13},{10,14},{11,... | collective-permute-start | bytes 663560 | tf_op jit(solution)/shard_map/ppermute | solution.py:294
  5.2 16.7 %collective-permute-start.6 = (bf16[256,768]{1,0:T(8,128)(2,1)S(1)}, bf16[256,768]{1,0:T(8,128)(2,1)S(1)}, u32[]{:S(2)}, u32[]{:S(2)}) collective-permute-start(bf16[256,768]{1,0:T(8,128)(2,1)S(1)} %get-tuple-element.102.refs_0_.cast_ref), channel_id=1, source_target_pairs={{0,1},{1,0},{2,3},{3,2},{4,5},{5,4},{6,7},{7,6},{8,9},{9,8},{10,11... | collective-permute-start | bytes 1179656 | tf_op jit(solution)/shard_map/ppermute | solution.py:294
  5.2 10.4 %collective-permute-start.5 = (bf16[144,768]{1,0:T(8,128)(2,1)S(1)}, bf16[144,768]{1,0:T(8,128)(2,1)S(1)}, u32[]{:S(2)}, u32[]{:S(2)}) collective-permute-start(bf16[144,768]{1,0:T(8,128)(2,1)S(1)} %get-tuple-element.100.a_ref), channel_id=1, source_target_pairs={{0,4},{1,5},{4,8},{5,9},{8,12},{9,13},{12,14},{13,15},{14,10},{15,... | collective-permute-start | bytes 663560 | tf_op jit(solution)/shard_map/ppermute | solution.py:294
  7.2 10.5 %collective-permute-start.4 = (bf16[128,768]{1,0:T(8,128)(2,1)S(1)}, bf16[128,768]{1,0:T(8,128)(2,1)S(1)}, u32[]{:S(2)}, u32[]{:S(2)}) collective-permute-start(bf16[128,768]{1,0:T(8,128)(2,1)S(1)} %get-tuple-element.101.b_ref), channel_id=1, source_target_pairs={{4,0},{5,1},{8,4},{9,5},{12,8},{13,9},{14,12},{15,13},{10,14},{11,... | collective-permute-start | bytes 589832 | tf_op jit(solution)/shard_map/ppermute | solution.py:294
  10.9 9.0 %collective-permute-start.3 = (bf16[128,768]{1,0:T(8,128)(2,1)S(1)}, bf16[128,768]{1,0:T(8,128)(2,1)S(1)}, u32[]{:S(2)}, u32[]{:S(2)}) collective-permute-start(bf16[128,768]{1,0:T(8,128)(2,1)S(1)} %collective-permute-done.1.b_ref), channel_id=1, source_target_pairs={{0,4},{1,5},{4,8},{5,9},{8,12},{9,13},{12,14},{13,15},{14,10},{15,... | collective-permute-start | bytes 589832 | tf_op jit(solution)/shard_map/ppermute | solution.py:294
  13.6 9.4 %collective-permute-start.2 = (bf16[144,768]{1,0:T(8,128)(2,1)S(1)}, bf16[144,768]{1,0:T(8,128)(2,1)S(1)}, u32[]{:S(2)}, u32[]{:S(2)}) collective-permute-start(bf16[144,768]{1,0:T(8,128)(2,1)S(1)} %collective-permute-done.a_ref), channel_id=1, source_target_pairs={{4,0},{5,1},{8,4},{9,5},{12,8},{13,9},{14,12},{15,13},{10,14},{11,... | collective-permute-start | bytes 663560 | tf_op jit(solution)/shard_map/ppermute | solution.py:294
  15.6 9.0 %collective-permute-start.10 = (bf16[144,768]{1,0:T(8,128)(2,1)S(1)}, bf16[144,768]{1,0:T(8,128)(2,1)S(1)}, u32[]{:S(2)}, u32[]{:S(2)}) collective-permute-start(bf16[144,768]{1,0:T(8,128)(2,1)S(1)} %collective-permute-done.5.a_ref), channel_id=1, source_target_pairs={{0,4},{1,5},{4,8},{5,9},{8,12},{9,13},{12,14},{13,15},{14,10},{15,... | collective-permute-start | bytes 663560 | tf_op jit(solution)/shard_map/ppermute | solution.py:294
  17.8 9.9 %collective-permute-start.9 = (bf16[128,768]{1,0:T(8,128)(2,1)S(1)}, bf16[128,768]{1,0:T(8,128)(2,1)S(1)}, u32[]{:S(2)}, u32[]{:S(2)}) collective-permute-start(bf16[128,768]{1,0:T(8,128)(2,1)S(1)} %collective-permute-done.4.b_ref), channel_id=1, source_target_pairs={{4,0},{5,1},{8,4},{9,5},{12,8},{13,9},{14,12},{15,13},{10,14},{11,... | collective-permute-start | bytes 589832 | tf_op jit(solution)/shard_map/ppermute | solution.py:294
  19.8 9.0 %collective-permute-start.8 = (bf16[128,768]{1,0:T(8,128)(2,1)S(1)}, bf16[128,768]{1,0:T(8,128)(2,1)S(1)}, u32[]{:S(2)}, u32[]{:S(2)}) collective-permute-start(bf16[128,768]{1,0:T(8,128)(2,1)S(1)} %collective-permute-done.3.b_ref), channel_id=1, source_target_pairs={{0,4},{1,5},{4,8},{5,9},{8,12},{9,13},{12,14},{13,15},{14,10},{15,... | collective-permute-start | bytes 589832 | tf_op jit(solution)/shard_map/ppermute | solution.py:294
  22.9 9.0 %collective-permute-start.7 = (bf16[144,768]{1,0:T(8,128)(2,1)S(1)}, bf16[144,768]{1,0:T(8,128)(2,1)S(1)}, u32[]{:S(2)}, u32[]{:S(2)}) collective-permute-start(bf16[144,768]{1,0:T(8,128)(2,1)S(1)} %collective-permute-done.2.a_ref), channel_id=1, source_target_pairs={{4,0},{5,1},{8,4},{9,5},{12,8},{13,9},{14,12},{15,13},{10,14},{11,... | collective-permute-start | bytes 663560 | tf_op jit(solution)/shard_map/ppermute | solution.py:294
  24.6 9.0 %collective-permute-start.14 = (bf16[144,768]{1,0:T(8,128)(2,1)S(1)}, bf16[144,768]{1,0:T(8,128)(2,1)S(1)}, u32[]{:S(2)}, u32[]{:S(2)}) collective-permute-start(bf16[144,768]{1,0:T(8,128)(2,1)S(1)} %collective-permute-done.10.a_ref), channel_id=1, source_target_pairs={{0,4},{1,5},{4,8},{5,9},{8,12},{9,13},{12,14},{13,15},{14,10},{15,... | collective-permute-start | bytes 663560 | tf_op jit(solution)/shard_map/ppermute | solution.py:294
  27.7 8.0 %collective-permute-start.13 = (bf16[128,768]{1,0:T(8,128)(2,1)S(1)}, bf16[128,768]{1,0:T(8,128)(2,1)S(1)}, u32[]{:S(2)}, u32[]{:S(2)}) collective-permute-start(bf16[128,768]{1,0:T(8,128)(2,1)S(1)} %collective-permute-done.9.b_ref), channel_id=1, source_target_pairs={{4,0},{5,1},{8,4},{9,5},{12,8},{13,9},{14,12},{15,13},{10,14},{11,... | collective-permute-start | bytes 589832 | tf_op jit(solution)/shard_map/ppermute | solution.py:294
  28.8 8.1 %collective-permute-start.12 = (bf16[128,768]{1,0:T(8,128)(2,1)S(1)}, bf16[128,768]{1,0:T(8,128)(2,1)S(1)}, u32[]{:S(2)}, u32[]{:S(2)}) collective-permute-start(bf16[128,768]{1,0:T(8,128)(2,1)S(1)} %collective-permute-done.8.b_ref), channel_id=1, source_target_pairs={{0,4},{1,5},{4,8},{5,9},{8,12},{9,13},{12,14},{13,15},{14,10},{15,... | collective-permute-start | bytes 589832 | tf_op jit(solution)/shard_map/ppermute | solution.py:294
  31.9 7.0 %collective-permute-start.11 = (bf16[144,768]{1,0:T(8,128)(2,1)S(1)}, bf16[144,768]{1,0:T(8,128)(2,1)S(1)}, u32[]{:S(2)}, u32[]{:S(2)}) collective-permute-start(bf16[144,768]{1,0:T(8,128)(2,1)S(1)} %collective-permute-done.7.a_ref), channel_id=1, source_target_pairs={{4,0},{5,1},{8,4},{9,5},{12,8},{13,9},{14,12},{15,13},{10,14},{11,... | collective-permute-start | bytes 663560 | tf_op jit(solution)/shard_map/ppermute | solution.py:294
  36.7 3.7 %collective-permute-start.17 = (f32[256,768]{1,0:T(8,128)S(1)}, f32[256,768]{1,0:T(8,128)S(1)}, u32[]{:S(2)}, u32[]{:S(2)}) collective-permute-start(f32[256,768]{1,0:T(8,128)S(1)} %get-tuple-element.156), channel_id=1, source_target_pairs={{0,1},{1,0},{2,3},{3,2},{4,5},{5,4},{6,7},{7,6},{8,9},{9,8},{10,11... | collective-permute-start | bytes 2359304 | tf_op jit(solution)/shard_map/ppermute | solution.py:294
  36.9 3.5 %copy-start = (f32[256,768]{1,0:T(8,128)S(1)}, f32[256,768]{1,0:T(8,128)}, u32[]{:S(2)}) copy-start(f32[256,768]{1,0:T(8,128)} %weights_ref.1) | copy-start | bytes 2359300
  36.9 3.5 %copy-start.1 = (f32[256,768]{1,0:T(8,128)S(1)}, f32[256,768]{1,0:T(8,128)}, u32[]{:S(2)}) copy-start(f32[256,768]{1,0:T(8,128)} %first_ref.1) | copy-start | bytes 2359300
  36.9 3.5 %copy-start.2 = (f32[256,768]{1,0:T(8,128)S(1)}, f32[256,768]{1,0:T(8,128)}, u32[]{:S(2)}) copy-start(f32[256,768]{1,0:T(8,128)} %second_ref.1) | copy-start | bytes 2359300
  36.9 2.7 %collective-permute-start.16 = (bf16[128,768]{1,0:T(8,128)(2,1)S(1)}, bf16[128,768]{1,0:T(8,128)(2,1)S(1)}, u32[]{:S(2)}, u32[]{:S(2)}) collective-permute-start(bf16[128,768]{1,0:T(8,128)(2,1)S(1)} %collective-permute-done.12.b_ref), channel_id=1, source_target_pairs={{0,1},{1,0},{2,3},{3,2},{4,5},{5,4},{6,7},{7,6},{8,9},{9,8},{10,11... | collective-permute-start | bytes 589832 | tf_op jit(solution)/shard_map/ppermute | solution.py:294
  38.9 1.5 %collective-permute-start.15 = (bf16[144,768]{1,0:T(8,128)(2,1)S(1)}, bf16[144,768]{1,0:T(8,128)(2,1)S(1)}, u32[]{:S(2)}, u32[]{:S(2)}) collective-permute-start(bf16[144,768]{1,0:T(8,128)(2,1)S(1)} %collective-permute-done.11.a_ref), channel_id=1, source_target_pairs={{0,1},{1,0},{2,3},{3,2},{4,5},{5,4},{6,7},{7,6},{8,9},{9,8},{10,11... | collective-permute-start | bytes 663560 | tf_op jit(solution)/shard_map/ppermute | solution.py:294

commit v10 on v9

--- a/solution.py
+++ b/solution.py
@@ -17,7 +17,7 @@
 
 WORD = 32
 LANES = 128
-PIECES = 4
+PIECE = 32
 VMEM_LIMIT = 32 * 1024 * 1024
 FLOPS = 5 * 10**8
 LATE_FLOPS = 10 * 10**8
@@ -129,7 +129,7 @@
     )(*(pltpu.with_memory_space_constraint(x, pltpu.HBM) for x in inputs))
 
 
-def signs_of(codes, owner, bits, height):
+def signs_of(codes, owner, bits, height, parts):
     docs = codes.shape[1]
     scale = power_of_two(owner * (height // LANES), bits, jnp.float32(2.0**64), -1)
     scaled = codes * scale
@@ -137,7 +137,7 @@
         jnp.ones((WORD, docs), jnp.int32), lax.broadcasted_iota(jnp.int32, (WORD, docs), 0)
     )
     spread = []
-    for part in range(height // LANES):
+    for part in parts:
         row = jnp.minimum(scaled * 2.0**-part, 512.0).astype(jnp.int32) - LANES
         word = row >> 5
         bit = jnp.left_shift(jnp.ones_like(row), row & (WORD - 1))
@@ -148,19 +148,24 @@
     return jnp.concatenate(spread, axis=0)
 
 
-def doubled_gradient(bits, owners, a_ref, b_ref, w_refs):
+def doubled_gradient(bits, owners, a_ref, b_ref, w_refs, parts=None):
     height = w_refs[0].shape[0]
     head = b_ref.shape[0]
     number = 2 * head
     docs = jnp.concatenate([a_ref[:head, :], b_ref[...]], axis=0)
     codes = jnp.concatenate([a_ref[head:, :number], a_ref[head:, number : 2 * number]], axis=0)
     codes = codes.astype(jnp.float32)
-    weights = jnp.concatenate([ref[...] for ref in w_refs], axis=0)
+    parts = range(height // LANES) if parts is None else parts
+    weights = jnp.concatenate(
+        [ref[part * LANES : (part + 1) * LANES, :] for ref in w_refs for part in parts], axis=0
+    )
     halved = lax.dot_general(
         weights, docs, (((1,), (1,)), ((), ())), preferred_element_type=jnp.float32
     )
     me = lax.axis_index("blk")
-    signs = jnp.concatenate([signs_of(codes, me ^ owner, bits, height) for owner in owners], axis=0)
+    signs = jnp.concatenate(
+        [signs_of(codes, me ^ owner, bits, height, parts) for owner in owners], axis=0
+    )
     signal = (jnp.tanh(halved) + signs).astype(jnp.bfloat16)
     return jnp.dot(signal, docs, preferred_element_type=jnp.float32)
 
@@ -213,13 +218,14 @@
     second_out,
     done,
 ):
-    part = doubled_gradient(bits, (0,), a_ref, b_ref, [cast_ref])
-    height = part.shape[0]
-    size = height // PIECES
     writes = []
-    for i in range(PIECES):
-        here = pl.ds(i * size, size)
-        gradient = 0.5 * (sum_ref[here, :] + other_ref[here, :] + part[i * size : (i + 1) * size])
+    for i in range(sum_ref.shape[0] // PIECE):
+        start = i * PIECE
+        here = pl.ds(start, PIECE)
+        if start % LANES == 0:
+            part = doubled_gradient(bits, (0,), a_ref, b_ref, [cast_ref], [start // LANES])
+        piece = part[start % LANES : start % LANES + PIECE]
+        gradient = 0.5 * (sum_ref[here, :] + other_ref[here, :] + piece)
         new_weights, new_first, new_second = adam_step(
             weights_ref[here, :], first_ref[here, :], second_ref[here, :], gradient
         )
@@ -246,7 +252,7 @@
         out_specs=[pl.BlockSpec(memory_space=pltpu.HBM)] * 3,
         out_shape=[shape] * 3,
         scratch_shapes=[pltpu.VMEM(weights.shape, jnp.float32)] * 3
-        + [pltpu.SemaphoreType.DMA((PIECES, 3))],
+        + [pltpu.SemaphoreType.DMA((weights.shape[0] // PIECE, 3))],
         compiler_params=pltpu.CompilerParams(vmem_limit_bytes=VMEM_LIMIT),
         cost_estimate=pl.CostEstimate(flops=END_FLOPS, bytes_accessed=10**6, transcendentals=0),
         name="finish",

time: 43.1 us -> 43.2 us (level)
  no operation moved by 1% of the time
where the time goes in v10:
time: 43.2 us; the launch traced here: 43 us
  starting transfers between devices  16.4 us (38%)
  waiting for transfers between devices  14.1 us (33%)
  Pallas kernels  11.8 us (27%)
  between operations  0.79 us (2%)
    ppermute x18, starting transfers between devices, send(): return lax.ppermute(value, 'blk', pairs)  16.4 us
    ppermute x18, waiting for transfers between devices, send(): return lax.ppermute(value, 'blk', pairs)  14.1 us
    pallas_call x8, Pallas kernels, add_gradient(): pl.pallas_call(functools.partial(gradient_kernel, bits, owners, not sums)...  7.72 us
    pallas_call x1, Pallas kernels, finish(): pl.pallas_call(functools.partial(finish_kernel, bits), in_specs=[pl.Block...  2.58 us
    pallas_call x1, Pallas kernels, prepare(): pl.pallas_call(functools.partial(prepare_kernel, (lines - 1).bit_length()...  1.48 us
  transfers between devices with their start and end apart: 18, of which 11 were waited for; matrix products, arithmetic and copies ran while one was open for 0% of the time, Pallas kernels for 18%

profile of v10, /device:TPU:0, one launch (start us, length us, event | category | flops | bytes accessed | tf_op | source)
XLA Modules:
  0.0 43.0 jit_solution(16321755602903198310)
XLA Ops:
  0.6 1.5 %prepare.1 = (bf16[144,768]{1,0:T(8,128)(2,1)S(1)}, bf16[128,768]{1,0:T(8,128)(2,1)S(1)}, bf16[256,768]{1,0:T(8,128)(2,1)S(1)}) custom-call(s32[32,256]{1,0:T(8,128)} %bitcast.3, s32[1,256]{1,0:T(1,128)} %bitcast.5, s32[32,128]{1,0:T(8,128)} %bitcast.4, bf16[256,768]{1,0:T(8,128)(2,1)} %docs_hbm.1, f32[256,768]{1,0:T(8,128)} %weights_ref.1), custom_call_target="tpu_custom_call" | custom-call | tf_op jit(solution)/shard_map/prepare/pallas_call | solution.py:111
  2.1 3.1 %collective-permute-start.1 = (bf16[128,768]{1,0:T(8,128)(2,1)S(1)}, bf16[128,768]{1,0:T(8,128)(2,1)S(1)}, u32[]{:S(2)}, u32[]{:S(2)}) collective-permute-start(bf16[128,768]{1,0:T(8,128)(2,1)S(1)} %get-tuple-element.101.b_ref), channel_id=1, source_target_pairs={{0,4},{1,5},{4,8},{5,9},{8,12},{9,13},{12,14},{13,15},{14,10},{15,... | collective-permute-start | bytes 589832 | tf_op jit(solution)/shard_map/ppermute | solution.py:300
  5.2 2.0 %collective-permute-start.5 = (bf16[144,768]{1,0:T(8,128)(2,1)S(1)}, bf16[144,768]{1,0:T(8,128)(2,1)S(1)}, u32[]{:S(2)}, u32[]{:S(2)}) collective-permute-start(bf16[144,768]{1,0:T(8,128)(2,1)S(1)} %get-tuple-element.100.a_ref), channel_id=1, source_target_pairs={{0,4},{1,5},{4,8},{5,9},{8,12},{9,13},{12,14},{13,15},{14,10},{15,... | collective-permute-start | bytes 663560 | tf_op jit(solution)/shard_map/ppermute | solution.py:300
  7.2 3.6 %collective-permute-done.1.b_ref = bf16[128,768]{1,0:T(8,128)(2,1)S(1)} collective-permute-done((bf16[128,768]{1,0:T(8,128)(2,1)S(1)}, bf16[128,768]{1,0:T(8,128)(2,1)S(1)}, u32[]{:S(2)}, u32[]{:S(2)}) %collective-permute-start.1) | collective-permute-done | bytes 196640 | tf_op jit(solution)/shard_map/ppermute | solution.py:300
  10.9 2.1 %collective-permute-start.3 = (bf16[128,768]{1,0:T(8,128)(2,1)S(1)}, bf16[128,768]{1,0:T(8,128)(2,1)S(1)}, u32[]{:S(2)}, u32[]{:S(2)}) collective-permute-start(bf16[128,768]{1,0:T(8,128)(2,1)S(1)} %collective-permute-done.1.b_ref), channel_id=1, source_target_pairs={{0,4},{1,5},{4,8},{5,9},{8,12},{9,13},{12,14},{13,15},{14,10},{15,... | collective-permute-start | bytes 589832 | tf_op jit(solution)/shard_map/ppermute | solution.py:300
  13.0 0.6 %collective-permute-done.a_ref = bf16[144,768]{1,0:T(8,128)(2,1)S(1)} collective-permute-done((bf16[144,768]{1,0:T(8,128)(2,1)S(1)}, bf16[144,768]{1,0:T(8,128)(2,1)S(1)}, u32[]{:S(2)}, u32[]{:S(2)}) %collective-permute-start) | collective-permute-done | bytes 221216 | tf_op jit(solution)/shard_map/ppermute | solution.py:300
  13.6 2.1 %collective-permute-done.5.a_ref = bf16[144,768]{1,0:T(8,128)(2,1)S(1)} collective-permute-done((bf16[144,768]{1,0:T(8,128)(2,1)S(1)}, bf16[144,768]{1,0:T(8,128)(2,1)S(1)}, u32[]{:S(2)}, u32[]{:S(2)}) %collective-permute-start.5) | collective-permute-done | bytes 221216 | tf_op jit(solution)/shard_map/ppermute | solution.py:300
  15.6 2.1 %collective-permute-start.10 = (bf16[144,768]{1,0:T(8,128)(2,1)S(1)}, bf16[144,768]{1,0:T(8,128)(2,1)S(1)}, u32[]{:S(2)}, u32[]{:S(2)}) collective-permute-start(bf16[144,768]{1,0:T(8,128)(2,1)S(1)} %collective-permute-done.5.a_ref), channel_id=1, source_target_pairs={{0,4},{1,5},{4,8},{5,9},{8,12},{9,13},{12,14},{13,15},{14,10},{15,... | collective-permute-start | bytes 663560 | tf_op jit(solution)/shard_map/ppermute | solution.py:300
  17.8 2.1 %collective-permute-done.3.b_ref = bf16[128,768]{1,0:T(8,128)(2,1)S(1)} collective-permute-done((bf16[128,768]{1,0:T(8,128)(2,1)S(1)}, bf16[128,768]{1,0:T(8,128)(2,1)S(1)}, u32[]{:S(2)}, u32[]{:S(2)}) %collective-permute-start.3) | collective-permute-done | bytes 196640 | tf_op jit(solution)/shard_map/ppermute | solution.py:300
  19.8 2.1 %collective-permute-start.8 = (bf16[128,768]{1,0:T(8,128)(2,1)S(1)}, bf16[128,768]{1,0:T(8,128)(2,1)S(1)}, u32[]{:S(2)}, u32[]{:S(2)}) collective-permute-start(bf16[128,768]{1,0:T(8,128)(2,1)S(1)} %collective-permute-done.3.b_ref), channel_id=1, source_target_pairs={{0,4},{1,5},{4,8},{5,9},{8,12},{9,13},{12,14},{13,15},{14,10},{15,... | collective-permute-start | bytes 589832 | tf_op jit(solution)/shard_map/ppermute | solution.py:300
  21.9 1.0 %gradient.8 = (f32[256,768]{1,0:T(8,128)S(1)}, f32[256,768]{1,0:T(8,128)S(1)}) custom-call(bf16[144,768]{1,0:T(8,128)(2,1)S(1)} %get-tuple-element.100.a_ref, bf16[128,768]{1,0:T(8,128)(2,1)S(1)} %get-tuple-element.101.b_ref, bf16[256,768]{1,0:T(8,128)(2,1)S(1)} %get-tuple-element.102.refs_0_.cast_ref, bf16[256,768]{1,0:T(8,128)(2,1)S(1)} %collective-permute-done.6.refs_1_), custom_call_target="tpu_custom_call" | custom-call | flops 500000000 | bytes 1000000 | tf_op jit(solution)/shard_map/gradient/pallas_call | solution.py:191
  22.9 0.1 collective-permute-start.7
  23.0 1.0 %gradient.9 = (f32[256,768]{1,0:T(8,128)S(1)}, f32[256,768]{1,0:T(8,128)S(1)}) custom-call(bf16[144,768]{1,0:T(8,128)(2,1)S(1)} %collective-permute-done.5.a_ref, bf16[128,768]{1,0:T(8,128)(2,1)S(1)} %collective-permute-done.1.b_ref, bf16[256,768]{1,0:T(8,128)(2,1)S(1)} %get-tuple-element.102.refs_0_.cast_ref, ...), custom_call_target="tpu_custom_call", output_to_operand_aliasing={{0}: (4, {}), {1}: (5, {})} | custom-call | flops 500000000 | bytes 1000000 | tf_op jit(solution)/shard_map/gradient/pallas_call | solution.py:191
  24.0 0.5 %collective-permute-done.10.a_ref = bf16[144,768]{1,0:T(8,128)(2,1)S(1)} collective-permute-done((bf16[144,768]{1,0:T(8,128)(2,1)S(1)}, bf16[144,768]{1,0:T(8,128)(2,1)S(1)}, u32[]{:S(2)}, u32[]{:S(2)}) %collective-permute-start.10) | collective-permute-done | bytes 221216 | tf_op jit(solution)/shard_map/ppermute | solution.py:300
  24.6 2.1 %collective-permute-start.14 = (bf16[144,768]{1,0:T(8,128)(2,1)S(1)}, bf16[144,768]{1,0:T(8,128)(2,1)S(1)}, u32[]{:S(2)}, u32[]{:S(2)}) collective-permute-start(bf16[144,768]{1,0:T(8,128)(2,1)S(1)} %collective-permute-done.10.a_ref), channel_id=1, source_target_pairs={{0,4},{1,5},{4,8},{5,9},{8,12},{9,13},{12,14},{13,15},{14,10},{15,... | collective-permute-start | bytes 663560 | tf_op jit(solution)/shard_map/ppermute | solution.py:300
  26.7 1.0 %gradient.10 = (f32[256,768]{1,0:T(8,128)S(1)}, f32[256,768]{1,0:T(8,128)S(1)}) custom-call(bf16[144,768]{1,0:T(8,128)(2,1)S(1)} %collective-permute-done.a_ref, bf16[128,768]{1,0:T(8,128)(2,1)S(1)} %collective-permute-done.4.b_ref, bf16[256,768]{1,0:T(8,128)(2,1)S(1)} %get-tuple-element.102.refs_0_.cast_ref, ...), custom_call_target="tpu_custom_call", output_to_operand_aliasing={{0}: (4, {}), {1}: (5, {})} | custom-call | flops 500000000 | bytes 1000000 | tf_op jit(solution)/shard_map/gradient/pallas_call | solution.py:191
  27.7 0.1 collective-permute-start.13
  27.8 1.0 %collective-permute-done.8.b_ref = bf16[128,768]{1,0:T(8,128)(2,1)S(1)} collective-permute-done((bf16[128,768]{1,0:T(8,128)(2,1)S(1)}, bf16[128,768]{1,0:T(8,128)(2,1)S(1)}, u32[]{:S(2)}, u32[]{:S(2)}) %collective-permute-start.8) | collective-permute-done | bytes 196640 | tf_op jit(solution)/shard_map/ppermute | solution.py:300
  28.8 2.1 %collective-permute-start.12 = (bf16[128,768]{1,0:T(8,128)(2,1)S(1)}, bf16[128,768]{1,0:T(8,128)(2,1)S(1)}, u32[]{:S(2)}, u32[]{:S(2)}) collective-permute-start(bf16[128,768]{1,0:T(8,128)(2,1)S(1)} %collective-permute-done.8.b_ref), channel_id=1, source_target_pairs={{0,4},{1,5},{4,8},{5,9},{8,12},{9,13},{12,14},{13,15},{14,10},{15,... | collective-permute-start | bytes 589832 | tf_op jit(solution)/shard_map/ppermute | solution.py:300
  30.9 1.0 %gradient.11 = (f32[256,768]{1,0:T(8,128)S(1)}, f32[256,768]{1,0:T(8,128)S(1)}) custom-call(bf16[144,768]{1,0:T(8,128)(2,1)S(1)} %collective-permute-done.10.a_ref, bf16[128,768]{1,0:T(8,128)(2,1)S(1)} %collective-permute-done.3.b_ref, bf16[256,768]{1,0:T(8,128)(2,1)S(1)} %get-tuple-element.102.refs_0_.cast_ref, ...), custom_call_target="tpu_custom_call", output_to_operand_aliasing={{0}: (4, {}), {1}: (5, {})} | custom-call | flops 1000000000 | bytes 1000000 | tf_op jit(solution)/shard_map/gradient/pallas_call | solution.py:191
  32.0 1.0 %gradient.12 = (f32[256,768]{1,0:T(8,128)S(1)}, f32[256,768]{1,0:T(8,128)S(1)}) custom-call(bf16[144,768]{1,0:T(8,128)(2,1)S(1)} %collective-permute-done.2.a_ref, bf16[128,768]{1,0:T(8,128)(2,1)S(1)} %collective-permute-done.9.b_ref, bf16[256,768]{1,0:T(8,128)(2,1)S(1)} %get-tuple-element.102.refs_0_.cast_ref, ...), custom_call_target="tpu_custom_call", output_to_operand_aliasing={{0}: (4, {}), {1}: (5, {})} | custom-call | flops 1000000000 | bytes 1000000 | tf_op jit(solution)/shard_map/gradient/pallas_call | solution.py:191
  33.0 0.5 %collective-permute-done.14.a_ref = bf16[144,768]{1,0:T(8,128)(2,1)S(1)} collective-permute-done((bf16[144,768]{1,0:T(8,128)(2,1)S(1)}, bf16[144,768]{1,0:T(8,128)(2,1)S(1)}, u32[]{:S(2)}, u32[]{:S(2)}) %collective-permute-start.14) | collective-permute-done | bytes 221216 | tf_op jit(solution)/shard_map/ppermute | solution.py:300
  33.5 1.0 %gradient.13 = (f32[256,768]{1,0:T(8,128)S(1)}, f32[256,768]{1,0:T(8,128)S(1)}) custom-call(bf16[144,768]{1,0:T(8,128)(2,1)S(1)} %collective-permute-done.14.a_ref, bf16[128,768]{1,0:T(8,128)(2,1)S(1)} %collective-permute-done.8.b_ref, bf16[256,768]{1,0:T(8,128)(2,1)S(1)} %get-tuple-element.102.refs_0_.cast_ref, ...), custom_call_target="tpu_custom_call", output_to_operand_aliasing={{0}: (4, {}), {1}: (5, {})} | custom-call | flops 1000000000 | bytes 1000000 | tf_op jit(solution)/shard_map/gradient/pallas_call | solution.py:191
  34.5 1.1 %collective-permute-done.13.b_ref = bf16[128,768]{1,0:T(8,128)(2,1)S(1)} collective-permute-done((bf16[128,768]{1,0:T(8,128)(2,1)S(1)}, bf16[128,768]{1,0:T(8,128)(2,1)S(1)}, u32[]{:S(2)}, u32[]{:S(2)}) %collective-permute-start.13) | collective-permute-done | bytes 196640 | tf_op jit(solution)/shard_map/ppermute | solution.py:300
  35.7 1.0 %gradient.14 = (f32[256,768]{1,0:T(8,128)S(1)}, f32[256,768]{1,0:T(8,128)S(1)}) custom-call(bf16[144,768]{1,0:T(8,128)(2,1)S(1)} %collective-permute-done.7.a_ref, bf16[128,768]{1,0:T(8,128)(2,1)S(1)} %collective-permute-done.13.b_ref, bf16[256,768]{1,0:T(8,128)(2,1)S(1)} %get-tuple-element.102.refs_0_.cast_ref, ...), custom_call_target="tpu_custom_call", output_to_operand_aliasing={{0}: (4, {}), {1}: (5, {})} | custom-call | flops 1000000000 | bytes 1000000 | tf_op jit(solution)/shard_map/gradient/pallas_call | solution.py:191
  36.7 0.1 collective-permute-start.17
  36.8 0.1 collective-permute-done.12.b_ref
  36.9 0.4 %collective-permute-start.16 = (bf16[128,768]{1,0:T(8,128)(2,1)S(1)}, bf16[128,768]{1,0:T(8,128)(2,1)S(1)}, u32[]{:S(2)}, u32[]{:S(2)}) collective-permute-start(bf16[128,768]{1,0:T(8,128)(2,1)S(1)} %collective-permute-done.12.b_ref), channel_id=1, source_target_pairs={{0,1},{1,0},{2,3},{3,2},{4,5},{5,4},{6,7},{7,6},{8,9},{9,8},{10,11... | collective-permute-start | bytes 589832 | tf_op jit(solution)/shard_map/ppermute | solution.py:300
  37.3 1.6 %collective-permute-done.11.a_ref = bf16[144,768]{1,0:T(8,128)(2,1)S(1)} collective-permute-done((bf16[144,768]{1,0:T(8,128)(2,1)S(1)}, bf16[144,768]{1,0:T(8,128)(2,1)S(1)}, u32[]{:S(2)}, u32[]{:S(2)}) %collective-permute-start.11) | collective-permute-done | bytes 221216 | tf_op jit(solution)/shard_map/ppermute | solution.py:300
  38.9 0.7 %gradient.15.sum_ref = f32[256,768]{1,0:T(8,128)S(1)} custom-call(bf16[144,768]{1,0:T(8,128)(2,1)S(1)} %collective-permute-done.11.a_ref, bf16[128,768]{1,0:T(8,128)(2,1)S(1)} %collective-permute-done.12.b_ref, bf16[256,768]{1,0:T(8,128)(2,1)S(1)} %get-tuple-element.102.refs_0_.cast_ref, ...), custom_call_target="tpu_custom_call", output_to_operand_aliasing={{}: (3, {})} | custom-call | flops 10000000000 | bytes 1000000 | tf_op jit(solution)/shard_map/gradient/pallas_call | solution.py:191
  39.6 0.8 %collective-permute-done.15.a_ref = bf16[144,768]{1,0:T(8,128)(2,1)S(1)} collective-permute-done((bf16[144,768]{1,0:T(8,128)(2,1)S(1)}, bf16[144,768]{1,0:T(8,128)(2,1)S(1)}, u32[]{:S(2)}, u32[]{:S(2)}) %collective-permute-start.15) | collective-permute-done | bytes 221216 | tf_op jit(solution)/shard_map/ppermute | solution.py:300
  40.4 2.6 %finish.1 = (f32[256,768]{1,0:T(8,128)}, f32[256,768]{1,0:T(8,128)}, f32[256,768]{1,0:T(8,128)}) custom-call(bf16[144,768]{1,0:T(8,128)(2,1)S(1)} %collective-permute-done.15.a_ref, bf16[128,768]{1,0:T(8,128)(2,1)S(1)} %collective-permute-done.16.b_ref, bf16[256,768]{1,0:T(8,128)(2,1)S(1)} %get-tuple-element.102.refs_0_.cast_ref, ...), custom_call_target="tpu_custom_call" | custom-call | flops 10000000000 | bytes 1000000 | tf_op jit(solution)/shard_map/finish/pallas_call | solution.py:249
  (20 shorter events, 0.1 us)
Async XLA Ops:
  2.1 8.7 %collective-permute-start.1 = (bf16[128,768]{1,0:T(8,128)(2,1)S(1)}, bf16[128,768]{1,0:T(8,128)(2,1)S(1)}, u32[]{:S(2)}, u32[]{:S(2)}) collective-permute-start(bf16[128,768]{1,0:T(8,128)(2,1)S(1)} %get-tuple-element.101.b_ref), channel_id=1, source_target_pairs={{0,4},{1,5},{4,8},{5,9},{8,12},{9,13},{12,14},{13,15},{14,10},{15,... | collective-permute-start | bytes 589832 | tf_op jit(solution)/shard_map/ppermute | solution.py:300
  5.2 8.4 %collective-permute-start = (bf16[144,768]{1,0:T(8,128)(2,1)S(1)}, bf16[144,768]{1,0:T(8,128)(2,1)S(1)}, u32[]{:S(2)}, u32[]{:S(2)}) collective-permute-start(bf16[144,768]{1,0:T(8,128)(2,1)S(1)} %get-tuple-element.100.a_ref), channel_id=1, source_target_pairs={{4,0},{5,1},{8,4},{9,5},{12,8},{13,9},{14,12},{15,13},{10,14},{11,... | collective-permute-start | bytes 663560 | tf_op jit(solution)/shard_map/ppermute | solution.py:300
  5.2 16.7 %collective-permute-start.6 = (bf16[256,768]{1,0:T(8,128)(2,1)S(1)}, bf16[256,768]{1,0:T(8,128)(2,1)S(1)}, u32[]{:S(2)}, u32[]{:S(2)}) collective-permute-start(bf16[256,768]{1,0:T(8,128)(2,1)S(1)} %get-tuple-element.102.refs_0_.cast_ref), channel_id=1, source_target_pairs={{0,1},{1,0},{2,3},{3,2},{4,5},{5,4},{6,7},{7,6},{8,9},{9,8},{10,11... | collective-permute-start | bytes 1179656 | tf_op jit(solution)/shard_map/ppermute | solution.py:300
  5.2 10.4 %collective-permute-start.5 = (bf16[144,768]{1,0:T(8,128)(2,1)S(1)}, bf16[144,768]{1,0:T(8,128)(2,1)S(1)}, u32[]{:S(2)}, u32[]{:S(2)}) collective-permute-start(bf16[144,768]{1,0:T(8,128)(2,1)S(1)} %get-tuple-element.100.a_ref), channel_id=1, source_target_pairs={{0,4},{1,5},{4,8},{5,9},{8,12},{9,13},{12,14},{13,15},{14,10},{15,... | collective-permute-start | bytes 663560 | tf_op jit(solution)/shard_map/ppermute | solution.py:300
  7.2 10.5 %collective-permute-start.4 = (bf16[128,768]{1,0:T(8,128)(2,1)S(1)}, bf16[128,768]{1,0:T(8,128)(2,1)S(1)}, u32[]{:S(2)}, u32[]{:S(2)}) collective-permute-start(bf16[128,768]{1,0:T(8,128)(2,1)S(1)} %get-tuple-element.101.b_ref), channel_id=1, source_target_pairs={{4,0},{5,1},{8,4},{9,5},{12,8},{13,9},{14,12},{15,13},{10,14},{11,... | collective-permute-start | bytes 589832 | tf_op jit(solution)/shard_map/ppermute | solution.py:300
  10.9 9.0 %collective-permute-start.3 = (bf16[128,768]{1,0:T(8,128)(2,1)S(1)}, bf16[128,768]{1,0:T(8,128)(2,1)S(1)}, u32[]{:S(2)}, u32[]{:S(2)}) collective-permute-start(bf16[128,768]{1,0:T(8,128)(2,1)S(1)} %collective-permute-done.1.b_ref), channel_id=1, source_target_pairs={{0,4},{1,5},{4,8},{5,9},{8,12},{9,13},{12,14},{13,15},{14,10},{15,... | collective-permute-start | bytes 589832 | tf_op jit(solution)/shard_map/ppermute | solution.py:300
  13.6 9.4 %collective-permute-start.2 = (bf16[144,768]{1,0:T(8,128)(2,1)S(1)}, bf16[144,768]{1,0:T(8,128)(2,1)S(1)}, u32[]{:S(2)}, u32[]{:S(2)}) collective-permute-start(bf16[144,768]{1,0:T(8,128)(2,1)S(1)} %collective-permute-done.a_ref), channel_id=1, source_target_pairs={{4,0},{5,1},{8,4},{9,5},{12,8},{13,9},{14,12},{15,13},{10,14},{11,... | collective-permute-start | bytes 663560 | tf_op jit(solution)/shard_map/ppermute | solution.py:300
  15.6 9.0 %collective-permute-start.10 = (bf16[144,768]{1,0:T(8,128)(2,1)S(1)}, bf16[144,768]{1,0:T(8,128)(2,1)S(1)}, u32[]{:S(2)}, u32[]{:S(2)}) collective-permute-start(bf16[144,768]{1,0:T(8,128)(2,1)S(1)} %collective-permute-done.5.a_ref), channel_id=1, source_target_pairs={{0,4},{1,5},{4,8},{5,9},{8,12},{9,13},{12,14},{13,15},{14,10},{15,... | collective-permute-start | bytes 663560 | tf_op jit(solution)/shard_map/ppermute | solution.py:300
  17.8 9.9 %collective-permute-start.9 = (bf16[128,768]{1,0:T(8,128)(2,1)S(1)}, bf16[128,768]{1,0:T(8,128)(2,1)S(1)}, u32[]{:S(2)}, u32[]{:S(2)}) collective-permute-start(bf16[128,768]{1,0:T(8,128)(2,1)S(1)} %collective-permute-done.4.b_ref), channel_id=1, source_target_pairs={{4,0},{5,1},{8,4},{9,5},{12,8},{13,9},{14,12},{15,13},{10,14},{11,... | collective-permute-start | bytes 589832 | tf_op jit(solution)/shard_map/ppermute | solution.py:300
  19.8 9.0 %collective-permute-start.8 = (bf16[128,768]{1,0:T(8,128)(2,1)S(1)}, bf16[128,768]{1,0:T(8,128)(2,1)S(1)}, u32[]{:S(2)}, u32[]{:S(2)}) collective-permute-start(bf16[128,768]{1,0:T(8,128)(2,1)S(1)} %collective-permute-done.3.b_ref), channel_id=1, source_target_pairs={{0,4},{1,5},{4,8},{5,9},{8,12},{9,13},{12,14},{13,15},{14,10},{15,... | collective-permute-start | bytes 589832 | tf_op jit(solution)/shard_map/ppermute | solution.py:300
  22.9 9.0 %collective-permute-start.7 = (bf16[144,768]{1,0:T(8,128)(2,1)S(1)}, bf16[144,768]{1,0:T(8,128)(2,1)S(1)}, u32[]{:S(2)}, u32[]{:S(2)}) collective-permute-start(bf16[144,768]{1,0:T(8,128)(2,1)S(1)} %collective-permute-done.2.a_ref), channel_id=1, source_target_pairs={{4,0},{5,1},{8,4},{9,5},{12,8},{13,9},{14,12},{15,13},{10,14},{11,... | collective-permute-start | bytes 663560 | tf_op jit(solution)/shard_map/ppermute | solution.py:300
  24.6 9.0 %collective-permute-start.14 = (bf16[144,768]{1,0:T(8,128)(2,1)S(1)}, bf16[144,768]{1,0:T(8,128)(2,1)S(1)}, u32[]{:S(2)}, u32[]{:S(2)}) collective-permute-start(bf16[144,768]{1,0:T(8,128)(2,1)S(1)} %collective-permute-done.10.a_ref), channel_id=1, source_target_pairs={{0,4},{1,5},{4,8},{5,9},{8,12},{9,13},{12,14},{13,15},{14,10},{15,... | collective-permute-start | bytes 663560 | tf_op jit(solution)/shard_map/ppermute | solution.py:300
  27.7 8.0 %collective-permute-start.13 = (bf16[128,768]{1,0:T(8,128)(2,1)S(1)}, bf16[128,768]{1,0:T(8,128)(2,1)S(1)}, u32[]{:S(2)}, u32[]{:S(2)}) collective-permute-start(bf16[128,768]{1,0:T(8,128)(2,1)S(1)} %collective-permute-done.9.b_ref), channel_id=1, source_target_pairs={{4,0},{5,1},{8,4},{9,5},{12,8},{13,9},{14,12},{15,13},{10,14},{11,... | collective-permute-start | bytes 589832 | tf_op jit(solution)/shard_map/ppermute | solution.py:300
  28.8 8.1 %collective-permute-start.12 = (bf16[128,768]{1,0:T(8,128)(2,1)S(1)}, bf16[128,768]{1,0:T(8,128)(2,1)S(1)}, u32[]{:S(2)}, u32[]{:S(2)}) collective-permute-start(bf16[128,768]{1,0:T(8,128)(2,1)S(1)} %collective-permute-done.8.b_ref), channel_id=1, source_target_pairs={{0,4},{1,5},{4,8},{5,9},{8,12},{9,13},{12,14},{13,15},{14,10},{15,... | collective-permute-start | bytes 589832 | tf_op jit(solution)/shard_map/ppermute | solution.py:300
  31.9 7.0 %collective-permute-start.11 = (bf16[144,768]{1,0:T(8,128)(2,1)S(1)}, bf16[144,768]{1,0:T(8,128)(2,1)S(1)}, u32[]{:S(2)}, u32[]{:S(2)}) collective-permute-start(bf16[144,768]{1,0:T(8,128)(2,1)S(1)} %collective-permute-done.7.a_ref), channel_id=1, source_target_pairs={{4,0},{5,1},{8,4},{9,5},{12,8},{13,9},{14,12},{15,13},{10,14},{11,... | collective-permute-start | bytes 663560 | tf_op jit(solution)/shard_map/ppermute | solution.py:300
  36.7 3.7 %collective-permute-start.17 = (f32[256,768]{1,0:T(8,128)S(1)}, f32[256,768]{1,0:T(8,128)S(1)}, u32[]{:S(2)}, u32[]{:S(2)}) collective-permute-start(f32[256,768]{1,0:T(8,128)S(1)} %get-tuple-element.156), channel_id=1, source_target_pairs={{0,1},{1,0},{2,3},{3,2},{4,5},{5,4},{6,7},{7,6},{8,9},{9,8},{10,11... | collective-permute-start | bytes 2359304 | tf_op jit(solution)/shard_map/ppermute | solution.py:300
  36.9 3.5 %copy-start = (f32[256,768]{1,0:T(8,128)S(1)}, f32[256,768]{1,0:T(8,128)}, u32[]{:S(2)}) copy-start(f32[256,768]{1,0:T(8,128)} %weights_ref.1) | copy-start | bytes 2359300
  36.9 3.5 %copy-start.1 = (f32[256,768]{1,0:T(8,128)S(1)}, f32[256,768]{1,0:T(8,128)}, u32[]{:S(2)}) copy-start(f32[256,768]{1,0:T(8,128)} %first_ref.1) | copy-start | bytes 2359300
  36.9 3.5 %copy-start.2 = (f32[256,768]{1,0:T(8,128)S(1)}, f32[256,768]{1,0:T(8,128)}, u32[]{:S(2)}) copy-start(f32[256,768]{1,0:T(8,128)} %second_ref.1) | copy-start | bytes 2359300
  36.9 2.7 %collective-permute-start.16 = (bf16[128,768]{1,0:T(8,128)(2,1)S(1)}, bf16[128,768]{1,0:T(8,128)(2,1)S(1)}, u32[]{:S(2)}, u32[]{:S(2)}) collective-permute-start(bf16[128,768]{1,0:T(8,128)(2,1)S(1)} %collective-permute-done.12.b_ref), channel_id=1, source_target_pairs={{0,1},{1,0},{2,3},{3,2},{4,5},{5,4},{6,7},{7,6},{8,9},{9,8},{10,11... | collective-permute-start | bytes 589832 | tf_op jit(solution)/shard_map/ppermute | solution.py:300
  38.9 1.5 %collective-permute-start.15 = (bf16[144,768]{1,0:T(8,128)(2,1)S(1)}, bf16[144,768]{1,0:T(8,128)(2,1)S(1)}, u32[]{:S(2)}, u32[]{:S(2)}) collective-permute-start(bf16[144,768]{1,0:T(8,128)(2,1)S(1)} %collective-permute-done.11.a_ref), channel_id=1, source_target_pairs={{0,1},{1,0},{2,3},{3,2},{4,5},{5,4},{6,7},{7,6},{8,9},{9,8},{10,11... | collective-permute-start | bytes 663560 | tf_op jit(solution)/shard_map/ppermute | solution.py:300

commit v11 on v9

--- a/solution.py
+++ b/solution.py
@@ -1,4 +1,5 @@
 import functools
+import math
 
 import jax
 import jax.numpy as jnp
@@ -38,14 +39,11 @@
     count_hbm,
     table_hbm,
     docs_hbm,
-    weights_hbm,
     a_ref,
     b_ref,
-    cast_ref,
     ids_ref,
     count_ref,
     table_ref,
-    weights_ref,
     done,
 ):
     slots, docs = ids_ref.shape
@@ -59,7 +57,6 @@
                 (count_hbm, count_ref),
                 (docs_hbm.at[pl.ds(0, head)], a_ref.at[pl.ds(0, head)]),
                 (docs_hbm.at[pl.ds(head, docs - head)], b_ref),
-                (weights_hbm, weights_ref),
             )
         )
     ]
@@ -99,34 +96,46 @@
         a_ref[head:, docs + start : docs + start + LANES] = code[slots // 2 :]
     for fetch in fetches[3:]:
         fetch.wait()
-    cast_ref[...] = weights_ref[...].astype(jnp.bfloat16) * 0.5
-
-
-def prepare(label_slot, pos_ids, pos_count, embeddings, weights, head):
+
+
+def prepare(label_slot, pos_ids, pos_count, embeddings, head):
     docs, slots = pos_ids.shape
     width = embeddings.shape[1]
     lines = label_slot.shape[0] // LANES
     table = label_slot.reshape(lines, LANES)
-    inputs = (pos_ids.T, pos_count.reshape(1, docs), table, embeddings, weights)
+    inputs = (pos_ids.T, pos_count.reshape(1, docs), table, embeddings)
     return pl.pallas_call(
         functools.partial(prepare_kernel, (lines - 1).bit_length()),
-        in_specs=[pl.BlockSpec(memory_space=pltpu.HBM)] * 5,
-        out_specs=[pl.BlockSpec(memory_space=pltpu.VMEM)] * 3,
+        in_specs=[pl.BlockSpec(memory_space=pltpu.HBM)] * 4,
+        out_specs=[pl.BlockSpec(memory_space=pltpu.VMEM)] * 2,
         out_shape=[
             jax.ShapeDtypeStruct((head + slots // 2, width), jnp.bfloat16),
             jax.ShapeDtypeStruct((docs - head, width), jnp.bfloat16),
-            jax.ShapeDtypeStruct(weights.shape, jnp.bfloat16),
         ],
         scratch_shapes=[
             pltpu.VMEM((slots, docs), jnp.int32),
             pltpu.VMEM((1, docs), jnp.int32),
             pltpu.VMEM((lines, LANES), jnp.int32),
-            pltpu.VMEM(weights.shape, jnp.float32),
-            pltpu.SemaphoreType.DMA((6,)),
+            pltpu.SemaphoreType.DMA((5,)),
         ],
         compiler_params=pltpu.CompilerParams(vmem_limit_bytes=VMEM_LIMIT),
         name="prepare",
     )(*(pltpu.with_memory_space_constraint(x, pltpu.HBM) for x in inputs))
+
+
+def cast_kernel(weights_ref, cast_ref):
+    cast_ref[...] = weights_ref[...].astype(jnp.bfloat16) * 0.5
+
+
+def halved_cast(weights):
+    return pl.pallas_call(
+        cast_kernel,
+        in_specs=[pl.BlockSpec(memory_space=pltpu.VMEM)],
+        out_specs=pl.BlockSpec(memory_space=pltpu.VMEM),
+        out_shape=jax.ShapeDtypeStruct(weights.shape, jnp.bfloat16),
+        compiler_params=pltpu.CompilerParams(vmem_limit_bytes=VMEM_LIMIT),
+        name="cast",
+    )(weights)
 
 
 def signs_of(codes, owner, bits, height):
@@ -219,9 +228,9 @@
     writes = []
     for i in range(PIECES):
         here = pl.ds(i * size, size)
-        gradient = 0.5 * (sum_ref[here, :] + other_ref[here, :] + part[i * size : (i + 1) * size])
+        doubled = sum_ref[here, :] + other_ref[here, :] + part[i * size : (i + 1) * size]
         new_weights, new_first, new_second = adam_step(
-            weights_ref[here, :], first_ref[here, :], second_ref[here, :], gradient
+            weights_ref[here, :], first_ref[here, :], second_ref[here, :], doubled
         )
         for k, (value, out, hbm) in enumerate(
             (
@@ -253,11 +262,12 @@
     )(a, b, cast, mine_sum, other_sum, weights, first_moment, second_moment)
 
 
-def adam_step(weights, first_moment, second_moment, gradient):
-    new_first = beta_one * first_moment + (1.0 - beta_one) * gradient
-    new_second = beta_two * second_moment + (1.0 - beta_two) * gradient * gradient
-    update = new_first / correct_one / (jnp.sqrt(new_second / correct_two) + adam_eps)
-    new_weights = weights - learn_rate * (update + decay_rate * weights)
+def adam_step(weights, first_moment, second_moment, doubled):
+    new_first = beta_one * first_moment + ((1.0 - beta_one) * 0.5) * doubled
+    new_second = beta_two * second_moment + ((1.0 - beta_two) * 0.25) * (doubled * doubled)
+    steep = correct_one / (learn_rate * math.sqrt(correct_two))
+    update = new_first / (jnp.sqrt(new_second) * steep + correct_one * adam_eps / learn_rate)
+    new_weights = weights * (1.0 - learn_rate * decay_rate) - update
     return (new_weights, new_first, new_second)
 
 
@@ -293,9 +303,10 @@
     def send(value, pairs):
         return lax.ppermute(value, "blk", pairs)
 
-    a, b, mine = prepare(label_slot, pos_ids, pos_count, embeddings, weights, head)
+    a, b = prepare(label_slot, pos_ids, pos_count, embeddings, head)
     coming = {"up_b": send(b, up), "down_a": send(a, down)}
     coming |= {"up_a": send(a, up), "down_b": send(b, down)}
+    mine = halved_cast(weights)
     cast = [mine, send(mine, swap)]
     sums = ()
     waiting = [(a, b)]

time: 43.1 us -> 42.8 us (level)
  local copies, waits for them, and re-layouts: 0.01 us -> 1.14 us
  waiting for transfers between devices: 14.1 us -> 13.5 us
  starting transfers between devices: 16.4 us -> 15.8 us
    unnamed x6 -> x8, local copies, waits for them, and re-layouts: 0.01 us -> 1.14 us
    ppermute x18, waiting for transfers between devices: 14.1 us -> 13.5 us  [send(): return lax.ppermute(value, 'blk', pairs)]
    ppermute x18, starting transfers between devices: 16.4 us -> 15.8 us  [send(): return lax.ppermute(value, 'blk', pairs)]
  transfers between devices with their start and end apart: 18 -> 18, of which waited for: 11 -> 12; matrix products, arithmetic and copies ran while one was open for 0% -> 0% of each run, Pallas kernels for 18% -> 18%
where the time goes in v11:
time: 42.8 us; the launch traced here: 42.6 us
  starting transfers between devices  15.8 us (37%)
  waiting for transfers between devices  13.5 us (32%)
  Pallas kernels  11.4 us (27%)
  local copies, waits for them, and re-layouts  1.14 us (3%)
  between operations  0.78 us (2%)
    ppermute x18, starting transfers between devices, send(): return lax.ppermute(value, 'blk', pairs)  15.8 us
    ppermute x18, waiting for transfers between devices, send(): return lax.ppermute(value, 'blk', pairs)  13.5 us
    pallas_call x8, Pallas kernels, add_gradient(): pl.pallas_call(functools.partial(gradient_kernel, bits, owners, not sums)...  7.72 us
    pallas_call x1, Pallas kernels, finish(): pl.pallas_call(functools.partial(finish_kernel, bits), in_specs=[pl.Block...  2.37 us
    pallas_call x1, Pallas kernels, prepare(): pl.pallas_call(functools.partial(prepare_kernel, (lines - 1).bit_length()...  1.25 us
    unnamed x8, local copies, waits for them, and re-layouts  1.14 us
  transfers between devices with their start and end apart: 18, of which 12 were waited for; matrix products, arithmetic and copies ran while one was open for 0% of the time, Pallas kernels for 18%

profile of v11, /device:TPU:0, one launch (start us, length us, event | category | flops | bytes accessed | tf_op | source)
XLA Modules:
  0.0 42.6 jit_solution(7686865527050174306)
XLA Ops:
  0.6 1.3 %prepare.1 = (bf16[144,768]{1,0:T(8,128)(2,1)S(1)}, bf16[128,768]{1,0:T(8,128)(2,1)S(1)}) custom-call(s32[32,256]{1,0:T(8,128)} %bitcast.3, s32[1,256]{1,0:T(1,128)} %bitcast.5, s32[32,128]{1,0:T(8,128)} %bitcast.4, bf16[256,768]{1,0:T(8,128)(2,1)} %docs_hbm.1), custom_call_target="tpu_custom_call" | custom-call | tf_op jit(solution)/shard_map/prepare/pallas_call | solution.py:107
  1.9 3.1 %collective-permute-start.1 = (bf16[128,768]{1,0:T(8,128)(2,1)S(1)}, bf16[128,768]{1,0:T(8,128)(2,1)S(1)}, u32[]{:S(2)}, u32[]{:S(2)}) collective-permute-start(bf16[128,768]{1,0:T(8,128)(2,1)S(1)} %get-tuple-element.100.b_ref), channel_id=1, source_target_pairs={{0,4},{1,5},{4,8},{5,9},{8,12},{9,13},{12,14},{13,15},{14,10},{15,... | collective-permute-start | bytes 589832 | tf_op jit(solution)/shard_map/ppermute | solution.py:304
  5.0 1.1 %copy-done = f32[256,768]{1,0:T(8,128)S(1)} copy-done((f32[256,768]{1,0:T(8,128)S(1)}, f32[256,768]{1,0:T(8,128)}, u32[]{:S(2)}) %copy-start) | copy-done | bytes 786456
  6.2 2.1 %collective-permute-start.5 = (bf16[144,768]{1,0:T(8,128)(2,1)S(1)}, bf16[144,768]{1,0:T(8,128)(2,1)S(1)}, u32[]{:S(2)}, u32[]{:S(2)}) collective-permute-start(bf16[144,768]{1,0:T(8,128)(2,1)S(1)} %get-tuple-element.99.a_ref), channel_id=1, source_target_pairs={{0,4},{1,5},{4,8},{5,9},{8,12},{9,13},{12,14},{13,15},{14,10},{15,... | collective-permute-start | bytes 663560 | tf_op jit(solution)/shard_map/ppermute | solution.py:304
  8.3 1.7 %collective-permute-done.1.b_ref = bf16[128,768]{1,0:T(8,128)(2,1)S(1)} collective-permute-done((bf16[128,768]{1,0:T(8,128)(2,1)S(1)}, bf16[128,768]{1,0:T(8,128)(2,1)S(1)}, u32[]{:S(2)}, u32[]{:S(2)}) %collective-permute-start.1) | collective-permute-done | bytes 196640 | tf_op jit(solution)/shard_map/ppermute | solution.py:304
  10.0 1.8 %collective-permute-start.3 = (bf16[128,768]{1,0:T(8,128)(2,1)S(1)}, bf16[128,768]{1,0:T(8,128)(2,1)S(1)}, u32[]{:S(2)}, u32[]{:S(2)}) collective-permute-start(bf16[128,768]{1,0:T(8,128)(2,1)S(1)} %collective-permute-done.1.b_ref), channel_id=1, source_target_pairs={{0,4},{1,5},{4,8},{5,9},{8,12},{9,13},{12,14},{13,15},{14,10},{15,... | collective-permute-start | bytes 589832 | tf_op jit(solution)/shard_map/ppermute | solution.py:304
  11.8 0.8 %collective-permute-done.a_ref = bf16[144,768]{1,0:T(8,128)(2,1)S(1)} collective-permute-done((bf16[144,768]{1,0:T(8,128)(2,1)S(1)}, bf16[144,768]{1,0:T(8,128)(2,1)S(1)}, u32[]{:S(2)}, u32[]{:S(2)}) %collective-permute-start) | collective-permute-done | bytes 221216 | tf_op jit(solution)/shard_map/ppermute | solution.py:304
  12.6 0.3 collective-permute-start.2
  12.9 1.9 %collective-permute-done.5.a_ref = bf16[144,768]{1,0:T(8,128)(2,1)S(1)} collective-permute-done((bf16[144,768]{1,0:T(8,128)(2,1)S(1)}, bf16[144,768]{1,0:T(8,128)(2,1)S(1)}, u32[]{:S(2)}, u32[]{:S(2)}) %collective-permute-start.5) | collective-permute-done | bytes 221216 | tf_op jit(solution)/shard_map/ppermute | solution.py:304
  14.7 1.9 %collective-permute-start.10 = (bf16[144,768]{1,0:T(8,128)(2,1)S(1)}, bf16[144,768]{1,0:T(8,128)(2,1)S(1)}, u32[]{:S(2)}, u32[]{:S(2)}) collective-permute-start(bf16[144,768]{1,0:T(8,128)(2,1)S(1)} %collective-permute-done.5.a_ref), channel_id=1, source_target_pairs={{0,4},{1,5},{4,8},{5,9},{8,12},{9,13},{12,14},{13,15},{14,10},{15,... | collective-permute-start | bytes 663560 | tf_op jit(solution)/shard_map/ppermute | solution.py:304
  16.8 0.3 collective-permute-start.9
  17.1 1.9 %collective-permute-done.3.b_ref = bf16[128,768]{1,0:T(8,128)(2,1)S(1)} collective-permute-done((bf16[128,768]{1,0:T(8,128)(2,1)S(1)}, bf16[128,768]{1,0:T(8,128)(2,1)S(1)}, u32[]{:S(2)}, u32[]{:S(2)}) %collective-permute-start.3) | collective-permute-done | bytes 196640 | tf_op jit(solution)/shard_map/ppermute | solution.py:304
  19.0 1.9 %collective-permute-start.8 = (bf16[128,768]{1,0:T(8,128)(2,1)S(1)}, bf16[128,768]{1,0:T(8,128)(2,1)S(1)}, u32[]{:S(2)}, u32[]{:S(2)}) collective-permute-start(bf16[128,768]{1,0:T(8,128)(2,1)S(1)} %collective-permute-done.3.b_ref), channel_id=1, source_target_pairs={{0,4},{1,5},{4,8},{5,9},{8,12},{9,13},{12,14},{13,15},{14,10},{15,... | collective-permute-start | bytes 589832 | tf_op jit(solution)/shard_map/ppermute | solution.py:304
  20.8 1.0 %gradient.8 = (f32[256,768]{1,0:T(8,128)S(1)}, f32[256,768]{1,0:T(8,128)S(1)}) custom-call(bf16[144,768]{1,0:T(8,128)(2,1)S(1)} %get-tuple-element.99.a_ref, bf16[128,768]{1,0:T(8,128)(2,1)S(1)} %get-tuple-element.100.b_ref, bf16[256,768]{1,0:T(8,128)(2,1)S(1)} %cast.1.refs_0_.cast_ref, bf16[256,768]{1,0:T(8,128)(2,1)S(1)} %collective-permute-done.6.refs_1_), custom_call_target="tpu_custom_call" | custom-call | flops 500000000 | bytes 1000000 | tf_op jit(solution)/shard_map/gradient/pallas_call | solution.py:195
  21.8 0.2 collective-permute-start.7
  22.0 1.0 %gradient.9 = (f32[256,768]{1,0:T(8,128)S(1)}, f32[256,768]{1,0:T(8,128)S(1)}) custom-call(bf16[144,768]{1,0:T(8,128)(2,1)S(1)} %collective-permute-done.5.a_ref, bf16[128,768]{1,0:T(8,128)(2,1)S(1)} %collective-permute-done.1.b_ref, bf16[256,768]{1,0:T(8,128)(2,1)S(1)} %cast.1.refs_0_.cast_ref, ...), custom_call_target="tpu_custom_call", output_to_operand_aliasing={{0}: (4, {}), {1}: (5, {})} | custom-call | flops 500000000 | bytes 1000000 | tf_op jit(solution)/shard_map/gradient/pallas_call | solution.py:195
  23.1 0.6 %collective-permute-done.10.a_ref = bf16[144,768]{1,0:T(8,128)(2,1)S(1)} collective-permute-done((bf16[144,768]{1,0:T(8,128)(2,1)S(1)}, bf16[144,768]{1,0:T(8,128)(2,1)S(1)}, u32[]{:S(2)}, u32[]{:S(2)}) %collective-permute-start.10) | collective-permute-done | bytes 221216 | tf_op jit(solution)/shard_map/ppermute | solution.py:304
  23.7 1.9 %collective-permute-start.14 = (bf16[144,768]{1,0:T(8,128)(2,1)S(1)}, bf16[144,768]{1,0:T(8,128)(2,1)S(1)}, u32[]{:S(2)}, u32[]{:S(2)}) collective-permute-start(bf16[144,768]{1,0:T(8,128)(2,1)S(1)} %collective-permute-done.10.a_ref), channel_id=1, source_target_pairs={{0,4},{1,5},{4,8},{5,9},{8,12},{9,13},{12,14},{13,15},{14,10},{15,... | collective-permute-start | bytes 663560 | tf_op jit(solution)/shard_map/ppermute | solution.py:304
  25.6 1.0 %gradient.10 = (f32[256,768]{1,0:T(8,128)S(1)}, f32[256,768]{1,0:T(8,128)S(1)}) custom-call(bf16[144,768]{1,0:T(8,128)(2,1)S(1)} %collective-permute-done.a_ref, bf16[128,768]{1,0:T(8,128)(2,1)S(1)} %collective-permute-done.4.b_ref, bf16[256,768]{1,0:T(8,128)(2,1)S(1)} %cast.1.refs_0_.cast_ref, ...), custom_call_target="tpu_custom_call", output_to_operand_aliasing={{0}: (4, {}), {1}: (5, {})} | custom-call | flops 500000000 | bytes 1000000 | tf_op jit(solution)/shard_map/gradient/pallas_call | solution.py:195
  26.8 1.1 %collective-permute-done.8.b_ref = bf16[128,768]{1,0:T(8,128)(2,1)S(1)} collective-permute-done((bf16[128,768]{1,0:T(8,128)(2,1)S(1)}, bf16[128,768]{1,0:T(8,128)(2,1)S(1)}, u32[]{:S(2)}, u32[]{:S(2)}) %collective-permute-start.8) | collective-permute-done | bytes 196640 | tf_op jit(solution)/shard_map/ppermute | solution.py:304
  27.9 1.9 %collective-permute-start.12 = (bf16[128,768]{1,0:T(8,128)(2,1)S(1)}, bf16[128,768]{1,0:T(8,128)(2,1)S(1)}, u32[]{:S(2)}, u32[]{:S(2)}) collective-permute-start(bf16[128,768]{1,0:T(8,128)(2,1)S(1)} %collective-permute-done.8.b_ref), channel_id=1, source_target_pairs={{0,4},{1,5},{4,8},{5,9},{8,12},{9,13},{12,14},{13,15},{14,10},{15,... | collective-permute-start | bytes 589832 | tf_op jit(solution)/shard_map/ppermute | solution.py:304
  29.8 1.0 %gradient.11 = (f32[256,768]{1,0:T(8,128)S(1)}, f32[256,768]{1,0:T(8,128)S(1)}) custom-call(bf16[144,768]{1,0:T(8,128)(2,1)S(1)} %collective-permute-done.10.a_ref, bf16[128,768]{1,0:T(8,128)(2,1)S(1)} %collective-permute-done.3.b_ref, bf16[256,768]{1,0:T(8,128)(2,1)S(1)} %cast.1.refs_0_.cast_ref, ...), custom_call_target="tpu_custom_call", output_to_operand_aliasing={{0}: (4, {}), {1}: (5, {})} | custom-call | flops 1000000000 | bytes 1000000 | tf_op jit(solution)/shard_map/gradient/pallas_call | solution.py:195
  31.0 1.0 %gradient.12 = (f32[256,768]{1,0:T(8,128)S(1)}, f32[256,768]{1,0:T(8,128)S(1)}) custom-call(bf16[144,768]{1,0:T(8,128)(2,1)S(1)} %collective-permute-done.2.a_ref, bf16[128,768]{1,0:T(8,128)(2,1)S(1)} %collective-permute-done.9.b_ref, bf16[256,768]{1,0:T(8,128)(2,1)S(1)} %cast.1.refs_0_.cast_ref, ...), custom_call_target="tpu_custom_call", output_to_operand_aliasing={{0}: (4, {}), {1}: (5, {})} | custom-call | flops 1000000000 | bytes 1000000 | tf_op jit(solution)/shard_map/gradient/pallas_call | solution.py:195
  32.0 0.6 %collective-permute-done.14.a_ref = bf16[144,768]{1,0:T(8,128)(2,1)S(1)} collective-permute-done((bf16[144,768]{1,0:T(8,128)(2,1)S(1)}, bf16[144,768]{1,0:T(8,128)(2,1)S(1)}, u32[]{:S(2)}, u32[]{:S(2)}) %collective-permute-start.14) | collective-permute-done | bytes 221216 | tf_op jit(solution)/shard_map/ppermute | solution.py:304
  32.7 1.0 %gradient.13 = (f32[256,768]{1,0:T(8,128)S(1)}, f32[256,768]{1,0:T(8,128)S(1)}) custom-call(bf16[144,768]{1,0:T(8,128)(2,1)S(1)} %collective-permute-done.14.a_ref, bf16[128,768]{1,0:T(8,128)(2,1)S(1)} %collective-permute-done.8.b_ref, bf16[256,768]{1,0:T(8,128)(2,1)S(1)} %cast.1.refs_0_.cast_ref, ...), custom_call_target="tpu_custom_call", output_to_operand_aliasing={{0}: (4, {}), {1}: (5, {})} | custom-call | flops 1000000000 | bytes 1000000 | tf_op jit(solution)/shard_map/gradient/pallas_call | solution.py:195
  33.7 1.0 %collective-permute-done.13.b_ref = bf16[128,768]{1,0:T(8,128)(2,1)S(1)} collective-permute-done((bf16[128,768]{1,0:T(8,128)(2,1)S(1)}, bf16[128,768]{1,0:T(8,128)(2,1)S(1)}, u32[]{:S(2)}, u32[]{:S(2)}) %collective-permute-start.13) | collective-permute-done | bytes 196640 | tf_op jit(solution)/shard_map/ppermute | solution.py:304
  34.7 1.0 %gradient.14 = (f32[256,768]{1,0:T(8,128)S(1)}, f32[256,768]{1,0:T(8,128)S(1)}) custom-call(bf16[144,768]{1,0:T(8,128)(2,1)S(1)} %collective-permute-done.7.a_ref, bf16[128,768]{1,0:T(8,128)(2,1)S(1)} %collective-permute-done.13.b_ref, bf16[256,768]{1,0:T(8,128)(2,1)S(1)} %cast.1.refs_0_.cast_ref, ...), custom_call_target="tpu_custom_call", output_to_operand_aliasing={{0}: (4, {}), {1}: (5, {})} | custom-call | flops 1000000000 | bytes 1000000 | tf_op jit(solution)/shard_map/gradient/pallas_call | solution.py:195
  35.8 0.9 %collective-permute-done.12.b_ref = bf16[128,768]{1,0:T(8,128)(2,1)S(1)} collective-permute-done((bf16[128,768]{1,0:T(8,128)(2,1)S(1)}, bf16[128,768]{1,0:T(8,128)(2,1)S(1)}, u32[]{:S(2)}, u32[]{:S(2)}) %collective-permute-start.12) | collective-permute-done | bytes 196640 | tf_op jit(solution)/shard_map/ppermute | solution.py:304
  36.7 2.0 %collective-permute-done.11.a_ref = bf16[144,768]{1,0:T(8,128)(2,1)S(1)} collective-permute-done((bf16[144,768]{1,0:T(8,128)(2,1)S(1)}, bf16[144,768]{1,0:T(8,128)(2,1)S(1)}, u32[]{:S(2)}, u32[]{:S(2)}) %collective-permute-start.11) | collective-permute-done | bytes 221216 | tf_op jit(solution)/shard_map/ppermute | solution.py:304
  38.7 0.7 %gradient.15.sum_ref = f32[256,768]{1,0:T(8,128)S(1)} custom-call(bf16[144,768]{1,0:T(8,128)(2,1)S(1)} %collective-permute-done.11.a_ref, bf16[128,768]{1,0:T(8,128)(2,1)S(1)} %collective-permute-done.12.b_ref, bf16[256,768]{1,0:T(8,128)(2,1)S(1)} %cast.1.refs_0_.cast_ref, f32[256,768]{1,0:T(8,128)S(1)} %get-tuple-element.153.refs_1_), custom_call_target="tpu_custom_call", output_to_operand_aliasing={{}: (3, {})} | custom-call | flops 10000000000 | bytes 1000000 | tf_op jit(solution)/shard_map/gradient/pallas_call | solution.py:195
  39.4 0.8 %collective-permute-done.15.a_ref = bf16[144,768]{1,0:T(8,128)(2,1)S(1)} collective-permute-done((bf16[144,768]{1,0:T(8,128)(2,1)S(1)}, bf16[144,768]{1,0:T(8,128)(2,1)S(1)}, u32[]{:S(2)}, u32[]{:S(2)}) %collective-permute-start.15) | collective-permute-done | bytes 221216 | tf_op jit(solution)/shard_map/ppermute | solution.py:304
  40.2 2.4 %finish.1 = (f32[256,768]{1,0:T(8,128)}, f32[256,768]{1,0:T(8,128)}, f32[256,768]{1,0:T(8,128)}) custom-call(bf16[144,768]{1,0:T(8,128)(2,1)S(1)} %collective-permute-done.15.a_ref, bf16[128,768]{1,0:T(8,128)(2,1)S(1)} %collective-permute-done.16.b_ref, bf16[256,768]{1,0:T(8,128)(2,1)S(1)} %cast.1.refs_0_.cast_ref, f32[256,768]{1,0:T(8,128)S(1)} %gradient.15.sum_ref, ...), custom_call_target="tpu_custom_call" | custom-call | flops 10000000000 | bytes 1000000 | tf_op jit(solution)/shard_map/finish/pallas_call | solution.py:252
  (23 shorter events, 0.9 us)
Async XLA Ops:
  1.9 8.1 %collective-permute-start.1 = (bf16[128,768]{1,0:T(8,128)(2,1)S(1)}, bf16[128,768]{1,0:T(8,128)(2,1)S(1)}, u32[]{:S(2)}, u32[]{:S(2)}) collective-permute-start(bf16[128,768]{1,0:T(8,128)(2,1)S(1)} %get-tuple-element.100.b_ref), channel_id=1, source_target_pairs={{0,4},{1,5},{4,8},{5,9},{8,12},{9,13},{12,14},{13,15},{14,10},{15,... | collective-permute-start | bytes 589832 | tf_op jit(solution)/shard_map/ppermute | solution.py:304
  5.0 7.6 %collective-permute-start = (bf16[144,768]{1,0:T(8,128)(2,1)S(1)}, bf16[144,768]{1,0:T(8,128)(2,1)S(1)}, u32[]{:S(2)}, u32[]{:S(2)}) collective-permute-start(bf16[144,768]{1,0:T(8,128)(2,1)S(1)} %get-tuple-element.99.a_ref), channel_id=1, source_target_pairs={{4,0},{5,1},{8,4},{9,5},{12,8},{13,9},{14,12},{15,13},{10,14},{11,... | collective-permute-start | bytes 663560 | tf_op jit(solution)/shard_map/ppermute | solution.py:304
  5.0 1.1 %copy-start = (f32[256,768]{1,0:T(8,128)S(1)}, f32[256,768]{1,0:T(8,128)}, u32[]{:S(2)}) copy-start(f32[256,768]{1,0:T(8,128)} %weights_ref.3) | copy-start | bytes 2359300
  6.2 14.7 %collective-permute-start.6 = (bf16[256,768]{1,0:T(8,128)(2,1)S(1)}, bf16[256,768]{1,0:T(8,128)(2,1)S(1)}, u32[]{:S(2)}, u32[]{:S(2)}) collective-permute-start(bf16[256,768]{1,0:T(8,128)(2,1)S(1)} %cast.1.refs_0_.cast_ref), channel_id=1, source_target_pairs={{0,1},{1,0},{2,3},{3,2},{4,5},{5,4},{6,7},{7,6},{8,9},{9,8},{10,11... | collective-permute-start | bytes 1179656 | tf_op jit(solution)/shard_map/ppermute | solution.py:304
  6.2 8.5 %collective-permute-start.5 = (bf16[144,768]{1,0:T(8,128)(2,1)S(1)}, bf16[144,768]{1,0:T(8,128)(2,1)S(1)}, u32[]{:S(2)}, u32[]{:S(2)}) collective-permute-start(bf16[144,768]{1,0:T(8,128)(2,1)S(1)} %get-tuple-element.99.a_ref), channel_id=1, source_target_pairs={{0,4},{1,5},{4,8},{5,9},{8,12},{9,13},{12,14},{13,15},{14,10},{15,... | collective-permute-start | bytes 663560 | tf_op jit(solution)/shard_map/ppermute | solution.py:304
  8.3 8.5 %collective-permute-start.4 = (bf16[128,768]{1,0:T(8,128)(2,1)S(1)}, bf16[128,768]{1,0:T(8,128)(2,1)S(1)}, u32[]{:S(2)}, u32[]{:S(2)}) collective-permute-start(bf16[128,768]{1,0:T(8,128)(2,1)S(1)} %get-tuple-element.100.b_ref), channel_id=1, source_target_pairs={{4,0},{5,1},{8,4},{9,5},{12,8},{13,9},{14,12},{15,13},{10,14},{11,... | collective-permute-start | bytes 589832 | tf_op jit(solution)/shard_map/ppermute | solution.py:304
  10.0 9.0 %collective-permute-start.3 = (bf16[128,768]{1,0:T(8,128)(2,1)S(1)}, bf16[128,768]{1,0:T(8,128)(2,1)S(1)}, u32[]{:S(2)}, u32[]{:S(2)}) collective-permute-start(bf16[128,768]{1,0:T(8,128)(2,1)S(1)} %collective-permute-done.1.b_ref), channel_id=1, source_target_pairs={{0,4},{1,5},{4,8},{5,9},{8,12},{9,13},{12,14},{13,15},{14,10},{15,... | collective-permute-start | bytes 589832 | tf_op jit(solution)/shard_map/ppermute | solution.py:304
  12.6 9.2 %collective-permute-start.2 = (bf16[144,768]{1,0:T(8,128)(2,1)S(1)}, bf16[144,768]{1,0:T(8,128)(2,1)S(1)}, u32[]{:S(2)}, u32[]{:S(2)}) collective-permute-start(bf16[144,768]{1,0:T(8,128)(2,1)S(1)} %collective-permute-done.a_ref), channel_id=1, source_target_pairs={{4,0},{5,1},{8,4},{9,5},{12,8},{13,9},{14,12},{15,13},{10,14},{11,... | collective-permute-start | bytes 663560 | tf_op jit(solution)/shard_map/ppermute | solution.py:304
  14.7 9.0 %collective-permute-start.10 = (bf16[144,768]{1,0:T(8,128)(2,1)S(1)}, bf16[144,768]{1,0:T(8,128)(2,1)S(1)}, u32[]{:S(2)}, u32[]{:S(2)}) collective-permute-start(bf16[144,768]{1,0:T(8,128)(2,1)S(1)} %collective-permute-done.5.a_ref), channel_id=1, source_target_pairs={{0,4},{1,5},{4,8},{5,9},{8,12},{9,13},{12,14},{13,15},{14,10},{15,... | collective-permute-start | bytes 663560 | tf_op jit(solution)/shard_map/ppermute | solution.py:304
  16.8 9.8 %collective-permute-start.9 = (bf16[128,768]{1,0:T(8,128)(2,1)S(1)}, bf16[128,768]{1,0:T(8,128)(2,1)S(1)}, u32[]{:S(2)}, u32[]{:S(2)}) collective-permute-start(bf16[128,768]{1,0:T(8,128)(2,1)S(1)} %collective-permute-done.4.b_ref), channel_id=1, source_target_pairs={{4,0},{5,1},{8,4},{9,5},{12,8},{13,9},{14,12},{15,13},{10,14},{11,... | collective-permute-start | bytes 589832 | tf_op jit(solution)/shard_map/ppermute | solution.py:304
  19.0 9.0 %collective-permute-start.8 = (bf16[128,768]{1,0:T(8,128)(2,1)S(1)}, bf16[128,768]{1,0:T(8,128)(2,1)S(1)}, u32[]{:S(2)}, u32[]{:S(2)}) collective-permute-start(bf16[128,768]{1,0:T(8,128)(2,1)S(1)} %collective-permute-done.3.b_ref), channel_id=1, source_target_pairs={{0,4},{1,5},{4,8},{5,9},{8,12},{9,13},{12,14},{13,15},{14,10},{15,... | collective-permute-start | bytes 589832 | tf_op jit(solution)/shard_map/ppermute | solution.py:304
  21.8 9.0 %collective-permute-start.7 = (bf16[144,768]{1,0:T(8,128)(2,1)S(1)}, bf16[144,768]{1,0:T(8,128)(2,1)S(1)}, u32[]{:S(2)}, u32[]{:S(2)}) collective-permute-start(bf16[144,768]{1,0:T(8,128)(2,1)S(1)} %collective-permute-done.2.a_ref), channel_id=1, source_target_pairs={{4,0},{5,1},{8,4},{9,5},{12,8},{13,9},{14,12},{15,13},{10,14},{11,... | collective-permute-start | bytes 663560 | tf_op jit(solution)/shard_map/ppermute | solution.py:304
  23.7 9.0 %collective-permute-start.14 = (bf16[144,768]{1,0:T(8,128)(2,1)S(1)}, bf16[144,768]{1,0:T(8,128)(2,1)S(1)}, u32[]{:S(2)}, u32[]{:S(2)}) collective-permute-start(bf16[144,768]{1,0:T(8,128)(2,1)S(1)} %collective-permute-done.10.a_ref), channel_id=1, source_target_pairs={{0,4},{1,5},{4,8},{5,9},{8,12},{9,13},{12,14},{13,15},{14,10},{15,... | collective-permute-start | bytes 663560 | tf_op jit(solution)/shard_map/ppermute | solution.py:304
  26.6 8.1 %collective-permute-start.13 = (bf16[128,768]{1,0:T(8,128)(2,1)S(1)}, bf16[128,768]{1,0:T(8,128)(2,1)S(1)}, u32[]{:S(2)}, u32[]{:S(2)}) collective-permute-start(bf16[128,768]{1,0:T(8,128)(2,1)S(1)} %collective-permute-done.9.b_ref), channel_id=1, source_target_pairs={{4,0},{5,1},{8,4},{9,5},{12,8},{13,9},{14,12},{15,13},{10,14},{11,... | collective-permute-start | bytes 589832 | tf_op jit(solution)/shard_map/ppermute | solution.py:304
  27.9 8.8 %collective-permute-start.12 = (bf16[128,768]{1,0:T(8,128)(2,1)S(1)}, bf16[128,768]{1,0:T(8,128)(2,1)S(1)}, u32[]{:S(2)}, u32[]{:S(2)}) collective-permute-start(bf16[128,768]{1,0:T(8,128)(2,1)S(1)} %collective-permute-done.8.b_ref), channel_id=1, source_target_pairs={{0,4},{1,5},{4,8},{5,9},{8,12},{9,13},{12,14},{13,15},{14,10},{15,... | collective-permute-start | bytes 589832 | tf_op jit(solution)/shard_map/ppermute | solution.py:304
  30.8 7.9 %collective-permute-start.11 = (bf16[144,768]{1,0:T(8,128)(2,1)S(1)}, bf16[144,768]{1,0:T(8,128)(2,1)S(1)}, u32[]{:S(2)}, u32[]{:S(2)}) collective-permute-start(bf16[144,768]{1,0:T(8,128)(2,1)S(1)} %collective-permute-done.7.a_ref), channel_id=1, source_target_pairs={{4,0},{5,1},{8,4},{9,5},{12,8},{13,9},{14,12},{15,13},{10,14},{11,... | collective-permute-start | bytes 663560 | tf_op jit(solution)/shard_map/ppermute | solution.py:304
  35.7 4.5 %collective-permute-start.17 = (f32[256,768]{1,0:T(8,128)S(1)}, f32[256,768]{1,0:T(8,128)S(1)}, u32[]{:S(2)}, u32[]{:S(2)}) collective-permute-start(f32[256,768]{1,0:T(8,128)S(1)} %get-tuple-element.154), channel_id=1, source_target_pairs={{0,1},{1,0},{2,3},{3,2},{4,5},{5,4},{6,7},{7,6},{8,9},{9,8},{10,11... | collective-permute-start | bytes 2359304 | tf_op jit(solution)/shard_map/ppermute | solution.py:304
  36.7 3.5 %copy-start.1 = (f32[256,768]{1,0:T(8,128)S(1)}, f32[256,768]{1,0:T(8,128)}, u32[]{:S(2)}) copy-start(f32[256,768]{1,0:T(8,128)} %weights_ref.3) | copy-start | bytes 2359300
  36.7 3.5 %copy-start.2 = (f32[256,768]{1,0:T(8,128)S(1)}, f32[256,768]{1,0:T(8,128)}, u32[]{:S(2)}) copy-start(f32[256,768]{1,0:T(8,128)} %first_ref.1) | copy-start | bytes 2359300
  36.7 3.5 %copy-start.3 = (f32[256,768]{1,0:T(8,128)S(1)}, f32[256,768]{1,0:T(8,128)}, u32[]{:S(2)}) copy-start(f32[256,768]{1,0:T(8,128)} %second_ref.1) | copy-start | bytes 2359300
  36.7 2.7 %collective-permute-start.16 = (bf16[128,768]{1,0:T(8,128)(2,1)S(1)}, bf16[128,768]{1,0:T(8,128)(2,1)S(1)}, u32[]{:S(2)}, u32[]{:S(2)}) collective-permute-start(bf16[128,768]{1,0:T(8,128)(2,1)S(1)} %collective-permute-done.12.b_ref), channel_id=1, source_target_pairs={{0,1},{1,0},{2,3},{3,2},{4,5},{5,4},{6,7},{7,6},{8,9},{9,8},{10,11... | collective-permute-start | bytes 589832 | tf_op jit(solution)/shard_map/ppermute | solution.py:304
  38.7 1.5 %collective-permute-start.15 = (bf16[144,768]{1,0:T(8,128)(2,1)S(1)}, bf16[144,768]{1,0:T(8,128)(2,1)S(1)}, u32[]{:S(2)}, u32[]{:S(2)}) collective-permute-start(bf16[144,768]{1,0:T(8,128)(2,1)S(1)} %collective-permute-done.11.a_ref), channel_id=1, source_target_pairs={{0,1},{1,0},{2,3},{3,2},{4,5},{5,4},{6,7},{7,6},{8,9},{9,8},{10,11... | collective-permute-start | bytes 663560 | tf_op jit(solution)/shard_map/ppermute | solution.py:304

commit v12 on v11

--- a/solution.py
+++ b/solution.py
@@ -20,7 +20,7 @@
 LANES = 128
 PIECES = 4
 VMEM_LIMIT = 32 * 1024 * 1024
-FLOPS = 5 * 10**8
+FLOPS = 2 * 10**8
 LATE_FLOPS = 10 * 10**8
 END_FLOPS = 100 * 10**8
 
@@ -48,6 +48,7 @@
 ):
     slots, docs = ids_ref.shape
     head = docs - b_ref.shape[0]
+    tiles = [pl.ds(start, LANES) for start in range(0, b_ref.shape[1], LANES)]
     fetches = [
         pltpu.make_async_copy(source, target, done.at[i])
         for i, (source, target) in enumerate(
@@ -55,8 +56,11 @@
                 (ids_hbm, ids_ref),
                 (table_hbm, table_ref),
                 (count_hbm, count_ref),
-                (docs_hbm.at[pl.ds(0, head)], a_ref.at[pl.ds(0, head)]),
                 (docs_hbm.at[pl.ds(head, docs - head)], b_ref),
+                *(
+                    (docs_hbm.at[pl.ds(0, head), tile], a_ref.at[pl.ds(j * head, head)])
+                    for j, tile in enumerate(tiles)
+                ),
             )
         )
     ]
@@ -85,15 +89,13 @@
     else:
         found = lax.fori_loop(0, pairs, pick, found, unroll=8)
     place = lax.broadcasted_iota(jnp.int32, (slots, LANES), 0)
-    a_ref[head:, :] = jnp.zeros((slots // 2, a_ref.shape[1]), jnp.bfloat16)
     for i, start in enumerate(starts):
         row = jnp.where((ids[i] >> 7) < pairs, found[i], found[i] >> 16) & 0xFFFF
         low = (LANES + (row & (LANES - 1))).astype(jnp.float32)
         code = power_of_two(row >> 7, bits, low * 2.0**-64, 1)
         code = jnp.where(place < count_ref[:, start : start + LANES], code, 0.0)
-        code = code.astype(jnp.bfloat16)
-        a_ref[head:, start : start + LANES] = code[: slots // 2]
-        a_ref[head:, docs + start : docs + start + LANES] = code[slots // 2 :]
+        first = len(tiles) * head + i * slots
+        a_ref[first : first + slots, :] = code.astype(jnp.bfloat16)
     for fetch in fetches[3:]:
         fetch.wait()
 
@@ -101,6 +103,7 @@
 def prepare(label_slot, pos_ids, pos_count, embeddings, head):
     docs, slots = pos_ids.shape
     width = embeddings.shape[1]
+    tall = width // LANES * head + slots * (docs // LANES)
     lines = label_slot.shape[0] // LANES
     table = label_slot.reshape(lines, LANES)
     inputs = (pos_ids.T, pos_count.reshape(1, docs), table, embeddings)
@@ -109,14 +112,14 @@
         in_specs=[pl.BlockSpec(memory_space=pltpu.HBM)] * 4,
         out_specs=[pl.BlockSpec(memory_space=pltpu.VMEM)] * 2,
         out_shape=[
-            jax.ShapeDtypeStruct((head + slots // 2, width), jnp.bfloat16),
+            jax.ShapeDtypeStruct((tall, LANES), jnp.bfloat16),
             jax.ShapeDtypeStruct((docs - head, width), jnp.bfloat16),
         ],
         scratch_shapes=[
             pltpu.VMEM((slots, docs), jnp.int32),
             pltpu.VMEM((1, docs), jnp.int32),
             pltpu.VMEM((lines, LANES), jnp.int32),
-            pltpu.SemaphoreType.DMA((5,)),
+            pltpu.SemaphoreType.DMA((4 + width // LANES,)),
         ],
         compiler_params=pltpu.CompilerParams(vmem_limit_bytes=VMEM_LIMIT),
         name="prepare",
@@ -159,10 +162,14 @@
 
 def doubled_gradient(bits, owners, a_ref, b_ref, w_refs):
     height = w_refs[0].shape[0]
-    head = b_ref.shape[0]
-    number = 2 * head
-    docs = jnp.concatenate([a_ref[:head, :], b_ref[...]], axis=0)
-    codes = jnp.concatenate([a_ref[head:, :number], a_ref[head:, number : 2 * number]], axis=0)
+    head, width = b_ref.shape
+    tiles = width // LANES
+    chunks = 2 * head // LANES
+    slots = (a_ref.shape[0] - tiles * head) // chunks
+    top = jnp.concatenate([a_ref[j * head : (j + 1) * head, :] for j in range(tiles)], axis=1)
+    docs = jnp.concatenate([top, b_ref[...]], axis=0)
+    starts = [tiles * head + i * slots for i in range(chunks)]
+    codes = jnp.concatenate([a_ref[start : start + slots, :] for start in starts], axis=1)
     codes = codes.astype(jnp.float32)
     weights = jnp.concatenate([ref[...] for ref in w_refs], axis=0)
     halved = lax.dot_general(
@@ -324,7 +331,7 @@
             if message in ("up_a", "down_b"):
                 side = message.split("_")[0]
                 waiting.append((came[side + "_a"], came[side + "_b"]))
-            if waiting and (last or (step > 1 and message != "down_b")):
+            if waiting and (last or (step > 1 and message != "up_b")):
                 sums = work(LATE_FLOPS if last else FLOPS)
     while waiting:
         sums = work(LATE_FLOPS)

time: 42.8 us -> 42.1 us (0.984)
  waiting for transfers between devices: 13.5 us -> 12 us
  starting transfers between devices: 15.8 us -> 16.5 us
    ppermute x18, waiting for transfers between devices: 13.5 us -> 12 us  [send(): return lax.ppermute(value, 'blk', pairs)]
    ppermute x18, starting transfers between devices: 15.8 us -> 16.5 us  [send(): return lax.ppermute(value, 'blk', pairs)]
  transfers between devices with their start and end apart: 18 -> 18, of which waited for: 12 -> 8; matrix products, arithmetic and copies ran while one was open for 0% -> 0% of each run, Pallas kernels for 18% -> 18%
where the time goes in v12:
time: 42.1 us; the launch traced here: 41.9 us
  starting transfers between devices  16.5 us (39%)
  waiting for transfers between devices  12 us (29%)
  Pallas kernels  11.4 us (27%)
  local copies, waits for them, and re-layouts  1.14 us (3%)
  between operations  0.81 us (2%)
    ppermute x18, starting transfers between devices, send(): return lax.ppermute(value, 'blk', pairs)  16.5 us
    ppermute x18, waiting for transfers between devices, send(): return lax.ppermute(value, 'blk', pairs)  12 us
    pallas_call x8, Pallas kernels, add_gradient(): pl.pallas_call(functools.partial(gradient_kernel, bits, owners, not sums)...  7.69 us
    pallas_call x1, Pallas kernels, finish(): pl.pallas_call(functools.partial(finish_kernel, bits), in_specs=[pl.Block...  2.35 us
    pallas_call x1, Pallas kernels, prepare(): pl.pallas_call(functools.partial(prepare_kernel, (lines - 1).bit_length()...  1.31 us
    unnamed x8, local copies, waits for them, and re-layouts  1.14 us
  transfers between devices with their start and end apart: 18, of which 8 were waited for; matrix products, arithmetic and copies ran while one was open for 0% of the time, Pallas kernels for 18%

profile of v12, /device:TPU:0, one launch (start us, length us, event | category | flops | bytes accessed | tf_op | source)
XLA Modules:
  0.0 41.9 jit_solution(4851079118931326963)
XLA Ops:
  0.6 1.3 %prepare.1 = (bf16[832,128]{1,0:T(8,128)(2,1)S(1)}, bf16[128,768]{1,0:T(8,128)(2,1)S(1)}) custom-call(s32[32,256]{1,0:T(8,128)} %bitcast.3, s32[1,256]{1,0:T(1,128)} %bitcast.5, s32[32,128]{1,0:T(8,128)} %bitcast.4, bf16[256,768]{1,0:T(8,128)(2,1)} %docs_hbm.1), custom_call_target="tpu_custom_call" | custom-call | tf_op jit(solution)/shard_map/prepare/pallas_call | solution.py:110
  1.9 3.1 %collective-permute-start.1 = (bf16[128,768]{1,0:T(8,128)(2,1)S(1)}, bf16[128,768]{1,0:T(8,128)(2,1)S(1)}, u32[]{:S(2)}, u32[]{:S(2)}) collective-permute-start(bf16[128,768]{1,0:T(8,128)(2,1)S(1)} %get-tuple-element.112.b_ref), channel_id=1, source_target_pairs={{0,4},{1,5},{4,8},{5,9},{8,12},{9,13},{12,14},{13,15},{14,10},{15,... | collective-permute-start | bytes 589832 | tf_op jit(solution)/shard_map/ppermute | solution.py:311
  5.0 2.0 %collective-permute-start.5 = (bf16[832,128]{1,0:T(8,128)(2,1)S(1)}, bf16[832,128]{1,0:T(8,128)(2,1)S(1)}, u32[]{:S(2)}, u32[]{:S(2)}) collective-permute-start(bf16[832,128]{1,0:T(8,128)(2,1)S(1)} %get-tuple-element.111.a_ref), channel_id=1, source_target_pairs={{0,4},{1,5},{4,8},{5,9},{8,12},{9,13},{12,14},{13,15},{14,10},{15,... | collective-permute-start | bytes 638984 | tf_op jit(solution)/shard_map/ppermute | solution.py:311
  7.0 1.1 %copy-done = f32[256,768]{1,0:T(8,128)S(1)} copy-done((f32[256,768]{1,0:T(8,128)S(1)}, f32[256,768]{1,0:T(8,128)}, u32[]{:S(2)}) %copy-start) | copy-done | bytes 786456
  8.2 0.1 collective-permute-start.10
  8.3 0.1 collective-permute-start.4
  8.4 2.3 %collective-permute-done.1.b_ref = bf16[128,768]{1,0:T(8,128)(2,1)S(1)} collective-permute-done((bf16[128,768]{1,0:T(8,128)(2,1)S(1)}, bf16[128,768]{1,0:T(8,128)(2,1)S(1)}, u32[]{:S(2)}, u32[]{:S(2)}) %collective-permute-start.1) | collective-permute-done | bytes 196640 | tf_op jit(solution)/shard_map/ppermute | solution.py:311
  10.7 2.1 %collective-permute-start.3 = (bf16[128,768]{1,0:T(8,128)(2,1)S(1)}, bf16[128,768]{1,0:T(8,128)(2,1)S(1)}, u32[]{:S(2)}, u32[]{:S(2)}) collective-permute-start(bf16[128,768]{1,0:T(8,128)(2,1)S(1)} %collective-permute-done.1.b_ref), channel_id=1, source_target_pairs={{0,4},{1,5},{4,8},{5,9},{8,12},{9,13},{12,14},{13,15},{14,10},{15,... | collective-permute-start | bytes 589832 | tf_op jit(solution)/shard_map/ppermute | solution.py:311
  12.8 2.4 %collective-permute-done.5.a_ref = bf16[832,128]{1,0:T(8,128)(2,1)S(1)} collective-permute-done((bf16[832,128]{1,0:T(8,128)(2,1)S(1)}, bf16[832,128]{1,0:T(8,128)(2,1)S(1)}, u32[]{:S(2)}, u32[]{:S(2)}) %collective-permute-start.5) | collective-permute-done | bytes 213024 | tf_op jit(solution)/shard_map/ppermute | solution.py:311
  15.3 2.1 %collective-permute-start.9 = (bf16[832,128]{1,0:T(8,128)(2,1)S(1)}, bf16[832,128]{1,0:T(8,128)(2,1)S(1)}, u32[]{:S(2)}, u32[]{:S(2)}) collective-permute-start(bf16[832,128]{1,0:T(8,128)(2,1)S(1)} %collective-permute-done.5.a_ref), channel_id=1, source_target_pairs={{0,4},{1,5},{4,8},{5,9},{8,12},{9,13},{12,14},{13,15},{14,10},{15,... | collective-permute-start | bytes 638984 | tf_op jit(solution)/shard_map/ppermute | solution.py:311
  17.4 2.1 %collective-permute-done.3.b_ref = bf16[128,768]{1,0:T(8,128)(2,1)S(1)} collective-permute-done((bf16[128,768]{1,0:T(8,128)(2,1)S(1)}, bf16[128,768]{1,0:T(8,128)(2,1)S(1)}, u32[]{:S(2)}, u32[]{:S(2)}) %collective-permute-start.3) | collective-permute-done | bytes 196640 | tf_op jit(solution)/shard_map/ppermute | solution.py:311
  19.5 2.1 %collective-permute-start.7 = (bf16[128,768]{1,0:T(8,128)(2,1)S(1)}, bf16[128,768]{1,0:T(8,128)(2,1)S(1)}, u32[]{:S(2)}, u32[]{:S(2)}) collective-permute-start(bf16[128,768]{1,0:T(8,128)(2,1)S(1)} %collective-permute-done.3.b_ref), channel_id=1, source_target_pairs={{0,4},{1,5},{4,8},{5,9},{8,12},{9,13},{12,14},{13,15},{14,10},{15,... | collective-permute-start | bytes 589832 | tf_op jit(solution)/shard_map/ppermute | solution.py:311
  21.6 1.0 %gradient.8 = (f32[256,768]{1,0:T(8,128)S(1)}, f32[256,768]{1,0:T(8,128)S(1)}) custom-call(bf16[832,128]{1,0:T(8,128)(2,1)S(1)} %get-tuple-element.111.a_ref, bf16[128,768]{1,0:T(8,128)(2,1)S(1)} %get-tuple-element.112.b_ref, bf16[256,768]{1,0:T(8,128)(2,1)S(1)} %cast.1.refs_0_.cast_ref, bf16[256,768]{1,0:T(8,128)(2,1)S(1)} %collective-permute-done.10.refs_1_), custom_call_target="tpu_custom_call" | custom-call | flops 200000000 | bytes 1000000 | tf_op jit(solution)/shard_map/gradient/pallas_call | solution.py:202
  22.6 1.4 %collective-permute-done.9.a_ref = bf16[832,128]{1,0:T(8,128)(2,1)S(1)} collective-permute-done((bf16[832,128]{1,0:T(8,128)(2,1)S(1)}, bf16[832,128]{1,0:T(8,128)(2,1)S(1)}, u32[]{:S(2)}, u32[]{:S(2)}) %collective-permute-start.9) | collective-permute-done | bytes 213024 | tf_op jit(solution)/shard_map/ppermute | solution.py:311
  24.0 2.1 %collective-permute-start.14 = (bf16[832,128]{1,0:T(8,128)(2,1)S(1)}, bf16[832,128]{1,0:T(8,128)(2,1)S(1)}, u32[]{:S(2)}, u32[]{:S(2)}) collective-permute-start(bf16[832,128]{1,0:T(8,128)(2,1)S(1)} %collective-permute-done.9.a_ref), channel_id=1, source_target_pairs={{0,4},{1,5},{4,8},{5,9},{8,12},{9,13},{12,14},{13,15},{14,10},{15,... | collective-permute-start | bytes 638984 | tf_op jit(solution)/shard_map/ppermute | solution.py:311
  26.2 1.0 %gradient.9 = (f32[256,768]{1,0:T(8,128)S(1)}, f32[256,768]{1,0:T(8,128)S(1)}) custom-call(bf16[832,128]{1,0:T(8,128)(2,1)S(1)} %collective-permute-done.5.a_ref, bf16[128,768]{1,0:T(8,128)(2,1)S(1)} %collective-permute-done.1.b_ref, bf16[256,768]{1,0:T(8,128)(2,1)S(1)} %cast.1.refs_0_.cast_ref, ...), custom_call_target="tpu_custom_call", output_to_operand_aliasing={{0}: (4, {}), {1}: (5, {})} | custom-call | flops 200000000 | bytes 1000000 | tf_op jit(solution)/shard_map/gradient/pallas_call | solution.py:202
  27.2 0.1 collective-permute-start.13
  27.2 1.0 %gradient.10 = (f32[256,768]{1,0:T(8,128)S(1)}, f32[256,768]{1,0:T(8,128)S(1)}) custom-call(bf16[832,128]{1,0:T(8,128)(2,1)S(1)} %collective-permute-done.a_ref, bf16[128,768]{1,0:T(8,128)(2,1)S(1)} %collective-permute-done.4.b_ref, bf16[256,768]{1,0:T(8,128)(2,1)S(1)} %cast.1.refs_0_.cast_ref, ...), custom_call_target="tpu_custom_call", output_to_operand_aliasing={{0}: (4, {}), {1}: (5, {})} | custom-call | flops 200000000 | bytes 1000000 | tf_op jit(solution)/shard_map/gradient/pallas_call | solution.py:202
  28.3 2.1 %collective-permute-start.12 = (bf16[128,768]{1,0:T(8,128)(2,1)S(1)}, bf16[128,768]{1,0:T(8,128)(2,1)S(1)}, u32[]{:S(2)}, u32[]{:S(2)}) collective-permute-start(bf16[128,768]{1,0:T(8,128)(2,1)S(1)} %collective-permute-done.7.b_ref), channel_id=1, source_target_pairs={{0,4},{1,5},{4,8},{5,9},{8,12},{9,13},{12,14},{13,15},{14,10},{15,... | collective-permute-start | bytes 589832 | tf_op jit(solution)/shard_map/ppermute | solution.py:311
  30.4 1.0 %gradient.11 = (f32[256,768]{1,0:T(8,128)S(1)}, f32[256,768]{1,0:T(8,128)S(1)}) custom-call(bf16[832,128]{1,0:T(8,128)(2,1)S(1)} %collective-permute-done.9.a_ref, bf16[128,768]{1,0:T(8,128)(2,1)S(1)} %collective-permute-done.3.b_ref, bf16[256,768]{1,0:T(8,128)(2,1)S(1)} %cast.1.refs_0_.cast_ref, ...), custom_call_target="tpu_custom_call", output_to_operand_aliasing={{0}: (4, {}), {1}: (5, {})} | custom-call | flops 1000000000 | bytes 1000000 | tf_op jit(solution)/shard_map/gradient/pallas_call | solution.py:202
  31.4 0.1 collective-permute-start.11
  31.5 1.0 %gradient.12 = (f32[256,768]{1,0:T(8,128)S(1)}, f32[256,768]{1,0:T(8,128)S(1)}) custom-call(bf16[832,128]{1,0:T(8,128)(2,1)S(1)} %collective-permute-done.2.a_ref, bf16[128,768]{1,0:T(8,128)(2,1)S(1)} %collective-permute-done.8.b_ref, bf16[256,768]{1,0:T(8,128)(2,1)S(1)} %cast.1.refs_0_.cast_ref, ...), custom_call_target="tpu_custom_call", output_to_operand_aliasing={{0}: (4, {}), {1}: (5, {})} | custom-call | flops 1000000000 | bytes 1000000 | tf_op jit(solution)/shard_map/gradient/pallas_call | solution.py:202
  32.5 0.3 collective-permute-done.14.a_ref
  32.8 1.0 %gradient.13 = (f32[256,768]{1,0:T(8,128)S(1)}, f32[256,768]{1,0:T(8,128)S(1)}) custom-call(bf16[832,128]{1,0:T(8,128)(2,1)S(1)} %collective-permute-done.14.a_ref, bf16[128,768]{1,0:T(8,128)(2,1)S(1)} %collective-permute-done.7.b_ref, bf16[256,768]{1,0:T(8,128)(2,1)S(1)} %cast.1.refs_0_.cast_ref, ...), custom_call_target="tpu_custom_call", output_to_operand_aliasing={{0}: (4, {}), {1}: (5, {})} | custom-call | flops 1000000000 | bytes 1000000 | tf_op jit(solution)/shard_map/gradient/pallas_call | solution.py:202
  33.8 1.2 %collective-permute-done.13.b_ref = bf16[128,768]{1,0:T(8,128)(2,1)S(1)} collective-permute-done((bf16[128,768]{1,0:T(8,128)(2,1)S(1)}, bf16[128,768]{1,0:T(8,128)(2,1)S(1)}, u32[]{:S(2)}, u32[]{:S(2)}) %collective-permute-start.13) | collective-permute-done | bytes 196640 | tf_op jit(solution)/shard_map/ppermute | solution.py:311
  35.1 1.0 %gradient.14 = (f32[256,768]{1,0:T(8,128)S(1)}, f32[256,768]{1,0:T(8,128)S(1)}) custom-call(bf16[832,128]{1,0:T(8,128)(2,1)S(1)} %collective-permute-done.6.a_ref, bf16[128,768]{1,0:T(8,128)(2,1)S(1)} %collective-permute-done.13.b_ref, bf16[256,768]{1,0:T(8,128)(2,1)S(1)} %cast.1.refs_0_.cast_ref, ...), custom_call_target="tpu_custom_call", output_to_operand_aliasing={{0}: (4, {}), {1}: (5, {})} | custom-call | flops 1000000000 | bytes 1000000 | tf_op jit(solution)/shard_map/gradient/pallas_call | solution.py:202
  36.1 0.1 collective-permute-start.17
  36.2 0.5 %collective-permute-start.16 = (bf16[128,768]{1,0:T(8,128)(2,1)S(1)}, bf16[128,768]{1,0:T(8,128)(2,1)S(1)}, u32[]{:S(2)}, u32[]{:S(2)}) collective-permute-start(bf16[128,768]{1,0:T(8,128)(2,1)S(1)} %collective-permute-done.12.b_ref), channel_id=1, source_target_pairs={{0,1},{1,0},{2,3},{3,2},{4,5},{5,4},{6,7},{7,6},{8,9},{9,8},{10,11... | collective-permute-start | bytes 589832 | tf_op jit(solution)/shard_map/ppermute | solution.py:311
  36.7 1.3 %collective-permute-done.11.a_ref = bf16[832,128]{1,0:T(8,128)(2,1)S(1)} collective-permute-done((bf16[832,128]{1,0:T(8,128)(2,1)S(1)}, bf16[832,128]{1,0:T(8,128)(2,1)S(1)}, u32[]{:S(2)}, u32[]{:S(2)}) %collective-permute-start.11) | collective-permute-done | bytes 213024 | tf_op jit(solution)/shard_map/ppermute | solution.py:311
  38.1 0.7 %gradient.15.sum_ref = f32[256,768]{1,0:T(8,128)S(1)} custom-call(bf16[832,128]{1,0:T(8,128)(2,1)S(1)} %collective-permute-done.11.a_ref, bf16[128,768]{1,0:T(8,128)(2,1)S(1)} %collective-permute-done.12.b_ref, bf16[256,768]{1,0:T(8,128)(2,1)S(1)} %cast.1.refs_0_.cast_ref, f32[256,768]{1,0:T(8,128)S(1)} %get-tuple-element.161.refs_1_), custom_call_target="tpu_custom_call", output_to_operand_aliasing={{}: (3, {})} | custom-call | flops 10000000000 | bytes 1000000 | tf_op jit(solution)/shard_map/gradient/pallas_call | solution.py:202
  38.7 0.8 %collective-permute-done.15.a_ref = bf16[832,128]{1,0:T(8,128)(2,1)S(1)} collective-permute-done((bf16[832,128]{1,0:T(8,128)(2,1)S(1)}, bf16[832,128]{1,0:T(8,128)(2,1)S(1)}, u32[]{:S(2)}, u32[]{:S(2)}) %collective-permute-start.15) | collective-permute-done | bytes 213024 | tf_op jit(solution)/shard_map/ppermute | solution.py:311
  39.6 2.3 %finish.1 = (f32[256,768]{1,0:T(8,128)}, f32[256,768]{1,0:T(8,128)}, f32[256,768]{1,0:T(8,128)}) custom-call(bf16[832,128]{1,0:T(8,128)(2,1)S(1)} %collective-permute-done.15.a_ref, bf16[128,768]{1,0:T(8,128)(2,1)S(1)} %collective-permute-done.16.b_ref, bf16[256,768]{1,0:T(8,128)(2,1)S(1)} %cast.1.refs_0_.cast_ref, f32[256,768]{1,0:T(8,128)S(1)} %gradient.15.sum_ref, ...), custom_call_target="tpu_custom_call" | custom-call | flops 10000000000 | bytes 1000000 | tf_op jit(solution)/shard_map/finish/pallas_call | solution.py:259
  (23 shorter events, 0.1 us)
Async XLA Ops:
  1.9 8.7 %collective-permute-start.1 = (bf16[128,768]{1,0:T(8,128)(2,1)S(1)}, bf16[128,768]{1,0:T(8,128)(2,1)S(1)}, u32[]{:S(2)}, u32[]{:S(2)}) collective-permute-start(bf16[128,768]{1,0:T(8,128)(2,1)S(1)} %get-tuple-element.112.b_ref), channel_id=1, source_target_pairs={{0,4},{1,5},{4,8},{5,9},{8,12},{9,13},{12,14},{13,15},{14,10},{15,... | collective-permute-start | bytes 589832 | tf_op jit(solution)/shard_map/ppermute | solution.py:311
  5.0 7.8 %collective-permute-start = (bf16[832,128]{1,0:T(8,128)(2,1)S(1)}, bf16[832,128]{1,0:T(8,128)(2,1)S(1)}, u32[]{:S(2)}, u32[]{:S(2)}) collective-permute-start(bf16[832,128]{1,0:T(8,128)(2,1)S(1)} %get-tuple-element.111.a_ref), channel_id=1, source_target_pairs={{4,0},{5,1},{8,4},{9,5},{12,8},{13,9},{14,12},{15,13},{10,14},{11,... | collective-permute-start | bytes 638984 | tf_op jit(solution)/shard_map/ppermute | solution.py:311
  5.0 10.2 %collective-permute-start.5 = (bf16[832,128]{1,0:T(8,128)(2,1)S(1)}, bf16[832,128]{1,0:T(8,128)(2,1)S(1)}, u32[]{:S(2)}, u32[]{:S(2)}) collective-permute-start(bf16[832,128]{1,0:T(8,128)(2,1)S(1)} %get-tuple-element.111.a_ref), channel_id=1, source_target_pairs={{0,4},{1,5},{4,8},{5,9},{8,12},{9,13},{12,14},{13,15},{14,10},{15,... | collective-permute-start | bytes 638984 | tf_op jit(solution)/shard_map/ppermute | solution.py:311
  7.0 1.1 %copy-start = (f32[256,768]{1,0:T(8,128)S(1)}, f32[256,768]{1,0:T(8,128)}, u32[]{:S(2)}) copy-start(f32[256,768]{1,0:T(8,128)} %weights_ref.3) | copy-start | bytes 2359300
  8.2 13.4 %collective-permute-start.10 = (bf16[256,768]{1,0:T(8,128)(2,1)S(1)}, bf16[256,768]{1,0:T(8,128)(2,1)S(1)}, u32[]{:S(2)}, u32[]{:S(2)}) collective-permute-start(bf16[256,768]{1,0:T(8,128)(2,1)S(1)} %cast.1.refs_0_.cast_ref), channel_id=1, source_target_pairs={{0,1},{1,0},{2,3},{3,2},{4,5},{5,4},{6,7},{7,6},{8,9},{9,8},{10,11... | collective-permute-start | bytes 1179656 | tf_op jit(solution)/shard_map/ppermute | solution.py:311
  8.3 9.1 %collective-permute-start.4 = (bf16[128,768]{1,0:T(8,128)(2,1)S(1)}, bf16[128,768]{1,0:T(8,128)(2,1)S(1)}, u32[]{:S(2)}, u32[]{:S(2)}) collective-permute-start(bf16[128,768]{1,0:T(8,128)(2,1)S(1)} %get-tuple-element.112.b_ref), channel_id=1, source_target_pairs={{4,0},{5,1},{8,4},{9,5},{12,8},{13,9},{14,12},{15,13},{10,14},{11,... | collective-permute-start | bytes 589832 | tf_op jit(solution)/shard_map/ppermute | solution.py:311
  10.7 8.8 %collective-permute-start.3 = (bf16[128,768]{1,0:T(8,128)(2,1)S(1)}, bf16[128,768]{1,0:T(8,128)(2,1)S(1)}, u32[]{:S(2)}, u32[]{:S(2)}) collective-permute-start(bf16[128,768]{1,0:T(8,128)(2,1)S(1)} %collective-permute-done.1.b_ref), channel_id=1, source_target_pairs={{0,4},{1,5},{4,8},{5,9},{8,12},{9,13},{12,14},{13,15},{14,10},{15,... | collective-permute-start | bytes 589832 | tf_op jit(solution)/shard_map/ppermute | solution.py:311
  12.8 8.8 %collective-permute-start.2 = (bf16[832,128]{1,0:T(8,128)(2,1)S(1)}, bf16[832,128]{1,0:T(8,128)(2,1)S(1)}, u32[]{:S(2)}, u32[]{:S(2)}) collective-permute-start(bf16[832,128]{1,0:T(8,128)(2,1)S(1)} %collective-permute-done.a_ref), channel_id=1, source_target_pairs={{4,0},{5,1},{8,4},{9,5},{12,8},{13,9},{14,12},{15,13},{10,14},{11,... | collective-permute-start | bytes 638984 | tf_op jit(solution)/shard_map/ppermute | solution.py:311
  15.3 8.8 %collective-permute-start.9 = (bf16[832,128]{1,0:T(8,128)(2,1)S(1)}, bf16[832,128]{1,0:T(8,128)(2,1)S(1)}, u32[]{:S(2)}, u32[]{:S(2)}) collective-permute-start(bf16[832,128]{1,0:T(8,128)(2,1)S(1)} %collective-permute-done.5.a_ref), channel_id=1, source_target_pairs={{0,4},{1,5},{4,8},{5,9},{8,12},{9,13},{12,14},{13,15},{14,10},{15,... | collective-permute-start | bytes 638984 | tf_op jit(solution)/shard_map/ppermute | solution.py:311
  17.4 9.8 %collective-permute-start.8 = (bf16[128,768]{1,0:T(8,128)(2,1)S(1)}, bf16[128,768]{1,0:T(8,128)(2,1)S(1)}, u32[]{:S(2)}, u32[]{:S(2)}) collective-permute-start(bf16[128,768]{1,0:T(8,128)(2,1)S(1)} %collective-permute-done.4.b_ref), channel_id=1, source_target_pairs={{4,0},{5,1},{8,4},{9,5},{12,8},{13,9},{14,12},{15,13},{10,14},{11,... | collective-permute-start | bytes 589832 | tf_op jit(solution)/shard_map/ppermute | solution.py:311
  19.5 8.8 %collective-permute-start.7 = (bf16[128,768]{1,0:T(8,128)(2,1)S(1)}, bf16[128,768]{1,0:T(8,128)(2,1)S(1)}, u32[]{:S(2)}, u32[]{:S(2)}) collective-permute-start(bf16[128,768]{1,0:T(8,128)(2,1)S(1)} %collective-permute-done.3.b_ref), channel_id=1, source_target_pairs={{0,4},{1,5},{4,8},{5,9},{8,12},{9,13},{12,14},{13,15},{14,10},{15,... | collective-permute-start | bytes 589832 | tf_op jit(solution)/shard_map/ppermute | solution.py:311
  21.6 9.8 %collective-permute-start.6 = (bf16[832,128]{1,0:T(8,128)(2,1)S(1)}, bf16[832,128]{1,0:T(8,128)(2,1)S(1)}, u32[]{:S(2)}, u32[]{:S(2)}) collective-permute-start(bf16[832,128]{1,0:T(8,128)(2,1)S(1)} %collective-permute-done.2.a_ref), channel_id=1, source_target_pairs={{4,0},{5,1},{8,4},{9,5},{12,8},{13,9},{14,12},{15,13},{10,14},{11,... | collective-permute-start | bytes 638984 | tf_op jit(solution)/shard_map/ppermute | solution.py:311
  24.0 8.8 %collective-permute-start.14 = (bf16[832,128]{1,0:T(8,128)(2,1)S(1)}, bf16[832,128]{1,0:T(8,128)(2,1)S(1)}, u32[]{:S(2)}, u32[]{:S(2)}) collective-permute-start(bf16[832,128]{1,0:T(8,128)(2,1)S(1)} %collective-permute-done.9.a_ref), channel_id=1, source_target_pairs={{0,4},{1,5},{4,8},{5,9},{8,12},{9,13},{12,14},{13,15},{14,10},{15,... | collective-permute-start | bytes 638984 | tf_op jit(solution)/shard_map/ppermute | solution.py:311
  27.2 7.9 %collective-permute-start.13 = (bf16[128,768]{1,0:T(8,128)(2,1)S(1)}, bf16[128,768]{1,0:T(8,128)(2,1)S(1)}, u32[]{:S(2)}, u32[]{:S(2)}) collective-permute-start(bf16[128,768]{1,0:T(8,128)(2,1)S(1)} %collective-permute-done.8.b_ref), channel_id=1, source_target_pairs={{4,0},{5,1},{8,4},{9,5},{12,8},{13,9},{14,12},{15,13},{10,14},{11,... | collective-permute-start | bytes 589832 | tf_op jit(solution)/shard_map/ppermute | solution.py:311
  28.3 7.9 %collective-permute-start.12 = (bf16[128,768]{1,0:T(8,128)(2,1)S(1)}, bf16[128,768]{1,0:T(8,128)(2,1)S(1)}, u32[]{:S(2)}, u32[]{:S(2)}) collective-permute-start(bf16[128,768]{1,0:T(8,128)(2,1)S(1)} %collective-permute-done.7.b_ref), channel_id=1, source_target_pairs={{0,4},{1,5},{4,8},{5,9},{8,12},{9,13},{12,14},{13,15},{14,10},{15,... | collective-permute-start | bytes 589832 | tf_op jit(solution)/shard_map/ppermute | solution.py:311
  31.4 6.7 %collective-permute-start.11 = (bf16[832,128]{1,0:T(8,128)(2,1)S(1)}, bf16[832,128]{1,0:T(8,128)(2,1)S(1)}, u32[]{:S(2)}, u32[]{:S(2)}) collective-permute-start(bf16[832,128]{1,0:T(8,128)(2,1)S(1)} %collective-permute-done.6.a_ref), channel_id=1, source_target_pairs={{4,0},{5,1},{8,4},{9,5},{12,8},{13,9},{14,12},{15,13},{10,14},{11,... | collective-permute-start | bytes 638984 | tf_op jit(solution)/shard_map/ppermute | solution.py:311
  36.1 3.4 %collective-permute-start.17 = (f32[256,768]{1,0:T(8,128)S(1)}, f32[256,768]{1,0:T(8,128)S(1)}, u32[]{:S(2)}, u32[]{:S(2)}) collective-permute-start(f32[256,768]{1,0:T(8,128)S(1)} %get-tuple-element.162), channel_id=1, source_target_pairs={{0,1},{1,0},{2,3},{3,2},{4,5},{5,4},{6,7},{7,6},{8,9},{9,8},{10,11... | collective-permute-start | bytes 2359304 | tf_op jit(solution)/shard_map/ppermute | solution.py:311
  36.2 3.3 %copy-start.1 = (f32[256,768]{1,0:T(8,128)S(1)}, f32[256,768]{1,0:T(8,128)}, u32[]{:S(2)}) copy-start(f32[256,768]{1,0:T(8,128)} %weights_ref.3) | copy-start | bytes 2359300
  36.2 3.3 %copy-start.2 = (f32[256,768]{1,0:T(8,128)S(1)}, f32[256,768]{1,0:T(8,128)}, u32[]{:S(2)}) copy-start(f32[256,768]{1,0:T(8,128)} %first_ref.1) | copy-start | bytes 2359300
  36.2 3.3 %copy-start.3 = (f32[256,768]{1,0:T(8,128)S(1)}, f32[256,768]{1,0:T(8,128)}, u32[]{:S(2)}) copy-start(f32[256,768]{1,0:T(8,128)} %second_ref.1) | copy-start | bytes 2359300
  36.2 2.5 %collective-permute-start.16 = (bf16[128,768]{1,0:T(8,128)(2,1)S(1)}, bf16[128,768]{1,0:T(8,128)(2,1)S(1)}, u32[]{:S(2)}, u32[]{:S(2)}) collective-permute-start(bf16[128,768]{1,0:T(8,128)(2,1)S(1)} %collective-permute-done.12.b_ref), channel_id=1, source_target_pairs={{0,1},{1,0},{2,3},{3,2},{4,5},{5,4},{6,7},{7,6},{8,9},{9,8},{10,11... | collective-permute-start | bytes 589832 | tf_op jit(solution)/shard_map/ppermute | solution.py:311
  38.1 1.5 %collective-permute-start.15 = (bf16[832,128]{1,0:T(8,128)(2,1)S(1)}, bf16[832,128]{1,0:T(8,128)(2,1)S(1)}, u32[]{:S(2)}, u32[]{:S(2)}) collective-permute-start(bf16[832,128]{1,0:T(8,128)(2,1)S(1)} %collective-permute-done.11.a_ref), channel_id=1, source_target_pairs={{0,1},{1,0},{2,3},{3,2},{4,5},{5,4},{6,7},{7,6},{8,9},{9,8},{10,11... | collective-permute-start | bytes 638984 | tf_op jit(solution)/shard_map/ppermute | solution.py:311

commit v13 on v12

--- a/solution.py
+++ b/solution.py
@@ -20,8 +20,9 @@
 LANES = 128
 PIECES = 4
 VMEM_LIMIT = 32 * 1024 * 1024
-FLOPS = 2 * 10**8
+FLOPS = 5 * 10**8
 LATE_FLOPS = 10 * 10**8
+PLAN = {(1,"down_b"):1,(2,"up_b"):1,(2,"up_a"):1,(3,"up_b"):1,(3,"up_a"):1,("last","up_b"):1,("last","down_a"):1,("last","up_a"):1,("last","down_b"):1}
 END_FLOPS = 100 * 10**8
 
 
@@ -39,11 +40,14 @@
     count_hbm,
     table_hbm,
     docs_hbm,
+    weights_hbm,
     a_ref,
     b_ref,
+    cast_ref,
     ids_ref,
     count_ref,
     table_ref,
+    weights_ref,
     done,
 ):
     slots, docs = ids_ref.shape
@@ -61,6 +65,7 @@
                     (docs_hbm.at[pl.ds(0, head), tile], a_ref.at[pl.ds(j * head, head)])
                     for j, tile in enumerate(tiles)
                 ),
+                (weights_hbm, weights_ref),
             )
         )
     ]
@@ -98,47 +103,35 @@
         a_ref[first : first + slots, :] = code.astype(jnp.bfloat16)
     for fetch in fetches[3:]:
         fetch.wait()
-
-
-def prepare(label_slot, pos_ids, pos_count, embeddings, head):
+    cast_ref[...] = weights_ref[...].astype(jnp.bfloat16) * 0.5
+
+
+def prepare(label_slot, pos_ids, pos_count, embeddings, weights, head):
     docs, slots = pos_ids.shape
     width = embeddings.shape[1]
     tall = width // LANES * head + slots * (docs // LANES)
     lines = label_slot.shape[0] // LANES
     table = label_slot.reshape(lines, LANES)
-    inputs = (pos_ids.T, pos_count.reshape(1, docs), table, embeddings)
+    inputs = (pos_ids.T, pos_count.reshape(1, docs), table, embeddings, weights)
     return pl.pallas_call(
         functools.partial(prepare_kernel, (lines - 1).bit_length()),
-        in_specs=[pl.BlockSpec(memory_space=pltpu.HBM)] * 4,
-        out_specs=[pl.BlockSpec(memory_space=pltpu.VMEM)] * 2,
+        in_specs=[pl.BlockSpec(memory_space=pltpu.HBM)] * 5,
+        out_specs=[pl.BlockSpec(memory_space=pltpu.VMEM)] * 3,
         out_shape=[
             jax.ShapeDtypeStruct((tall, LANES), jnp.bfloat16),
             jax.ShapeDtypeStruct((docs - head, width), jnp.bfloat16),
+            jax.ShapeDtypeStruct(weights.shape, jnp.bfloat16),
         ],
         scratch_shapes=[
             pltpu.VMEM((slots, docs), jnp.int32),
             pltpu.VMEM((1, docs), jnp.int32),
             pltpu.VMEM((lines, LANES), jnp.int32),
-            pltpu.SemaphoreType.DMA((4 + width // LANES,)),
+            pltpu.VMEM(weights.shape, jnp.float32),
+            pltpu.SemaphoreType.DMA((5 + width // LANES,)),
         ],
         compiler_params=pltpu.CompilerParams(vmem_limit_bytes=VMEM_LIMIT),
         name="prepare",
     )(*(pltpu.with_memory_space_constraint(x, pltpu.HBM) for x in inputs))
-
-
-def cast_kernel(weights_ref, cast_ref):
-    cast_ref[...] = weights_ref[...].astype(jnp.bfloat16) * 0.5
-
-
-def halved_cast(weights):
-    return pl.pallas_call(
-        cast_kernel,
-        in_specs=[pl.BlockSpec(memory_space=pltpu.VMEM)],
-        out_specs=pl.BlockSpec(memory_space=pltpu.VMEM),
-        out_shape=jax.ShapeDtypeStruct(weights.shape, jnp.bfloat16),
-        compiler_params=pltpu.CompilerParams(vmem_limit_bytes=VMEM_LIMIT),
-        name="cast",
-    )(weights)
 
 
 def signs_of(codes, owner, bits, height):
@@ -310,10 +303,9 @@
     def send(value, pairs):
         return lax.ppermute(value, "blk", pairs)
 
-    a, b = prepare(label_slot, pos_ids, pos_count, embeddings, head)
+    a, b, mine = prepare(label_slot, pos_ids, pos_count, embeddings, weights, head)
     coming = {"up_b": send(b, up), "down_a": send(a, down)}
     coming |= {"up_a": send(a, up), "down_b": send(b, down)}
-    mine = halved_cast(weights)
     cast = [mine, send(mine, swap)]
     sums = ()
     waiting = [(a, b)]
@@ -331,8 +323,9 @@
             if message in ("up_a", "down_b"):
                 side = message.split("_")[0]
                 waiting.append((came[side + "_a"], came[side + "_b"]))
-            if waiting and (last or (step > 1 and message != "up_b")):
-                sums = work(LATE_FLOPS if last else FLOPS)
+            for _ in range(PLAN.get((min(step, 3) if not last else "last", message), 0)):
+                if waiting:
+                    sums = work(LATE_FLOPS if last else FLOPS)
     while waiting:
         sums = work(LATE_FLOPS)
     mine_sum, other_sum = sums

time: 42.1 us -> 43 us (1.021)
  waiting for transfers between devices: 12 us -> 14.9 us
  local copies, waits for them, and re-layouts: 1.14 us -> 0.01 us
  starting transfers between devices: 16.5 us -> 15.5 us
    ppermute x18, waiting for transfers between devices: 12 us -> 14.9 us  [send(): return lax.ppermute(value, 'blk', pairs)]
    unnamed x8 -> x6, local copies, waits for them, and re-layouts: 1.14 us -> 0.01 us
    ppermute x18, starting transfers between devices: 16.5 us -> 15.5 us  [send(): return lax.ppermute(value, 'blk', pairs)]
  transfers between devices with their start and end apart: 18 -> 18, of which waited for: 8 -> 11; matrix products, arithmetic and copies ran while one was open for 0% -> 0% of each run, Pallas kernels for 18% -> 18%
where the time goes in v13:
time: 43 us; the launch traced here: 42.8 us
  starting transfers between devices  15.5 us (36%)
  waiting for transfers between devices  14.9 us (35%)
  Pallas kernels  11.6 us (27%)
  between operations  0.77 us (2%)
    ppermute x18, starting transfers between devices, send(): return lax.ppermute(value, 'blk', pairs)  15.5 us
    ppermute x18, waiting for transfers between devices, send(): return lax.ppermute(value, 'blk', pairs)  14.9 us
    pallas_call x8, Pallas kernels, add_gradient(): pl.pallas_call(functools.partial(gradient_kernel, bits, owners, not sums)...  7.69 us
    pallas_call x1, Pallas kernels, finish(): pl.pallas_call(functools.partial(finish_kernel, bits), in_specs=[pl.Block...  2.35 us
    pallas_call x1, Pallas kernels, prepare(): pl.pallas_call(functools.partial(prepare_kernel, (lines - 1).bit_length()...  1.54 us
  transfers between devices with their start and end apart: 18, of which 11 were waited for; matrix products, arithmetic and copies ran while one was open for 0% of the time, Pallas kernels for 18%

profile of v13, /device:TPU:0, one launch (start us, length us, event | category | flops | bytes accessed | tf_op | source)
XLA Modules:
  0.0 42.8 jit_solution(14108347429687588519)
XLA Ops:
  0.6 1.5 %prepare.1 = (bf16[832,128]{1,0:T(8,128)(2,1)S(1)}, bf16[128,768]{1,0:T(8,128)(2,1)S(1)}, bf16[256,768]{1,0:T(8,128)(2,1)S(1)}) custom-call(s32[32,256]{1,0:T(8,128)} %bitcast.3, s32[1,256]{1,0:T(1,128)} %bitcast.5, s32[32,128]{1,0:T(8,128)} %bitcast.4, bf16[256,768]{1,0:T(8,128)(2,1)} %docs_hbm.1, f32[256,768]{1,0:T(8,128)} %weights_ref.1), custom_call_target="tpu_custom_call" | custom-call | tf_op jit(solution)/shard_map/prepare/pallas_call | solution.py:116
  2.2 0.5 %collective-permute-start.6 = (bf16[256,768]{1,0:T(8,128)(2,1)S(1)}, bf16[256,768]{1,0:T(8,128)(2,1)S(1)}, u32[]{:S(2)}, u32[]{:S(2)}) collective-permute-start(bf16[256,768]{1,0:T(8,128)(2,1)S(1)} %get-tuple-element.94.refs_0_.cast_ref), channel_id=1, source_target_pairs={{0,1},{1,0},{2,3},{3,2},{4,5},{5,4},{6,7},{7,6},{8,9},{9,8},{10,11... | collective-permute-start | bytes 1179656 | tf_op jit(solution)/shard_map/ppermute | solution.py:304
  2.7 2.6 %collective-permute-start.1 = (bf16[128,768]{1,0:T(8,128)(2,1)S(1)}, bf16[128,768]{1,0:T(8,128)(2,1)S(1)}, u32[]{:S(2)}, u32[]{:S(2)}) collective-permute-start(bf16[128,768]{1,0:T(8,128)(2,1)S(1)} %get-tuple-element.93.b_ref), channel_id=1, source_target_pairs={{0,4},{1,5},{4,8},{5,9},{8,12},{9,13},{12,14},{13,15},{14,10},{15,... | collective-permute-start | bytes 589832 | tf_op jit(solution)/shard_map/ppermute | solution.py:304
  5.4 2.0 %collective-permute-start.5 = (bf16[832,128]{1,0:T(8,128)(2,1)S(1)}, bf16[832,128]{1,0:T(8,128)(2,1)S(1)}, u32[]{:S(2)}, u32[]{:S(2)}) collective-permute-start(bf16[832,128]{1,0:T(8,128)(2,1)S(1)} %get-tuple-element.92.a_ref), channel_id=1, source_target_pairs={{0,4},{1,5},{4,8},{5,9},{8,12},{9,13},{12,14},{13,15},{14,10},{15,... | collective-permute-start | bytes 638984 | tf_op jit(solution)/shard_map/ppermute | solution.py:304
  7.4 3.6 %collective-permute-done.1.b_ref = bf16[128,768]{1,0:T(8,128)(2,1)S(1)} collective-permute-done((bf16[128,768]{1,0:T(8,128)(2,1)S(1)}, bf16[128,768]{1,0:T(8,128)(2,1)S(1)}, u32[]{:S(2)}, u32[]{:S(2)}) %collective-permute-start.1) | collective-permute-done | bytes 196640 | tf_op jit(solution)/shard_map/ppermute | solution.py:304
  11.0 2.0 %collective-permute-start.3 = (bf16[128,768]{1,0:T(8,128)(2,1)S(1)}, bf16[128,768]{1,0:T(8,128)(2,1)S(1)}, u32[]{:S(2)}, u32[]{:S(2)}) collective-permute-start(bf16[128,768]{1,0:T(8,128)(2,1)S(1)} %collective-permute-done.1.b_ref), channel_id=1, source_target_pairs={{0,4},{1,5},{4,8},{5,9},{8,12},{9,13},{12,14},{13,15},{14,10},{15,... | collective-permute-start | bytes 589832 | tf_op jit(solution)/shard_map/ppermute | solution.py:304
  13.0 0.4 collective-permute-done.a_ref
  13.4 2.2 %collective-permute-done.5.a_ref = bf16[832,128]{1,0:T(8,128)(2,1)S(1)} collective-permute-done((bf16[832,128]{1,0:T(8,128)(2,1)S(1)}, bf16[832,128]{1,0:T(8,128)(2,1)S(1)}, u32[]{:S(2)}, u32[]{:S(2)}) %collective-permute-start.5) | collective-permute-done | bytes 213024 | tf_op jit(solution)/shard_map/ppermute | solution.py:304
  15.6 2.0 %collective-permute-start.10 = (bf16[832,128]{1,0:T(8,128)(2,1)S(1)}, bf16[832,128]{1,0:T(8,128)(2,1)S(1)}, u32[]{:S(2)}, u32[]{:S(2)}) collective-permute-start(bf16[832,128]{1,0:T(8,128)(2,1)S(1)} %collective-permute-done.5.a_ref), channel_id=1, source_target_pairs={{0,4},{1,5},{4,8},{5,9},{8,12},{9,13},{12,14},{13,15},{14,10},{15,... | collective-permute-start | bytes 638984 | tf_op jit(solution)/shard_map/ppermute | solution.py:304
  17.6 1.0 %gradient.8 = (f32[256,768]{1,0:T(8,128)S(1)}, f32[256,768]{1,0:T(8,128)S(1)}) custom-call(bf16[832,128]{1,0:T(8,128)(2,1)S(1)} %get-tuple-element.92.a_ref, bf16[128,768]{1,0:T(8,128)(2,1)S(1)} %get-tuple-element.93.b_ref, bf16[256,768]{1,0:T(8,128)(2,1)S(1)} %get-tuple-element.94.refs_0_.cast_ref, bf16[256,768]{1,0:T(8,128)(2,1)S(1)} %collective-permute-done.6.refs_1_), custom_call_target="tpu_custom_call" | custom-call | flops 500000000 | bytes 1000000 | tf_op jit(solution)/shard_map/gradient/pallas_call | solution.py:195
  18.6 1.2 %collective-permute-done.3.b_ref = bf16[128,768]{1,0:T(8,128)(2,1)S(1)} collective-permute-done((bf16[128,768]{1,0:T(8,128)(2,1)S(1)}, bf16[128,768]{1,0:T(8,128)(2,1)S(1)}, u32[]{:S(2)}, u32[]{:S(2)}) %collective-permute-start.3) | collective-permute-done | bytes 196640 | tf_op jit(solution)/shard_map/ppermute | solution.py:304
  19.8 2.0 %collective-permute-start.8 = (bf16[128,768]{1,0:T(8,128)(2,1)S(1)}, bf16[128,768]{1,0:T(8,128)(2,1)S(1)}, u32[]{:S(2)}, u32[]{:S(2)}) collective-permute-start(bf16[128,768]{1,0:T(8,128)(2,1)S(1)} %collective-permute-done.3.b_ref), channel_id=1, source_target_pairs={{0,4},{1,5},{4,8},{5,9},{8,12},{9,13},{12,14},{13,15},{14,10},{15,... | collective-permute-start | bytes 589832 | tf_op jit(solution)/shard_map/ppermute | solution.py:304
  21.8 1.0 %gradient.9 = (f32[256,768]{1,0:T(8,128)S(1)}, f32[256,768]{1,0:T(8,128)S(1)}) custom-call(bf16[832,128]{1,0:T(8,128)(2,1)S(1)} %collective-permute-done.5.a_ref, bf16[128,768]{1,0:T(8,128)(2,1)S(1)} %collective-permute-done.1.b_ref, bf16[256,768]{1,0:T(8,128)(2,1)S(1)} %get-tuple-element.94.refs_0_.cast_ref, ...), custom_call_target="tpu_custom_call", output_to_operand_aliasing={{0}: (4, {}), {1}: (5, {})} | custom-call | flops 500000000 | bytes 1000000 | tf_op jit(solution)/shard_map/gradient/pallas_call | solution.py:195
  22.8 0.1 collective-permute-start.7
  22.9 1.5 %collective-permute-done.10.a_ref = bf16[832,128]{1,0:T(8,128)(2,1)S(1)} collective-permute-done((bf16[832,128]{1,0:T(8,128)(2,1)S(1)}, bf16[832,128]{1,0:T(8,128)(2,1)S(1)}, u32[]{:S(2)}, u32[]{:S(2)}) %collective-permute-start.10) | collective-permute-done | bytes 213024 | tf_op jit(solution)/shard_map/ppermute | solution.py:304
  24.4 2.0 %collective-permute-start.14 = (bf16[832,128]{1,0:T(8,128)(2,1)S(1)}, bf16[832,128]{1,0:T(8,128)(2,1)S(1)}, u32[]{:S(2)}, u32[]{:S(2)}) collective-permute-start(bf16[832,128]{1,0:T(8,128)(2,1)S(1)} %collective-permute-done.10.a_ref), channel_id=1, source_target_pairs={{0,4},{1,5},{4,8},{5,9},{8,12},{9,13},{12,14},{13,15},{14,10},{15,... | collective-permute-start | bytes 638984 | tf_op jit(solution)/shard_map/ppermute | solution.py:304
  26.4 1.0 %gradient.10 = (f32[256,768]{1,0:T(8,128)S(1)}, f32[256,768]{1,0:T(8,128)S(1)}) custom-call(bf16[832,128]{1,0:T(8,128)(2,1)S(1)} %collective-permute-done.a_ref, bf16[128,768]{1,0:T(8,128)(2,1)S(1)} %collective-permute-done.4.b_ref, bf16[256,768]{1,0:T(8,128)(2,1)S(1)} %get-tuple-element.94.refs_0_.cast_ref, ...), custom_call_target="tpu_custom_call", output_to_operand_aliasing={{0}: (4, {}), {1}: (5, {})} | custom-call | flops 500000000 | bytes 1000000 | tf_op jit(solution)/shard_map/gradient/pallas_call | solution.py:195
  27.4 0.1 collective-permute-start.13
  27.5 1.1 %collective-permute-done.8.b_ref = bf16[128,768]{1,0:T(8,128)(2,1)S(1)} collective-permute-done((bf16[128,768]{1,0:T(8,128)(2,1)S(1)}, bf16[128,768]{1,0:T(8,128)(2,1)S(1)}, u32[]{:S(2)}, u32[]{:S(2)}) %collective-permute-start.8) | collective-permute-done | bytes 196640 | tf_op jit(solution)/shard_map/ppermute | solution.py:304
  28.6 2.0 %collective-permute-start.12 = (bf16[128,768]{1,0:T(8,128)(2,1)S(1)}, bf16[128,768]{1,0:T(8,128)(2,1)S(1)}, u32[]{:S(2)}, u32[]{:S(2)}) collective-permute-start(bf16[128,768]{1,0:T(8,128)(2,1)S(1)} %collective-permute-done.8.b_ref), channel_id=1, source_target_pairs={{0,4},{1,5},{4,8},{5,9},{8,12},{9,13},{12,14},{13,15},{14,10},{15,... | collective-permute-start | bytes 589832 | tf_op jit(solution)/shard_map/ppermute | solution.py:304
  30.6 1.0 %gradient.11 = (f32[256,768]{1,0:T(8,128)S(1)}, f32[256,768]{1,0:T(8,128)S(1)}) custom-call(bf16[832,128]{1,0:T(8,128)(2,1)S(1)} %collective-permute-done.10.a_ref, bf16[128,768]{1,0:T(8,128)(2,1)S(1)} %collective-permute-done.3.b_ref, bf16[256,768]{1,0:T(8,128)(2,1)S(1)} %get-tuple-element.94.refs_0_.cast_ref, ...), custom_call_target="tpu_custom_call", output_to_operand_aliasing={{0}: (4, {}), {1}: (5, {})} | custom-call | flops 1000000000 | bytes 1000000 | tf_op jit(solution)/shard_map/gradient/pallas_call | solution.py:195
  31.6 0.1 collective-permute-start.11
  31.7 1.0 %gradient.12 = (f32[256,768]{1,0:T(8,128)S(1)}, f32[256,768]{1,0:T(8,128)S(1)}) custom-call(bf16[832,128]{1,0:T(8,128)(2,1)S(1)} %collective-permute-done.2.a_ref, bf16[128,768]{1,0:T(8,128)(2,1)S(1)} %collective-permute-done.9.b_ref, bf16[256,768]{1,0:T(8,128)(2,1)S(1)} %get-tuple-element.94.refs_0_.cast_ref, ...), custom_call_target="tpu_custom_call", output_to_operand_aliasing={{0}: (4, {}), {1}: (5, {})} | custom-call | flops 1000000000 | bytes 1000000 | tf_op jit(solution)/shard_map/gradient/pallas_call | solution.py:195
  32.7 0.4 %collective-permute-done.14.a_ref = bf16[832,128]{1,0:T(8,128)(2,1)S(1)} collective-permute-done((bf16[832,128]{1,0:T(8,128)(2,1)S(1)}, bf16[832,128]{1,0:T(8,128)(2,1)S(1)}, u32[]{:S(2)}, u32[]{:S(2)}) %collective-permute-start.14) | collective-permute-done | bytes 213024 | tf_op jit(solution)/shard_map/ppermute | solution.py:304
  33.1 1.0 %gradient.13 = (f32[256,768]{1,0:T(8,128)S(1)}, f32[256,768]{1,0:T(8,128)S(1)}) custom-call(bf16[832,128]{1,0:T(8,128)(2,1)S(1)} %collective-permute-done.14.a_ref, bf16[128,768]{1,0:T(8,128)(2,1)S(1)} %collective-permute-done.8.b_ref, bf16[256,768]{1,0:T(8,128)(2,1)S(1)} %get-tuple-element.94.refs_0_.cast_ref, ...), custom_call_target="tpu_custom_call", output_to_operand_aliasing={{0}: (4, {}), {1}: (5, {})} | custom-call | flops 1000000000 | bytes 1000000 | tf_op jit(solution)/shard_map/gradient/pallas_call | solution.py:195
  34.2 1.1 %collective-permute-done.13.b_ref = bf16[128,768]{1,0:T(8,128)(2,1)S(1)} collective-permute-done((bf16[128,768]{1,0:T(8,128)(2,1)S(1)}, bf16[128,768]{1,0:T(8,128)(2,1)S(1)}, u32[]{:S(2)}, u32[]{:S(2)}) %collective-permute-start.13) | collective-permute-done | bytes 196640 | tf_op jit(solution)/shard_map/ppermute | solution.py:304
  35.3 1.0 %gradient.14 = (f32[256,768]{1,0:T(8,128)S(1)}, f32[256,768]{1,0:T(8,128)S(1)}) custom-call(bf16[832,128]{1,0:T(8,128)(2,1)S(1)} %collective-permute-done.7.a_ref, bf16[128,768]{1,0:T(8,128)(2,1)S(1)} %collective-permute-done.13.b_ref, bf16[256,768]{1,0:T(8,128)(2,1)S(1)} %get-tuple-element.94.refs_0_.cast_ref, ...), custom_call_target="tpu_custom_call", output_to_operand_aliasing={{0}: (4, {}), {1}: (5, {})} | custom-call | flops 1000000000 | bytes 1000000 | tf_op jit(solution)/shard_map/gradient/pallas_call | solution.py:195
  36.4 0.7 %collective-permute-done.12.b_ref = bf16[128,768]{1,0:T(8,128)(2,1)S(1)} collective-permute-done((bf16[128,768]{1,0:T(8,128)(2,1)S(1)}, bf16[128,768]{1,0:T(8,128)(2,1)S(1)}, u32[]{:S(2)}, u32[]{:S(2)}) %collective-permute-start.12) | collective-permute-done | bytes 196640 | tf_op jit(solution)/shard_map/ppermute | solution.py:304
  37.1 1.9 %collective-permute-done.11.a_ref = bf16[832,128]{1,0:T(8,128)(2,1)S(1)} collective-permute-done((bf16[832,128]{1,0:T(8,128)(2,1)S(1)}, bf16[832,128]{1,0:T(8,128)(2,1)S(1)}, u32[]{:S(2)}, u32[]{:S(2)}) %collective-permute-start.11) | collective-permute-done | bytes 213024 | tf_op jit(solution)/shard_map/ppermute | solution.py:304
  39.0 0.7 %gradient.15.sum_ref = f32[256,768]{1,0:T(8,128)S(1)} custom-call(bf16[832,128]{1,0:T(8,128)(2,1)S(1)} %collective-permute-done.11.a_ref, bf16[128,768]{1,0:T(8,128)(2,1)S(1)} %collective-permute-done.12.b_ref, bf16[256,768]{1,0:T(8,128)(2,1)S(1)} %get-tuple-element.94.refs_0_.cast_ref, ...), custom_call_target="tpu_custom_call", output_to_operand_aliasing={{}: (3, {})} | custom-call | flops 10000000000 | bytes 1000000 | tf_op jit(solution)/shard_map/gradient/pallas_call | solution.py:195
  39.7 0.8 %collective-permute-done.15.a_ref = bf16[832,128]{1,0:T(8,128)(2,1)S(1)} collective-permute-done((bf16[832,128]{1,0:T(8,128)(2,1)S(1)}, bf16[832,128]{1,0:T(8,128)(2,1)S(1)}, u32[]{:S(2)}, u32[]{:S(2)}) %collective-permute-start.15) | collective-permute-done | bytes 213024 | tf_op jit(solution)/shard_map/ppermute | solution.py:304
  40.5 2.3 %finish.1 = (f32[256,768]{1,0:T(8,128)}, f32[256,768]{1,0:T(8,128)}, f32[256,768]{1,0:T(8,128)}) custom-call(bf16[832,128]{1,0:T(8,128)(2,1)S(1)} %collective-permute-done.15.a_ref, bf16[128,768]{1,0:T(8,128)(2,1)S(1)} %collective-permute-done.16.b_ref, bf16[256,768]{1,0:T(8,128)(2,1)S(1)} %get-tuple-element.94.refs_0_.cast_ref, ...), custom_call_target="tpu_custom_call" | custom-call | flops 10000000000 | bytes 1000000 | tf_op jit(solution)/shard_map/finish/pallas_call | solution.py:252
  (20 shorter events, 0.2 us)
Async XLA Ops:
  2.2 15.5 %collective-permute-start.6 = (bf16[256,768]{1,0:T(8,128)(2,1)S(1)}, bf16[256,768]{1,0:T(8,128)(2,1)S(1)}, u32[]{:S(2)}, u32[]{:S(2)}) collective-permute-start(bf16[256,768]{1,0:T(8,128)(2,1)S(1)} %get-tuple-element.94.refs_0_.cast_ref), channel_id=1, source_target_pairs={{0,1},{1,0},{2,3},{3,2},{4,5},{5,4},{6,7},{7,6},{8,9},{9,8},{10,11... | collective-permute-start | bytes 1179656 | tf_op jit(solution)/shard_map/ppermute | solution.py:304
  2.7 8.3 %collective-permute-start.1 = (bf16[128,768]{1,0:T(8,128)(2,1)S(1)}, bf16[128,768]{1,0:T(8,128)(2,1)S(1)}, u32[]{:S(2)}, u32[]{:S(2)}) collective-permute-start(bf16[128,768]{1,0:T(8,128)(2,1)S(1)} %get-tuple-element.93.b_ref), channel_id=1, source_target_pairs={{0,4},{1,5},{4,8},{5,9},{8,12},{9,13},{12,14},{13,15},{14,10},{15,... | collective-permute-start | bytes 589832 | tf_op jit(solution)/shard_map/ppermute | solution.py:304
  5.3 8.1 %collective-permute-start = (bf16[832,128]{1,0:T(8,128)(2,1)S(1)}, bf16[832,128]{1,0:T(8,128)(2,1)S(1)}, u32[]{:S(2)}, u32[]{:S(2)}) collective-permute-start(bf16[832,128]{1,0:T(8,128)(2,1)S(1)} %get-tuple-element.92.a_ref), channel_id=1, source_target_pairs={{4,0},{5,1},{8,4},{9,5},{12,8},{13,9},{14,12},{15,13},{10,14},{11,... | collective-permute-start | bytes 638984 | tf_op jit(solution)/shard_map/ppermute | solution.py:304
  5.4 10.2 %collective-permute-start.5 = (bf16[832,128]{1,0:T(8,128)(2,1)S(1)}, bf16[832,128]{1,0:T(8,128)(2,1)S(1)}, u32[]{:S(2)}, u32[]{:S(2)}) collective-permute-start(bf16[832,128]{1,0:T(8,128)(2,1)S(1)} %get-tuple-element.92.a_ref), channel_id=1, source_target_pairs={{0,4},{1,5},{4,8},{5,9},{8,12},{9,13},{12,14},{13,15},{14,10},{15,... | collective-permute-start | bytes 638984 | tf_op jit(solution)/shard_map/ppermute | solution.py:304
  7.4 10.3 %collective-permute-start.4 = (bf16[128,768]{1,0:T(8,128)(2,1)S(1)}, bf16[128,768]{1,0:T(8,128)(2,1)S(1)}, u32[]{:S(2)}, u32[]{:S(2)}) collective-permute-start(bf16[128,768]{1,0:T(8,128)(2,1)S(1)} %get-tuple-element.93.b_ref), channel_id=1, source_target_pairs={{4,0},{5,1},{8,4},{9,5},{12,8},{13,9},{14,12},{15,13},{10,14},{11,... | collective-permute-start | bytes 589832 | tf_op jit(solution)/shard_map/ppermute | solution.py:304
  11.0 8.8 %collective-permute-start.3 = (bf16[128,768]{1,0:T(8,128)(2,1)S(1)}, bf16[128,768]{1,0:T(8,128)(2,1)S(1)}, u32[]{:S(2)}, u32[]{:S(2)}) collective-permute-start(bf16[128,768]{1,0:T(8,128)(2,1)S(1)} %collective-permute-done.1.b_ref), channel_id=1, source_target_pairs={{0,4},{1,5},{4,8},{5,9},{8,12},{9,13},{12,14},{13,15},{14,10},{15,... | collective-permute-start | bytes 589832 | tf_op jit(solution)/shard_map/ppermute | solution.py:304
  13.4 9.4 %collective-permute-start.2 = (bf16[832,128]{1,0:T(8,128)(2,1)S(1)}, bf16[832,128]{1,0:T(8,128)(2,1)S(1)}, u32[]{:S(2)}, u32[]{:S(2)}) collective-permute-start(bf16[832,128]{1,0:T(8,128)(2,1)S(1)} %collective-permute-done.a_ref), channel_id=1, source_target_pairs={{4,0},{5,1},{8,4},{9,5},{12,8},{13,9},{14,12},{15,13},{10,14},{11,... | collective-permute-start | bytes 638984 | tf_op jit(solution)/shard_map/ppermute | solution.py:304
  15.6 8.8 %collective-permute-start.10 = (bf16[832,128]{1,0:T(8,128)(2,1)S(1)}, bf16[832,128]{1,0:T(8,128)(2,1)S(1)}, u32[]{:S(2)}, u32[]{:S(2)}) collective-permute-start(bf16[832,128]{1,0:T(8,128)(2,1)S(1)} %collective-permute-done.5.a_ref), channel_id=1, source_target_pairs={{0,4},{1,5},{4,8},{5,9},{8,12},{9,13},{12,14},{13,15},{14,10},{15,... | collective-permute-start | bytes 638984 | tf_op jit(solution)/shard_map/ppermute | solution.py:304
  17.6 9.8 %collective-permute-start.9 = (bf16[128,768]{1,0:T(8,128)(2,1)S(1)}, bf16[128,768]{1,0:T(8,128)(2,1)S(1)}, u32[]{:S(2)}, u32[]{:S(2)}) collective-permute-start(bf16[128,768]{1,0:T(8,128)(2,1)S(1)} %collective-permute-done.4.b_ref), channel_id=1, source_target_pairs={{4,0},{5,1},{8,4},{9,5},{12,8},{13,9},{14,12},{15,13},{10,14},{11,... | collective-permute-start | bytes 589832 | tf_op jit(solution)/shard_map/ppermute | solution.py:304
  19.8 8.8 %collective-permute-start.8 = (bf16[128,768]{1,0:T(8,128)(2,1)S(1)}, bf16[128,768]{1,0:T(8,128)(2,1)S(1)}, u32[]{:S(2)}, u32[]{:S(2)}) collective-permute-start(bf16[128,768]{1,0:T(8,128)(2,1)S(1)} %collective-permute-done.3.b_ref), channel_id=1, source_target_pairs={{0,4},{1,5},{4,8},{5,9},{8,12},{9,13},{12,14},{13,15},{14,10},{15,... | collective-permute-start | bytes 589832 | tf_op jit(solution)/shard_map/ppermute | solution.py:304
  22.8 8.8 %collective-permute-start.7 = (bf16[832,128]{1,0:T(8,128)(2,1)S(1)}, bf16[832,128]{1,0:T(8,128)(2,1)S(1)}, u32[]{:S(2)}, u32[]{:S(2)}) collective-permute-start(bf16[832,128]{1,0:T(8,128)(2,1)S(1)} %collective-permute-done.2.a_ref), channel_id=1, source_target_pairs={{4,0},{5,1},{8,4},{9,5},{12,8},{13,9},{14,12},{15,13},{10,14},{11,... | collective-permute-start | bytes 638984 | tf_op jit(solution)/shard_map/ppermute | solution.py:304
  24.4 8.8 %collective-permute-start.14 = (bf16[832,128]{1,0:T(8,128)(2,1)S(1)}, bf16[832,128]{1,0:T(8,128)(2,1)S(1)}, u32[]{:S(2)}, u32[]{:S(2)}) collective-permute-start(bf16[832,128]{1,0:T(8,128)(2,1)S(1)} %collective-permute-done.10.a_ref), channel_id=1, source_target_pairs={{0,4},{1,5},{4,8},{5,9},{8,12},{9,13},{12,14},{13,15},{14,10},{15,... | collective-permute-start | bytes 638984 | tf_op jit(solution)/shard_map/ppermute | solution.py:304
  27.4 7.9 %collective-permute-start.13 = (bf16[128,768]{1,0:T(8,128)(2,1)S(1)}, bf16[128,768]{1,0:T(8,128)(2,1)S(1)}, u32[]{:S(2)}, u32[]{:S(2)}) collective-permute-start(bf16[128,768]{1,0:T(8,128)(2,1)S(1)} %collective-permute-done.9.b_ref), channel_id=1, source_target_pairs={{4,0},{5,1},{8,4},{9,5},{12,8},{13,9},{14,12},{15,13},{10,14},{11,... | collective-permute-start | bytes 589832 | tf_op jit(solution)/shard_map/ppermute | solution.py:304
  28.6 8.5 %collective-permute-start.12 = (bf16[128,768]{1,0:T(8,128)(2,1)S(1)}, bf16[128,768]{1,0:T(8,128)(2,1)S(1)}, u32[]{:S(2)}, u32[]{:S(2)}) collective-permute-start(bf16[128,768]{1,0:T(8,128)(2,1)S(1)} %collective-permute-done.8.b_ref), channel_id=1, source_target_pairs={{0,4},{1,5},{4,8},{5,9},{8,12},{9,13},{12,14},{13,15},{14,10},{15,... | collective-permute-start | bytes 589832 | tf_op jit(solution)/shard_map/ppermute | solution.py:304
  31.6 7.4 %collective-permute-start.11 = (bf16[832,128]{1,0:T(8,128)(2,1)S(1)}, bf16[832,128]{1,0:T(8,128)(2,1)S(1)}, u32[]{:S(2)}, u32[]{:S(2)}) collective-permute-start(bf16[832,128]{1,0:T(8,128)(2,1)S(1)} %collective-permute-done.7.a_ref), channel_id=1, source_target_pairs={{4,0},{5,1},{8,4},{9,5},{12,8},{13,9},{14,12},{15,13},{10,14},{11,... | collective-permute-start | bytes 638984 | tf_op jit(solution)/shard_map/ppermute | solution.py:304
  36.3 4.1 %collective-permute-start.17 = (f32[256,768]{1,0:T(8,128)S(1)}, f32[256,768]{1,0:T(8,128)S(1)}, u32[]{:S(2)}, u32[]{:S(2)}) collective-permute-start(f32[256,768]{1,0:T(8,128)S(1)} %get-tuple-element.152), channel_id=1, source_target_pairs={{0,1},{1,0},{2,3},{3,2},{4,5},{5,4},{6,7},{7,6},{8,9},{9,8},{10,11... | collective-permute-start | bytes 2359304 | tf_op jit(solution)/shard_map/ppermute | solution.py:304
  37.1 3.3 %copy-start = (f32[256,768]{1,0:T(8,128)S(1)}, f32[256,768]{1,0:T(8,128)}, u32[]{:S(2)}) copy-start(f32[256,768]{1,0:T(8,128)} %weights_ref.1) | copy-start | bytes 2359300
  37.1 3.3 %copy-start.1 = (f32[256,768]{1,0:T(8,128)S(1)}, f32[256,768]{1,0:T(8,128)}, u32[]{:S(2)}) copy-start(f32[256,768]{1,0:T(8,128)} %first_ref.1) | copy-start | bytes 2359300
  37.1 3.3 %copy-start.2 = (f32[256,768]{1,0:T(8,128)S(1)}, f32[256,768]{1,0:T(8,128)}, u32[]{:S(2)}) copy-start(f32[256,768]{1,0:T(8,128)} %second_ref.1) | copy-start | bytes 2359300
  37.1 2.5 %collective-permute-start.16 = (bf16[128,768]{1,0:T(8,128)(2,1)S(1)}, bf16[128,768]{1,0:T(8,128)(2,1)S(1)}, u32[]{:S(2)}, u32[]{:S(2)}) collective-permute-start(bf16[128,768]{1,0:T(8,128)(2,1)S(1)} %collective-permute-done.12.b_ref), channel_id=1, source_target_pairs={{0,1},{1,0},{2,3},{3,2},{4,5},{5,4},{6,7},{7,6},{8,9},{9,8},{10,11... | collective-permute-start | bytes 589832 | tf_op jit(solution)/shard_map/ppermute | solution.py:304
  39.0 1.5 %collective-permute-start.15 = (bf16[832,128]{1,0:T(8,128)(2,1)S(1)}, bf16[832,128]{1,0:T(8,128)(2,1)S(1)}, u32[]{:S(2)}, u32[]{:S(2)}) collective-permute-start(bf16[832,128]{1,0:T(8,128)(2,1)S(1)} %collective-permute-done.11.a_ref), channel_id=1, source_target_pairs={{0,1},{1,0},{2,3},{3,2},{4,5},{5,4},{6,7},{7,6},{8,9},{9,8},{10,11... | collective-permute-start | bytes 638984 | tf_op jit(solution)/shard_map/ppermute | solution.py:304

commit v14 on v12

--- a/solution.py
+++ b/solution.py
@@ -282,8 +282,10 @@
     path = list(range(0, blocks // 2, across))
     if across == 2:
         path += list(range(1, blocks // 2, 2))[::-1]
-    steps = zip(path, path[1:] + path[:1])
-    return [(2 * here + core, 2 * there + core) for here, there in steps for core in range(2)]
+    pairs = []
+    for here, there in zip(path, path[1:] + path[:1]):
+        pairs += [(2 * here, 2 * there), (2 * there + 1, 2 * here + 1)]
+    return pairs
 
 
 together = lax.optimization_barrier

time: 42.1 us -> 40.8 us (0.969)
  waiting for transfers between devices: 12 us -> 10.1 us
  starting transfers between devices: 16.5 us -> 17.2 us
    ppermute x18, waiting for transfers between devices: 12 us -> 10.1 us  [send(): return lax.ppermute(value, 'blk', pairs)]
    ppermute x18, starting transfers between devices: 16.5 us -> 17.2 us  [send(): return lax.ppermute(value, 'blk', pairs)]
  transfers between devices with their start and end apart: 18 -> 18, of which waited for: 8 -> 12; matrix products, arithmetic and copies ran while one was open for 0% -> 0% of each run, Pallas kernels for 18% -> 19%
where the time goes in v14:
time: 40.8 us; the launch traced here: 40.6 us
  starting transfers between devices  17.2 us (42%)
  Pallas kernels  11.4 us (28%)
  waiting for transfers between devices  10.1 us (25%)
  local copies, waits for them, and re-layouts  1.14 us (3%)
  between operations  0.78 us (2%)
    ppermute x18, starting transfers between devices, send(): return lax.ppermute(value, 'blk', pairs)  17.2 us
    ppermute x18, waiting for transfers between devices, send(): return lax.ppermute(value, 'blk', pairs)  10.1 us
    pallas_call x8, Pallas kernels, add_gradient(): pl.pallas_call(functools.partial(gradient_kernel, bits, owners, not sums)...  7.69 us
    pallas_call x1, Pallas kernels, finish(): pl.pallas_call(functools.partial(finish_kernel, bits), in_specs=[pl.Block...  2.35 us
    pallas_call x1, Pallas kernels, prepare(): pl.pallas_call(functools.partial(prepare_kernel, (lines - 1).bit_length()...  1.31 us
    unnamed x8, local copies, waits for them, and re-layouts  1.14 us
  transfers between devices with their start and end apart: 18, of which 12 were waited for; matrix products, arithmetic and copies ran while one was open for 0% of the time, Pallas kernels for 19%

profile of v14, /device:TPU:0, one launch (start us, length us, event | category | flops | bytes accessed | tf_op | source)
XLA Modules:
  0.0 40.6 jit_solution(6395182453526803060)
XLA Ops:
  0.6 1.3 %prepare.1 = (bf16[832,128]{1,0:T(8,128)(2,1)S(1)}, bf16[128,768]{1,0:T(8,128)(2,1)S(1)}) custom-call(s32[32,256]{1,0:T(8,128)} %bitcast.3, s32[1,256]{1,0:T(1,128)} %bitcast.5, s32[32,128]{1,0:T(8,128)} %bitcast.4, bf16[256,768]{1,0:T(8,128)(2,1)} %docs_hbm.1), custom_call_target="tpu_custom_call" | custom-call | tf_op jit(solution)/shard_map/prepare/pallas_call | solution.py:110
  1.9 3.1 %collective-permute-start.1 = (bf16[128,768]{1,0:T(8,128)(2,1)S(1)}, bf16[128,768]{1,0:T(8,128)(2,1)S(1)}, u32[]{:S(2)}, u32[]{:S(2)}) collective-permute-start(bf16[128,768]{1,0:T(8,128)(2,1)S(1)} %get-tuple-element.112.b_ref), channel_id=1, source_target_pairs={{0,4},{5,1},{4,8},{9,5},{8,12},{13,9},{12,14},{15,13},{14,10},{11,... | collective-permute-start | bytes 589832 | tf_op jit(solution)/shard_map/ppermute | solution.py:313
  5.0 2.0 %collective-permute-start.5 = (bf16[832,128]{1,0:T(8,128)(2,1)S(1)}, bf16[832,128]{1,0:T(8,128)(2,1)S(1)}, u32[]{:S(2)}, u32[]{:S(2)}) collective-permute-start(bf16[832,128]{1,0:T(8,128)(2,1)S(1)} %get-tuple-element.111.a_ref), channel_id=1, source_target_pairs={{0,4},{5,1},{4,8},{9,5},{8,12},{13,9},{12,14},{15,13},{14,10},{11,... | collective-permute-start | bytes 638984 | tf_op jit(solution)/shard_map/ppermute | solution.py:313
  7.0 1.1 %copy-done = f32[256,768]{1,0:T(8,128)S(1)} copy-done((f32[256,768]{1,0:T(8,128)S(1)}, f32[256,768]{1,0:T(8,128)}, u32[]{:S(2)}) %copy-start) | copy-done | bytes 786456
  8.3 0.5 %collective-permute-start.4 = (bf16[128,768]{1,0:T(8,128)(2,1)S(1)}, bf16[128,768]{1,0:T(8,128)(2,1)S(1)}, u32[]{:S(2)}, u32[]{:S(2)}) collective-permute-start(bf16[128,768]{1,0:T(8,128)(2,1)S(1)} %get-tuple-element.112.b_ref), channel_id=1, source_target_pairs={{4,0},{1,5},{8,4},{5,9},{12,8},{9,13},{14,12},{13,15},{10,14},{15,... | collective-permute-start | bytes 589832 | tf_op jit(solution)/shard_map/ppermute | solution.py:313
  8.8 1.4 %collective-permute-done.1.b_ref = bf16[128,768]{1,0:T(8,128)(2,1)S(1)} collective-permute-done((bf16[128,768]{1,0:T(8,128)(2,1)S(1)}, bf16[128,768]{1,0:T(8,128)(2,1)S(1)}, u32[]{:S(2)}, u32[]{:S(2)}) %collective-permute-start.1) | collective-permute-done | bytes 196640 | tf_op jit(solution)/shard_map/ppermute | solution.py:313
  10.2 1.7 %collective-permute-start.3 = (bf16[128,768]{1,0:T(8,128)(2,1)S(1)}, bf16[128,768]{1,0:T(8,128)(2,1)S(1)}, u32[]{:S(2)}, u32[]{:S(2)}) collective-permute-start(bf16[128,768]{1,0:T(8,128)(2,1)S(1)} %collective-permute-done.1.b_ref), channel_id=1, source_target_pairs={{0,4},{5,1},{4,8},{9,5},{8,12},{13,9},{12,14},{15,13},{14,10},{11,... | collective-permute-start | bytes 589832 | tf_op jit(solution)/shard_map/ppermute | solution.py:313
  12.4 0.8 %collective-permute-start.2 = (bf16[832,128]{1,0:T(8,128)(2,1)S(1)}, bf16[832,128]{1,0:T(8,128)(2,1)S(1)}, u32[]{:S(2)}, u32[]{:S(2)}) collective-permute-start(bf16[832,128]{1,0:T(8,128)(2,1)S(1)} %collective-permute-done.a_ref), channel_id=1, source_target_pairs={{4,0},{1,5},{8,4},{5,9},{12,8},{9,13},{14,12},{13,15},{10,14},{15,... | collective-permute-start | bytes 638984 | tf_op jit(solution)/shard_map/ppermute | solution.py:313
  13.2 1.6 %collective-permute-done.5.a_ref = bf16[832,128]{1,0:T(8,128)(2,1)S(1)} collective-permute-done((bf16[832,128]{1,0:T(8,128)(2,1)S(1)}, bf16[832,128]{1,0:T(8,128)(2,1)S(1)}, u32[]{:S(2)}, u32[]{:S(2)}) %collective-permute-start.5) | collective-permute-done | bytes 213024 | tf_op jit(solution)/shard_map/ppermute | solution.py:313
  14.7 0.6 %collective-permute-start.9 = (bf16[832,128]{1,0:T(8,128)(2,1)S(1)}, bf16[832,128]{1,0:T(8,128)(2,1)S(1)}, u32[]{:S(2)}, u32[]{:S(2)}) collective-permute-start(bf16[832,128]{1,0:T(8,128)(2,1)S(1)} %collective-permute-done.5.a_ref), channel_id=1, source_target_pairs={{0,4},{5,1},{4,8},{9,5},{8,12},{13,9},{12,14},{15,13},{14,10},{11,... | collective-permute-start | bytes 638984 | tf_op jit(solution)/shard_map/ppermute | solution.py:313
  15.3 0.9 %collective-permute-done.4.b_ref = bf16[128,768]{1,0:T(8,128)(2,1)S(1)} collective-permute-done((bf16[128,768]{1,0:T(8,128)(2,1)S(1)}, bf16[128,768]{1,0:T(8,128)(2,1)S(1)}, u32[]{:S(2)}, u32[]{:S(2)}) %collective-permute-start.4) | collective-permute-done | bytes 196640 | tf_op jit(solution)/shard_map/ppermute | solution.py:313
  16.2 1.2 %collective-permute-start.8 = (bf16[128,768]{1,0:T(8,128)(2,1)S(1)}, bf16[128,768]{1,0:T(8,128)(2,1)S(1)}, u32[]{:S(2)}, u32[]{:S(2)}) collective-permute-start(bf16[128,768]{1,0:T(8,128)(2,1)S(1)} %collective-permute-done.4.b_ref), channel_id=1, source_target_pairs={{4,0},{1,5},{8,4},{5,9},{12,8},{9,13},{14,12},{13,15},{10,14},{15,... | collective-permute-start | bytes 589832 | tf_op jit(solution)/shard_map/ppermute | solution.py:313
  17.4 1.6 %collective-permute-done.3.b_ref = bf16[128,768]{1,0:T(8,128)(2,1)S(1)} collective-permute-done((bf16[128,768]{1,0:T(8,128)(2,1)S(1)}, bf16[128,768]{1,0:T(8,128)(2,1)S(1)}, u32[]{:S(2)}, u32[]{:S(2)}) %collective-permute-start.3) | collective-permute-done | bytes 196640 | tf_op jit(solution)/shard_map/ppermute | solution.py:313
  18.9 0.8 %collective-permute-start.7 = (bf16[128,768]{1,0:T(8,128)(2,1)S(1)}, bf16[128,768]{1,0:T(8,128)(2,1)S(1)}, u32[]{:S(2)}, u32[]{:S(2)}) collective-permute-start(bf16[128,768]{1,0:T(8,128)(2,1)S(1)} %collective-permute-done.3.b_ref), channel_id=1, source_target_pairs={{0,4},{5,1},{4,8},{9,5},{8,12},{13,9},{12,14},{15,13},{14,10},{11,... | collective-permute-start | bytes 589832 | tf_op jit(solution)/shard_map/ppermute | solution.py:313
  19.7 1.0 %collective-permute-done.2.a_ref = bf16[832,128]{1,0:T(8,128)(2,1)S(1)} collective-permute-done((bf16[832,128]{1,0:T(8,128)(2,1)S(1)}, bf16[832,128]{1,0:T(8,128)(2,1)S(1)}, u32[]{:S(2)}, u32[]{:S(2)}) %collective-permute-start.2) | collective-permute-done | bytes 213024 | tf_op jit(solution)/shard_map/ppermute | solution.py:313
  20.8 1.2 %collective-permute-start.6 = (bf16[832,128]{1,0:T(8,128)(2,1)S(1)}, bf16[832,128]{1,0:T(8,128)(2,1)S(1)}, u32[]{:S(2)}, u32[]{:S(2)}) collective-permute-start(bf16[832,128]{1,0:T(8,128)(2,1)S(1)} %collective-permute-done.2.a_ref), channel_id=1, source_target_pairs={{4,0},{1,5},{8,4},{5,9},{12,8},{9,13},{14,12},{13,15},{10,14},{15,... | collective-permute-start | bytes 638984 | tf_op jit(solution)/shard_map/ppermute | solution.py:313
  22.0 1.0 %gradient.8 = (f32[256,768]{1,0:T(8,128)S(1)}, f32[256,768]{1,0:T(8,128)S(1)}) custom-call(bf16[832,128]{1,0:T(8,128)(2,1)S(1)} %get-tuple-element.111.a_ref, bf16[128,768]{1,0:T(8,128)(2,1)S(1)} %get-tuple-element.112.b_ref, bf16[256,768]{1,0:T(8,128)(2,1)S(1)} %cast.1.refs_0_.cast_ref, bf16[256,768]{1,0:T(8,128)(2,1)S(1)} %collective-permute-done.10.refs_1_), custom_call_target="tpu_custom_call" | custom-call | flops 200000000 | bytes 1000000 | tf_op jit(solution)/shard_map/gradient/pallas_call | solution.py:202
  22.9 0.6 %collective-permute-done.9.a_ref = bf16[832,128]{1,0:T(8,128)(2,1)S(1)} collective-permute-done((bf16[832,128]{1,0:T(8,128)(2,1)S(1)}, bf16[832,128]{1,0:T(8,128)(2,1)S(1)}, u32[]{:S(2)}, u32[]{:S(2)}) %collective-permute-start.9) | collective-permute-done | bytes 213024 | tf_op jit(solution)/shard_map/ppermute | solution.py:313
  23.5 0.8 %collective-permute-start.14 = (bf16[832,128]{1,0:T(8,128)(2,1)S(1)}, bf16[832,128]{1,0:T(8,128)(2,1)S(1)}, u32[]{:S(2)}, u32[]{:S(2)}) collective-permute-start(bf16[832,128]{1,0:T(8,128)(2,1)S(1)} %collective-permute-done.9.a_ref), channel_id=1, source_target_pairs={{0,4},{5,1},{4,8},{9,5},{8,12},{13,9},{12,14},{15,13},{14,10},{11,... | collective-permute-start | bytes 638984 | tf_op jit(solution)/shard_map/ppermute | solution.py:313
  24.3 1.0 %gradient.9 = (f32[256,768]{1,0:T(8,128)S(1)}, f32[256,768]{1,0:T(8,128)S(1)}) custom-call(bf16[832,128]{1,0:T(8,128)(2,1)S(1)} %collective-permute-done.5.a_ref, bf16[128,768]{1,0:T(8,128)(2,1)S(1)} %collective-permute-done.1.b_ref, bf16[256,768]{1,0:T(8,128)(2,1)S(1)} %cast.1.refs_0_.cast_ref, ...), custom_call_target="tpu_custom_call", output_to_operand_aliasing={{0}: (4, {}), {1}: (5, {})} | custom-call | flops 200000000 | bytes 1000000 | tf_op jit(solution)/shard_map/gradient/pallas_call | solution.py:202
  25.3 1.7 %collective-permute-start.13 = (bf16[128,768]{1,0:T(8,128)(2,1)S(1)}, bf16[128,768]{1,0:T(8,128)(2,1)S(1)}, u32[]{:S(2)}, u32[]{:S(2)}) collective-permute-start(bf16[128,768]{1,0:T(8,128)(2,1)S(1)} %collective-permute-done.8.b_ref), channel_id=1, source_target_pairs={{4,0},{1,5},{8,4},{5,9},{12,8},{9,13},{14,12},{13,15},{10,14},{15,... | collective-permute-start | bytes 589832 | tf_op jit(solution)/shard_map/ppermute | solution.py:313
  27.0 1.0 %gradient.10 = (f32[256,768]{1,0:T(8,128)S(1)}, f32[256,768]{1,0:T(8,128)S(1)}) custom-call(bf16[832,128]{1,0:T(8,128)(2,1)S(1)} %collective-permute-done.a_ref, bf16[128,768]{1,0:T(8,128)(2,1)S(1)} %collective-permute-done.4.b_ref, bf16[256,768]{1,0:T(8,128)(2,1)S(1)} %cast.1.refs_0_.cast_ref, ...), custom_call_target="tpu_custom_call", output_to_operand_aliasing={{0}: (4, {}), {1}: (5, {})} | custom-call | flops 200000000 | bytes 1000000 | tf_op jit(solution)/shard_map/gradient/pallas_call | solution.py:202
  28.0 0.5 %collective-permute-start.12 = (bf16[128,768]{1,0:T(8,128)(2,1)S(1)}, bf16[128,768]{1,0:T(8,128)(2,1)S(1)}, u32[]{:S(2)}, u32[]{:S(2)}) collective-permute-start(bf16[128,768]{1,0:T(8,128)(2,1)S(1)} %collective-permute-done.7.b_ref), channel_id=1, source_target_pairs={{0,4},{5,1},{4,8},{9,5},{8,12},{13,9},{12,14},{15,13},{14,10},{11,... | collective-permute-start | bytes 589832 | tf_op jit(solution)/shard_map/ppermute | solution.py:313
  28.5 1.0 %gradient.11 = (f32[256,768]{1,0:T(8,128)S(1)}, f32[256,768]{1,0:T(8,128)S(1)}) custom-call(bf16[832,128]{1,0:T(8,128)(2,1)S(1)} %collective-permute-done.9.a_ref, bf16[128,768]{1,0:T(8,128)(2,1)S(1)} %collective-permute-done.3.b_ref, bf16[256,768]{1,0:T(8,128)(2,1)S(1)} %cast.1.refs_0_.cast_ref, ...), custom_call_target="tpu_custom_call", output_to_operand_aliasing={{0}: (4, {}), {1}: (5, {})} | custom-call | flops 1000000000 | bytes 1000000 | tf_op jit(solution)/shard_map/gradient/pallas_call | solution.py:202
  29.5 1.7 %collective-permute-start.11 = (bf16[832,128]{1,0:T(8,128)(2,1)S(1)}, bf16[832,128]{1,0:T(8,128)(2,1)S(1)}, u32[]{:S(2)}, u32[]{:S(2)}) collective-permute-start(bf16[832,128]{1,0:T(8,128)(2,1)S(1)} %collective-permute-done.6.a_ref), channel_id=1, source_target_pairs={{4,0},{1,5},{8,4},{5,9},{12,8},{9,13},{14,12},{13,15},{10,14},{15,... | collective-permute-start | bytes 638984 | tf_op jit(solution)/shard_map/ppermute | solution.py:313
  31.2 1.0 %gradient.12 = (f32[256,768]{1,0:T(8,128)S(1)}, f32[256,768]{1,0:T(8,128)S(1)}) custom-call(bf16[832,128]{1,0:T(8,128)(2,1)S(1)} %collective-permute-done.2.a_ref, bf16[128,768]{1,0:T(8,128)(2,1)S(1)} %collective-permute-done.8.b_ref, bf16[256,768]{1,0:T(8,128)(2,1)S(1)} %cast.1.refs_0_.cast_ref, ...), custom_call_target="tpu_custom_call", output_to_operand_aliasing={{0}: (4, {}), {1}: (5, {})} | custom-call | flops 1000000000 | bytes 1000000 | tf_op jit(solution)/shard_map/gradient/pallas_call | solution.py:202
  32.3 1.0 %gradient.13 = (f32[256,768]{1,0:T(8,128)S(1)}, f32[256,768]{1,0:T(8,128)S(1)}) custom-call(bf16[832,128]{1,0:T(8,128)(2,1)S(1)} %collective-permute-done.14.a_ref, bf16[128,768]{1,0:T(8,128)(2,1)S(1)} %collective-permute-done.7.b_ref, bf16[256,768]{1,0:T(8,128)(2,1)S(1)} %cast.1.refs_0_.cast_ref, ...), custom_call_target="tpu_custom_call", output_to_operand_aliasing={{0}: (4, {}), {1}: (5, {})} | custom-call | flops 1000000000 | bytes 1000000 | tf_op jit(solution)/shard_map/gradient/pallas_call | solution.py:202
  33.8 1.0 %gradient.14 = (f32[256,768]{1,0:T(8,128)S(1)}, f32[256,768]{1,0:T(8,128)S(1)}) custom-call(bf16[832,128]{1,0:T(8,128)(2,1)S(1)} %collective-permute-done.6.a_ref, bf16[128,768]{1,0:T(8,128)(2,1)S(1)} %collective-permute-done.13.b_ref, bf16[256,768]{1,0:T(8,128)(2,1)S(1)} %cast.1.refs_0_.cast_ref, ...), custom_call_target="tpu_custom_call", output_to_operand_aliasing={{0}: (4, {}), {1}: (5, {})} | custom-call | flops 1000000000 | bytes 1000000 | tf_op jit(solution)/shard_map/gradient/pallas_call | solution.py:202
  34.8 1.6 %collective-permute-done.12.b_ref = bf16[128,768]{1,0:T(8,128)(2,1)S(1)} collective-permute-done((bf16[128,768]{1,0:T(8,128)(2,1)S(1)}, bf16[128,768]{1,0:T(8,128)(2,1)S(1)}, u32[]{:S(2)}, u32[]{:S(2)}) %collective-permute-start.12) | collective-permute-done | bytes 196640 | tf_op jit(solution)/shard_map/ppermute | solution.py:313
  36.5 0.5 %collective-permute-start.15 = (bf16[832,128]{1,0:T(8,128)(2,1)S(1)}, bf16[832,128]{1,0:T(8,128)(2,1)S(1)}, u32[]{:S(2)}, u32[]{:S(2)}) collective-permute-start(bf16[832,128]{1,0:T(8,128)(2,1)S(1)} %collective-permute-done.11.a_ref), channel_id=1, source_target_pairs={{0,1},{1,0},{2,3},{3,2},{4,5},{5,4},{6,7},{7,6},{8,9},{9,8},{10,11... | collective-permute-start | bytes 638984 | tf_op jit(solution)/shard_map/ppermute | solution.py:313
  37.0 0.7 %gradient.15.sum_ref = f32[256,768]{1,0:T(8,128)S(1)} custom-call(bf16[832,128]{1,0:T(8,128)(2,1)S(1)} %collective-permute-done.11.a_ref, bf16[128,768]{1,0:T(8,128)(2,1)S(1)} %collective-permute-done.12.b_ref, bf16[256,768]{1,0:T(8,128)(2,1)S(1)} %cast.1.refs_0_.cast_ref, f32[256,768]{1,0:T(8,128)S(1)} %get-tuple-element.161.refs_1_), custom_call_target="tpu_custom_call", output_to_operand_aliasing={{}: (3, {})} | custom-call | flops 10000000000 | bytes 1000000 | tf_op jit(solution)/shard_map/gradient/pallas_call | solution.py:202
  38.3 2.3 %finish.1 = (f32[256,768]{1,0:T(8,128)}, f32[256,768]{1,0:T(8,128)}, f32[256,768]{1,0:T(8,128)}) custom-call(bf16[832,128]{1,0:T(8,128)(2,1)S(1)} %collective-permute-done.15.a_ref, bf16[128,768]{1,0:T(8,128)(2,1)S(1)} %collective-permute-done.16.b_ref, bf16[256,768]{1,0:T(8,128)(2,1)S(1)} %cast.1.refs_0_.cast_ref, f32[256,768]{1,0:T(8,128)S(1)} %gradient.15.sum_ref, ...), custom_call_target="tpu_custom_call" | custom-call | flops 10000000000 | bytes 1000000 | tf_op jit(solution)/shard_map/finish/pallas_call | solution.py:259
  (23 shorter events, 1.8 us)
Async XLA Ops:
  1.9 8.2 %collective-permute-start.1 = (bf16[128,768]{1,0:T(8,128)(2,1)S(1)}, bf16[128,768]{1,0:T(8,128)(2,1)S(1)}, u32[]{:S(2)}, u32[]{:S(2)}) collective-permute-start(bf16[128,768]{1,0:T(8,128)(2,1)S(1)} %get-tuple-element.112.b_ref), channel_id=1, source_target_pairs={{0,4},{5,1},{4,8},{9,5},{8,12},{13,9},{12,14},{15,13},{14,10},{11,... | collective-permute-start | bytes 589832 | tf_op jit(solution)/shard_map/ppermute | solution.py:313
  5.0 7.4 %collective-permute-start = (bf16[832,128]{1,0:T(8,128)(2,1)S(1)}, bf16[832,128]{1,0:T(8,128)(2,1)S(1)}, u32[]{:S(2)}, u32[]{:S(2)}) collective-permute-start(bf16[832,128]{1,0:T(8,128)(2,1)S(1)} %get-tuple-element.111.a_ref), channel_id=1, source_target_pairs={{4,0},{1,5},{8,4},{5,9},{12,8},{9,13},{14,12},{13,15},{10,14},{15,... | collective-permute-start | bytes 638984 | tf_op jit(solution)/shard_map/ppermute | solution.py:313
  5.0 9.7 %collective-permute-start.5 = (bf16[832,128]{1,0:T(8,128)(2,1)S(1)}, bf16[832,128]{1,0:T(8,128)(2,1)S(1)}, u32[]{:S(2)}, u32[]{:S(2)}) collective-permute-start(bf16[832,128]{1,0:T(8,128)(2,1)S(1)} %get-tuple-element.111.a_ref), channel_id=1, source_target_pairs={{0,4},{5,1},{4,8},{9,5},{8,12},{13,9},{12,14},{15,13},{14,10},{11,... | collective-permute-start | bytes 638984 | tf_op jit(solution)/shard_map/ppermute | solution.py:313
  7.0 1.1 %copy-start = (f32[256,768]{1,0:T(8,128)S(1)}, f32[256,768]{1,0:T(8,128)}, u32[]{:S(2)}) copy-start(f32[256,768]{1,0:T(8,128)} %weights_ref.3) | copy-start | bytes 2359300
  8.2 13.7 %collective-permute-start.10 = (bf16[256,768]{1,0:T(8,128)(2,1)S(1)}, bf16[256,768]{1,0:T(8,128)(2,1)S(1)}, u32[]{:S(2)}, u32[]{:S(2)}) collective-permute-start(bf16[256,768]{1,0:T(8,128)(2,1)S(1)} %cast.1.refs_0_.cast_ref), channel_id=1, source_target_pairs={{0,1},{1,0},{2,3},{3,2},{4,5},{5,4},{6,7},{7,6},{8,9},{9,8},{10,11... | collective-permute-start | bytes 1179656 | tf_op jit(solution)/shard_map/ppermute | solution.py:313
  8.3 7.9 %collective-permute-start.4 = (bf16[128,768]{1,0:T(8,128)(2,1)S(1)}, bf16[128,768]{1,0:T(8,128)(2,1)S(1)}, u32[]{:S(2)}, u32[]{:S(2)}) collective-permute-start(bf16[128,768]{1,0:T(8,128)(2,1)S(1)} %get-tuple-element.112.b_ref), channel_id=1, source_target_pairs={{4,0},{1,5},{8,4},{5,9},{12,8},{9,13},{14,12},{13,15},{10,14},{15,... | collective-permute-start | bytes 589832 | tf_op jit(solution)/shard_map/ppermute | solution.py:313
  10.2 8.8 %collective-permute-start.3 = (bf16[128,768]{1,0:T(8,128)(2,1)S(1)}, bf16[128,768]{1,0:T(8,128)(2,1)S(1)}, u32[]{:S(2)}, u32[]{:S(2)}) collective-permute-start(bf16[128,768]{1,0:T(8,128)(2,1)S(1)} %collective-permute-done.1.b_ref), channel_id=1, source_target_pairs={{0,4},{5,1},{4,8},{9,5},{8,12},{13,9},{12,14},{15,13},{14,10},{11,... | collective-permute-start | bytes 589832 | tf_op jit(solution)/shard_map/ppermute | solution.py:313
  12.4 8.4 %collective-permute-start.2 = (bf16[832,128]{1,0:T(8,128)(2,1)S(1)}, bf16[832,128]{1,0:T(8,128)(2,1)S(1)}, u32[]{:S(2)}, u32[]{:S(2)}) collective-permute-start(bf16[832,128]{1,0:T(8,128)(2,1)S(1)} %collective-permute-done.a_ref), channel_id=1, source_target_pairs={{4,0},{1,5},{8,4},{5,9},{12,8},{9,13},{14,12},{13,15},{10,14},{15,... | collective-permute-start | bytes 638984 | tf_op jit(solution)/shard_map/ppermute | solution.py:313
  14.7 8.8 %collective-permute-start.9 = (bf16[832,128]{1,0:T(8,128)(2,1)S(1)}, bf16[832,128]{1,0:T(8,128)(2,1)S(1)}, u32[]{:S(2)}, u32[]{:S(2)}) collective-permute-start(bf16[832,128]{1,0:T(8,128)(2,1)S(1)} %collective-permute-done.5.a_ref), channel_id=1, source_target_pairs={{0,4},{5,1},{4,8},{9,5},{8,12},{13,9},{12,14},{15,13},{14,10},{11,... | collective-permute-start | bytes 638984 | tf_op jit(solution)/shard_map/ppermute | solution.py:313
  16.2 9.1 %collective-permute-start.8 = (bf16[128,768]{1,0:T(8,128)(2,1)S(1)}, bf16[128,768]{1,0:T(8,128)(2,1)S(1)}, u32[]{:S(2)}, u32[]{:S(2)}) collective-permute-start(bf16[128,768]{1,0:T(8,128)(2,1)S(1)} %collective-permute-done.4.b_ref), channel_id=1, source_target_pairs={{4,0},{1,5},{8,4},{5,9},{12,8},{9,13},{14,12},{13,15},{10,14},{15,... | collective-permute-start | bytes 589832 | tf_op jit(solution)/shard_map/ppermute | solution.py:313
  18.9 9.1 %collective-permute-start.7 = (bf16[128,768]{1,0:T(8,128)(2,1)S(1)}, bf16[128,768]{1,0:T(8,128)(2,1)S(1)}, u32[]{:S(2)}, u32[]{:S(2)}) collective-permute-start(bf16[128,768]{1,0:T(8,128)(2,1)S(1)} %collective-permute-done.3.b_ref), channel_id=1, source_target_pairs={{0,4},{5,1},{4,8},{9,5},{8,12},{13,9},{12,14},{15,13},{14,10},{11,... | collective-permute-start | bytes 589832 | tf_op jit(solution)/shard_map/ppermute | solution.py:313
  20.8 8.8 %collective-permute-start.6 = (bf16[832,128]{1,0:T(8,128)(2,1)S(1)}, bf16[832,128]{1,0:T(8,128)(2,1)S(1)}, u32[]{:S(2)}, u32[]{:S(2)}) collective-permute-start(bf16[832,128]{1,0:T(8,128)(2,1)S(1)} %collective-permute-done.2.a_ref), channel_id=1, source_target_pairs={{4,0},{1,5},{8,4},{5,9},{12,8},{9,13},{14,12},{13,15},{10,14},{15,... | collective-permute-start | bytes 638984 | tf_op jit(solution)/shard_map/ppermute | solution.py:313
  23.5 8.8 %collective-permute-start.14 = (bf16[832,128]{1,0:T(8,128)(2,1)S(1)}, bf16[832,128]{1,0:T(8,128)(2,1)S(1)}, u32[]{:S(2)}, u32[]{:S(2)}) collective-permute-start(bf16[832,128]{1,0:T(8,128)(2,1)S(1)} %collective-permute-done.9.a_ref), channel_id=1, source_target_pairs={{0,4},{5,1},{4,8},{9,5},{8,12},{13,9},{12,14},{15,13},{14,10},{11,... | collective-permute-start | bytes 638984 | tf_op jit(solution)/shard_map/ppermute | solution.py:313
  25.3 8.4 %collective-permute-start.13 = (bf16[128,768]{1,0:T(8,128)(2,1)S(1)}, bf16[128,768]{1,0:T(8,128)(2,1)S(1)}, u32[]{:S(2)}, u32[]{:S(2)}) collective-permute-start(bf16[128,768]{1,0:T(8,128)(2,1)S(1)} %collective-permute-done.8.b_ref), channel_id=1, source_target_pairs={{4,0},{1,5},{8,4},{5,9},{12,8},{9,13},{14,12},{13,15},{10,14},{15,... | collective-permute-start | bytes 589832 | tf_op jit(solution)/shard_map/ppermute | solution.py:313
  28.0 8.5 %collective-permute-start.12 = (bf16[128,768]{1,0:T(8,128)(2,1)S(1)}, bf16[128,768]{1,0:T(8,128)(2,1)S(1)}, u32[]{:S(2)}, u32[]{:S(2)}) collective-permute-start(bf16[128,768]{1,0:T(8,128)(2,1)S(1)} %collective-permute-done.7.b_ref), channel_id=1, source_target_pairs={{0,4},{5,1},{4,8},{9,5},{8,12},{13,9},{12,14},{15,13},{14,10},{11,... | collective-permute-start | bytes 589832 | tf_op jit(solution)/shard_map/ppermute | solution.py:313
  29.5 7.0 %collective-permute-start.11 = (bf16[832,128]{1,0:T(8,128)(2,1)S(1)}, bf16[832,128]{1,0:T(8,128)(2,1)S(1)}, u32[]{:S(2)}, u32[]{:S(2)}) collective-permute-start(bf16[832,128]{1,0:T(8,128)(2,1)S(1)} %collective-permute-done.6.a_ref), channel_id=1, source_target_pairs={{4,0},{1,5},{8,4},{5,9},{12,8},{9,13},{14,12},{13,15},{10,14},{15,... | collective-permute-start | bytes 638984 | tf_op jit(solution)/shard_map/ppermute | solution.py:313
  34.8 3.5 %collective-permute-start.17 = (f32[256,768]{1,0:T(8,128)S(1)}, f32[256,768]{1,0:T(8,128)S(1)}, u32[]{:S(2)}, u32[]{:S(2)}) collective-permute-start(f32[256,768]{1,0:T(8,128)S(1)} %get-tuple-element.162), channel_id=1, source_target_pairs={{0,1},{1,0},{2,3},{3,2},{4,5},{5,4},{6,7},{7,6},{8,9},{9,8},{10,11... | collective-permute-start | bytes 2359304 | tf_op jit(solution)/shard_map/ppermute | solution.py:313
  36.5 1.8 %copy-start.1 = (f32[256,768]{1,0:T(8,128)S(1)}, f32[256,768]{1,0:T(8,128)}, u32[]{:S(2)}) copy-start(f32[256,768]{1,0:T(8,128)} %weights_ref.3) | copy-start | bytes 2359300
  36.5 1.8 %copy-start.2 = (f32[256,768]{1,0:T(8,128)S(1)}, f32[256,768]{1,0:T(8,128)}, u32[]{:S(2)}) copy-start(f32[256,768]{1,0:T(8,128)} %first_ref.1) | copy-start | bytes 2359300
  36.5 1.8 %copy-start.3 = (f32[256,768]{1,0:T(8,128)S(1)}, f32[256,768]{1,0:T(8,128)}, u32[]{:S(2)}) copy-start(f32[256,768]{1,0:T(8,128)} %second_ref.1) | copy-start | bytes 2359300
  36.5 1.4 %collective-permute-start.16 = (bf16[128,768]{1,0:T(8,128)(2,1)S(1)}, bf16[128,768]{1,0:T(8,128)(2,1)S(1)}, u32[]{:S(2)}, u32[]{:S(2)}) collective-permute-start(bf16[128,768]{1,0:T(8,128)(2,1)S(1)} %collective-permute-done.12.b_ref), channel_id=1, source_target_pairs={{0,1},{1,0},{2,3},{3,2},{4,5},{5,4},{6,7},{7,6},{8,9},{9,8},{10,11... | collective-permute-start | bytes 589832 | tf_op jit(solution)/shard_map/ppermute | solution.py:313
  36.5 1.7 %collective-permute-start.15 = (bf16[832,128]{1,0:T(8,128)(2,1)S(1)}, bf16[832,128]{1,0:T(8,128)(2,1)S(1)}, u32[]{:S(2)}, u32[]{:S(2)}) collective-permute-start(bf16[832,128]{1,0:T(8,128)(2,1)S(1)} %collective-permute-done.11.a_ref), channel_id=1, source_target_pairs={{0,1},{1,0},{2,3},{3,2},{4,5},{5,4},{6,7},{7,6},{8,9},{9,8},{10,11... | collective-permute-start | bytes 638984 | tf_op jit(solution)/shard_map/ppermute | solution.py:313

commit v15 on v14

--- a/solution.py
+++ b/solution.py
@@ -333,7 +333,11 @@
             if message in ("up_a", "down_b"):
                 side = message.split("_")[0]
                 waiting.append((came[side + "_a"], came[side + "_b"]))
-            if waiting and (last or (step > 1 and message != "up_b")):
+            if last:
+                number = 2 if message == "down_a" else 1
+            else:
+                number = 1 if step > 1 and message in ("down_a", "up_a") else 0
+            for _ in range(min(number, len(waiting))):
                 sums = work(LATE_FLOPS if last else FLOPS)
     while waiting:
         sums = work(LATE_FLOPS)

time: 40.8 us -> 40.8 us (level)
  transfers between devices with their start and end apart: 18 -> 18, of which waited for: 12 -> 11; matrix products, arithmetic and copies ran while one was open for 0% -> 0% of each run, Pallas kernels for 19% -> 19%
where the time goes in v15:
time: 40.8 us; the launch traced here: 40.6 us
  starting transfers between devices  17.5 us (43%)
  Pallas kernels  11.4 us (28%)
  waiting for transfers between devices  9.77 us (24%)
  local copies, waits for them, and re-layouts  1.14 us (3%)
  between operations  0.79 us (2%)
    ppermute x18, starting transfers between devices, send(): return lax.ppermute(value, 'blk', pairs)  17.5 us
    ppermute x18, waiting for transfers between devices, send(): return lax.ppermute(value, 'blk', pairs)  9.77 us
    pallas_call x8, Pallas kernels, add_gradient(): pl.pallas_call(functools.partial(gradient_kernel, bits, owners, not sums)...  7.7 us
    pallas_call x1, Pallas kernels, finish(): pl.pallas_call(functools.partial(finish_kernel, bits), in_specs=[pl.Block...  2.35 us
    pallas_call x1, Pallas kernels, prepare(): pl.pallas_call(functools.partial(prepare_kernel, (lines - 1).bit_length()...  1.31 us
    unnamed x8, local copies, waits for them, and re-layouts  1.14 us
  transfers between devices with their start and end apart: 18, of which 11 were waited for; matrix products, arithmetic and copies ran while one was open for 0% of the time, Pallas kernels for 19%

profile of v15, /device:TPU:0, one launch (start us, length us, event | category | flops | bytes accessed | tf_op | source)
XLA Modules:
  0.0 40.6 jit_solution(13972510760149604858)
XLA Ops:
  0.6 1.3 %prepare.1 = (bf16[832,128]{1,0:T(8,128)(2,1)S(1)}, bf16[128,768]{1,0:T(8,128)(2,1)S(1)}) custom-call(s32[32,256]{1,0:T(8,128)} %bitcast.3, s32[1,256]{1,0:T(1,128)} %bitcast.5, s32[32,128]{1,0:T(8,128)} %bitcast.4, bf16[256,768]{1,0:T(8,128)(2,1)} %docs_hbm.1), custom_call_target="tpu_custom_call" | custom-call | tf_op jit(solution)/shard_map/prepare/pallas_call | solution.py:110
  1.9 3.1 %collective-permute-start.1 = (bf16[128,768]{1,0:T(8,128)(2,1)S(1)}, bf16[128,768]{1,0:T(8,128)(2,1)S(1)}, u32[]{:S(2)}, u32[]{:S(2)}) collective-permute-start(bf16[128,768]{1,0:T(8,128)(2,1)S(1)} %get-tuple-element.116.b_ref), channel_id=1, source_target_pairs={{0,4},{5,1},{4,8},{9,5},{8,12},{13,9},{12,14},{15,13},{14,10},{11,... | collective-permute-start | bytes 589832 | tf_op jit(solution)/shard_map/ppermute | solution.py:313
  5.0 2.0 %collective-permute-start.5 = (bf16[832,128]{1,0:T(8,128)(2,1)S(1)}, bf16[832,128]{1,0:T(8,128)(2,1)S(1)}, u32[]{:S(2)}, u32[]{:S(2)}) collective-permute-start(bf16[832,128]{1,0:T(8,128)(2,1)S(1)} %get-tuple-element.115.a_ref), channel_id=1, source_target_pairs={{0,4},{5,1},{4,8},{9,5},{8,12},{13,9},{12,14},{15,13},{14,10},{11,... | collective-permute-start | bytes 638984 | tf_op jit(solution)/shard_map/ppermute | solution.py:313
  7.0 1.1 %copy-done = f32[256,768]{1,0:T(8,128)S(1)} copy-done((f32[256,768]{1,0:T(8,128)S(1)}, f32[256,768]{1,0:T(8,128)}, u32[]{:S(2)}) %copy-start) | copy-done | bytes 786456
  8.8 1.4 %collective-permute-done.1.b_ref = bf16[128,768]{1,0:T(8,128)(2,1)S(1)} collective-permute-done((bf16[128,768]{1,0:T(8,128)(2,1)S(1)}, bf16[128,768]{1,0:T(8,128)(2,1)S(1)}, u32[]{:S(2)}, u32[]{:S(2)}) %collective-permute-start.1) | collective-permute-done | bytes 196640 | tf_op jit(solution)/shard_map/ppermute | solution.py:313
  10.2 1.7 %collective-permute-start.3 = (bf16[128,768]{1,0:T(8,128)(2,1)S(1)}, bf16[128,768]{1,0:T(8,128)(2,1)S(1)}, u32[]{:S(2)}, u32[]{:S(2)}) collective-permute-start(bf16[128,768]{1,0:T(8,128)(2,1)S(1)} %collective-permute-done.1.b_ref), channel_id=1, source_target_pairs={{0,4},{5,1},{4,8},{9,5},{8,12},{13,9},{12,14},{15,13},{14,10},{11,... | collective-permute-start | bytes 589832 | tf_op jit(solution)/shard_map/ppermute | solution.py:313
  12.4 0.8 %collective-permute-start.2 = (bf16[832,128]{1,0:T(8,128)(2,1)S(1)}, bf16[832,128]{1,0:T(8,128)(2,1)S(1)}, u32[]{:S(2)}, u32[]{:S(2)}) collective-permute-start(bf16[832,128]{1,0:T(8,128)(2,1)S(1)} %collective-permute-done.a_ref), channel_id=1, source_target_pairs={{4,0},{1,5},{8,4},{5,9},{12,8},{9,13},{14,12},{13,15},{10,14},{15,... | collective-permute-start | bytes 638984 | tf_op jit(solution)/shard_map/ppermute | solution.py:313
  13.2 1.6 %collective-permute-done.5.a_ref = bf16[832,128]{1,0:T(8,128)(2,1)S(1)} collective-permute-done((bf16[832,128]{1,0:T(8,128)(2,1)S(1)}, bf16[832,128]{1,0:T(8,128)(2,1)S(1)}, u32[]{:S(2)}, u32[]{:S(2)}) %collective-permute-start.5) | collective-permute-done | bytes 213024 | tf_op jit(solution)/shard_map/ppermute | solution.py:313
  14.7 0.6 %collective-permute-start.9 = (bf16[832,128]{1,0:T(8,128)(2,1)S(1)}, bf16[832,128]{1,0:T(8,128)(2,1)S(1)}, u32[]{:S(2)}, u32[]{:S(2)}) collective-permute-start(bf16[832,128]{1,0:T(8,128)(2,1)S(1)} %collective-permute-done.5.a_ref), channel_id=1, source_target_pairs={{0,4},{5,1},{4,8},{9,5},{8,12},{13,9},{12,14},{15,13},{14,10},{11,... | collective-permute-start | bytes 638984 | tf_op jit(solution)/shard_map/ppermute | solution.py:313
  15.3 0.9 %collective-permute-done.4.b_ref = bf16[128,768]{1,0:T(8,128)(2,1)S(1)} collective-permute-done((bf16[128,768]{1,0:T(8,128)(2,1)S(1)}, bf16[128,768]{1,0:T(8,128)(2,1)S(1)}, u32[]{:S(2)}, u32[]{:S(2)}) %collective-permute-start.4) | collective-permute-done | bytes 196640 | tf_op jit(solution)/shard_map/ppermute | solution.py:313
  16.2 1.2 %collective-permute-start.8 = (bf16[128,768]{1,0:T(8,128)(2,1)S(1)}, bf16[128,768]{1,0:T(8,128)(2,1)S(1)}, u32[]{:S(2)}, u32[]{:S(2)}) collective-permute-start(bf16[128,768]{1,0:T(8,128)(2,1)S(1)} %collective-permute-done.4.b_ref), channel_id=1, source_target_pairs={{4,0},{1,5},{8,4},{5,9},{12,8},{9,13},{14,12},{13,15},{10,14},{15,... | collective-permute-start | bytes 589832 | tf_op jit(solution)/shard_map/ppermute | solution.py:313
  17.4 1.6 %collective-permute-done.3.b_ref = bf16[128,768]{1,0:T(8,128)(2,1)S(1)} collective-permute-done((bf16[128,768]{1,0:T(8,128)(2,1)S(1)}, bf16[128,768]{1,0:T(8,128)(2,1)S(1)}, u32[]{:S(2)}, u32[]{:S(2)}) %collective-permute-start.3) | collective-permute-done | bytes 196640 | tf_op jit(solution)/shard_map/ppermute | solution.py:313
  18.9 0.8 %collective-permute-start.7 = (bf16[128,768]{1,0:T(8,128)(2,1)S(1)}, bf16[128,768]{1,0:T(8,128)(2,1)S(1)}, u32[]{:S(2)}, u32[]{:S(2)}) collective-permute-start(bf16[128,768]{1,0:T(8,128)(2,1)S(1)} %collective-permute-done.3.b_ref), channel_id=1, source_target_pairs={{0,4},{5,1},{4,8},{9,5},{8,12},{13,9},{12,14},{15,13},{14,10},{11,... | collective-permute-start | bytes 589832 | tf_op jit(solution)/shard_map/ppermute | solution.py:313
  19.7 1.0 %collective-permute-done.2.a_ref = bf16[832,128]{1,0:T(8,128)(2,1)S(1)} collective-permute-done((bf16[832,128]{1,0:T(8,128)(2,1)S(1)}, bf16[832,128]{1,0:T(8,128)(2,1)S(1)}, u32[]{:S(2)}, u32[]{:S(2)}) %collective-permute-start.2) | collective-permute-done | bytes 213024 | tf_op jit(solution)/shard_map/ppermute | solution.py:313
  20.8 1.2 %collective-permute-start.6 = (bf16[832,128]{1,0:T(8,128)(2,1)S(1)}, bf16[832,128]{1,0:T(8,128)(2,1)S(1)}, u32[]{:S(2)}, u32[]{:S(2)}) collective-permute-start(bf16[832,128]{1,0:T(8,128)(2,1)S(1)} %collective-permute-done.2.a_ref), channel_id=1, source_target_pairs={{4,0},{1,5},{8,4},{5,9},{12,8},{9,13},{14,12},{13,15},{10,14},{15,... | collective-permute-start | bytes 638984 | tf_op jit(solution)/shard_map/ppermute | solution.py:313
  22.0 1.0 %gradient.8 = (f32[256,768]{1,0:T(8,128)S(1)}, f32[256,768]{1,0:T(8,128)S(1)}) custom-call(bf16[832,128]{1,0:T(8,128)(2,1)S(1)} %get-tuple-element.115.a_ref, bf16[128,768]{1,0:T(8,128)(2,1)S(1)} %get-tuple-element.116.b_ref, bf16[256,768]{1,0:T(8,128)(2,1)S(1)} %cast.1.refs_0_.cast_ref, bf16[256,768]{1,0:T(8,128)(2,1)S(1)} %collective-permute-done.10.refs_1_), custom_call_target="tpu_custom_call" | custom-call | flops 200000000 | bytes 1000000 | tf_op jit(solution)/shard_map/gradient/pallas_call | solution.py:202
  22.9 0.6 %collective-permute-done.9.a_ref = bf16[832,128]{1,0:T(8,128)(2,1)S(1)} collective-permute-done((bf16[832,128]{1,0:T(8,128)(2,1)S(1)}, bf16[832,128]{1,0:T(8,128)(2,1)S(1)}, u32[]{:S(2)}, u32[]{:S(2)}) %collective-permute-start.9) | collective-permute-done | bytes 213024 | tf_op jit(solution)/shard_map/ppermute | solution.py:313
  23.5 0.8 %collective-permute-start.14 = (bf16[832,128]{1,0:T(8,128)(2,1)S(1)}, bf16[832,128]{1,0:T(8,128)(2,1)S(1)}, u32[]{:S(2)}, u32[]{:S(2)}) collective-permute-start(bf16[832,128]{1,0:T(8,128)(2,1)S(1)} %collective-permute-done.9.a_ref), channel_id=1, source_target_pairs={{0,4},{5,1},{4,8},{9,5},{8,12},{13,9},{12,14},{15,13},{14,10},{11,... | collective-permute-start | bytes 638984 | tf_op jit(solution)/shard_map/ppermute | solution.py:313
  24.3 1.0 %gradient.9 = (f32[256,768]{1,0:T(8,128)S(1)}, f32[256,768]{1,0:T(8,128)S(1)}) custom-call(bf16[832,128]{1,0:T(8,128)(2,1)S(1)} %collective-permute-done.5.a_ref, bf16[128,768]{1,0:T(8,128)(2,1)S(1)} %collective-permute-done.1.b_ref, bf16[256,768]{1,0:T(8,128)(2,1)S(1)} %cast.1.refs_0_.cast_ref, ...), custom_call_target="tpu_custom_call", output_to_operand_aliasing={{0}: (4, {}), {1}: (5, {})} | custom-call | flops 200000000 | bytes 1000000 | tf_op jit(solution)/shard_map/gradient/pallas_call | solution.py:202
  25.3 1.7 %collective-permute-start.13 = (bf16[128,768]{1,0:T(8,128)(2,1)S(1)}, bf16[128,768]{1,0:T(8,128)(2,1)S(1)}, u32[]{:S(2)}, u32[]{:S(2)}) collective-permute-start(bf16[128,768]{1,0:T(8,128)(2,1)S(1)} %collective-permute-done.8.b_ref), channel_id=1, source_target_pairs={{4,0},{1,5},{8,4},{5,9},{12,8},{9,13},{14,12},{13,15},{10,14},{15,... | collective-permute-start | bytes 589832 | tf_op jit(solution)/shard_map/ppermute | solution.py:313
  27.0 0.7 %collective-permute-done.7.b_ref = bf16[128,768]{1,0:T(8,128)(2,1)S(1)} collective-permute-done((bf16[128,768]{1,0:T(8,128)(2,1)S(1)}, bf16[128,768]{1,0:T(8,128)(2,1)S(1)}, u32[]{:S(2)}, u32[]{:S(2)}) %collective-permute-start.7) | collective-permute-done | bytes 196640 | tf_op jit(solution)/shard_map/ppermute | solution.py:313
  27.7 0.8 %collective-permute-start.12 = (bf16[128,768]{1,0:T(8,128)(2,1)S(1)}, bf16[128,768]{1,0:T(8,128)(2,1)S(1)}, u32[]{:S(2)}, u32[]{:S(2)}) collective-permute-start(bf16[128,768]{1,0:T(8,128)(2,1)S(1)} %collective-permute-done.7.b_ref), channel_id=1, source_target_pairs={{0,4},{5,1},{4,8},{9,5},{8,12},{13,9},{12,14},{15,13},{14,10},{11,... | collective-permute-start | bytes 589832 | tf_op jit(solution)/shard_map/ppermute | solution.py:313
  28.5 1.0 %gradient.10 = (f32[256,768]{1,0:T(8,128)S(1)}, f32[256,768]{1,0:T(8,128)S(1)}) custom-call(bf16[832,128]{1,0:T(8,128)(2,1)S(1)} %collective-permute-done.a_ref, bf16[128,768]{1,0:T(8,128)(2,1)S(1)} %collective-permute-done.4.b_ref, bf16[256,768]{1,0:T(8,128)(2,1)S(1)} %cast.1.refs_0_.cast_ref, ...), custom_call_target="tpu_custom_call", output_to_operand_aliasing={{0}: (4, {}), {1}: (5, {})} | custom-call | flops 1000000000 | bytes 1000000 | tf_op jit(solution)/shard_map/gradient/pallas_call | solution.py:202
  29.5 1.7 %collective-permute-start.11 = (bf16[832,128]{1,0:T(8,128)(2,1)S(1)}, bf16[832,128]{1,0:T(8,128)(2,1)S(1)}, u32[]{:S(2)}, u32[]{:S(2)}) collective-permute-start(bf16[832,128]{1,0:T(8,128)(2,1)S(1)} %collective-permute-done.6.a_ref), channel_id=1, source_target_pairs={{4,0},{1,5},{8,4},{5,9},{12,8},{9,13},{14,12},{13,15},{10,14},{15,... | collective-permute-start | bytes 638984 | tf_op jit(solution)/shard_map/ppermute | solution.py:313
  31.2 1.0 %gradient.11 = (f32[256,768]{1,0:T(8,128)S(1)}, f32[256,768]{1,0:T(8,128)S(1)}) custom-call(bf16[832,128]{1,0:T(8,128)(2,1)S(1)} %collective-permute-done.9.a_ref, bf16[128,768]{1,0:T(8,128)(2,1)S(1)} %collective-permute-done.3.b_ref, bf16[256,768]{1,0:T(8,128)(2,1)S(1)} %cast.1.refs_0_.cast_ref, ...), custom_call_target="tpu_custom_call", output_to_operand_aliasing={{0}: (4, {}), {1}: (5, {})} | custom-call | flops 1000000000 | bytes 1000000 | tf_op jit(solution)/shard_map/gradient/pallas_call | solution.py:202
  32.2 1.0 %gradient.12 = (f32[256,768]{1,0:T(8,128)S(1)}, f32[256,768]{1,0:T(8,128)S(1)}) custom-call(bf16[832,128]{1,0:T(8,128)(2,1)S(1)} %collective-permute-done.2.a_ref, bf16[128,768]{1,0:T(8,128)(2,1)S(1)} %collective-permute-done.8.b_ref, bf16[256,768]{1,0:T(8,128)(2,1)S(1)} %cast.1.refs_0_.cast_ref, ...), custom_call_target="tpu_custom_call", output_to_operand_aliasing={{0}: (4, {}), {1}: (5, {})} | custom-call | flops 1000000000 | bytes 1000000 | tf_op jit(solution)/shard_map/gradient/pallas_call | solution.py:202
  33.3 1.0 %gradient.13 = (f32[256,768]{1,0:T(8,128)S(1)}, f32[256,768]{1,0:T(8,128)S(1)}) custom-call(bf16[832,128]{1,0:T(8,128)(2,1)S(1)} %collective-permute-done.14.a_ref, bf16[128,768]{1,0:T(8,128)(2,1)S(1)} %collective-permute-done.7.b_ref, bf16[256,768]{1,0:T(8,128)(2,1)S(1)} %cast.1.refs_0_.cast_ref, ...), custom_call_target="tpu_custom_call", output_to_operand_aliasing={{0}: (4, {}), {1}: (5, {})} | custom-call | flops 1000000000 | bytes 1000000 | tf_op jit(solution)/shard_map/gradient/pallas_call | solution.py:202
  34.3 1.0 %gradient.14 = (f32[256,768]{1,0:T(8,128)S(1)}, f32[256,768]{1,0:T(8,128)S(1)}) custom-call(bf16[832,128]{1,0:T(8,128)(2,1)S(1)} %collective-permute-done.6.a_ref, bf16[128,768]{1,0:T(8,128)(2,1)S(1)} %collective-permute-done.13.b_ref, bf16[256,768]{1,0:T(8,128)(2,1)S(1)} %cast.1.refs_0_.cast_ref, ...), custom_call_target="tpu_custom_call", output_to_operand_aliasing={{0}: (4, {}), {1}: (5, {})} | custom-call | flops 1000000000 | bytes 1000000 | tf_op jit(solution)/shard_map/gradient/pallas_call | solution.py:202
  35.4 1.1 %collective-permute-done.12.b_ref = bf16[128,768]{1,0:T(8,128)(2,1)S(1)} collective-permute-done((bf16[128,768]{1,0:T(8,128)(2,1)S(1)}, bf16[128,768]{1,0:T(8,128)(2,1)S(1)}, u32[]{:S(2)}, u32[]{:S(2)}) %collective-permute-start.12) | collective-permute-done | bytes 196640 | tf_op jit(solution)/shard_map/ppermute | solution.py:313
  36.5 0.5 %collective-permute-start.15 = (bf16[832,128]{1,0:T(8,128)(2,1)S(1)}, bf16[832,128]{1,0:T(8,128)(2,1)S(1)}, u32[]{:S(2)}, u32[]{:S(2)}) collective-permute-start(bf16[832,128]{1,0:T(8,128)(2,1)S(1)} %collective-permute-done.11.a_ref), channel_id=1, source_target_pairs={{0,1},{1,0},{2,3},{3,2},{4,5},{5,4},{6,7},{7,6},{8,9},{9,8},{10,11... | collective-permute-start | bytes 638984 | tf_op jit(solution)/shard_map/ppermute | solution.py:313
  37.0 0.7 %gradient.15.sum_ref = f32[256,768]{1,0:T(8,128)S(1)} custom-call(bf16[832,128]{1,0:T(8,128)(2,1)S(1)} %collective-permute-done.11.a_ref, bf16[128,768]{1,0:T(8,128)(2,1)S(1)} %collective-permute-done.12.b_ref, bf16[256,768]{1,0:T(8,128)(2,1)S(1)} %cast.1.refs_0_.cast_ref, f32[256,768]{1,0:T(8,128)S(1)} %get-tuple-element.169.refs_1_), custom_call_target="tpu_custom_call", output_to_operand_aliasing={{}: (3, {})} | custom-call | flops 10000000000 | bytes 1000000 | tf_op jit(solution)/shard_map/gradient/pallas_call | solution.py:202
  38.3 2.3 %finish.1 = (f32[256,768]{1,0:T(8,128)}, f32[256,768]{1,0:T(8,128)}, f32[256,768]{1,0:T(8,128)}) custom-call(bf16[832,128]{1,0:T(8,128)(2,1)S(1)} %collective-permute-done.15.a_ref, bf16[128,768]{1,0:T(8,128)(2,1)S(1)} %collective-permute-done.16.b_ref, bf16[256,768]{1,0:T(8,128)(2,1)S(1)} %cast.1.refs_0_.cast_ref, f32[256,768]{1,0:T(8,128)S(1)} %gradient.15.sum_ref, ...), custom_call_target="tpu_custom_call" | custom-call | flops 10000000000 | bytes 1000000 | tf_op jit(solution)/shard_map/finish/pallas_call | solution.py:259
  (23 shorter events, 1.8 us)
Async XLA Ops:
  1.9 8.2 %collective-permute-start.1 = (bf16[128,768]{1,0:T(8,128)(2,1)S(1)}, bf16[128,768]{1,0:T(8,128)(2,1)S(1)}, u32[]{:S(2)}, u32[]{:S(2)}) collective-permute-start(bf16[128,768]{1,0:T(8,128)(2,1)S(1)} %get-tuple-element.116.b_ref), channel_id=1, source_target_pairs={{0,4},{5,1},{4,8},{9,5},{8,12},{13,9},{12,14},{15,13},{14,10},{11,... | collective-permute-start | bytes 589832 | tf_op jit(solution)/shard_map/ppermute | solution.py:313
  5.0 7.4 %collective-permute-start = (bf16[832,128]{1,0:T(8,128)(2,1)S(1)}, bf16[832,128]{1,0:T(8,128)(2,1)S(1)}, u32[]{:S(2)}, u32[]{:S(2)}) collective-permute-start(bf16[832,128]{1,0:T(8,128)(2,1)S(1)} %get-tuple-element.115.a_ref), channel_id=1, source_target_pairs={{4,0},{1,5},{8,4},{5,9},{12,8},{9,13},{14,12},{13,15},{10,14},{15,... | collective-permute-start | bytes 638984 | tf_op jit(solution)/shard_map/ppermute | solution.py:313
  5.0 9.7 %collective-permute-start.5 = (bf16[832,128]{1,0:T(8,128)(2,1)S(1)}, bf16[832,128]{1,0:T(8,128)(2,1)S(1)}, u32[]{:S(2)}, u32[]{:S(2)}) collective-permute-start(bf16[832,128]{1,0:T(8,128)(2,1)S(1)} %get-tuple-element.115.a_ref), channel_id=1, source_target_pairs={{0,4},{5,1},{4,8},{9,5},{8,12},{13,9},{12,14},{15,13},{14,10},{11,... | collective-permute-start | bytes 638984 | tf_op jit(solution)/shard_map/ppermute | solution.py:313
  7.0 1.1 %copy-start = (f32[256,768]{1,0:T(8,128)S(1)}, f32[256,768]{1,0:T(8,128)}, u32[]{:S(2)}) copy-start(f32[256,768]{1,0:T(8,128)} %weights_ref.3) | copy-start | bytes 2359300
  8.2 13.7 %collective-permute-start.10 = (bf16[256,768]{1,0:T(8,128)(2,1)S(1)}, bf16[256,768]{1,0:T(8,128)(2,1)S(1)}, u32[]{:S(2)}, u32[]{:S(2)}) collective-permute-start(bf16[256,768]{1,0:T(8,128)(2,1)S(1)} %cast.1.refs_0_.cast_ref), channel_id=1, source_target_pairs={{0,1},{1,0},{2,3},{3,2},{4,5},{5,4},{6,7},{7,6},{8,9},{9,8},{10,11... | collective-permute-start | bytes 1179656 | tf_op jit(solution)/shard_map/ppermute | solution.py:313
  8.3 7.9 %collective-permute-start.4 = (bf16[128,768]{1,0:T(8,128)(2,1)S(1)}, bf16[128,768]{1,0:T(8,128)(2,1)S(1)}, u32[]{:S(2)}, u32[]{:S(2)}) collective-permute-start(bf16[128,768]{1,0:T(8,128)(2,1)S(1)} %get-tuple-element.116.b_ref), channel_id=1, source_target_pairs={{4,0},{1,5},{8,4},{5,9},{12,8},{9,13},{14,12},{13,15},{10,14},{15,... | collective-permute-start | bytes 589832 | tf_op jit(solution)/shard_map/ppermute | solution.py:313
  10.2 8.8 %collective-permute-start.3 = (bf16[128,768]{1,0:T(8,128)(2,1)S(1)}, bf16[128,768]{1,0:T(8,128)(2,1)S(1)}, u32[]{:S(2)}, u32[]{:S(2)}) collective-permute-start(bf16[128,768]{1,0:T(8,128)(2,1)S(1)} %collective-permute-done.1.b_ref), channel_id=1, source_target_pairs={{0,4},{5,1},{4,8},{9,5},{8,12},{13,9},{12,14},{15,13},{14,10},{11,... | collective-permute-start | bytes 589832 | tf_op jit(solution)/shard_map/ppermute | solution.py:313
  12.4 8.4 %collective-permute-start.2 = (bf16[832,128]{1,0:T(8,128)(2,1)S(1)}, bf16[832,128]{1,0:T(8,128)(2,1)S(1)}, u32[]{:S(2)}, u32[]{:S(2)}) collective-permute-start(bf16[832,128]{1,0:T(8,128)(2,1)S(1)} %collective-permute-done.a_ref), channel_id=1, source_target_pairs={{4,0},{1,5},{8,4},{5,9},{12,8},{9,13},{14,12},{13,15},{10,14},{15,... | collective-permute-start | bytes 638984 | tf_op jit(solution)/shard_map/ppermute | solution.py:313
  14.7 8.8 %collective-permute-start.9 = (bf16[832,128]{1,0:T(8,128)(2,1)S(1)}, bf16[832,128]{1,0:T(8,128)(2,1)S(1)}, u32[]{:S(2)}, u32[]{:S(2)}) collective-permute-start(bf16[832,128]{1,0:T(8,128)(2,1)S(1)} %collective-permute-done.5.a_ref), channel_id=1, source_target_pairs={{0,4},{5,1},{4,8},{9,5},{8,12},{13,9},{12,14},{15,13},{14,10},{11,... | collective-permute-start | bytes 638984 | tf_op jit(solution)/shard_map/ppermute | solution.py:313
  16.2 9.1 %collective-permute-start.8 = (bf16[128,768]{1,0:T(8,128)(2,1)S(1)}, bf16[128,768]{1,0:T(8,128)(2,1)S(1)}, u32[]{:S(2)}, u32[]{:S(2)}) collective-permute-start(bf16[128,768]{1,0:T(8,128)(2,1)S(1)} %collective-permute-done.4.b_ref), channel_id=1, source_target_pairs={{4,0},{1,5},{8,4},{5,9},{12,8},{9,13},{14,12},{13,15},{10,14},{15,... | collective-permute-start | bytes 589832 | tf_op jit(solution)/shard_map/ppermute | solution.py:313
  18.9 8.8 %collective-permute-start.7 = (bf16[128,768]{1,0:T(8,128)(2,1)S(1)}, bf16[128,768]{1,0:T(8,128)(2,1)S(1)}, u32[]{:S(2)}, u32[]{:S(2)}) collective-permute-start(bf16[128,768]{1,0:T(8,128)(2,1)S(1)} %collective-permute-done.3.b_ref), channel_id=1, source_target_pairs={{0,4},{5,1},{4,8},{9,5},{8,12},{13,9},{12,14},{15,13},{14,10},{11,... | collective-permute-start | bytes 589832 | tf_op jit(solution)/shard_map/ppermute | solution.py:313
  20.8 8.8 %collective-permute-start.6 = (bf16[832,128]{1,0:T(8,128)(2,1)S(1)}, bf16[832,128]{1,0:T(8,128)(2,1)S(1)}, u32[]{:S(2)}, u32[]{:S(2)}) collective-permute-start(bf16[832,128]{1,0:T(8,128)(2,1)S(1)} %collective-permute-done.2.a_ref), channel_id=1, source_target_pairs={{4,0},{1,5},{8,4},{5,9},{12,8},{9,13},{14,12},{13,15},{10,14},{15,... | collective-permute-start | bytes 638984 | tf_op jit(solution)/shard_map/ppermute | solution.py:313
  23.5 9.7 %collective-permute-start.14 = (bf16[832,128]{1,0:T(8,128)(2,1)S(1)}, bf16[832,128]{1,0:T(8,128)(2,1)S(1)}, u32[]{:S(2)}, u32[]{:S(2)}) collective-permute-start(bf16[832,128]{1,0:T(8,128)(2,1)S(1)} %collective-permute-done.9.a_ref), channel_id=1, source_target_pairs={{0,4},{5,1},{4,8},{9,5},{8,12},{13,9},{12,14},{15,13},{14,10},{11,... | collective-permute-start | bytes 638984 | tf_op jit(solution)/shard_map/ppermute | solution.py:313
  25.3 9.0 %collective-permute-start.13 = (bf16[128,768]{1,0:T(8,128)(2,1)S(1)}, bf16[128,768]{1,0:T(8,128)(2,1)S(1)}, u32[]{:S(2)}, u32[]{:S(2)}) collective-permute-start(bf16[128,768]{1,0:T(8,128)(2,1)S(1)} %collective-permute-done.8.b_ref), channel_id=1, source_target_pairs={{4,0},{1,5},{8,4},{5,9},{12,8},{9,13},{14,12},{13,15},{10,14},{15,... | collective-permute-start | bytes 589832 | tf_op jit(solution)/shard_map/ppermute | solution.py:313
  27.7 8.8 %collective-permute-start.12 = (bf16[128,768]{1,0:T(8,128)(2,1)S(1)}, bf16[128,768]{1,0:T(8,128)(2,1)S(1)}, u32[]{:S(2)}, u32[]{:S(2)}) collective-permute-start(bf16[128,768]{1,0:T(8,128)(2,1)S(1)} %collective-permute-done.7.b_ref), channel_id=1, source_target_pairs={{0,4},{5,1},{4,8},{9,5},{8,12},{13,9},{12,14},{15,13},{14,10},{11,... | collective-permute-start | bytes 589832 | tf_op jit(solution)/shard_map/ppermute | solution.py:313
  29.5 7.0 %collective-permute-start.11 = (bf16[832,128]{1,0:T(8,128)(2,1)S(1)}, bf16[832,128]{1,0:T(8,128)(2,1)S(1)}, u32[]{:S(2)}, u32[]{:S(2)}) collective-permute-start(bf16[832,128]{1,0:T(8,128)(2,1)S(1)} %collective-permute-done.6.a_ref), channel_id=1, source_target_pairs={{4,0},{1,5},{8,4},{5,9},{12,8},{9,13},{14,12},{13,15},{10,14},{15,... | collective-permute-start | bytes 638984 | tf_op jit(solution)/shard_map/ppermute | solution.py:313
  35.3 2.9 %collective-permute-start.17 = (f32[256,768]{1,0:T(8,128)S(1)}, f32[256,768]{1,0:T(8,128)S(1)}, u32[]{:S(2)}, u32[]{:S(2)}) collective-permute-start(f32[256,768]{1,0:T(8,128)S(1)} %get-tuple-element.170), channel_id=1, source_target_pairs={{0,1},{1,0},{2,3},{3,2},{4,5},{5,4},{6,7},{7,6},{8,9},{9,8},{10,11... | collective-permute-start | bytes 2359304 | tf_op jit(solution)/shard_map/ppermute | solution.py:313
  36.5 1.8 %copy-start.1 = (f32[256,768]{1,0:T(8,128)S(1)}, f32[256,768]{1,0:T(8,128)}, u32[]{:S(2)}) copy-start(f32[256,768]{1,0:T(8,128)} %weights_ref.3) | copy-start | bytes 2359300
  36.5 1.8 %copy-start.2 = (f32[256,768]{1,0:T(8,128)S(1)}, f32[256,768]{1,0:T(8,128)}, u32[]{:S(2)}) copy-start(f32[256,768]{1,0:T(8,128)} %first_ref.1) | copy-start | bytes 2359300
  36.5 1.8 %copy-start.3 = (f32[256,768]{1,0:T(8,128)S(1)}, f32[256,768]{1,0:T(8,128)}, u32[]{:S(2)}) copy-start(f32[256,768]{1,0:T(8,128)} %second_ref.1) | copy-start | bytes 2359300
  36.5 1.4 %collective-permute-start.16 = (bf16[128,768]{1,0:T(8,128)(2,1)S(1)}, bf16[128,768]{1,0:T(8,128)(2,1)S(1)}, u32[]{:S(2)}, u32[]{:S(2)}) collective-permute-start(bf16[128,768]{1,0:T(8,128)(2,1)S(1)} %collective-permute-done.12.b_ref), channel_id=1, source_target_pairs={{0,1},{1,0},{2,3},{3,2},{4,5},{5,4},{6,7},{7,6},{8,9},{9,8},{10,11... | collective-permute-start | bytes 589832 | tf_op jit(solution)/shard_map/ppermute | solution.py:313
  36.5 1.7 %collective-permute-start.15 = (bf16[832,128]{1,0:T(8,128)(2,1)S(1)}, bf16[832,128]{1,0:T(8,128)(2,1)S(1)}, u32[]{:S(2)}, u32[]{:S(2)}) collective-permute-start(bf16[832,128]{1,0:T(8,128)(2,1)S(1)} %collective-permute-done.11.a_ref), channel_id=1, source_target_pairs={{0,1},{1,0},{2,3},{3,2},{4,5},{5,4},{6,7},{7,6},{8,9},{9,8},{10,11... | collective-permute-start | bytes 638984 | tf_op jit(solution)/shard_map/ppermute | solution.py:313

commit v16 on v15

--- a/solution.py
+++ b/solution.py
@@ -39,16 +39,16 @@
     count_hbm,
     table_hbm,
     docs_hbm,
+    _,
     a_ref,
-    b_ref,
     ids_ref,
     count_ref,
     table_ref,
     done,
 ):
     slots, docs = ids_ref.shape
-    head = docs - b_ref.shape[0]
-    tiles = [pl.ds(start, LANES) for start in range(0, b_ref.shape[1], LANES)]
+    tiles = [pl.ds(start, LANES) for start in range(0, docs_hbm.shape[1], LANES)]
+    head = (a_ref.shape[0] - slots * (docs // LANES)) // len(tiles)
     fetches = [
         pltpu.make_async_copy(source, target, done.at[i])
         for i, (source, target) in enumerate(
@@ -56,7 +56,6 @@
                 (ids_hbm, ids_ref),
                 (table_hbm, table_ref),
                 (count_hbm, count_ref),
-                (docs_hbm.at[pl.ds(head, docs - head)], b_ref),
                 *(
                     (docs_hbm.at[pl.ds(0, head), tile], a_ref.at[pl.ds(j * head, head)])
                     for j, tile in enumerate(tiles)
@@ -100,7 +99,26 @@
         fetch.wait()
 
 
-def prepare(label_slot, pos_ids, pos_count, embeddings, head):
+def fetch_kernel(head, docs_hbm, b_ref, done):
+    fetch = pltpu.make_async_copy(docs_hbm.at[pl.ds(head, b_ref.shape[0])], b_ref, done)
+    fetch.start()
+    fetch.wait()
+
+
+def fetch_later(embeddings, head):
+    docs, width = embeddings.shape
+    return pl.pallas_call(
+        functools.partial(fetch_kernel, head),
+        in_specs=[pl.BlockSpec(memory_space=pltpu.HBM)],
+        out_specs=pl.BlockSpec(memory_space=pltpu.VMEM),
+        out_shape=jax.ShapeDtypeStruct((docs - head, width), jnp.bfloat16),
+        scratch_shapes=[pltpu.SemaphoreType.DMA],
+        compiler_params=pltpu.CompilerParams(vmem_limit_bytes=VMEM_LIMIT),
+        name="fetch",
+    )(pltpu.with_memory_space_constraint(embeddings, pltpu.HBM))
+
+
+def prepare(label_slot, pos_ids, pos_count, embeddings, b, head):
     docs, slots = pos_ids.shape
     width = embeddings.shape[1]
     tall = width // LANES * head + slots * (docs // LANES)
@@ -109,21 +127,18 @@
     inputs = (pos_ids.T, pos_count.reshape(1, docs), table, embeddings)
     return pl.pallas_call(
         functools.partial(prepare_kernel, (lines - 1).bit_length()),
-        in_specs=[pl.BlockSpec(memory_space=pltpu.HBM)] * 4,
-        out_specs=[pl.BlockSpec(memory_space=pltpu.VMEM)] * 2,
-        out_shape=[
-            jax.ShapeDtypeStruct((tall, LANES), jnp.bfloat16),
-            jax.ShapeDtypeStruct((docs - head, width), jnp.bfloat16),
-        ],
+        in_specs=[pl.BlockSpec(memory_space=pltpu.HBM)] * 4 + [pl.BlockSpec(memory_space=pl.ANY)],
+        out_specs=pl.BlockSpec(memory_space=pltpu.VMEM),
+        out_shape=jax.ShapeDtypeStruct((tall, LANES), jnp.bfloat16),
         scratch_shapes=[
             pltpu.VMEM((slots, docs), jnp.int32),
             pltpu.VMEM((1, docs), jnp.int32),
             pltpu.VMEM((lines, LANES), jnp.int32),
-            pltpu.SemaphoreType.DMA((4 + width // LANES,)),
+            pltpu.SemaphoreType.DMA((3 + width // LANES,)),
         ],
         compiler_params=pltpu.CompilerParams(vmem_limit_bytes=VMEM_LIMIT),
         name="prepare",
-    )(*(pltpu.with_memory_space_constraint(x, pltpu.HBM) for x in inputs))
+    )(*(pltpu.with_memory_space_constraint(x, pltpu.HBM) for x in inputs), b)
 
 
 def cast_kernel(weights_ref, cast_ref):
@@ -312,8 +327,10 @@
     def send(value, pairs):
         return lax.ppermute(value, "blk", pairs)
 
-    a, b = prepare(label_slot, pos_ids, pos_count, embeddings, head)
-    coming = {"up_b": send(b, up), "down_a": send(a, down)}
+    b = fetch_later(embeddings, head)
+    coming = {"up_b": send(b, up)}
+    a = prepare(label_slot, pos_ids, pos_count, embeddings, b, head)
+    coming["down_a"] = send(a, down)
     coming |= {"up_a": send(a, up), "down_b": send(b, down)}
     mine = halved_cast(weights)
     cast = [mine, send(mine, swap)]

time: 40.8 us -> 41.1 us (level)
  starting transfers between devices: 17.5 us -> 21.9 us
  waiting for transfers between devices: 9.77 us -> 5.8 us
  local copies, waits for them, and re-layouts: 1.14 us -> 0.01 us
  Pallas kernels: 11.4 us -> 12.4 us
    ppermute x18, starting transfers between devices: 17.5 us -> 21.9 us  [send(): return lax.ppermute(value, 'blk', pairs)]
    ppermute x18, waiting for transfers between devices: 9.77 us -> 5.8 us  [send(): return lax.ppermute(value, 'blk', pairs)]
    unnamed x8 -> x6, local copies, waits for them, and re-layouts: 1.14 us -> 0.01 us
    pallas_call x0 -> x1, Pallas kernels: none -> 1.01 us  [fetch_later(): pl.pallas_call(functools.partial(fetch_kernel, head), in_specs=[pl.BlockS...]
  transfers between devices with their start and end apart: 18 -> 18, of which waited for: 11 -> 11; matrix products, arithmetic and copies ran while one was open for 0% -> 0% of each run, Pallas kernels for 19% -> 22%
where the time goes in v16:
time: 41.1 us; the launch traced here: 40.9 us
  starting transfers between devices  21.9 us (53%)
  Pallas kernels  12.4 us (30%)
  waiting for transfers between devices  5.8 us (14%)
  between operations  0.79 us (2%)
    ppermute x18, starting transfers between devices, send(): return lax.ppermute(value, 'blk', pairs)  21.9 us
    pallas_call x8, Pallas kernels, add_gradient(): pl.pallas_call(functools.partial(gradient_kernel, bits, owners, not sums)...  7.69 us
    ppermute x18, waiting for transfers between devices, send(): return lax.ppermute(value, 'blk', pairs)  5.8 us
    pallas_call x1, Pallas kernels, finish(): pl.pallas_call(functools.partial(finish_kernel, bits), in_specs=[pl.Block...  2.35 us
    pallas_call x1, Pallas kernels, prepare(): pl.pallas_call(functools.partial(prepare_kernel, (lines - 1).bit_length()...  1.29 us
    pallas_call x1, Pallas kernels, fetch_later(): pl.pallas_call(functools.partial(fetch_kernel, head), in_specs=[pl.BlockS...  1.01 us
  transfers between devices with their start and end apart: 18, of which 11 were waited for; matrix products, arithmetic and copies ran while one was open for 0% of the time, Pallas kernels for 22%

profile of v16, /device:TPU:0, one launch (start us, length us, event | category | flops | bytes accessed | tf_op | source)
XLA Modules:
  0.0 40.9 jit_solution(15519950913077140455)
XLA Ops:
  0.6 1.0 %fetch.1._.b_ref = bf16[128,768]{1,0:T(8,128)(2,1)S(1)} custom-call(bf16[256,768]{1,0:T(8,128)(2,1)} %docs_hbm.3), custom_call_target="tpu_custom_call" | custom-call | tf_op jit(solution)/shard_map/fetch/pallas_call | solution.py:110
  1.7 3.1 %collective-permute-start.1 = (bf16[128,768]{1,0:T(8,128)(2,1)S(1)}, bf16[128,768]{1,0:T(8,128)(2,1)S(1)}, u32[]{:S(2)}, u32[]{:S(2)}) collective-permute-start(bf16[128,768]{1,0:T(8,128)(2,1)S(1)} %fetch.1._.b_ref), channel_id=1, source_target_pairs={{0,4},{5,1},{4,8},{9,5},{8,12},{13,9},{12,14},{15,13},{14,10},{11,... | collective-permute-start | bytes 589832 | tf_op jit(solution)/shard_map/ppermute | solution.py:328
  4.7 1.3 %prepare.1.a_ref = bf16[832,128]{1,0:T(8,128)(2,1)S(1)} custom-call(s32[32,256]{1,0:T(8,128)} %bitcast.3, s32[1,256]{1,0:T(1,128)} %bitcast.5, s32[32,128]{1,0:T(8,128)} %bitcast.4, bf16[256,768]{1,0:T(8,128)(2,1)} %docs_hbm.3, bf16[128,768]{1,0:T(8,128)(2,1)S(1)} %fetch.1._.b_ref), custom_call_target="tpu_custom_call" | custom-call | tf_op jit(solution)/shard_map/prepare/pallas_call | solution.py:128
  6.1 2.0 %collective-permute-start.5 = (bf16[832,128]{1,0:T(8,128)(2,1)S(1)}, bf16[832,128]{1,0:T(8,128)(2,1)S(1)}, u32[]{:S(2)}, u32[]{:S(2)}) collective-permute-start(bf16[832,128]{1,0:T(8,128)(2,1)S(1)} %prepare.1.a_ref), channel_id=1, source_target_pairs={{0,4},{5,1},{4,8},{9,5},{8,12},{13,9},{12,14},{15,13},{14,10},{11,... | collective-permute-start | bytes 638984 | tf_op jit(solution)/shard_map/ppermute | solution.py:328
  8.2 0.5 %collective-permute-start.4 = (bf16[128,768]{1,0:T(8,128)(2,1)S(1)}, bf16[128,768]{1,0:T(8,128)(2,1)S(1)}, u32[]{:S(2)}, u32[]{:S(2)}) collective-permute-start(bf16[128,768]{1,0:T(8,128)(2,1)S(1)} %fetch.1._.b_ref), channel_id=1, source_target_pairs={{4,0},{1,5},{8,4},{5,9},{12,8},{9,13},{14,12},{13,15},{10,14},{15,... | collective-permute-start | bytes 589832 | tf_op jit(solution)/shard_map/ppermute | solution.py:328
  8.8 1.0 %collective-permute-done.1.b_ref = bf16[128,768]{1,0:T(8,128)(2,1)S(1)} collective-permute-done((bf16[128,768]{1,0:T(8,128)(2,1)S(1)}, bf16[128,768]{1,0:T(8,128)(2,1)S(1)}, u32[]{:S(2)}, u32[]{:S(2)}) %collective-permute-start.1) | collective-permute-done | bytes 196640 | tf_op jit(solution)/shard_map/ppermute | solution.py:328
  9.8 2.5 %collective-permute-start.3 = (bf16[128,768]{1,0:T(8,128)(2,1)S(1)}, bf16[128,768]{1,0:T(8,128)(2,1)S(1)}, u32[]{:S(2)}, u32[]{:S(2)}) collective-permute-start(bf16[128,768]{1,0:T(8,128)(2,1)S(1)} %collective-permute-done.1.b_ref), channel_id=1, source_target_pairs={{0,4},{5,1},{4,8},{9,5},{8,12},{13,9},{12,14},{15,13},{14,10},{11,... | collective-permute-start | bytes 589832 | tf_op jit(solution)/shard_map/ppermute | solution.py:328
  12.3 0.7 %collective-permute-done.a_ref = bf16[832,128]{1,0:T(8,128)(2,1)S(1)} collective-permute-done((bf16[832,128]{1,0:T(8,128)(2,1)S(1)}, bf16[832,128]{1,0:T(8,128)(2,1)S(1)}, u32[]{:S(2)}, u32[]{:S(2)}) %collective-permute-start) | collective-permute-done | bytes 213024 | tf_op jit(solution)/shard_map/ppermute | solution.py:328
  12.9 1.0 %collective-permute-start.2 = (bf16[832,128]{1,0:T(8,128)(2,1)S(1)}, bf16[832,128]{1,0:T(8,128)(2,1)S(1)}, u32[]{:S(2)}, u32[]{:S(2)}) collective-permute-start(bf16[832,128]{1,0:T(8,128)(2,1)S(1)} %collective-permute-done.a_ref), channel_id=1, source_target_pairs={{4,0},{1,5},{8,4},{5,9},{12,8},{9,13},{14,12},{13,15},{10,14},{15,... | collective-permute-start | bytes 638984 | tf_op jit(solution)/shard_map/ppermute | solution.py:328
  14.0 0.4 collective-permute-done.5.a_ref
  14.4 2.5 %collective-permute-start.9 = (bf16[832,128]{1,0:T(8,128)(2,1)S(1)}, bf16[832,128]{1,0:T(8,128)(2,1)S(1)}, u32[]{:S(2)}, u32[]{:S(2)}) collective-permute-start(bf16[832,128]{1,0:T(8,128)(2,1)S(1)} %collective-permute-done.5.a_ref), channel_id=1, source_target_pairs={{0,4},{5,1},{4,8},{9,5},{8,12},{13,9},{12,14},{15,13},{14,10},{11,... | collective-permute-start | bytes 638984 | tf_op jit(solution)/shard_map/ppermute | solution.py:328
  17.1 1.0 %collective-permute-start.8 = (bf16[128,768]{1,0:T(8,128)(2,1)S(1)}, bf16[128,768]{1,0:T(8,128)(2,1)S(1)}, u32[]{:S(2)}, u32[]{:S(2)}) collective-permute-start(bf16[128,768]{1,0:T(8,128)(2,1)S(1)} %collective-permute-done.4.b_ref), channel_id=1, source_target_pairs={{4,0},{1,5},{8,4},{5,9},{12,8},{9,13},{14,12},{13,15},{10,14},{15,... | collective-permute-start | bytes 589832 | tf_op jit(solution)/shard_map/ppermute | solution.py:328
  18.2 0.4 collective-permute-done.3.b_ref
  18.6 2.5 %collective-permute-start.7 = (bf16[128,768]{1,0:T(8,128)(2,1)S(1)}, bf16[128,768]{1,0:T(8,128)(2,1)S(1)}, u32[]{:S(2)}, u32[]{:S(2)}) collective-permute-start(bf16[128,768]{1,0:T(8,128)(2,1)S(1)} %collective-permute-done.3.b_ref), channel_id=1, source_target_pairs={{0,4},{5,1},{4,8},{9,5},{8,12},{13,9},{12,14},{15,13},{14,10},{11,... | collective-permute-start | bytes 589832 | tf_op jit(solution)/shard_map/ppermute | solution.py:328
  21.0 0.7 %collective-permute-done.2.a_ref = bf16[832,128]{1,0:T(8,128)(2,1)S(1)} collective-permute-done((bf16[832,128]{1,0:T(8,128)(2,1)S(1)}, bf16[832,128]{1,0:T(8,128)(2,1)S(1)}, u32[]{:S(2)}, u32[]{:S(2)}) %collective-permute-start.2) | collective-permute-done | bytes 213024 | tf_op jit(solution)/shard_map/ppermute | solution.py:328
  21.7 1.0 %collective-permute-start.6 = (bf16[832,128]{1,0:T(8,128)(2,1)S(1)}, bf16[832,128]{1,0:T(8,128)(2,1)S(1)}, u32[]{:S(2)}, u32[]{:S(2)}) collective-permute-start(bf16[832,128]{1,0:T(8,128)(2,1)S(1)} %collective-permute-done.2.a_ref), channel_id=1, source_target_pairs={{4,0},{1,5},{8,4},{5,9},{12,8},{9,13},{14,12},{13,15},{10,14},{15,... | collective-permute-start | bytes 638984 | tf_op jit(solution)/shard_map/ppermute | solution.py:328
  22.7 1.0 %gradient.8 = (f32[256,768]{1,0:T(8,128)S(1)}, f32[256,768]{1,0:T(8,128)S(1)}) custom-call(bf16[832,128]{1,0:T(8,128)(2,1)S(1)} %prepare.1.a_ref, bf16[128,768]{1,0:T(8,128)(2,1)S(1)} %fetch.1._.b_ref, bf16[256,768]{1,0:T(8,128)(2,1)S(1)} %cast.1.refs_0_.cast_ref, bf16[256,768]{1,0:T(8,128)(2,1)S(1)} %collective-permute-done.10.refs_1_), custom_call_target="tpu_custom_call" | custom-call | flops 200000000 | bytes 1000000 | tf_op jit(solution)/shard_map/gradient/pallas_call | solution.py:217
  23.7 1.9 %collective-permute-start.14 = (bf16[832,128]{1,0:T(8,128)(2,1)S(1)}, bf16[832,128]{1,0:T(8,128)(2,1)S(1)}, u32[]{:S(2)}, u32[]{:S(2)}) collective-permute-start(bf16[832,128]{1,0:T(8,128)(2,1)S(1)} %collective-permute-done.9.a_ref), channel_id=1, source_target_pairs={{0,4},{5,1},{4,8},{9,5},{8,12},{13,9},{12,14},{15,13},{14,10},{11,... | collective-permute-start | bytes 638984 | tf_op jit(solution)/shard_map/ppermute | solution.py:328
  25.6 1.0 %gradient.9 = (f32[256,768]{1,0:T(8,128)S(1)}, f32[256,768]{1,0:T(8,128)S(1)}) custom-call(bf16[832,128]{1,0:T(8,128)(2,1)S(1)} %collective-permute-done.5.a_ref, bf16[128,768]{1,0:T(8,128)(2,1)S(1)} %collective-permute-done.1.b_ref, bf16[256,768]{1,0:T(8,128)(2,1)S(1)} %cast.1.refs_0_.cast_ref, ...), custom_call_target="tpu_custom_call", output_to_operand_aliasing={{0}: (4, {}), {1}: (5, {})} | custom-call | flops 200000000 | bytes 1000000 | tf_op jit(solution)/shard_map/gradient/pallas_call | solution.py:217
  26.6 0.5 %collective-permute-start.13 = (bf16[128,768]{1,0:T(8,128)(2,1)S(1)}, bf16[128,768]{1,0:T(8,128)(2,1)S(1)}, u32[]{:S(2)}, u32[]{:S(2)}) collective-permute-start(bf16[128,768]{1,0:T(8,128)(2,1)S(1)} %collective-permute-done.8.b_ref), channel_id=1, source_target_pairs={{4,0},{1,5},{8,4},{5,9},{12,8},{9,13},{14,12},{13,15},{10,14},{15,... | collective-permute-start | bytes 589832 | tf_op jit(solution)/shard_map/ppermute | solution.py:328
  27.3 2.5 %collective-permute-start.12 = (bf16[128,768]{1,0:T(8,128)(2,1)S(1)}, bf16[128,768]{1,0:T(8,128)(2,1)S(1)}, u32[]{:S(2)}, u32[]{:S(2)}) collective-permute-start(bf16[128,768]{1,0:T(8,128)(2,1)S(1)} %collective-permute-done.7.b_ref), channel_id=1, source_target_pairs={{0,4},{5,1},{4,8},{9,5},{8,12},{13,9},{12,14},{15,13},{14,10},{11,... | collective-permute-start | bytes 589832 | tf_op jit(solution)/shard_map/ppermute | solution.py:328
  29.8 1.0 %gradient.10 = (f32[256,768]{1,0:T(8,128)S(1)}, f32[256,768]{1,0:T(8,128)S(1)}) custom-call(bf16[832,128]{1,0:T(8,128)(2,1)S(1)} %collective-permute-done.a_ref, bf16[128,768]{1,0:T(8,128)(2,1)S(1)} %collective-permute-done.4.b_ref, bf16[256,768]{1,0:T(8,128)(2,1)S(1)} %cast.1.refs_0_.cast_ref, ...), custom_call_target="tpu_custom_call", output_to_operand_aliasing={{0}: (4, {}), {1}: (5, {})} | custom-call | flops 1000000000 | bytes 1000000 | tf_op jit(solution)/shard_map/gradient/pallas_call | solution.py:217
  30.8 0.7 %collective-permute-start.11 = (bf16[832,128]{1,0:T(8,128)(2,1)S(1)}, bf16[832,128]{1,0:T(8,128)(2,1)S(1)}, u32[]{:S(2)}, u32[]{:S(2)}) collective-permute-start(bf16[832,128]{1,0:T(8,128)(2,1)S(1)} %collective-permute-done.6.a_ref), channel_id=1, source_target_pairs={{4,0},{1,5},{8,4},{5,9},{12,8},{9,13},{14,12},{13,15},{10,14},{15,... | collective-permute-start | bytes 638984 | tf_op jit(solution)/shard_map/ppermute | solution.py:328
  31.5 1.0 %gradient.11 = (f32[256,768]{1,0:T(8,128)S(1)}, f32[256,768]{1,0:T(8,128)S(1)}) custom-call(bf16[832,128]{1,0:T(8,128)(2,1)S(1)} %collective-permute-done.9.a_ref, bf16[128,768]{1,0:T(8,128)(2,1)S(1)} %collective-permute-done.3.b_ref, bf16[256,768]{1,0:T(8,128)(2,1)S(1)} %cast.1.refs_0_.cast_ref, ...), custom_call_target="tpu_custom_call", output_to_operand_aliasing={{0}: (4, {}), {1}: (5, {})} | custom-call | flops 1000000000 | bytes 1000000 | tf_op jit(solution)/shard_map/gradient/pallas_call | solution.py:217
  32.5 1.0 %gradient.12 = (f32[256,768]{1,0:T(8,128)S(1)}, f32[256,768]{1,0:T(8,128)S(1)}) custom-call(bf16[832,128]{1,0:T(8,128)(2,1)S(1)} %collective-permute-done.2.a_ref, bf16[128,768]{1,0:T(8,128)(2,1)S(1)} %collective-permute-done.8.b_ref, bf16[256,768]{1,0:T(8,128)(2,1)S(1)} %cast.1.refs_0_.cast_ref, ...), custom_call_target="tpu_custom_call", output_to_operand_aliasing={{0}: (4, {}), {1}: (5, {})} | custom-call | flops 1000000000 | bytes 1000000 | tf_op jit(solution)/shard_map/gradient/pallas_call | solution.py:217
  33.6 1.0 %gradient.13 = (f32[256,768]{1,0:T(8,128)S(1)}, f32[256,768]{1,0:T(8,128)S(1)}) custom-call(bf16[832,128]{1,0:T(8,128)(2,1)S(1)} %collective-permute-done.14.a_ref, bf16[128,768]{1,0:T(8,128)(2,1)S(1)} %collective-permute-done.7.b_ref, bf16[256,768]{1,0:T(8,128)(2,1)S(1)} %cast.1.refs_0_.cast_ref, ...), custom_call_target="tpu_custom_call", output_to_operand_aliasing={{0}: (4, {}), {1}: (5, {})} | custom-call | flops 1000000000 | bytes 1000000 | tf_op jit(solution)/shard_map/gradient/pallas_call | solution.py:217
  34.6 1.0 %gradient.14 = (f32[256,768]{1,0:T(8,128)S(1)}, f32[256,768]{1,0:T(8,128)S(1)}) custom-call(bf16[832,128]{1,0:T(8,128)(2,1)S(1)} %collective-permute-done.6.a_ref, bf16[128,768]{1,0:T(8,128)(2,1)S(1)} %collective-permute-done.13.b_ref, bf16[256,768]{1,0:T(8,128)(2,1)S(1)} %cast.1.refs_0_.cast_ref, ...), custom_call_target="tpu_custom_call", output_to_operand_aliasing={{0}: (4, {}), {1}: (5, {})} | custom-call | flops 1000000000 | bytes 1000000 | tf_op jit(solution)/shard_map/gradient/pallas_call | solution.py:217
  35.7 0.7 %collective-permute-done.12.b_ref = bf16[128,768]{1,0:T(8,128)(2,1)S(1)} collective-permute-done((bf16[128,768]{1,0:T(8,128)(2,1)S(1)}, bf16[128,768]{1,0:T(8,128)(2,1)S(1)}, u32[]{:S(2)}, u32[]{:S(2)}) %collective-permute-start.12) | collective-permute-done | bytes 196640 | tf_op jit(solution)/shard_map/ppermute | solution.py:328
  36.4 0.5 %collective-permute-done.11.a_ref = bf16[832,128]{1,0:T(8,128)(2,1)S(1)} collective-permute-done((bf16[832,128]{1,0:T(8,128)(2,1)S(1)}, bf16[832,128]{1,0:T(8,128)(2,1)S(1)}, u32[]{:S(2)}, u32[]{:S(2)}) %collective-permute-start.11) | collective-permute-done | bytes 213024 | tf_op jit(solution)/shard_map/ppermute | solution.py:328
  37.0 0.7 %gradient.15.sum_ref = f32[256,768]{1,0:T(8,128)S(1)} custom-call(bf16[832,128]{1,0:T(8,128)(2,1)S(1)} %collective-permute-done.11.a_ref, bf16[128,768]{1,0:T(8,128)(2,1)S(1)} %collective-permute-done.12.b_ref, bf16[256,768]{1,0:T(8,128)(2,1)S(1)} %cast.1.refs_0_.cast_ref, f32[256,768]{1,0:T(8,128)S(1)} %get-tuple-element.165.refs_1_), custom_call_target="tpu_custom_call", output_to_operand_aliasing={{}: (3, {})} | custom-call | flops 10000000000 | bytes 1000000 | tf_op jit(solution)/shard_map/gradient/pallas_call | solution.py:217
  37.6 0.6 %collective-permute-done.16.b_ref = bf16[128,768]{1,0:T(8,128)(2,1)S(1)} collective-permute-done((bf16[128,768]{1,0:T(8,128)(2,1)S(1)}, bf16[128,768]{1,0:T(8,128)(2,1)S(1)}, u32[]{:S(2)}, u32[]{:S(2)}) %collective-permute-start.16) | collective-permute-done | bytes 196640 | tf_op jit(solution)/shard_map/ppermute | solution.py:328
  38.6 2.3 %finish.1 = (f32[256,768]{1,0:T(8,128)}, f32[256,768]{1,0:T(8,128)}, f32[256,768]{1,0:T(8,128)}) custom-call(bf16[832,128]{1,0:T(8,128)(2,1)S(1)} %collective-permute-done.15.a_ref, bf16[128,768]{1,0:T(8,128)(2,1)S(1)} %collective-permute-done.16.b_ref, bf16[256,768]{1,0:T(8,128)(2,1)S(1)} %cast.1.refs_0_.cast_ref, f32[256,768]{1,0:T(8,128)S(1)} %gradient.15.sum_ref, ...), custom_call_target="tpu_custom_call" | custom-call | flops 10000000000 | bytes 1000000 | tf_op jit(solution)/shard_map/finish/pallas_call | solution.py:274
  (22 shorter events, 1.3 us)
Async XLA Ops:
  0.6 7.5 %copy-start = (f32[256,768]{1,0:T(8,128)S(1)}, f32[256,768]{1,0:T(8,128)}, u32[]{:S(2)}) copy-start(f32[256,768]{1,0:T(8,128)} %weights_ref.3) | copy-start | bytes 2359300
  1.7 8.1 %collective-permute-start.1 = (bf16[128,768]{1,0:T(8,128)(2,1)S(1)}, bf16[128,768]{1,0:T(8,128)(2,1)S(1)}, u32[]{:S(2)}, u32[]{:S(2)}) collective-permute-start(bf16[128,768]{1,0:T(8,128)(2,1)S(1)} %fetch.1._.b_ref), channel_id=1, source_target_pairs={{0,4},{5,1},{4,8},{9,5},{8,12},{13,9},{12,14},{15,13},{14,10},{11,... | collective-permute-start | bytes 589832 | tf_op jit(solution)/shard_map/ppermute | solution.py:328
  6.0 6.9 %collective-permute-start = (bf16[832,128]{1,0:T(8,128)(2,1)S(1)}, bf16[832,128]{1,0:T(8,128)(2,1)S(1)}, u32[]{:S(2)}, u32[]{:S(2)}) collective-permute-start(bf16[832,128]{1,0:T(8,128)(2,1)S(1)} %prepare.1.a_ref), channel_id=1, source_target_pairs={{4,0},{1,5},{8,4},{5,9},{12,8},{9,13},{14,12},{13,15},{10,14},{15,... | collective-permute-start | bytes 638984 | tf_op jit(solution)/shard_map/ppermute | solution.py:328
  6.1 8.3 %collective-permute-start.5 = (bf16[832,128]{1,0:T(8,128)(2,1)S(1)}, bf16[832,128]{1,0:T(8,128)(2,1)S(1)}, u32[]{:S(2)}, u32[]{:S(2)}) collective-permute-start(bf16[832,128]{1,0:T(8,128)(2,1)S(1)} %prepare.1.a_ref), channel_id=1, source_target_pairs={{0,4},{5,1},{4,8},{9,5},{8,12},{13,9},{12,14},{15,13},{14,10},{11,... | collective-permute-start | bytes 638984 | tf_op jit(solution)/shard_map/ppermute | solution.py:328
  8.2 14.6 %collective-permute-start.10 = (bf16[256,768]{1,0:T(8,128)(2,1)S(1)}, bf16[256,768]{1,0:T(8,128)(2,1)S(1)}, u32[]{:S(2)}, u32[]{:S(2)}) collective-permute-start(bf16[256,768]{1,0:T(8,128)(2,1)S(1)} %cast.1.refs_0_.cast_ref), channel_id=1, source_target_pairs={{0,1},{1,0},{2,3},{3,2},{4,5},{5,4},{6,7},{7,6},{8,9},{9,8},{10,11... | collective-permute-start | bytes 1179656 | tf_op jit(solution)/shard_map/ppermute | solution.py:328
  8.2 8.9 %collective-permute-start.4 = (bf16[128,768]{1,0:T(8,128)(2,1)S(1)}, bf16[128,768]{1,0:T(8,128)(2,1)S(1)}, u32[]{:S(2)}, u32[]{:S(2)}) collective-permute-start(bf16[128,768]{1,0:T(8,128)(2,1)S(1)} %fetch.1._.b_ref), channel_id=1, source_target_pairs={{4,0},{1,5},{8,4},{5,9},{12,8},{9,13},{14,12},{13,15},{10,14},{15,... | collective-permute-start | bytes 589832 | tf_op jit(solution)/shard_map/ppermute | solution.py:328
  9.8 8.8 %collective-permute-start.3 = (bf16[128,768]{1,0:T(8,128)(2,1)S(1)}, bf16[128,768]{1,0:T(8,128)(2,1)S(1)}, u32[]{:S(2)}, u32[]{:S(2)}) collective-permute-start(bf16[128,768]{1,0:T(8,128)(2,1)S(1)} %collective-permute-done.1.b_ref), channel_id=1, source_target_pairs={{0,4},{5,1},{4,8},{9,5},{8,12},{13,9},{12,14},{15,13},{14,10},{11,... | collective-permute-start | bytes 589832 | tf_op jit(solution)/shard_map/ppermute | solution.py:328
  12.9 8.8 %collective-permute-start.2 = (bf16[832,128]{1,0:T(8,128)(2,1)S(1)}, bf16[832,128]{1,0:T(8,128)(2,1)S(1)}, u32[]{:S(2)}, u32[]{:S(2)}) collective-permute-start(bf16[832,128]{1,0:T(8,128)(2,1)S(1)} %collective-permute-done.a_ref), channel_id=1, source_target_pairs={{4,0},{1,5},{8,4},{5,9},{12,8},{9,13},{14,12},{13,15},{10,14},{15,... | collective-permute-start | bytes 638984 | tf_op jit(solution)/shard_map/ppermute | solution.py:328
  14.4 9.4 %collective-permute-start.9 = (bf16[832,128]{1,0:T(8,128)(2,1)S(1)}, bf16[832,128]{1,0:T(8,128)(2,1)S(1)}, u32[]{:S(2)}, u32[]{:S(2)}) collective-permute-start(bf16[832,128]{1,0:T(8,128)(2,1)S(1)} %collective-permute-done.5.a_ref), channel_id=1, source_target_pairs={{0,4},{5,1},{4,8},{9,5},{8,12},{13,9},{12,14},{15,13},{14,10},{11,... | collective-permute-start | bytes 638984 | tf_op jit(solution)/shard_map/ppermute | solution.py:328
  17.1 9.5 %collective-permute-start.8 = (bf16[128,768]{1,0:T(8,128)(2,1)S(1)}, bf16[128,768]{1,0:T(8,128)(2,1)S(1)}, u32[]{:S(2)}, u32[]{:S(2)}) collective-permute-start(bf16[128,768]{1,0:T(8,128)(2,1)S(1)} %collective-permute-done.4.b_ref), channel_id=1, source_target_pairs={{4,0},{1,5},{8,4},{5,9},{12,8},{9,13},{14,12},{13,15},{10,14},{15,... | collective-permute-start | bytes 589832 | tf_op jit(solution)/shard_map/ppermute | solution.py:328
  18.6 8.8 %collective-permute-start.7 = (bf16[128,768]{1,0:T(8,128)(2,1)S(1)}, bf16[128,768]{1,0:T(8,128)(2,1)S(1)}, u32[]{:S(2)}, u32[]{:S(2)}) collective-permute-start(bf16[128,768]{1,0:T(8,128)(2,1)S(1)} %collective-permute-done.3.b_ref), channel_id=1, source_target_pairs={{0,4},{5,1},{4,8},{9,5},{8,12},{13,9},{12,14},{15,13},{14,10},{11,... | collective-permute-start | bytes 589832 | tf_op jit(solution)/shard_map/ppermute | solution.py:328
  21.7 9.1 %collective-permute-start.6 = (bf16[832,128]{1,0:T(8,128)(2,1)S(1)}, bf16[832,128]{1,0:T(8,128)(2,1)S(1)}, u32[]{:S(2)}, u32[]{:S(2)}) collective-permute-start(bf16[832,128]{1,0:T(8,128)(2,1)S(1)} %collective-permute-done.2.a_ref), channel_id=1, source_target_pairs={{4,0},{1,5},{8,4},{5,9},{12,8},{9,13},{14,12},{13,15},{10,14},{15,... | collective-permute-start | bytes 638984 | tf_op jit(solution)/shard_map/ppermute | solution.py:328
  23.7 9.8 %collective-permute-start.14 = (bf16[832,128]{1,0:T(8,128)(2,1)S(1)}, bf16[832,128]{1,0:T(8,128)(2,1)S(1)}, u32[]{:S(2)}, u32[]{:S(2)}) collective-permute-start(bf16[832,128]{1,0:T(8,128)(2,1)S(1)} %collective-permute-done.9.a_ref), channel_id=1, source_target_pairs={{0,4},{5,1},{4,8},{9,5},{8,12},{13,9},{12,14},{15,13},{14,10},{11,... | collective-permute-start | bytes 638984 | tf_op jit(solution)/shard_map/ppermute | solution.py:328
  26.6 7.9 %collective-permute-start.13 = (bf16[128,768]{1,0:T(8,128)(2,1)S(1)}, bf16[128,768]{1,0:T(8,128)(2,1)S(1)}, u32[]{:S(2)}, u32[]{:S(2)}) collective-permute-start(bf16[128,768]{1,0:T(8,128)(2,1)S(1)} %collective-permute-done.8.b_ref), channel_id=1, source_target_pairs={{4,0},{1,5},{8,4},{5,9},{12,8},{9,13},{14,12},{13,15},{10,14},{15,... | collective-permute-start | bytes 589832 | tf_op jit(solution)/shard_map/ppermute | solution.py:328
  27.3 9.0 %collective-permute-start.12 = (bf16[128,768]{1,0:T(8,128)(2,1)S(1)}, bf16[128,768]{1,0:T(8,128)(2,1)S(1)}, u32[]{:S(2)}, u32[]{:S(2)}) collective-permute-start(bf16[128,768]{1,0:T(8,128)(2,1)S(1)} %collective-permute-done.7.b_ref), channel_id=1, source_target_pairs={{0,4},{5,1},{4,8},{9,5},{8,12},{13,9},{12,14},{15,13},{14,10},{11,... | collective-permute-start | bytes 589832 | tf_op jit(solution)/shard_map/ppermute | solution.py:328
  30.8 6.0 %collective-permute-start.11 = (bf16[832,128]{1,0:T(8,128)(2,1)S(1)}, bf16[832,128]{1,0:T(8,128)(2,1)S(1)}, u32[]{:S(2)}, u32[]{:S(2)}) collective-permute-start(bf16[832,128]{1,0:T(8,128)(2,1)S(1)} %collective-permute-done.6.a_ref), channel_id=1, source_target_pairs={{4,0},{1,5},{8,4},{5,9},{12,8},{9,13},{14,12},{13,15},{10,14},{15,... | collective-permute-start | bytes 638984 | tf_op jit(solution)/shard_map/ppermute | solution.py:328
  35.6 2.9 %collective-permute-start.17 = (f32[256,768]{1,0:T(8,128)S(1)}, f32[256,768]{1,0:T(8,128)S(1)}, u32[]{:S(2)}, u32[]{:S(2)}) collective-permute-start(f32[256,768]{1,0:T(8,128)S(1)} %get-tuple-element.166), channel_id=1, source_target_pairs={{0,1},{1,0},{2,3},{3,2},{4,5},{5,4},{6,7},{7,6},{8,9},{9,8},{10,11... | collective-permute-start | bytes 2359304 | tf_op jit(solution)/shard_map/ppermute | solution.py:328
  36.4 2.2 %copy-start.1 = (f32[256,768]{1,0:T(8,128)S(1)}, f32[256,768]{1,0:T(8,128)}, u32[]{:S(2)}) copy-start(f32[256,768]{1,0:T(8,128)} %first_ref.1) | copy-start | bytes 2359300
  36.4 2.2 %copy-start.2 = (f32[256,768]{1,0:T(8,128)S(1)}, f32[256,768]{1,0:T(8,128)}, u32[]{:S(2)}) copy-start(f32[256,768]{1,0:T(8,128)} %second_ref.1) | copy-start | bytes 2359300
  36.4 1.8 %collective-permute-start.16 = (bf16[128,768]{1,0:T(8,128)(2,1)S(1)}, bf16[128,768]{1,0:T(8,128)(2,1)S(1)}, u32[]{:S(2)}, u32[]{:S(2)}) collective-permute-start(bf16[128,768]{1,0:T(8,128)(2,1)S(1)} %collective-permute-done.12.b_ref), channel_id=1, source_target_pairs={{0,1},{1,0},{2,3},{3,2},{4,5},{5,4},{6,7},{7,6},{8,9},{9,8},{10,11... | collective-permute-start | bytes 589832 | tf_op jit(solution)/shard_map/ppermute | solution.py:328
  36.9 1.7 %collective-permute-start.15 = (bf16[832,128]{1,0:T(8,128)(2,1)S(1)}, bf16[832,128]{1,0:T(8,128)(2,1)S(1)}, u32[]{:S(2)}, u32[]{:S(2)}) collective-permute-start(bf16[832,128]{1,0:T(8,128)(2,1)S(1)} %collective-permute-done.11.a_ref), channel_id=1, source_target_pairs={{0,1},{1,0},{2,3},{3,2},{4,5},{5,4},{6,7},{7,6},{8,9},{9,8},{10,11... | collective-permute-start | bytes 638984 | tf_op jit(solution)/shard_map/ppermute | solution.py:328

commit v17 on v15

--- a/solution.py
+++ b/solution.py
@@ -33,41 +33,63 @@
     return value
 
 
-def prepare_kernel(
-    bits,
+def fetch_kernel(
     ids_hbm,
     count_hbm,
     table_hbm,
     docs_hbm,
-    a_ref,
     b_ref,
+    top_ref,
     ids_ref,
     count_ref,
     table_ref,
     done,
 ):
-    slots, docs = ids_ref.shape
+    docs, width = docs_hbm.shape
     head = docs - b_ref.shape[0]
-    tiles = [pl.ds(start, LANES) for start in range(0, b_ref.shape[1], LANES)]
-    fetches = [
-        pltpu.make_async_copy(source, target, done.at[i])
-        for i, (source, target) in enumerate(
-            (
-                (ids_hbm, ids_ref),
-                (table_hbm, table_ref),
-                (count_hbm, count_ref),
-                (docs_hbm.at[pl.ds(head, docs - head)], b_ref),
-                *(
-                    (docs_hbm.at[pl.ds(0, head), tile], a_ref.at[pl.ds(j * head, head)])
-                    for j, tile in enumerate(tiles)
-                ),
-            )
-        )
+    pairs = [
+        (docs_hbm.at[pl.ds(head, docs - head)], b_ref),
+        (ids_hbm, ids_ref),
+        (table_hbm, table_ref),
+        (count_hbm, count_ref),
     ]
+    for j in range(width // LANES):
+        tile = docs_hbm.at[pl.ds(0, head), pl.ds(j * LANES, LANES)]
+        pairs.append((tile, top_ref.at[pl.ds(j * head, head)]))
+    fetches = [pltpu.make_async_copy(*pair, done.at[k]) for k, pair in enumerate(pairs)]
     for fetch in fetches:
         fetch.start()
-    for fetch in fetches[:3]:
+    for fetch in fetches:
         fetch.wait()
+
+
+def fetch(label_slot, pos_ids, pos_count, embeddings, head):
+    docs, slots = pos_ids.shape
+    width = embeddings.shape[1]
+    lines = label_slot.shape[0] // LANES
+    table = label_slot.reshape(lines, LANES)
+    inputs = (pos_ids.T, pos_count.reshape(1, docs), table, embeddings)
+    return pl.pallas_call(
+        fetch_kernel,
+        in_specs=[pl.BlockSpec(memory_space=pltpu.HBM)] * 4,
+        out_specs=[pl.BlockSpec(memory_space=pltpu.VMEM)] * 5,
+        out_shape=[
+            jax.ShapeDtypeStruct((docs - head, width), jnp.bfloat16),
+            jax.ShapeDtypeStruct((width // LANES * head, LANES), jnp.bfloat16),
+            jax.ShapeDtypeStruct((slots, docs), jnp.int32),
+            jax.ShapeDtypeStruct((1, docs), jnp.int32),
+            jax.ShapeDtypeStruct((lines, LANES), jnp.int32),
+        ],
+        scratch_shapes=[pltpu.SemaphoreType.DMA((4 + width // LANES,))],
+        compiler_params=pltpu.CompilerParams(vmem_limit_bytes=VMEM_LIMIT),
+        name="fetch",
+    )(*(pltpu.with_memory_space_constraint(x, pltpu.HBM) for x in inputs))
+
+
+def prepare_kernel(bits, top_ref, ids_ref, count_ref, table_ref, a_ref):
+    slots, docs = ids_ref.shape
+    top = top_ref.shape[0]
+    a_ref[:top, :] = top_ref[...]
     pairs = table_ref.shape[0] // 2
     starts = range(0, docs, LANES)
     ids = [ids_ref[:, start : start + LANES] for start in starts]
@@ -94,36 +116,21 @@
         low = (LANES + (row & (LANES - 1))).astype(jnp.float32)
         code = power_of_two(row >> 7, bits, low * 2.0**-64, 1)
         code = jnp.where(place < count_ref[:, start : start + LANES], code, 0.0)
-        first = len(tiles) * head + i * slots
+        first = top + i * slots
         a_ref[first : first + slots, :] = code.astype(jnp.bfloat16)
-    for fetch in fetches[3:]:
-        fetch.wait()
-
-
-def prepare(label_slot, pos_ids, pos_count, embeddings, head):
-    docs, slots = pos_ids.shape
-    width = embeddings.shape[1]
-    tall = width // LANES * head + slots * (docs // LANES)
-    lines = label_slot.shape[0] // LANES
-    table = label_slot.reshape(lines, LANES)
-    inputs = (pos_ids.T, pos_count.reshape(1, docs), table, embeddings)
-    return pl.pallas_call(
-        functools.partial(prepare_kernel, (lines - 1).bit_length()),
-        in_specs=[pl.BlockSpec(memory_space=pltpu.HBM)] * 4,
-        out_specs=[pl.BlockSpec(memory_space=pltpu.VMEM)] * 2,
-        out_shape=[
-            jax.ShapeDtypeStruct((tall, LANES), jnp.bfloat16),
-            jax.ShapeDtypeStruct((docs - head, width), jnp.bfloat16),
-        ],
-        scratch_shapes=[
-            pltpu.VMEM((slots, docs), jnp.int32),
-            pltpu.VMEM((1, docs), jnp.int32),
-            pltpu.VMEM((lines, LANES), jnp.int32),
-            pltpu.SemaphoreType.DMA((4 + width // LANES,)),
-        ],
+
+
+def prepare(top, ids, count, table):
+    slots, docs = ids.shape
+    vmem = pl.BlockSpec(memory_space=pltpu.VMEM)
+    return pl.pallas_call(
+        functools.partial(prepare_kernel, (table.shape[0] - 1).bit_length()),
+        in_specs=[vmem] * 4,
+        out_specs=vmem,
+        out_shape=jax.ShapeDtypeStruct((top.shape[0] + slots * docs // LANES, LANES), jnp.bfloat16),
         compiler_params=pltpu.CompilerParams(vmem_limit_bytes=VMEM_LIMIT),
         name="prepare",
-    )(*(pltpu.with_memory_space_constraint(x, pltpu.HBM) for x in inputs))
+    )(top, ids, count, table)
 
 
 def cast_kernel(weights_ref, cast_ref):
@@ -312,8 +319,10 @@
     def send(value, pairs):
         return lax.ppermute(value, "blk", pairs)
 
-    a, b = prepare(label_slot, pos_ids, pos_count, embeddings, head)
-    coming = {"up_b": send(b, up), "down_a": send(a, down)}
+    b, *rest = fetch(label_slot, pos_ids, pos_count, embeddings, head)
+    coming = {"up_b": send(b, up)}
+    a = prepare(*rest)
+    coming["down_a"] = send(a, down)
     coming |= {"up_a": send(a, up), "down_b": send(b, down)}
     mine = halved_cast(weights)
     cast = [mine, send(mine, swap)]

time: 40.8 us -> 40.7 us (level)
  starting transfers between devices: 17.5 us -> 21.9 us
  waiting for transfers between devices: 9.77 us -> 6.15 us
  local copies, waits for them, and re-layouts: 1.14 us -> 0.01 us
    ppermute x18, starting transfers between devices: 17.5 us -> 21.9 us  [send(): return lax.ppermute(value, 'blk', pairs)]
    ppermute x18, waiting for transfers between devices: 9.77 us -> 6.15 us  [send(): return lax.ppermute(value, 'blk', pairs)]
    unnamed x8 -> x6, local copies, waits for them, and re-layouts: 1.14 us -> 0.01 us
    pallas_call x1 -> x2, Pallas kernels: 1.31 us -> 1.58 us  [the longest x1 1.14 us: fetch(): pl.pallas_call(fetch_kernel, in_specs=[pl.BlockSpec(memory_space=pltpu.HB...]
  transfers between devices with their start and end apart: 18 -> 18, of which waited for: 11 -> 10; matrix products, arithmetic and copies ran while one was open for 0% -> 0% of each run, Pallas kernels for 19% -> 20%
where the time goes in v17:
time: 40.7 us; the launch traced here: 40.5 us
  starting transfers between devices  21.9 us (54%)
  Pallas kernels  11.7 us (29%)
  waiting for transfers between devices  6.15 us (15%)
  between operations  0.81 us (2%)
    ppermute x18, starting transfers between devices, send(): return lax.ppermute(value, 'blk', pairs)  21.9 us
    pallas_call x8, Pallas kernels, add_gradient(): pl.pallas_call(functools.partial(gradient_kernel, bits, owners, not sums)...  7.7 us
    ppermute x18, waiting for transfers between devices, send(): return lax.ppermute(value, 'blk', pairs)  6.15 us
    pallas_call x1, Pallas kernels, finish(): pl.pallas_call(functools.partial(finish_kernel, bits), in_specs=[pl.Block...  2.35 us
    pallas_call x1, Pallas kernels, fetch(): pl.pallas_call(fetch_kernel, in_specs=[pl.BlockSpec(memory_space=pltpu.HB...  1.14 us
  transfers between devices with their start and end apart: 18, of which 10 were waited for; matrix products, arithmetic and copies ran while one was open for 0% of the time, Pallas kernels for 20%

profile of v17, /device:TPU:0, one launch (start us, length us, event | category | flops | bytes accessed | tf_op | source)
XLA Modules:
  0.0 40.5 jit_solution(7574780991092311302)
XLA Ops:
  0.6 1.1 %fetch.1 = (bf16[128,768]{1,0:T(8,128)(2,1)S(1)}, bf16[768,128]{1,0:T(8,128)(2,1)S(1)}, s32[32,256]{1,0:T(8,128)S(1)}, s32[1,256]{1,0:T(1,128)S(1)}, s32[32,128]{1,0:T(8,128)S(1)}) custom-call(s32[32,256]{1,0:T(8,128)} %bitcast.3, s32[1,256]{1,0:T(1,128)} %bitcast.5, s32[32,128]{1,0:T(8,128)} %bitcast.4, bf16[256,768]{1,0:T(8,128)(2,1)} %docs_hbm.1), custom_call_target="tpu_custom_call" | custom-call | tf_op jit(solution)/shard_map/fetch/pallas_call | solution.py:72
  1.8 3.1 %collective-permute-start.1 = (bf16[128,768]{1,0:T(8,128)(2,1)S(1)}, bf16[128,768]{1,0:T(8,128)(2,1)S(1)}, u32[]{:S(2)}, u32[]{:S(2)}) collective-permute-start(bf16[128,768]{1,0:T(8,128)(2,1)S(1)} %get-tuple-element.122.b_ref), channel_id=1, source_target_pairs={{0,4},{5,1},{4,8},{9,5},{8,12},{13,9},{12,14},{15,13},{14,10},{11,... | collective-permute-start | bytes 589832 | tf_op jit(solution)/shard_map/ppermute | solution.py:320
  4.9 0.4 %prepare.1.a_ref = bf16[832,128]{1,0:T(8,128)(2,1)S(1)} custom-call(bf16[768,128]{1,0:T(8,128)(2,1)S(1)} %get-tuple-element.90.top_ref, s32[32,256]{1,0:T(8,128)S(1)} %get-tuple-element.91.ids_ref, s32[1,256]{1,0:T(1,128)S(1)} %get-tuple-element.92.count_ref, s32[32,128]{1,0:T(8,128)S(1)} %get-tuple-element.93.table_ref), custom_call_target="tpu_custom_call" | custom-call | tf_op jit(solution)/shard_map/prepare/pallas_call | solution.py:126
  5.4 2.0 %collective-permute-start.5 = (bf16[832,128]{1,0:T(8,128)(2,1)S(1)}, bf16[832,128]{1,0:T(8,128)(2,1)S(1)}, u32[]{:S(2)}, u32[]{:S(2)}) collective-permute-start(bf16[832,128]{1,0:T(8,128)(2,1)S(1)} %prepare.1.a_ref), channel_id=1, source_target_pairs={{0,4},{5,1},{4,8},{9,5},{8,12},{13,9},{12,14},{15,13},{14,10},{11,... | collective-permute-start | bytes 638984 | tf_op jit(solution)/shard_map/ppermute | solution.py:320
  7.5 0.5 %collective-permute-start.4 = (bf16[128,768]{1,0:T(8,128)(2,1)S(1)}, bf16[128,768]{1,0:T(8,128)(2,1)S(1)}, u32[]{:S(2)}, u32[]{:S(2)}) collective-permute-start(bf16[128,768]{1,0:T(8,128)(2,1)S(1)} %get-tuple-element.122.b_ref), channel_id=1, source_target_pairs={{4,0},{1,5},{8,4},{5,9},{12,8},{9,13},{14,12},{13,15},{10,14},{15,... | collective-permute-start | bytes 589832 | tf_op jit(solution)/shard_map/ppermute | solution.py:320
  8.0 1.7 %collective-permute-done.1.b_ref = bf16[128,768]{1,0:T(8,128)(2,1)S(1)} collective-permute-done((bf16[128,768]{1,0:T(8,128)(2,1)S(1)}, bf16[128,768]{1,0:T(8,128)(2,1)S(1)}, u32[]{:S(2)}, u32[]{:S(2)}) %collective-permute-start.1) | collective-permute-done | bytes 196640 | tf_op jit(solution)/shard_map/ppermute | solution.py:320
  9.7 2.5 %collective-permute-start.3 = (bf16[128,768]{1,0:T(8,128)(2,1)S(1)}, bf16[128,768]{1,0:T(8,128)(2,1)S(1)}, u32[]{:S(2)}, u32[]{:S(2)}) collective-permute-start(bf16[128,768]{1,0:T(8,128)(2,1)S(1)} %collective-permute-done.1.b_ref), channel_id=1, source_target_pairs={{0,4},{5,1},{4,8},{9,5},{8,12},{13,9},{12,14},{15,13},{14,10},{11,... | collective-permute-start | bytes 589832 | tf_op jit(solution)/shard_map/ppermute | solution.py:320
  12.5 1.1 %collective-permute-start.2 = (bf16[832,128]{1,0:T(8,128)(2,1)S(1)}, bf16[832,128]{1,0:T(8,128)(2,1)S(1)}, u32[]{:S(2)}, u32[]{:S(2)}) collective-permute-start(bf16[832,128]{1,0:T(8,128)(2,1)S(1)} %collective-permute-done.a_ref), channel_id=1, source_target_pairs={{4,0},{1,5},{8,4},{5,9},{12,8},{9,13},{14,12},{13,15},{10,14},{15,... | collective-permute-start | bytes 638984 | tf_op jit(solution)/shard_map/ppermute | solution.py:320
  13.6 0.6 %collective-permute-done.5.a_ref = bf16[832,128]{1,0:T(8,128)(2,1)S(1)} collective-permute-done((bf16[832,128]{1,0:T(8,128)(2,1)S(1)}, bf16[832,128]{1,0:T(8,128)(2,1)S(1)}, u32[]{:S(2)}, u32[]{:S(2)}) %collective-permute-start.5) | collective-permute-done | bytes 213024 | tf_op jit(solution)/shard_map/ppermute | solution.py:320
  14.2 2.5 %collective-permute-start.9 = (bf16[832,128]{1,0:T(8,128)(2,1)S(1)}, bf16[832,128]{1,0:T(8,128)(2,1)S(1)}, u32[]{:S(2)}, u32[]{:S(2)}) collective-permute-start(bf16[832,128]{1,0:T(8,128)(2,1)S(1)} %collective-permute-done.5.a_ref), channel_id=1, source_target_pairs={{0,4},{5,1},{4,8},{9,5},{8,12},{13,9},{12,14},{15,13},{14,10},{11,... | collective-permute-start | bytes 638984 | tf_op jit(solution)/shard_map/ppermute | solution.py:320
  16.7 1.1 %collective-permute-start.8 = (bf16[128,768]{1,0:T(8,128)(2,1)S(1)}, bf16[128,768]{1,0:T(8,128)(2,1)S(1)}, u32[]{:S(2)}, u32[]{:S(2)}) collective-permute-start(bf16[128,768]{1,0:T(8,128)(2,1)S(1)} %collective-permute-done.4.b_ref), channel_id=1, source_target_pairs={{4,0},{1,5},{8,4},{5,9},{12,8},{9,13},{14,12},{13,15},{10,14},{15,... | collective-permute-start | bytes 589832 | tf_op jit(solution)/shard_map/ppermute | solution.py:320
  17.8 0.7 %collective-permute-done.3.b_ref = bf16[128,768]{1,0:T(8,128)(2,1)S(1)} collective-permute-done((bf16[128,768]{1,0:T(8,128)(2,1)S(1)}, bf16[128,768]{1,0:T(8,128)(2,1)S(1)}, u32[]{:S(2)}, u32[]{:S(2)}) %collective-permute-start.3) | collective-permute-done | bytes 196640 | tf_op jit(solution)/shard_map/ppermute | solution.py:320
  18.4 2.5 %collective-permute-start.7 = (bf16[128,768]{1,0:T(8,128)(2,1)S(1)}, bf16[128,768]{1,0:T(8,128)(2,1)S(1)}, u32[]{:S(2)}, u32[]{:S(2)}) collective-permute-start(bf16[128,768]{1,0:T(8,128)(2,1)S(1)} %collective-permute-done.3.b_ref), channel_id=1, source_target_pairs={{0,4},{5,1},{4,8},{9,5},{8,12},{13,9},{12,14},{15,13},{14,10},{11,... | collective-permute-start | bytes 589832 | tf_op jit(solution)/shard_map/ppermute | solution.py:320
  20.9 0.3 collective-permute-done.2.a_ref
  21.2 1.1 %collective-permute-start.6 = (bf16[832,128]{1,0:T(8,128)(2,1)S(1)}, bf16[832,128]{1,0:T(8,128)(2,1)S(1)}, u32[]{:S(2)}, u32[]{:S(2)}) collective-permute-start(bf16[832,128]{1,0:T(8,128)(2,1)S(1)} %collective-permute-done.2.a_ref), channel_id=1, source_target_pairs={{4,0},{1,5},{8,4},{5,9},{12,8},{9,13},{14,12},{13,15},{10,14},{15,... | collective-permute-start | bytes 638984 | tf_op jit(solution)/shard_map/ppermute | solution.py:320
  22.3 1.0 %gradient.8 = (f32[256,768]{1,0:T(8,128)S(1)}, f32[256,768]{1,0:T(8,128)S(1)}) custom-call(bf16[832,128]{1,0:T(8,128)(2,1)S(1)} %prepare.1.a_ref, bf16[128,768]{1,0:T(8,128)(2,1)S(1)} %get-tuple-element.122.b_ref, bf16[256,768]{1,0:T(8,128)(2,1)S(1)} %cast.1.refs_0_.cast_ref, bf16[256,768]{1,0:T(8,128)(2,1)S(1)} %collective-permute-done.10.refs_1_), custom_call_target="tpu_custom_call" | custom-call | flops 200000000 | bytes 1000000 | tf_op jit(solution)/shard_map/gradient/pallas_call | solution.py:209
  23.3 2.1 %collective-permute-start.14 = (bf16[832,128]{1,0:T(8,128)(2,1)S(1)}, bf16[832,128]{1,0:T(8,128)(2,1)S(1)}, u32[]{:S(2)}, u32[]{:S(2)}) collective-permute-start(bf16[832,128]{1,0:T(8,128)(2,1)S(1)} %collective-permute-done.9.a_ref), channel_id=1, source_target_pairs={{0,4},{5,1},{4,8},{9,5},{8,12},{13,9},{12,14},{15,13},{14,10},{11,... | collective-permute-start | bytes 638984 | tf_op jit(solution)/shard_map/ppermute | solution.py:320
  25.5 1.0 %gradient.9 = (f32[256,768]{1,0:T(8,128)S(1)}, f32[256,768]{1,0:T(8,128)S(1)}) custom-call(bf16[832,128]{1,0:T(8,128)(2,1)S(1)} %collective-permute-done.5.a_ref, bf16[128,768]{1,0:T(8,128)(2,1)S(1)} %collective-permute-done.1.b_ref, bf16[256,768]{1,0:T(8,128)(2,1)S(1)} %cast.1.refs_0_.cast_ref, ...), custom_call_target="tpu_custom_call", output_to_operand_aliasing={{0}: (4, {}), {1}: (5, {})} | custom-call | flops 200000000 | bytes 1000000 | tf_op jit(solution)/shard_map/gradient/pallas_call | solution.py:209
  26.6 0.6 %collective-permute-done.7.b_ref = bf16[128,768]{1,0:T(8,128)(2,1)S(1)} collective-permute-done((bf16[128,768]{1,0:T(8,128)(2,1)S(1)}, bf16[128,768]{1,0:T(8,128)(2,1)S(1)}, u32[]{:S(2)}, u32[]{:S(2)}) %collective-permute-start.7) | collective-permute-done | bytes 196640 | tf_op jit(solution)/shard_map/ppermute | solution.py:320
  27.2 2.5 %collective-permute-start.12 = (bf16[128,768]{1,0:T(8,128)(2,1)S(1)}, bf16[128,768]{1,0:T(8,128)(2,1)S(1)}, u32[]{:S(2)}, u32[]{:S(2)}) collective-permute-start(bf16[128,768]{1,0:T(8,128)(2,1)S(1)} %collective-permute-done.7.b_ref), channel_id=1, source_target_pairs={{0,4},{5,1},{4,8},{9,5},{8,12},{13,9},{12,14},{15,13},{14,10},{11,... | collective-permute-start | bytes 589832 | tf_op jit(solution)/shard_map/ppermute | solution.py:320
  29.7 1.0 %gradient.10 = (f32[256,768]{1,0:T(8,128)S(1)}, f32[256,768]{1,0:T(8,128)S(1)}) custom-call(bf16[832,128]{1,0:T(8,128)(2,1)S(1)} %collective-permute-done.a_ref, bf16[128,768]{1,0:T(8,128)(2,1)S(1)} %collective-permute-done.4.b_ref, bf16[256,768]{1,0:T(8,128)(2,1)S(1)} %cast.1.refs_0_.cast_ref, ...), custom_call_target="tpu_custom_call", output_to_operand_aliasing={{0}: (4, {}), {1}: (5, {})} | custom-call | flops 1000000000 | bytes 1000000 | tf_op jit(solution)/shard_map/gradient/pallas_call | solution.py:209
  30.7 0.4 %collective-permute-start.11 = (bf16[832,128]{1,0:T(8,128)(2,1)S(1)}, bf16[832,128]{1,0:T(8,128)(2,1)S(1)}, u32[]{:S(2)}, u32[]{:S(2)}) collective-permute-start(bf16[832,128]{1,0:T(8,128)(2,1)S(1)} %collective-permute-done.6.a_ref), channel_id=1, source_target_pairs={{4,0},{1,5},{8,4},{5,9},{12,8},{9,13},{14,12},{13,15},{10,14},{15,... | collective-permute-start | bytes 638984 | tf_op jit(solution)/shard_map/ppermute | solution.py:320
  31.1 1.0 %gradient.11 = (f32[256,768]{1,0:T(8,128)S(1)}, f32[256,768]{1,0:T(8,128)S(1)}) custom-call(bf16[832,128]{1,0:T(8,128)(2,1)S(1)} %collective-permute-done.9.a_ref, bf16[128,768]{1,0:T(8,128)(2,1)S(1)} %collective-permute-done.3.b_ref, bf16[256,768]{1,0:T(8,128)(2,1)S(1)} %cast.1.refs_0_.cast_ref, ...), custom_call_target="tpu_custom_call", output_to_operand_aliasing={{0}: (4, {}), {1}: (5, {})} | custom-call | flops 1000000000 | bytes 1000000 | tf_op jit(solution)/shard_map/gradient/pallas_call | solution.py:209
  32.1 1.0 %gradient.12 = (f32[256,768]{1,0:T(8,128)S(1)}, f32[256,768]{1,0:T(8,128)S(1)}) custom-call(bf16[832,128]{1,0:T(8,128)(2,1)S(1)} %collective-permute-done.2.a_ref, bf16[128,768]{1,0:T(8,128)(2,1)S(1)} %collective-permute-done.8.b_ref, bf16[256,768]{1,0:T(8,128)(2,1)S(1)} %cast.1.refs_0_.cast_ref, ...), custom_call_target="tpu_custom_call", output_to_operand_aliasing={{0}: (4, {}), {1}: (5, {})} | custom-call | flops 1000000000 | bytes 1000000 | tf_op jit(solution)/shard_map/gradient/pallas_call | solution.py:209
  33.2 1.0 %gradient.13 = (f32[256,768]{1,0:T(8,128)S(1)}, f32[256,768]{1,0:T(8,128)S(1)}) custom-call(bf16[832,128]{1,0:T(8,128)(2,1)S(1)} %collective-permute-done.14.a_ref, bf16[128,768]{1,0:T(8,128)(2,1)S(1)} %collective-permute-done.7.b_ref, bf16[256,768]{1,0:T(8,128)(2,1)S(1)} %cast.1.refs_0_.cast_ref, ...), custom_call_target="tpu_custom_call", output_to_operand_aliasing={{0}: (4, {}), {1}: (5, {})} | custom-call | flops 1000000000 | bytes 1000000 | tf_op jit(solution)/shard_map/gradient/pallas_call | solution.py:209
  34.2 1.0 %gradient.14 = (f32[256,768]{1,0:T(8,128)S(1)}, f32[256,768]{1,0:T(8,128)S(1)}) custom-call(bf16[832,128]{1,0:T(8,128)(2,1)S(1)} %collective-permute-done.6.a_ref, bf16[128,768]{1,0:T(8,128)(2,1)S(1)} %collective-permute-done.13.b_ref, bf16[256,768]{1,0:T(8,128)(2,1)S(1)} %cast.1.refs_0_.cast_ref, ...), custom_call_target="tpu_custom_call", output_to_operand_aliasing={{0}: (4, {}), {1}: (5, {})} | custom-call | flops 1000000000 | bytes 1000000 | tf_op jit(solution)/shard_map/gradient/pallas_call | solution.py:209
  35.3 0.7 %collective-permute-done.12.b_ref = bf16[128,768]{1,0:T(8,128)(2,1)S(1)} collective-permute-done((bf16[128,768]{1,0:T(8,128)(2,1)S(1)}, bf16[128,768]{1,0:T(8,128)(2,1)S(1)}, u32[]{:S(2)}, u32[]{:S(2)}) %collective-permute-start.12) | collective-permute-done | bytes 196640 | tf_op jit(solution)/shard_map/ppermute | solution.py:320
  36.0 0.6 %collective-permute-done.11.a_ref = bf16[832,128]{1,0:T(8,128)(2,1)S(1)} collective-permute-done((bf16[832,128]{1,0:T(8,128)(2,1)S(1)}, bf16[832,128]{1,0:T(8,128)(2,1)S(1)}, u32[]{:S(2)}, u32[]{:S(2)}) %collective-permute-start.11) | collective-permute-done | bytes 213024 | tf_op jit(solution)/shard_map/ppermute | solution.py:320
  36.9 0.7 %gradient.15.sum_ref = f32[256,768]{1,0:T(8,128)S(1)} custom-call(bf16[832,128]{1,0:T(8,128)(2,1)S(1)} %collective-permute-done.11.a_ref, bf16[128,768]{1,0:T(8,128)(2,1)S(1)} %collective-permute-done.12.b_ref, bf16[256,768]{1,0:T(8,128)(2,1)S(1)} %cast.1.refs_0_.cast_ref, f32[256,768]{1,0:T(8,128)S(1)} %get-tuple-element.175.refs_1_), custom_call_target="tpu_custom_call", output_to_operand_aliasing={{}: (3, {})} | custom-call | flops 10000000000 | bytes 1000000 | tf_op jit(solution)/shard_map/gradient/pallas_call | solution.py:209
  37.6 0.3 collective-permute-done.16.b_ref
  37.8 0.3 collective-permute-done.15.a_ref
  38.2 2.3 %finish.1 = (f32[256,768]{1,0:T(8,128)}, f32[256,768]{1,0:T(8,128)}, f32[256,768]{1,0:T(8,128)}) custom-call(bf16[832,128]{1,0:T(8,128)(2,1)S(1)} %collective-permute-done.15.a_ref, bf16[128,768]{1,0:T(8,128)(2,1)S(1)} %collective-permute-done.16.b_ref, bf16[256,768]{1,0:T(8,128)(2,1)S(1)} %cast.1.refs_0_.cast_ref, f32[256,768]{1,0:T(8,128)S(1)} %gradient.15.sum_ref, ...), custom_call_target="tpu_custom_call" | custom-call | flops 10000000000 | bytes 1000000 | tf_op jit(solution)/shard_map/finish/pallas_call | solution.py:266
  (22 shorter events, 0.9 us)
Async XLA Ops:
  0.6 6.8 %copy-start = (f32[256,768]{1,0:T(8,128)S(1)}, f32[256,768]{1,0:T(8,128)}, u32[]{:S(2)}) copy-start(f32[256,768]{1,0:T(8,128)} %weights_ref.3) | copy-start | bytes 2359300
  1.8 7.9 %collective-permute-start.1 = (bf16[128,768]{1,0:T(8,128)(2,1)S(1)}, bf16[128,768]{1,0:T(8,128)(2,1)S(1)}, u32[]{:S(2)}, u32[]{:S(2)}) collective-permute-start(bf16[128,768]{1,0:T(8,128)(2,1)S(1)} %get-tuple-element.122.b_ref), channel_id=1, source_target_pairs={{0,4},{5,1},{4,8},{9,5},{8,12},{13,9},{12,14},{15,13},{14,10},{11,... | collective-permute-start | bytes 589832 | tf_op jit(solution)/shard_map/ppermute | solution.py:320
  5.3 7.2 %collective-permute-start = (bf16[832,128]{1,0:T(8,128)(2,1)S(1)}, bf16[832,128]{1,0:T(8,128)(2,1)S(1)}, u32[]{:S(2)}, u32[]{:S(2)}) collective-permute-start(bf16[832,128]{1,0:T(8,128)(2,1)S(1)} %prepare.1.a_ref), channel_id=1, source_target_pairs={{4,0},{1,5},{8,4},{5,9},{12,8},{9,13},{14,12},{13,15},{10,14},{15,... | collective-permute-start | bytes 638984 | tf_op jit(solution)/shard_map/ppermute | solution.py:320
  5.4 8.8 %collective-permute-start.5 = (bf16[832,128]{1,0:T(8,128)(2,1)S(1)}, bf16[832,128]{1,0:T(8,128)(2,1)S(1)}, u32[]{:S(2)}, u32[]{:S(2)}) collective-permute-start(bf16[832,128]{1,0:T(8,128)(2,1)S(1)} %prepare.1.a_ref), channel_id=1, source_target_pairs={{0,4},{5,1},{4,8},{9,5},{8,12},{13,9},{12,14},{15,13},{14,10},{11,... | collective-permute-start | bytes 638984 | tf_op jit(solution)/shard_map/ppermute | solution.py:320
  7.5 14.9 %collective-permute-start.10 = (bf16[256,768]{1,0:T(8,128)(2,1)S(1)}, bf16[256,768]{1,0:T(8,128)(2,1)S(1)}, u32[]{:S(2)}, u32[]{:S(2)}) collective-permute-start(bf16[256,768]{1,0:T(8,128)(2,1)S(1)} %cast.1.refs_0_.cast_ref), channel_id=1, source_target_pairs={{0,1},{1,0},{2,3},{3,2},{4,5},{5,4},{6,7},{7,6},{8,9},{9,8},{10,11... | collective-permute-start | bytes 1179656 | tf_op jit(solution)/shard_map/ppermute | solution.py:320
  7.5 9.2 %collective-permute-start.4 = (bf16[128,768]{1,0:T(8,128)(2,1)S(1)}, bf16[128,768]{1,0:T(8,128)(2,1)S(1)}, u32[]{:S(2)}, u32[]{:S(2)}) collective-permute-start(bf16[128,768]{1,0:T(8,128)(2,1)S(1)} %get-tuple-element.122.b_ref), channel_id=1, source_target_pairs={{4,0},{1,5},{8,4},{5,9},{12,8},{9,13},{14,12},{13,15},{10,14},{15,... | collective-permute-start | bytes 589832 | tf_op jit(solution)/shard_map/ppermute | solution.py:320
  9.7 8.7 %collective-permute-start.3 = (bf16[128,768]{1,0:T(8,128)(2,1)S(1)}, bf16[128,768]{1,0:T(8,128)(2,1)S(1)}, u32[]{:S(2)}, u32[]{:S(2)}) collective-permute-start(bf16[128,768]{1,0:T(8,128)(2,1)S(1)} %collective-permute-done.1.b_ref), channel_id=1, source_target_pairs={{0,4},{5,1},{4,8},{9,5},{8,12},{13,9},{12,14},{15,13},{14,10},{11,... | collective-permute-start | bytes 589832 | tf_op jit(solution)/shard_map/ppermute | solution.py:320
  12.5 8.8 %collective-permute-start.2 = (bf16[832,128]{1,0:T(8,128)(2,1)S(1)}, bf16[832,128]{1,0:T(8,128)(2,1)S(1)}, u32[]{:S(2)}, u32[]{:S(2)}) collective-permute-start(bf16[832,128]{1,0:T(8,128)(2,1)S(1)} %collective-permute-done.a_ref), channel_id=1, source_target_pairs={{4,0},{1,5},{8,4},{5,9},{12,8},{9,13},{14,12},{13,15},{10,14},{15,... | collective-permute-start | bytes 638984 | tf_op jit(solution)/shard_map/ppermute | solution.py:320
  14.2 9.1 %collective-permute-start.9 = (bf16[832,128]{1,0:T(8,128)(2,1)S(1)}, bf16[832,128]{1,0:T(8,128)(2,1)S(1)}, u32[]{:S(2)}, u32[]{:S(2)}) collective-permute-start(bf16[832,128]{1,0:T(8,128)(2,1)S(1)} %collective-permute-done.5.a_ref), channel_id=1, source_target_pairs={{0,4},{5,1},{4,8},{9,5},{8,12},{13,9},{12,14},{15,13},{14,10},{11,... | collective-permute-start | bytes 638984 | tf_op jit(solution)/shard_map/ppermute | solution.py:320
  16.7 9.8 %collective-permute-start.8 = (bf16[128,768]{1,0:T(8,128)(2,1)S(1)}, bf16[128,768]{1,0:T(8,128)(2,1)S(1)}, u32[]{:S(2)}, u32[]{:S(2)}) collective-permute-start(bf16[128,768]{1,0:T(8,128)(2,1)S(1)} %collective-permute-done.4.b_ref), channel_id=1, source_target_pairs={{4,0},{1,5},{8,4},{5,9},{12,8},{9,13},{14,12},{13,15},{10,14},{15,... | collective-permute-start | bytes 589832 | tf_op jit(solution)/shard_map/ppermute | solution.py:320
  18.4 8.8 %collective-permute-start.7 = (bf16[128,768]{1,0:T(8,128)(2,1)S(1)}, bf16[128,768]{1,0:T(8,128)(2,1)S(1)}, u32[]{:S(2)}, u32[]{:S(2)}) collective-permute-start(bf16[128,768]{1,0:T(8,128)(2,1)S(1)} %collective-permute-done.3.b_ref), channel_id=1, source_target_pairs={{0,4},{5,1},{4,8},{9,5},{8,12},{13,9},{12,14},{15,13},{14,10},{11,... | collective-permute-start | bytes 589832 | tf_op jit(solution)/shard_map/ppermute | solution.py:320
  21.2 9.5 %collective-permute-start.6 = (bf16[832,128]{1,0:T(8,128)(2,1)S(1)}, bf16[832,128]{1,0:T(8,128)(2,1)S(1)}, u32[]{:S(2)}, u32[]{:S(2)}) collective-permute-start(bf16[832,128]{1,0:T(8,128)(2,1)S(1)} %collective-permute-done.2.a_ref), channel_id=1, source_target_pairs={{4,0},{1,5},{8,4},{5,9},{12,8},{9,13},{14,12},{13,15},{10,14},{15,... | collective-permute-start | bytes 638984 | tf_op jit(solution)/shard_map/ppermute | solution.py:320
  23.3 9.8 %collective-permute-start.14 = (bf16[832,128]{1,0:T(8,128)(2,1)S(1)}, bf16[832,128]{1,0:T(8,128)(2,1)S(1)}, u32[]{:S(2)}, u32[]{:S(2)}) collective-permute-start(bf16[832,128]{1,0:T(8,128)(2,1)S(1)} %collective-permute-done.9.a_ref), channel_id=1, source_target_pairs={{0,4},{5,1},{4,8},{9,5},{8,12},{13,9},{12,14},{15,13},{14,10},{11,... | collective-permute-start | bytes 638984 | tf_op jit(solution)/shard_map/ppermute | solution.py:320
  26.5 7.7 %collective-permute-start.13 = (bf16[128,768]{1,0:T(8,128)(2,1)S(1)}, bf16[128,768]{1,0:T(8,128)(2,1)S(1)}, u32[]{:S(2)}, u32[]{:S(2)}) collective-permute-start(bf16[128,768]{1,0:T(8,128)(2,1)S(1)} %collective-permute-done.8.b_ref), channel_id=1, source_target_pairs={{4,0},{1,5},{8,4},{5,9},{12,8},{9,13},{14,12},{13,15},{10,14},{15,... | collective-permute-start | bytes 589832 | tf_op jit(solution)/shard_map/ppermute | solution.py:320
  27.2 8.8 %collective-permute-start.12 = (bf16[128,768]{1,0:T(8,128)(2,1)S(1)}, bf16[128,768]{1,0:T(8,128)(2,1)S(1)}, u32[]{:S(2)}, u32[]{:S(2)}) collective-permute-start(bf16[128,768]{1,0:T(8,128)(2,1)S(1)} %collective-permute-done.7.b_ref), channel_id=1, source_target_pairs={{0,4},{5,1},{4,8},{9,5},{8,12},{13,9},{12,14},{15,13},{14,10},{11,... | collective-permute-start | bytes 589832 | tf_op jit(solution)/shard_map/ppermute | solution.py:320
  30.7 5.9 %collective-permute-start.11 = (bf16[832,128]{1,0:T(8,128)(2,1)S(1)}, bf16[832,128]{1,0:T(8,128)(2,1)S(1)}, u32[]{:S(2)}, u32[]{:S(2)}) collective-permute-start(bf16[832,128]{1,0:T(8,128)(2,1)S(1)} %collective-permute-done.6.a_ref), channel_id=1, source_target_pairs={{4,0},{1,5},{8,4},{5,9},{12,8},{9,13},{14,12},{13,15},{10,14},{15,... | collective-permute-start | bytes 638984 | tf_op jit(solution)/shard_map/ppermute | solution.py:320
  35.2 2.9 %collective-permute-start.17 = (f32[256,768]{1,0:T(8,128)S(1)}, f32[256,768]{1,0:T(8,128)S(1)}, u32[]{:S(2)}, u32[]{:S(2)}) collective-permute-start(f32[256,768]{1,0:T(8,128)S(1)} %get-tuple-element.176), channel_id=1, source_target_pairs={{0,1},{1,0},{2,3},{3,2},{4,5},{5,4},{6,7},{7,6},{8,9},{9,8},{10,11... | collective-permute-start | bytes 2359304 | tf_op jit(solution)/shard_map/ppermute | solution.py:320
  36.0 2.2 %copy-start.1 = (f32[256,768]{1,0:T(8,128)S(1)}, f32[256,768]{1,0:T(8,128)}, u32[]{:S(2)}) copy-start(f32[256,768]{1,0:T(8,128)} %first_ref.1) | copy-start | bytes 2359300
  36.0 2.2 %copy-start.2 = (f32[256,768]{1,0:T(8,128)S(1)}, f32[256,768]{1,0:T(8,128)}, u32[]{:S(2)}) copy-start(f32[256,768]{1,0:T(8,128)} %second_ref.1) | copy-start | bytes 2359300
  36.0 1.9 %collective-permute-start.16 = (bf16[128,768]{1,0:T(8,128)(2,1)S(1)}, bf16[128,768]{1,0:T(8,128)(2,1)S(1)}, u32[]{:S(2)}, u32[]{:S(2)}) collective-permute-start(bf16[128,768]{1,0:T(8,128)(2,1)S(1)} %collective-permute-done.12.b_ref), channel_id=1, source_target_pairs={{0,1},{1,0},{2,3},{3,2},{4,5},{5,4},{6,7},{7,6},{8,9},{9,8},{10,11... | collective-permute-start | bytes 589832 | tf_op jit(solution)/shard_map/ppermute | solution.py:320
  36.6 1.5 %collective-permute-start.15 = (bf16[832,128]{1,0:T(8,128)(2,1)S(1)}, bf16[832,128]{1,0:T(8,128)(2,1)S(1)}, u32[]{:S(2)}, u32[]{:S(2)}) collective-permute-start(bf16[832,128]{1,0:T(8,128)(2,1)S(1)} %collective-permute-done.11.a_ref), channel_id=1, source_target_pairs={{0,1},{1,0},{2,3},{3,2},{4,5},{5,4},{6,7},{7,6},{8,9},{9,8},{10,11... | collective-permute-start | bytes 638984 | tf_op jit(solution)/shard_map/ppermute | solution.py:320

commit v18 on v17

--- a/solution.py
+++ b/solution.py
@@ -18,7 +18,7 @@
 
 WORD = 32
 LANES = 128
-PIECES = 4
+PIECES = 2
 VMEM_LIMIT = 32 * 1024 * 1024
 FLOPS = 2 * 10**8
 LATE_FLOPS = 10 * 10**8
@@ -45,17 +45,15 @@
     table_ref,
     done,
 ):
-    docs, width = docs_hbm.shape
+    docs = docs_hbm.shape[0]
     head = docs - b_ref.shape[0]
     pairs = [
         (docs_hbm.at[pl.ds(head, docs - head)], b_ref),
+        (docs_hbm.at[pl.ds(0, head)], top_ref),
         (ids_hbm, ids_ref),
         (table_hbm, table_ref),
         (count_hbm, count_ref),
     ]
-    for j in range(width // LANES):
-        tile = docs_hbm.at[pl.ds(0, head), pl.ds(j * LANES, LANES)]
-        pairs.append((tile, top_ref.at[pl.ds(j * head, head)]))
     fetches = [pltpu.make_async_copy(*pair, done.at[k]) for k, pair in enumerate(pairs)]
     for fetch in fetches:
         fetch.start()
@@ -75,12 +73,12 @@
         out_specs=[pl.BlockSpec(memory_space=pltpu.VMEM)] * 5,
         out_shape=[
             jax.ShapeDtypeStruct((docs - head, width), jnp.bfloat16),
-            jax.ShapeDtypeStruct((width // LANES * head, LANES), jnp.bfloat16),
+            jax.ShapeDtypeStruct((head, width), jnp.bfloat16),
             jax.ShapeDtypeStruct((slots, docs), jnp.int32),
             jax.ShapeDtypeStruct((1, docs), jnp.int32),
             jax.ShapeDtypeStruct((lines, LANES), jnp.int32),
         ],
-        scratch_shapes=[pltpu.SemaphoreType.DMA((4 + width // LANES,))],
+        scratch_shapes=[pltpu.SemaphoreType.DMA((5,))],
         compiler_params=pltpu.CompilerParams(vmem_limit_bytes=VMEM_LIMIT),
         name="fetch",
     )(*(pltpu.with_memory_space_constraint(x, pltpu.HBM) for x in inputs))
@@ -88,8 +86,10 @@
 
 def prepare_kernel(bits, top_ref, ids_ref, count_ref, table_ref, a_ref):
     slots, docs = ids_ref.shape
-    top = top_ref.shape[0]
-    a_ref[:top, :] = top_ref[...]
+    head, width = top_ref.shape
+    top = width // LANES * head
+    for j in range(width // LANES):
+        a_ref[j * head : (j + 1) * head, :] = top_ref[:, j * LANES : (j + 1) * LANES]
     pairs = table_ref.shape[0] // 2
     starts = range(0, docs, LANES)
     ids = [ids_ref[:, start : start + LANES] for start in starts]
@@ -127,7 +127,7 @@
         functools.partial(prepare_kernel, (table.shape[0] - 1).bit_length()),
         in_specs=[vmem] * 4,
         out_specs=vmem,
-        out_shape=jax.ShapeDtypeStruct((top.shape[0] + slots * docs // LANES, LANES), jnp.bfloat16),
+        out_shape=jax.ShapeDtypeStruct(((top.size + slots * docs) // LANES, LANES), jnp.bfloat16),
         compiler_params=pltpu.CompilerParams(vmem_limit_bytes=VMEM_LIMIT),
         name="prepare",
     )(top, ids, count, table)

time: 40.7 us -> 40.7 us (level)
  no operation moved by 1% of the time
where the time goes in v18:
time: 40.7 us; the launch traced here: 40.5 us
  starting transfers between devices  21.9 us (54%)
  Pallas kernels  11.7 us (29%)
  waiting for transfers between devices  6.14 us (15%)
  between operations  0.81 us (2%)
    ppermute x18, starting transfers between devices, send(): return lax.ppermute(value, 'blk', pairs)  21.9 us
    pallas_call x8, Pallas kernels, add_gradient(): pl.pallas_call(functools.partial(gradient_kernel, bits, owners, not sums)...  7.7 us
    ppermute x18, waiting for transfers between devices, send(): return lax.ppermute(value, 'blk', pairs)  6.14 us
    pallas_call x1, Pallas kernels, finish(): pl.pallas_call(functools.partial(finish_kernel, bits), in_specs=[pl.Block...  2.35 us
    pallas_call x1, Pallas kernels, fetch(): pl.pallas_call(fetch_kernel, in_specs=[pl.BlockSpec(memory_space=pltpu.HB...  1.14 us
  transfers between devices with their start and end apart: 18, of which 10 were waited for; matrix products, arithmetic and copies ran while one was open for 0% of the time, Pallas kernels for 20%

profile of v18, /device:TPU:0, one launch (start us, length us, event | category | flops | bytes accessed | tf_op | source)
XLA Modules:
  0.0 40.5 jit_solution(7882839408019458370)
XLA Ops:
  0.6 1.1 %fetch.1 = (bf16[128,768]{1,0:T(8,128)(2,1)S(1)}, bf16[128,768]{1,0:T(8,128)(2,1)S(1)}, s32[32,256]{1,0:T(8,128)S(1)}, s32[1,256]{1,0:T(1,128)S(1)}, s32[32,128]{1,0:T(8,128)S(1)}) custom-call(s32[32,256]{1,0:T(8,128)} %bitcast.3, s32[1,256]{1,0:T(1,128)} %bitcast.5, s32[32,128]{1,0:T(8,128)} %bitcast.4, bf16[256,768]{1,0:T(8,128)(2,1)} %docs_hbm.1), custom_call_target="tpu_custom_call" | custom-call | tf_op jit(solution)/shard_map/fetch/pallas_call | solution.py:70
  1.8 3.1 %collective-permute-start.1 = (bf16[128,768]{1,0:T(8,128)(2,1)S(1)}, bf16[128,768]{1,0:T(8,128)(2,1)S(1)}, u32[]{:S(2)}, u32[]{:S(2)}) collective-permute-start(bf16[128,768]{1,0:T(8,128)(2,1)S(1)} %get-tuple-element.122.b_ref), channel_id=1, source_target_pairs={{0,4},{5,1},{4,8},{9,5},{8,12},{13,9},{12,14},{15,13},{14,10},{11,... | collective-permute-start | bytes 589832 | tf_op jit(solution)/shard_map/ppermute | solution.py:320
  4.9 0.4 %prepare.1.a_ref = bf16[832,128]{1,0:T(8,128)(2,1)S(1)} custom-call(bf16[128,768]{1,0:T(8,128)(2,1)S(1)} %get-tuple-element.90.top_ref, s32[32,256]{1,0:T(8,128)S(1)} %get-tuple-element.91.ids_ref, s32[1,256]{1,0:T(1,128)S(1)} %get-tuple-element.92.count_ref, s32[32,128]{1,0:T(8,128)S(1)} %get-tuple-element.93.table_ref), custom_call_target="tpu_custom_call" | custom-call | tf_op jit(solution)/shard_map/prepare/pallas_call | solution.py:126
  5.4 2.0 %collective-permute-start.5 = (bf16[832,128]{1,0:T(8,128)(2,1)S(1)}, bf16[832,128]{1,0:T(8,128)(2,1)S(1)}, u32[]{:S(2)}, u32[]{:S(2)}) collective-permute-start(bf16[832,128]{1,0:T(8,128)(2,1)S(1)} %prepare.1.a_ref), channel_id=1, source_target_pairs={{0,4},{5,1},{4,8},{9,5},{8,12},{13,9},{12,14},{15,13},{14,10},{11,... | collective-permute-start | bytes 638984 | tf_op jit(solution)/shard_map/ppermute | solution.py:320
  7.5 0.5 %collective-permute-start.4 = (bf16[128,768]{1,0:T(8,128)(2,1)S(1)}, bf16[128,768]{1,0:T(8,128)(2,1)S(1)}, u32[]{:S(2)}, u32[]{:S(2)}) collective-permute-start(bf16[128,768]{1,0:T(8,128)(2,1)S(1)} %get-tuple-element.122.b_ref), channel_id=1, source_target_pairs={{4,0},{1,5},{8,4},{5,9},{12,8},{9,13},{14,12},{13,15},{10,14},{15,... | collective-permute-start | bytes 589832 | tf_op jit(solution)/shard_map/ppermute | solution.py:320
  8.0 1.7 %collective-permute-done.1.b_ref = bf16[128,768]{1,0:T(8,128)(2,1)S(1)} collective-permute-done((bf16[128,768]{1,0:T(8,128)(2,1)S(1)}, bf16[128,768]{1,0:T(8,128)(2,1)S(1)}, u32[]{:S(2)}, u32[]{:S(2)}) %collective-permute-start.1) | collective-permute-done | bytes 196640 | tf_op jit(solution)/shard_map/ppermute | solution.py:320
  9.7 2.5 %collective-permute-start.3 = (bf16[128,768]{1,0:T(8,128)(2,1)S(1)}, bf16[128,768]{1,0:T(8,128)(2,1)S(1)}, u32[]{:S(2)}, u32[]{:S(2)}) collective-permute-start(bf16[128,768]{1,0:T(8,128)(2,1)S(1)} %collective-permute-done.1.b_ref), channel_id=1, source_target_pairs={{0,4},{5,1},{4,8},{9,5},{8,12},{13,9},{12,14},{15,13},{14,10},{11,... | collective-permute-start | bytes 589832 | tf_op jit(solution)/shard_map/ppermute | solution.py:320
  12.5 1.1 %collective-permute-start.2 = (bf16[832,128]{1,0:T(8,128)(2,1)S(1)}, bf16[832,128]{1,0:T(8,128)(2,1)S(1)}, u32[]{:S(2)}, u32[]{:S(2)}) collective-permute-start(bf16[832,128]{1,0:T(8,128)(2,1)S(1)} %collective-permute-done.a_ref), channel_id=1, source_target_pairs={{4,0},{1,5},{8,4},{5,9},{12,8},{9,13},{14,12},{13,15},{10,14},{15,... | collective-permute-start | bytes 638984 | tf_op jit(solution)/shard_map/ppermute | solution.py:320
  13.6 0.7 %collective-permute-done.5.a_ref = bf16[832,128]{1,0:T(8,128)(2,1)S(1)} collective-permute-done((bf16[832,128]{1,0:T(8,128)(2,1)S(1)}, bf16[832,128]{1,0:T(8,128)(2,1)S(1)}, u32[]{:S(2)}, u32[]{:S(2)}) %collective-permute-start.5) | collective-permute-done | bytes 213024 | tf_op jit(solution)/shard_map/ppermute | solution.py:320
  14.2 2.5 %collective-permute-start.9 = (bf16[832,128]{1,0:T(8,128)(2,1)S(1)}, bf16[832,128]{1,0:T(8,128)(2,1)S(1)}, u32[]{:S(2)}, u32[]{:S(2)}) collective-permute-start(bf16[832,128]{1,0:T(8,128)(2,1)S(1)} %collective-permute-done.5.a_ref), channel_id=1, source_target_pairs={{0,4},{5,1},{4,8},{9,5},{8,12},{13,9},{12,14},{15,13},{14,10},{11,... | collective-permute-start | bytes 638984 | tf_op jit(solution)/shard_map/ppermute | solution.py:320
  16.7 1.1 %collective-permute-start.8 = (bf16[128,768]{1,0:T(8,128)(2,1)S(1)}, bf16[128,768]{1,0:T(8,128)(2,1)S(1)}, u32[]{:S(2)}, u32[]{:S(2)}) collective-permute-start(bf16[128,768]{1,0:T(8,128)(2,1)S(1)} %collective-permute-done.4.b_ref), channel_id=1, source_target_pairs={{4,0},{1,5},{8,4},{5,9},{12,8},{9,13},{14,12},{13,15},{10,14},{15,... | collective-permute-start | bytes 589832 | tf_op jit(solution)/shard_map/ppermute | solution.py:320
  17.8 0.7 %collective-permute-done.3.b_ref = bf16[128,768]{1,0:T(8,128)(2,1)S(1)} collective-permute-done((bf16[128,768]{1,0:T(8,128)(2,1)S(1)}, bf16[128,768]{1,0:T(8,128)(2,1)S(1)}, u32[]{:S(2)}, u32[]{:S(2)}) %collective-permute-start.3) | collective-permute-done | bytes 196640 | tf_op jit(solution)/shard_map/ppermute | solution.py:320
  18.4 2.5 %collective-permute-start.7 = (bf16[128,768]{1,0:T(8,128)(2,1)S(1)}, bf16[128,768]{1,0:T(8,128)(2,1)S(1)}, u32[]{:S(2)}, u32[]{:S(2)}) collective-permute-start(bf16[128,768]{1,0:T(8,128)(2,1)S(1)} %collective-permute-done.3.b_ref), channel_id=1, source_target_pairs={{0,4},{5,1},{4,8},{9,5},{8,12},{13,9},{12,14},{15,13},{14,10},{11,... | collective-permute-start | bytes 589832 | tf_op jit(solution)/shard_map/ppermute | solution.py:320
  20.9 0.3 collective-permute-done.2.a_ref
  21.2 1.1 %collective-permute-start.6 = (bf16[832,128]{1,0:T(8,128)(2,1)S(1)}, bf16[832,128]{1,0:T(8,128)(2,1)S(1)}, u32[]{:S(2)}, u32[]{:S(2)}) collective-permute-start(bf16[832,128]{1,0:T(8,128)(2,1)S(1)} %collective-permute-done.2.a_ref), channel_id=1, source_target_pairs={{4,0},{1,5},{8,4},{5,9},{12,8},{9,13},{14,12},{13,15},{10,14},{15,... | collective-permute-start | bytes 638984 | tf_op jit(solution)/shard_map/ppermute | solution.py:320
  22.3 1.0 %gradient.8 = (f32[256,768]{1,0:T(8,128)S(1)}, f32[256,768]{1,0:T(8,128)S(1)}) custom-call(bf16[832,128]{1,0:T(8,128)(2,1)S(1)} %prepare.1.a_ref, bf16[128,768]{1,0:T(8,128)(2,1)S(1)} %get-tuple-element.122.b_ref, bf16[256,768]{1,0:T(8,128)(2,1)S(1)} %cast.1.refs_0_.cast_ref, bf16[256,768]{1,0:T(8,128)(2,1)S(1)} %collective-permute-done.10.refs_1_), custom_call_target="tpu_custom_call" | custom-call | flops 200000000 | bytes 1000000 | tf_op jit(solution)/shard_map/gradient/pallas_call | solution.py:209
  23.3 2.1 %collective-permute-start.14 = (bf16[832,128]{1,0:T(8,128)(2,1)S(1)}, bf16[832,128]{1,0:T(8,128)(2,1)S(1)}, u32[]{:S(2)}, u32[]{:S(2)}) collective-permute-start(bf16[832,128]{1,0:T(8,128)(2,1)S(1)} %collective-permute-done.9.a_ref), channel_id=1, source_target_pairs={{0,4},{5,1},{4,8},{9,5},{8,12},{13,9},{12,14},{15,13},{14,10},{11,... | collective-permute-start | bytes 638984 | tf_op jit(solution)/shard_map/ppermute | solution.py:320
  25.5 1.0 %gradient.9 = (f32[256,768]{1,0:T(8,128)S(1)}, f32[256,768]{1,0:T(8,128)S(1)}) custom-call(bf16[832,128]{1,0:T(8,128)(2,1)S(1)} %collective-permute-done.5.a_ref, bf16[128,768]{1,0:T(8,128)(2,1)S(1)} %collective-permute-done.1.b_ref, bf16[256,768]{1,0:T(8,128)(2,1)S(1)} %cast.1.refs_0_.cast_ref, ...), custom_call_target="tpu_custom_call", output_to_operand_aliasing={{0}: (4, {}), {1}: (5, {})} | custom-call | flops 200000000 | bytes 1000000 | tf_op jit(solution)/shard_map/gradient/pallas_call | solution.py:209
  26.6 0.6 %collective-permute-done.7.b_ref = bf16[128,768]{1,0:T(8,128)(2,1)S(1)} collective-permute-done((bf16[128,768]{1,0:T(8,128)(2,1)S(1)}, bf16[128,768]{1,0:T(8,128)(2,1)S(1)}, u32[]{:S(2)}, u32[]{:S(2)}) %collective-permute-start.7) | collective-permute-done | bytes 196640 | tf_op jit(solution)/shard_map/ppermute | solution.py:320
  27.2 2.5 %collective-permute-start.12 = (bf16[128,768]{1,0:T(8,128)(2,1)S(1)}, bf16[128,768]{1,0:T(8,128)(2,1)S(1)}, u32[]{:S(2)}, u32[]{:S(2)}) collective-permute-start(bf16[128,768]{1,0:T(8,128)(2,1)S(1)} %collective-permute-done.7.b_ref), channel_id=1, source_target_pairs={{0,4},{5,1},{4,8},{9,5},{8,12},{13,9},{12,14},{15,13},{14,10},{11,... | collective-permute-start | bytes 589832 | tf_op jit(solution)/shard_map/ppermute | solution.py:320
  29.7 1.0 %gradient.10 = (f32[256,768]{1,0:T(8,128)S(1)}, f32[256,768]{1,0:T(8,128)S(1)}) custom-call(bf16[832,128]{1,0:T(8,128)(2,1)S(1)} %collective-permute-done.a_ref, bf16[128,768]{1,0:T(8,128)(2,1)S(1)} %collective-permute-done.4.b_ref, bf16[256,768]{1,0:T(8,128)(2,1)S(1)} %cast.1.refs_0_.cast_ref, ...), custom_call_target="tpu_custom_call", output_to_operand_aliasing={{0}: (4, {}), {1}: (5, {})} | custom-call | flops 1000000000 | bytes 1000000 | tf_op jit(solution)/shard_map/gradient/pallas_call | solution.py:209
  30.7 0.4 %collective-permute-start.11 = (bf16[832,128]{1,0:T(8,128)(2,1)S(1)}, bf16[832,128]{1,0:T(8,128)(2,1)S(1)}, u32[]{:S(2)}, u32[]{:S(2)}) collective-permute-start(bf16[832,128]{1,0:T(8,128)(2,1)S(1)} %collective-permute-done.6.a_ref), channel_id=1, source_target_pairs={{4,0},{1,5},{8,4},{5,9},{12,8},{9,13},{14,12},{13,15},{10,14},{15,... | collective-permute-start | bytes 638984 | tf_op jit(solution)/shard_map/ppermute | solution.py:320
  31.1 1.0 %gradient.11 = (f32[256,768]{1,0:T(8,128)S(1)}, f32[256,768]{1,0:T(8,128)S(1)}) custom-call(bf16[832,128]{1,0:T(8,128)(2,1)S(1)} %collective-permute-done.9.a_ref, bf16[128,768]{1,0:T(8,128)(2,1)S(1)} %collective-permute-done.3.b_ref, bf16[256,768]{1,0:T(8,128)(2,1)S(1)} %cast.1.refs_0_.cast_ref, ...), custom_call_target="tpu_custom_call", output_to_operand_aliasing={{0}: (4, {}), {1}: (5, {})} | custom-call | flops 1000000000 | bytes 1000000 | tf_op jit(solution)/shard_map/gradient/pallas_call | solution.py:209
  32.1 1.0 %gradient.12 = (f32[256,768]{1,0:T(8,128)S(1)}, f32[256,768]{1,0:T(8,128)S(1)}) custom-call(bf16[832,128]{1,0:T(8,128)(2,1)S(1)} %collective-permute-done.2.a_ref, bf16[128,768]{1,0:T(8,128)(2,1)S(1)} %collective-permute-done.8.b_ref, bf16[256,768]{1,0:T(8,128)(2,1)S(1)} %cast.1.refs_0_.cast_ref, ...), custom_call_target="tpu_custom_call", output_to_operand_aliasing={{0}: (4, {}), {1}: (5, {})} | custom-call | flops 1000000000 | bytes 1000000 | tf_op jit(solution)/shard_map/gradient/pallas_call | solution.py:209
  33.2 1.0 %gradient.13 = (f32[256,768]{1,0:T(8,128)S(1)}, f32[256,768]{1,0:T(8,128)S(1)}) custom-call(bf16[832,128]{1,0:T(8,128)(2,1)S(1)} %collective-permute-done.14.a_ref, bf16[128,768]{1,0:T(8,128)(2,1)S(1)} %collective-permute-done.7.b_ref, bf16[256,768]{1,0:T(8,128)(2,1)S(1)} %cast.1.refs_0_.cast_ref, ...), custom_call_target="tpu_custom_call", output_to_operand_aliasing={{0}: (4, {}), {1}: (5, {})} | custom-call | flops 1000000000 | bytes 1000000 | tf_op jit(solution)/shard_map/gradient/pallas_call | solution.py:209
  34.2 1.0 %gradient.14 = (f32[256,768]{1,0:T(8,128)S(1)}, f32[256,768]{1,0:T(8,128)S(1)}) custom-call(bf16[832,128]{1,0:T(8,128)(2,1)S(1)} %collective-permute-done.6.a_ref, bf16[128,768]{1,0:T(8,128)(2,1)S(1)} %collective-permute-done.13.b_ref, bf16[256,768]{1,0:T(8,128)(2,1)S(1)} %cast.1.refs_0_.cast_ref, ...), custom_call_target="tpu_custom_call", output_to_operand_aliasing={{0}: (4, {}), {1}: (5, {})} | custom-call | flops 1000000000 | bytes 1000000 | tf_op jit(solution)/shard_map/gradient/pallas_call | solution.py:209
  35.3 0.7 %collective-permute-done.12.b_ref = bf16[128,768]{1,0:T(8,128)(2,1)S(1)} collective-permute-done((bf16[128,768]{1,0:T(8,128)(2,1)S(1)}, bf16[128,768]{1,0:T(8,128)(2,1)S(1)}, u32[]{:S(2)}, u32[]{:S(2)}) %collective-permute-start.12) | collective-permute-done | bytes 196640 | tf_op jit(solution)/shard_map/ppermute | solution.py:320
  36.0 0.6 %collective-permute-done.11.a_ref = bf16[832,128]{1,0:T(8,128)(2,1)S(1)} collective-permute-done((bf16[832,128]{1,0:T(8,128)(2,1)S(1)}, bf16[832,128]{1,0:T(8,128)(2,1)S(1)}, u32[]{:S(2)}, u32[]{:S(2)}) %collective-permute-start.11) | collective-permute-done | bytes 213024 | tf_op jit(solution)/shard_map/ppermute | solution.py:320
  36.9 0.7 %gradient.15.sum_ref = f32[256,768]{1,0:T(8,128)S(1)} custom-call(bf16[832,128]{1,0:T(8,128)(2,1)S(1)} %collective-permute-done.11.a_ref, bf16[128,768]{1,0:T(8,128)(2,1)S(1)} %collective-permute-done.12.b_ref, bf16[256,768]{1,0:T(8,128)(2,1)S(1)} %cast.1.refs_0_.cast_ref, f32[256,768]{1,0:T(8,128)S(1)} %get-tuple-element.175.refs_1_), custom_call_target="tpu_custom_call", output_to_operand_aliasing={{}: (3, {})} | custom-call | flops 10000000000 | bytes 1000000 | tf_op jit(solution)/shard_map/gradient/pallas_call | solution.py:209
  37.6 0.3 collective-permute-done.16.b_ref
  37.8 0.3 collective-permute-done.15.a_ref
  38.2 2.3 %finish.1 = (f32[256,768]{1,0:T(8,128)}, f32[256,768]{1,0:T(8,128)}, f32[256,768]{1,0:T(8,128)}) custom-call(bf16[832,128]{1,0:T(8,128)(2,1)S(1)} %collective-permute-done.15.a_ref, bf16[128,768]{1,0:T(8,128)(2,1)S(1)} %collective-permute-done.16.b_ref, bf16[256,768]{1,0:T(8,128)(2,1)S(1)} %cast.1.refs_0_.cast_ref, f32[256,768]{1,0:T(8,128)S(1)} %gradient.15.sum_ref, ...), custom_call_target="tpu_custom_call" | custom-call | flops 10000000000 | bytes 1000000 | tf_op jit(solution)/shard_map/finish/pallas_call | solution.py:266
  (22 shorter events, 0.9 us)
Async XLA Ops:
  0.6 6.8 %copy-start = (f32[256,768]{1,0:T(8,128)S(1)}, f32[256,768]{1,0:T(8,128)}, u32[]{:S(2)}) copy-start(f32[256,768]{1,0:T(8,128)} %weights_ref.3) | copy-start | bytes 2359300
  1.8 7.9 %collective-permute-start.1 = (bf16[128,768]{1,0:T(8,128)(2,1)S(1)}, bf16[128,768]{1,0:T(8,128)(2,1)S(1)}, u32[]{:S(2)}, u32[]{:S(2)}) collective-permute-start(bf16[128,768]{1,0:T(8,128)(2,1)S(1)} %get-tuple-element.122.b_ref), channel_id=1, source_target_pairs={{0,4},{5,1},{4,8},{9,5},{8,12},{13,9},{12,14},{15,13},{14,10},{11,... | collective-permute-start | bytes 589832 | tf_op jit(solution)/shard_map/ppermute | solution.py:320
  5.3 7.1 %collective-permute-start = (bf16[832,128]{1,0:T(8,128)(2,1)S(1)}, bf16[832,128]{1,0:T(8,128)(2,1)S(1)}, u32[]{:S(2)}, u32[]{:S(2)}) collective-permute-start(bf16[832,128]{1,0:T(8,128)(2,1)S(1)} %prepare.1.a_ref), channel_id=1, source_target_pairs={{4,0},{1,5},{8,4},{5,9},{12,8},{9,13},{14,12},{13,15},{10,14},{15,... | collective-permute-start | bytes 638984 | tf_op jit(solution)/shard_map/ppermute | solution.py:320
  5.4 8.8 %collective-permute-start.5 = (bf16[832,128]{1,0:T(8,128)(2,1)S(1)}, bf16[832,128]{1,0:T(8,128)(2,1)S(1)}, u32[]{:S(2)}, u32[]{:S(2)}) collective-permute-start(bf16[832,128]{1,0:T(8,128)(2,1)S(1)} %prepare.1.a_ref), channel_id=1, source_target_pairs={{0,4},{5,1},{4,8},{9,5},{8,12},{13,9},{12,14},{15,13},{14,10},{11,... | collective-permute-start | bytes 638984 | tf_op jit(solution)/shard_map/ppermute | solution.py:320
  7.5 14.9 %collective-permute-start.10 = (bf16[256,768]{1,0:T(8,128)(2,1)S(1)}, bf16[256,768]{1,0:T(8,128)(2,1)S(1)}, u32[]{:S(2)}, u32[]{:S(2)}) collective-permute-start(bf16[256,768]{1,0:T(8,128)(2,1)S(1)} %cast.1.refs_0_.cast_ref), channel_id=1, source_target_pairs={{0,1},{1,0},{2,3},{3,2},{4,5},{5,4},{6,7},{7,6},{8,9},{9,8},{10,11... | collective-permute-start | bytes 1179656 | tf_op jit(solution)/shard_map/ppermute | solution.py:320
  7.5 9.2 %collective-permute-start.4 = (bf16[128,768]{1,0:T(8,128)(2,1)S(1)}, bf16[128,768]{1,0:T(8,128)(2,1)S(1)}, u32[]{:S(2)}, u32[]{:S(2)}) collective-permute-start(bf16[128,768]{1,0:T(8,128)(2,1)S(1)} %get-tuple-element.122.b_ref), channel_id=1, source_target_pairs={{4,0},{1,5},{8,4},{5,9},{12,8},{9,13},{14,12},{13,15},{10,14},{15,... | collective-permute-start | bytes 589832 | tf_op jit(solution)/shard_map/ppermute | solution.py:320
  9.7 8.7 %collective-permute-start.3 = (bf16[128,768]{1,0:T(8,128)(2,1)S(1)}, bf16[128,768]{1,0:T(8,128)(2,1)S(1)}, u32[]{:S(2)}, u32[]{:S(2)}) collective-permute-start(bf16[128,768]{1,0:T(8,128)(2,1)S(1)} %collective-permute-done.1.b_ref), channel_id=1, source_target_pairs={{0,4},{5,1},{4,8},{9,5},{8,12},{13,9},{12,14},{15,13},{14,10},{11,... | collective-permute-start | bytes 589832 | tf_op jit(solution)/shard_map/ppermute | solution.py:320
  12.5 8.8 %collective-permute-start.2 = (bf16[832,128]{1,0:T(8,128)(2,1)S(1)}, bf16[832,128]{1,0:T(8,128)(2,1)S(1)}, u32[]{:S(2)}, u32[]{:S(2)}) collective-permute-start(bf16[832,128]{1,0:T(8,128)(2,1)S(1)} %collective-permute-done.a_ref), channel_id=1, source_target_pairs={{4,0},{1,5},{8,4},{5,9},{12,8},{9,13},{14,12},{13,15},{10,14},{15,... | collective-permute-start | bytes 638984 | tf_op jit(solution)/shard_map/ppermute | solution.py:320
  14.2 9.1 %collective-permute-start.9 = (bf16[832,128]{1,0:T(8,128)(2,1)S(1)}, bf16[832,128]{1,0:T(8,128)(2,1)S(1)}, u32[]{:S(2)}, u32[]{:S(2)}) collective-permute-start(bf16[832,128]{1,0:T(8,128)(2,1)S(1)} %collective-permute-done.5.a_ref), channel_id=1, source_target_pairs={{0,4},{5,1},{4,8},{9,5},{8,12},{13,9},{12,14},{15,13},{14,10},{11,... | collective-permute-start | bytes 638984 | tf_op jit(solution)/shard_map/ppermute | solution.py:320
  16.7 9.8 %collective-permute-start.8 = (bf16[128,768]{1,0:T(8,128)(2,1)S(1)}, bf16[128,768]{1,0:T(8,128)(2,1)S(1)}, u32[]{:S(2)}, u32[]{:S(2)}) collective-permute-start(bf16[128,768]{1,0:T(8,128)(2,1)S(1)} %collective-permute-done.4.b_ref), channel_id=1, source_target_pairs={{4,0},{1,5},{8,4},{5,9},{12,8},{9,13},{14,12},{13,15},{10,14},{15,... | collective-permute-start | bytes 589832 | tf_op jit(solution)/shard_map/ppermute | solution.py:320
  18.4 8.8 %collective-permute-start.7 = (bf16[128,768]{1,0:T(8,128)(2,1)S(1)}, bf16[128,768]{1,0:T(8,128)(2,1)S(1)}, u32[]{:S(2)}, u32[]{:S(2)}) collective-permute-start(bf16[128,768]{1,0:T(8,128)(2,1)S(1)} %collective-permute-done.3.b_ref), channel_id=1, source_target_pairs={{0,4},{5,1},{4,8},{9,5},{8,12},{13,9},{12,14},{15,13},{14,10},{11,... | collective-permute-start | bytes 589832 | tf_op jit(solution)/shard_map/ppermute | solution.py:320
  21.2 9.5 %collective-permute-start.6 = (bf16[832,128]{1,0:T(8,128)(2,1)S(1)}, bf16[832,128]{1,0:T(8,128)(2,1)S(1)}, u32[]{:S(2)}, u32[]{:S(2)}) collective-permute-start(bf16[832,128]{1,0:T(8,128)(2,1)S(1)} %collective-permute-done.2.a_ref), channel_id=1, source_target_pairs={{4,0},{1,5},{8,4},{5,9},{12,8},{9,13},{14,12},{13,15},{10,14},{15,... | collective-permute-start | bytes 638984 | tf_op jit(solution)/shard_map/ppermute | solution.py:320
  23.3 9.8 %collective-permute-start.14 = (bf16[832,128]{1,0:T(8,128)(2,1)S(1)}, bf16[832,128]{1,0:T(8,128)(2,1)S(1)}, u32[]{:S(2)}, u32[]{:S(2)}) collective-permute-start(bf16[832,128]{1,0:T(8,128)(2,1)S(1)} %collective-permute-done.9.a_ref), channel_id=1, source_target_pairs={{0,4},{5,1},{4,8},{9,5},{8,12},{13,9},{12,14},{15,13},{14,10},{11,... | collective-permute-start | bytes 638984 | tf_op jit(solution)/shard_map/ppermute | solution.py:320
  26.5 7.7 %collective-permute-start.13 = (bf16[128,768]{1,0:T(8,128)(2,1)S(1)}, bf16[128,768]{1,0:T(8,128)(2,1)S(1)}, u32[]{:S(2)}, u32[]{:S(2)}) collective-permute-start(bf16[128,768]{1,0:T(8,128)(2,1)S(1)} %collective-permute-done.8.b_ref), channel_id=1, source_target_pairs={{4,0},{1,5},{8,4},{5,9},{12,8},{9,13},{14,12},{13,15},{10,14},{15,... | collective-permute-start | bytes 589832 | tf_op jit(solution)/shard_map/ppermute | solution.py:320
  27.2 8.8 %collective-permute-start.12 = (bf16[128,768]{1,0:T(8,128)(2,1)S(1)}, bf16[128,768]{1,0:T(8,128)(2,1)S(1)}, u32[]{:S(2)}, u32[]{:S(2)}) collective-permute-start(bf16[128,768]{1,0:T(8,128)(2,1)S(1)} %collective-permute-done.7.b_ref), channel_id=1, source_target_pairs={{0,4},{5,1},{4,8},{9,5},{8,12},{13,9},{12,14},{15,13},{14,10},{11,... | collective-permute-start | bytes 589832 | tf_op jit(solution)/shard_map/ppermute | solution.py:320
  30.7 5.9 %collective-permute-start.11 = (bf16[832,128]{1,0:T(8,128)(2,1)S(1)}, bf16[832,128]{1,0:T(8,128)(2,1)S(1)}, u32[]{:S(2)}, u32[]{:S(2)}) collective-permute-start(bf16[832,128]{1,0:T(8,128)(2,1)S(1)} %collective-permute-done.6.a_ref), channel_id=1, source_target_pairs={{4,0},{1,5},{8,4},{5,9},{12,8},{9,13},{14,12},{13,15},{10,14},{15,... | collective-permute-start | bytes 638984 | tf_op jit(solution)/shard_map/ppermute | solution.py:320
  35.2 2.9 %collective-permute-start.17 = (f32[256,768]{1,0:T(8,128)S(1)}, f32[256,768]{1,0:T(8,128)S(1)}, u32[]{:S(2)}, u32[]{:S(2)}) collective-permute-start(f32[256,768]{1,0:T(8,128)S(1)} %get-tuple-element.176), channel_id=1, source_target_pairs={{0,1},{1,0},{2,3},{3,2},{4,5},{5,4},{6,7},{7,6},{8,9},{9,8},{10,11... | collective-permute-start | bytes 2359304 | tf_op jit(solution)/shard_map/ppermute | solution.py:320
  36.0 2.2 %copy-start.1 = (f32[256,768]{1,0:T(8,128)S(1)}, f32[256,768]{1,0:T(8,128)}, u32[]{:S(2)}) copy-start(f32[256,768]{1,0:T(8,128)} %first_ref.1) | copy-start | bytes 2359300
  36.0 2.2 %copy-start.2 = (f32[256,768]{1,0:T(8,128)S(1)}, f32[256,768]{1,0:T(8,128)}, u32[]{:S(2)}) copy-start(f32[256,768]{1,0:T(8,128)} %second_ref.1) | copy-start | bytes 2359300
  36.0 1.9 %collective-permute-start.16 = (bf16[128,768]{1,0:T(8,128)(2,1)S(1)}, bf16[128,768]{1,0:T(8,128)(2,1)S(1)}, u32[]{:S(2)}, u32[]{:S(2)}) collective-permute-start(bf16[128,768]{1,0:T(8,128)(2,1)S(1)} %collective-permute-done.12.b_ref), channel_id=1, source_target_pairs={{0,1},{1,0},{2,3},{3,2},{4,5},{5,4},{6,7},{7,6},{8,9},{9,8},{10,11... | collective-permute-start | bytes 589832 | tf_op jit(solution)/shard_map/ppermute | solution.py:320
  36.6 1.5 %collective-permute-start.15 = (bf16[832,128]{1,0:T(8,128)(2,1)S(1)}, bf16[832,128]{1,0:T(8,128)(2,1)S(1)}, u32[]{:S(2)}, u32[]{:S(2)}) collective-permute-start(bf16[832,128]{1,0:T(8,128)(2,1)S(1)} %collective-permute-done.11.a_ref), channel_id=1, source_target_pairs={{0,1},{1,0},{2,3},{3,2},{4,5},{5,4},{6,7},{7,6},{8,9},{9,8},{10,11... | collective-permute-start | bytes 638984 | tf_op jit(solution)/shard_map/ppermute | solution.py:320

commit v19 on v18

--- a/solution.py
+++ b/solution.py
@@ -20,7 +20,7 @@
 LANES = 128
 PIECES = 2
 VMEM_LIMIT = 32 * 1024 * 1024
-FLOPS = 2 * 10**8
+FLOPS = 8 * 10**8
 LATE_FLOPS = 10 * 10**8
 END_FLOPS = 100 * 10**8
 
@@ -169,9 +169,10 @@
 
 def doubled_gradient(bits, owners, a_ref, b_ref, w_refs):
     height = w_refs[0].shape[0]
-    head, width = b_ref.shape
+    bits, head = bits
+    later, width = b_ref.shape
     tiles = width // LANES
-    chunks = 2 * head // LANES
+    chunks = (head + later) // LANES
     slots = (a_ref.shape[0] - tiles * head) // chunks
     top = jnp.concatenate([a_ref[j * head : (j + 1) * head, :] for j in range(tiles)], axis=1)
     docs = jnp.concatenate([top, b_ref[...]], axis=0)
@@ -314,7 +315,8 @@
     down = [(there, here) for here, there in up]
     swap = [(i, i ^ 1) for i in range(blocks)]
     bits = (label_slot.shape[0] // LANES - 1).bit_length()
-    head = embeddings.shape[0] // 2
+    head = embeddings.shape[0] * 7 // 16
+    layout = (bits, head)
 
     def send(value, pairs):
         return lax.ppermute(value, "blk", pairs)
@@ -330,7 +332,7 @@
     waiting = [(a, b)]
 
     def work(flops):
-        return add_gradient(bits, (0, 1), *waiting.pop(0), cast, sums, flops)
+        return add_gradient(layout, (0, 1), *waiting.pop(0), cast, sums, flops)
 
     for step in range(1, half_way):
         last = step == half_way - 1
@@ -356,9 +358,9 @@
     beside_b = send(last_b, swap)
     last_a, mine_sum = together((coming["down_a"], mine_sum))
     beside_a = send(last_a, swap)
-    (mine_sum,) = add_gradient(bits, (0,), last_a, last_b, [mine], [mine_sum], END_FLOPS)
+    (mine_sum,) = add_gradient(layout, (0,), last_a, last_b, [mine], [mine_sum], END_FLOPS)
     state = (weights, first_moment, second_moment)
-    return finish(bits, beside_a, beside_b, mine, mine_sum, got, *state)
+    return finish(layout, beside_a, beside_b, mine, mine_sum, got, *state)
 
 
 def solution(mesh):

time: 40.7 us -> 42.8 us (1.052)
  waiting for transfers between devices: 6.14 us -> 10.3 us
  starting transfers between devices: 21.9 us -> 18.7 us
  local copies, waits for them, and re-layouts: 0.01 us -> 1.14 us
    ppermute x18, waiting for transfers between devices: 6.14 us -> 10.3 us  [send(): return lax.ppermute(value, 'blk', pairs)]
    ppermute x18, starting transfers between devices: 21.9 us -> 18.7 us  [send(): return lax.ppermute(value, 'blk', pairs)]
    unnamed x6 -> x8, local copies, waits for them, and re-layouts: 0.01 us -> 1.14 us
  transfers between devices with their start and end apart: 18 -> 18, of which waited for: 10 -> 11; matrix products, arithmetic and copies ran while one was open for 0% -> 0% of each run, Pallas kernels for 20% -> 19%
where the time goes in v19:
time: 42.8 us; the launch traced here: 42.6 us
  starting transfers between devices  18.7 us (44%)
  Pallas kernels  11.6 us (27%)
  waiting for transfers between devices  10.3 us (24%)
  local copies, waits for them, and re-layouts  1.14 us (3%)
  between operations  0.78 us (2%)
    ppermute x18, starting transfers between devices, send(): return lax.ppermute(value, 'blk', pairs)  18.7 us
    ppermute x18, waiting for transfers between devices, send(): return lax.ppermute(value, 'blk', pairs)  10.3 us
    pallas_call x8, Pallas kernels, add_gradient(): pl.pallas_call(functools.partial(gradient_kernel, bits, owners, not sums)...  7.72 us
    pallas_call x1, Pallas kernels, finish(): pl.pallas_call(functools.partial(finish_kernel, bits), in_specs=[pl.Block...  2.35 us
    unnamed x8, local copies, waits for them, and re-layouts  1.14 us
    pallas_call x1, Pallas kernels, fetch(): pl.pallas_call(fetch_kernel, in_specs=[pl.BlockSpec(memory_space=pltpu.HB...  1.08 us
  transfers between devices with their start and end apart: 18, of which 11 were waited for; matrix products, arithmetic and copies ran while one was open for 0% of the time, Pallas kernels for 19%

profile of v19, /device:TPU:0, one launch (start us, length us, event | category | flops | bytes accessed | tf_op | source)
XLA Modules:
  0.0 42.6 jit_solution(14689351405461608511)
XLA Ops:
  0.6 1.1 %fetch.1 = (bf16[144,768]{1,0:T(8,128)(2,1)S(1)}, bf16[112,768]{1,0:T(8,128)(2,1)S(1)}, s32[32,256]{1,0:T(8,128)S(1)}, s32[1,256]{1,0:T(1,128)S(1)}, s32[32,128]{1,0:T(8,128)S(1)}) custom-call(s32[32,256]{1,0:T(8,128)} %bitcast.3, s32[1,256]{1,0:T(1,128)} %bitcast.5, s32[32,128]{1,0:T(8,128)} %bitcast.4, bf16[256,768]{1,0:T(8,128)(2,1)} %docs_hbm.1), custom_call_target="tpu_custom_call" | custom-call | tf_op jit(solution)/shard_map/fetch/pallas_call | solution.py:70
  1.7 3.1 %collective-permute-start.1 = (bf16[144,768]{1,0:T(8,128)(2,1)S(1)}, bf16[144,768]{1,0:T(8,128)(2,1)S(1)}, u32[]{:S(2)}, u32[]{:S(2)}) collective-permute-start(bf16[144,768]{1,0:T(8,128)(2,1)S(1)} %get-tuple-element.122.b_ref), channel_id=1, source_target_pairs={{0,4},{5,1},{4,8},{9,5},{8,12},{13,9},{12,14},{15,13},{14,10},{11,... | collective-permute-start | bytes 663560 | tf_op jit(solution)/shard_map/ppermute | solution.py:322
  4.8 1.1 %copy-done = f32[256,768]{1,0:T(8,128)S(1)} copy-done((f32[256,768]{1,0:T(8,128)S(1)}, f32[256,768]{1,0:T(8,128)}, u32[]{:S(2)}) %copy-start) | copy-done | bytes 786456
  6.5 1.1 %collective-permute-start = (bf16[736,128]{1,0:T(8,128)(2,1)S(1)}, bf16[736,128]{1,0:T(8,128)(2,1)S(1)}, u32[]{:S(2)}, u32[]{:S(2)}) collective-permute-start(bf16[736,128]{1,0:T(8,128)(2,1)S(1)} %prepare.1.a_ref), channel_id=1, source_target_pairs={{4,0},{1,5},{8,4},{5,9},{12,8},{9,13},{14,12},{13,15},{10,14},{15,... | collective-permute-start | bytes 565256 | tf_op jit(solution)/shard_map/ppermute | solution.py:322
  7.6 1.0 %collective-permute-start.5 = (bf16[736,128]{1,0:T(8,128)(2,1)S(1)}, bf16[736,128]{1,0:T(8,128)(2,1)S(1)}, u32[]{:S(2)}, u32[]{:S(2)}) collective-permute-start(bf16[736,128]{1,0:T(8,128)(2,1)S(1)} %prepare.1.a_ref), channel_id=1, source_target_pairs={{0,4},{5,1},{4,8},{9,5},{8,12},{13,9},{12,14},{15,13},{14,10},{11,... | collective-permute-start | bytes 565256 | tf_op jit(solution)/shard_map/ppermute | solution.py:322
  8.6 1.1 %collective-permute-start.4 = (bf16[144,768]{1,0:T(8,128)(2,1)S(1)}, bf16[144,768]{1,0:T(8,128)(2,1)S(1)}, u32[]{:S(2)}, u32[]{:S(2)}) collective-permute-start(bf16[144,768]{1,0:T(8,128)(2,1)S(1)} %get-tuple-element.122.b_ref), channel_id=1, source_target_pairs={{4,0},{1,5},{8,4},{5,9},{12,8},{9,13},{14,12},{13,15},{10,14},{15,... | collective-permute-start | bytes 663560 | tf_op jit(solution)/shard_map/ppermute | solution.py:322
  9.6 1.1 %collective-permute-start.3 = (bf16[144,768]{1,0:T(8,128)(2,1)S(1)}, bf16[144,768]{1,0:T(8,128)(2,1)S(1)}, u32[]{:S(2)}, u32[]{:S(2)}) collective-permute-start(bf16[144,768]{1,0:T(8,128)(2,1)S(1)} %collective-permute-done.1.b_ref), channel_id=1, source_target_pairs={{0,4},{5,1},{4,8},{9,5},{8,12},{13,9},{12,14},{15,13},{14,10},{11,... | collective-permute-start | bytes 663560 | tf_op jit(solution)/shard_map/ppermute | solution.py:322
  10.7 2.6 %collective-permute-done.a_ref = bf16[736,128]{1,0:T(8,128)(2,1)S(1)} collective-permute-done((bf16[736,128]{1,0:T(8,128)(2,1)S(1)}, bf16[736,128]{1,0:T(8,128)(2,1)S(1)}, u32[]{:S(2)}, u32[]{:S(2)}) %collective-permute-start) | collective-permute-done | bytes 188448 | tf_op jit(solution)/shard_map/ppermute | solution.py:322
  13.4 1.6 %collective-permute-start.2 = (bf16[736,128]{1,0:T(8,128)(2,1)S(1)}, bf16[736,128]{1,0:T(8,128)(2,1)S(1)}, u32[]{:S(2)}, u32[]{:S(2)}) collective-permute-start(bf16[736,128]{1,0:T(8,128)(2,1)S(1)} %collective-permute-done.a_ref), channel_id=1, source_target_pairs={{4,0},{1,5},{8,4},{5,9},{12,8},{9,13},{14,12},{13,15},{10,14},{15,... | collective-permute-start | bytes 565256 | tf_op jit(solution)/shard_map/ppermute | solution.py:322
  15.3 0.9 %collective-permute-start.9 = (bf16[736,128]{1,0:T(8,128)(2,1)S(1)}, bf16[736,128]{1,0:T(8,128)(2,1)S(1)}, u32[]{:S(2)}, u32[]{:S(2)}) collective-permute-start(bf16[736,128]{1,0:T(8,128)(2,1)S(1)} %collective-permute-done.5.a_ref), channel_id=1, source_target_pairs={{0,4},{5,1},{4,8},{9,5},{8,12},{13,9},{12,14},{15,13},{14,10},{11,... | collective-permute-start | bytes 565256 | tf_op jit(solution)/shard_map/ppermute | solution.py:322
  16.2 1.9 %collective-permute-done.4.b_ref = bf16[144,768]{1,0:T(8,128)(2,1)S(1)} collective-permute-done((bf16[144,768]{1,0:T(8,128)(2,1)S(1)}, bf16[144,768]{1,0:T(8,128)(2,1)S(1)}, u32[]{:S(2)}, u32[]{:S(2)}) %collective-permute-start.4) | collective-permute-done | bytes 221216 | tf_op jit(solution)/shard_map/ppermute | solution.py:322
  18.1 1.6 %collective-permute-start.8 = (bf16[144,768]{1,0:T(8,128)(2,1)S(1)}, bf16[144,768]{1,0:T(8,128)(2,1)S(1)}, u32[]{:S(2)}, u32[]{:S(2)}) collective-permute-start(bf16[144,768]{1,0:T(8,128)(2,1)S(1)} %collective-permute-done.4.b_ref), channel_id=1, source_target_pairs={{4,0},{1,5},{8,4},{5,9},{12,8},{9,13},{14,12},{13,15},{10,14},{15,... | collective-permute-start | bytes 663560 | tf_op jit(solution)/shard_map/ppermute | solution.py:322
  20.0 0.9 %collective-permute-start.7 = (bf16[144,768]{1,0:T(8,128)(2,1)S(1)}, bf16[144,768]{1,0:T(8,128)(2,1)S(1)}, u32[]{:S(2)}, u32[]{:S(2)}) collective-permute-start(bf16[144,768]{1,0:T(8,128)(2,1)S(1)} %collective-permute-done.3.b_ref), channel_id=1, source_target_pairs={{0,4},{5,1},{4,8},{9,5},{8,12},{13,9},{12,14},{15,13},{14,10},{11,... | collective-permute-start | bytes 663560 | tf_op jit(solution)/shard_map/ppermute | solution.py:322
  20.9 1.2 %collective-permute-done.2.a_ref = bf16[736,128]{1,0:T(8,128)(2,1)S(1)} collective-permute-done((bf16[736,128]{1,0:T(8,128)(2,1)S(1)}, bf16[736,128]{1,0:T(8,128)(2,1)S(1)}, u32[]{:S(2)}, u32[]{:S(2)}) %collective-permute-start.2) | collective-permute-done | bytes 188448 | tf_op jit(solution)/shard_map/ppermute | solution.py:322
  22.1 1.6 %collective-permute-start.6 = (bf16[736,128]{1,0:T(8,128)(2,1)S(1)}, bf16[736,128]{1,0:T(8,128)(2,1)S(1)}, u32[]{:S(2)}, u32[]{:S(2)}) collective-permute-start(bf16[736,128]{1,0:T(8,128)(2,1)S(1)} %collective-permute-done.2.a_ref), channel_id=1, source_target_pairs={{4,0},{1,5},{8,4},{5,9},{12,8},{9,13},{14,12},{13,15},{10,14},{15,... | collective-permute-start | bytes 565256 | tf_op jit(solution)/shard_map/ppermute | solution.py:322
  23.8 1.0 %gradient.8 = (f32[256,768]{1,0:T(8,128)S(1)}, f32[256,768]{1,0:T(8,128)S(1)}) custom-call(bf16[736,128]{1,0:T(8,128)(2,1)S(1)} %prepare.1.a_ref, bf16[144,768]{1,0:T(8,128)(2,1)S(1)} %get-tuple-element.122.b_ref, bf16[256,768]{1,0:T(8,128)(2,1)S(1)} %cast.1.refs_0_.cast_ref, bf16[256,768]{1,0:T(8,128)(2,1)S(1)} %collective-permute-done.10.refs_1_), custom_call_target="tpu_custom_call" | custom-call | flops 800000000 | bytes 1000000 | tf_op jit(solution)/shard_map/gradient/pallas_call | solution.py:210
  25.2 1.0 %gradient.9 = (f32[256,768]{1,0:T(8,128)S(1)}, f32[256,768]{1,0:T(8,128)S(1)}) custom-call(bf16[736,128]{1,0:T(8,128)(2,1)S(1)} %collective-permute-done.5.a_ref, bf16[144,768]{1,0:T(8,128)(2,1)S(1)} %collective-permute-done.1.b_ref, bf16[256,768]{1,0:T(8,128)(2,1)S(1)} %cast.1.refs_0_.cast_ref, ...), custom_call_target="tpu_custom_call", output_to_operand_aliasing={{0}: (4, {}), {1}: (5, {})} | custom-call | flops 800000000 | bytes 1000000 | tf_op jit(solution)/shard_map/gradient/pallas_call | solution.py:210
  26.2 0.6 %collective-permute-done.8.b_ref = bf16[144,768]{1,0:T(8,128)(2,1)S(1)} collective-permute-done((bf16[144,768]{1,0:T(8,128)(2,1)S(1)}, bf16[144,768]{1,0:T(8,128)(2,1)S(1)}, u32[]{:S(2)}, u32[]{:S(2)}) %collective-permute-start.8) | collective-permute-done | bytes 221216 | tf_op jit(solution)/shard_map/ppermute | solution.py:322
  26.9 1.6 %collective-permute-start.13 = (bf16[144,768]{1,0:T(8,128)(2,1)S(1)}, bf16[144,768]{1,0:T(8,128)(2,1)S(1)}, u32[]{:S(2)}, u32[]{:S(2)}) collective-permute-start(bf16[144,768]{1,0:T(8,128)(2,1)S(1)} %collective-permute-done.8.b_ref), channel_id=1, source_target_pairs={{4,0},{1,5},{8,4},{5,9},{12,8},{9,13},{14,12},{13,15},{10,14},{15,... | collective-permute-start | bytes 663560 | tf_op jit(solution)/shard_map/ppermute | solution.py:322
  28.8 1.0 %gradient.10 = (f32[256,768]{1,0:T(8,128)S(1)}, f32[256,768]{1,0:T(8,128)S(1)}) custom-call(bf16[736,128]{1,0:T(8,128)(2,1)S(1)} %collective-permute-done.a_ref, bf16[144,768]{1,0:T(8,128)(2,1)S(1)} %collective-permute-done.4.b_ref, bf16[256,768]{1,0:T(8,128)(2,1)S(1)} %cast.1.refs_0_.cast_ref, ...), custom_call_target="tpu_custom_call", output_to_operand_aliasing={{0}: (4, {}), {1}: (5, {})} | custom-call | flops 1000000000 | bytes 1000000 | tf_op jit(solution)/shard_map/gradient/pallas_call | solution.py:210
  29.8 1.1 %collective-permute-done.6.a_ref = bf16[736,128]{1,0:T(8,128)(2,1)S(1)} collective-permute-done((bf16[736,128]{1,0:T(8,128)(2,1)S(1)}, bf16[736,128]{1,0:T(8,128)(2,1)S(1)}, u32[]{:S(2)}, u32[]{:S(2)}) %collective-permute-start.6) | collective-permute-done | bytes 188448 | tf_op jit(solution)/shard_map/ppermute | solution.py:322
  30.9 1.6 %collective-permute-start.12 = (bf16[144,768]{1,0:T(8,128)(2,1)S(1)}, bf16[144,768]{1,0:T(8,128)(2,1)S(1)}, u32[]{:S(2)}, u32[]{:S(2)}) collective-permute-start(bf16[144,768]{1,0:T(8,128)(2,1)S(1)} %collective-permute-done.7.b_ref), channel_id=1, source_target_pairs={{0,4},{5,1},{4,8},{9,5},{8,12},{13,9},{12,14},{15,13},{14,10},{11,... | collective-permute-start | bytes 663560 | tf_op jit(solution)/shard_map/ppermute | solution.py:322
  32.9 1.0 %gradient.11 = (f32[256,768]{1,0:T(8,128)S(1)}, f32[256,768]{1,0:T(8,128)S(1)}) custom-call(bf16[736,128]{1,0:T(8,128)(2,1)S(1)} %collective-permute-done.9.a_ref, bf16[144,768]{1,0:T(8,128)(2,1)S(1)} %collective-permute-done.3.b_ref, bf16[256,768]{1,0:T(8,128)(2,1)S(1)} %cast.1.refs_0_.cast_ref, ...), custom_call_target="tpu_custom_call", output_to_operand_aliasing={{0}: (4, {}), {1}: (5, {})} | custom-call | flops 1000000000 | bytes 1000000 | tf_op jit(solution)/shard_map/gradient/pallas_call | solution.py:210
  34.0 1.0 %gradient.12 = (f32[256,768]{1,0:T(8,128)S(1)}, f32[256,768]{1,0:T(8,128)S(1)}) custom-call(bf16[736,128]{1,0:T(8,128)(2,1)S(1)} %collective-permute-done.2.a_ref, bf16[144,768]{1,0:T(8,128)(2,1)S(1)} %collective-permute-done.8.b_ref, bf16[256,768]{1,0:T(8,128)(2,1)S(1)} %cast.1.refs_0_.cast_ref, ...), custom_call_target="tpu_custom_call", output_to_operand_aliasing={{0}: (4, {}), {1}: (5, {})} | custom-call | flops 1000000000 | bytes 1000000 | tf_op jit(solution)/shard_map/gradient/pallas_call | solution.py:210
  35.0 1.0 %gradient.13 = (f32[256,768]{1,0:T(8,128)S(1)}, f32[256,768]{1,0:T(8,128)S(1)}) custom-call(bf16[736,128]{1,0:T(8,128)(2,1)S(1)} %collective-permute-done.14.a_ref, bf16[144,768]{1,0:T(8,128)(2,1)S(1)} %collective-permute-done.7.b_ref, bf16[256,768]{1,0:T(8,128)(2,1)S(1)} %cast.1.refs_0_.cast_ref, ...), custom_call_target="tpu_custom_call", output_to_operand_aliasing={{0}: (4, {}), {1}: (5, {})} | custom-call | flops 1000000000 | bytes 1000000 | tf_op jit(solution)/shard_map/gradient/pallas_call | solution.py:210
  36.0 1.0 %gradient.14 = (f32[256,768]{1,0:T(8,128)S(1)}, f32[256,768]{1,0:T(8,128)S(1)}) custom-call(bf16[736,128]{1,0:T(8,128)(2,1)S(1)} %collective-permute-done.6.a_ref, bf16[144,768]{1,0:T(8,128)(2,1)S(1)} %collective-permute-done.13.b_ref, bf16[256,768]{1,0:T(8,128)(2,1)S(1)} %cast.1.refs_0_.cast_ref, ...), custom_call_target="tpu_custom_call", output_to_operand_aliasing={{0}: (4, {}), {1}: (5, {})} | custom-call | flops 1000000000 | bytes 1000000 | tf_op jit(solution)/shard_map/gradient/pallas_call | solution.py:210
  37.1 0.9 %collective-permute-done.12.b_ref = bf16[144,768]{1,0:T(8,128)(2,1)S(1)} collective-permute-done((bf16[144,768]{1,0:T(8,128)(2,1)S(1)}, bf16[144,768]{1,0:T(8,128)(2,1)S(1)}, u32[]{:S(2)}, u32[]{:S(2)}) %collective-permute-start.12) | collective-permute-done | bytes 221216 | tf_op jit(solution)/shard_map/ppermute | solution.py:322
  38.0 0.5 %collective-permute-done.11.a_ref = bf16[736,128]{1,0:T(8,128)(2,1)S(1)} collective-permute-done((bf16[736,128]{1,0:T(8,128)(2,1)S(1)}, bf16[736,128]{1,0:T(8,128)(2,1)S(1)}, u32[]{:S(2)}, u32[]{:S(2)}) %collective-permute-start.11) | collective-permute-done | bytes 188448 | tf_op jit(solution)/shard_map/ppermute | solution.py:322
  38.5 0.5 %collective-permute-start.15 = (bf16[736,128]{1,0:T(8,128)(2,1)S(1)}, bf16[736,128]{1,0:T(8,128)(2,1)S(1)}, u32[]{:S(2)}, u32[]{:S(2)}) collective-permute-start(bf16[736,128]{1,0:T(8,128)(2,1)S(1)} %collective-permute-done.11.a_ref), channel_id=1, source_target_pairs={{0,1},{1,0},{2,3},{3,2},{4,5},{5,4},{6,7},{7,6},{8,9},{9,8},{10,11... | collective-permute-start | bytes 565256 | tf_op jit(solution)/shard_map/ppermute | solution.py:322
  39.0 0.7 %gradient.15.sum_ref = f32[256,768]{1,0:T(8,128)S(1)} custom-call(bf16[736,128]{1,0:T(8,128)(2,1)S(1)} %collective-permute-done.11.a_ref, bf16[144,768]{1,0:T(8,128)(2,1)S(1)} %collective-permute-done.12.b_ref, bf16[256,768]{1,0:T(8,128)(2,1)S(1)} %cast.1.refs_0_.cast_ref, f32[256,768]{1,0:T(8,128)S(1)} %get-tuple-element.175.refs_1_), custom_call_target="tpu_custom_call", output_to_operand_aliasing={{}: (3, {})} | custom-call | flops 10000000000 | bytes 1000000 | tf_op jit(solution)/shard_map/gradient/pallas_call | solution.py:210
  39.6 0.6 %collective-permute-done.15.a_ref = bf16[736,128]{1,0:T(8,128)(2,1)S(1)} collective-permute-done((bf16[736,128]{1,0:T(8,128)(2,1)S(1)}, bf16[736,128]{1,0:T(8,128)(2,1)S(1)}, u32[]{:S(2)}, u32[]{:S(2)}) %collective-permute-start.15) | collective-permute-done | bytes 188448 | tf_op jit(solution)/shard_map/ppermute | solution.py:322
  40.3 2.4 %finish.1 = (f32[256,768]{1,0:T(8,128)}, f32[256,768]{1,0:T(8,128)}, f32[256,768]{1,0:T(8,128)}) custom-call(bf16[736,128]{1,0:T(8,128)(2,1)S(1)} %collective-permute-done.15.a_ref, bf16[144,768]{1,0:T(8,128)(2,1)S(1)} %collective-permute-done.16.b_ref, bf16[256,768]{1,0:T(8,128)(2,1)S(1)} %cast.1.refs_0_.cast_ref, f32[256,768]{1,0:T(8,128)S(1)} %gradient.15.sum_ref, ...), custom_call_target="tpu_custom_call" | custom-call | flops 10000000000 | bytes 1000000 | tf_op jit(solution)/shard_map/finish/pallas_call | solution.py:267
  (24 shorter events, 2.4 us)
Async XLA Ops:
  1.7 7.9 %collective-permute-start.1 = (bf16[144,768]{1,0:T(8,128)(2,1)S(1)}, bf16[144,768]{1,0:T(8,128)(2,1)S(1)}, u32[]{:S(2)}, u32[]{:S(2)}) collective-permute-start(bf16[144,768]{1,0:T(8,128)(2,1)S(1)} %get-tuple-element.122.b_ref), channel_id=1, source_target_pairs={{0,4},{5,1},{4,8},{9,5},{8,12},{13,9},{12,14},{15,13},{14,10},{11,... | collective-permute-start | bytes 663560 | tf_op jit(solution)/shard_map/ppermute | solution.py:322
  4.8 1.1 %copy-start = (f32[256,768]{1,0:T(8,128)S(1)}, f32[256,768]{1,0:T(8,128)}, u32[]{:S(2)}) copy-start(f32[256,768]{1,0:T(8,128)} %weights_ref.3) | copy-start | bytes 2359300
  6.0 17.8 %collective-permute-start.10 = (bf16[256,768]{1,0:T(8,128)(2,1)S(1)}, bf16[256,768]{1,0:T(8,128)(2,1)S(1)}, u32[]{:S(2)}, u32[]{:S(2)}) collective-permute-start(bf16[256,768]{1,0:T(8,128)(2,1)S(1)} %cast.1.refs_0_.cast_ref), channel_id=1, source_target_pairs={{0,1},{1,0},{2,3},{3,2},{4,5},{5,4},{6,7},{7,6},{8,9},{9,8},{10,11... | collective-permute-start | bytes 1179656 | tf_op jit(solution)/shard_map/ppermute | solution.py:322
  6.5 6.9 %collective-permute-start = (bf16[736,128]{1,0:T(8,128)(2,1)S(1)}, bf16[736,128]{1,0:T(8,128)(2,1)S(1)}, u32[]{:S(2)}, u32[]{:S(2)}) collective-permute-start(bf16[736,128]{1,0:T(8,128)(2,1)S(1)} %prepare.1.a_ref), channel_id=1, source_target_pairs={{4,0},{1,5},{8,4},{5,9},{12,8},{9,13},{14,12},{13,15},{10,14},{15,... | collective-permute-start | bytes 565256 | tf_op jit(solution)/shard_map/ppermute | solution.py:322
  7.6 7.7 %collective-permute-start.5 = (bf16[736,128]{1,0:T(8,128)(2,1)S(1)}, bf16[736,128]{1,0:T(8,128)(2,1)S(1)}, u32[]{:S(2)}, u32[]{:S(2)}) collective-permute-start(bf16[736,128]{1,0:T(8,128)(2,1)S(1)} %prepare.1.a_ref), channel_id=1, source_target_pairs={{0,4},{5,1},{4,8},{9,5},{8,12},{13,9},{12,14},{15,13},{14,10},{11,... | collective-permute-start | bytes 565256 | tf_op jit(solution)/shard_map/ppermute | solution.py:322
  8.6 9.5 %collective-permute-start.4 = (bf16[144,768]{1,0:T(8,128)(2,1)S(1)}, bf16[144,768]{1,0:T(8,128)(2,1)S(1)}, u32[]{:S(2)}, u32[]{:S(2)}) collective-permute-start(bf16[144,768]{1,0:T(8,128)(2,1)S(1)} %get-tuple-element.122.b_ref), channel_id=1, source_target_pairs={{4,0},{1,5},{8,4},{5,9},{12,8},{9,13},{14,12},{13,15},{10,14},{15,... | collective-permute-start | bytes 663560 | tf_op jit(solution)/shard_map/ppermute | solution.py:322
  9.6 10.4 %collective-permute-start.3 = (bf16[144,768]{1,0:T(8,128)(2,1)S(1)}, bf16[144,768]{1,0:T(8,128)(2,1)S(1)}, u32[]{:S(2)}, u32[]{:S(2)}) collective-permute-start(bf16[144,768]{1,0:T(8,128)(2,1)S(1)} %collective-permute-done.1.b_ref), channel_id=1, source_target_pairs={{0,4},{5,1},{4,8},{9,5},{8,12},{13,9},{12,14},{15,13},{14,10},{11,... | collective-permute-start | bytes 663560 | tf_op jit(solution)/shard_map/ppermute | solution.py:322
  13.4 8.8 %collective-permute-start.2 = (bf16[736,128]{1,0:T(8,128)(2,1)S(1)}, bf16[736,128]{1,0:T(8,128)(2,1)S(1)}, u32[]{:S(2)}, u32[]{:S(2)}) collective-permute-start(bf16[736,128]{1,0:T(8,128)(2,1)S(1)} %collective-permute-done.a_ref), channel_id=1, source_target_pairs={{4,0},{1,5},{8,4},{5,9},{12,8},{9,13},{14,12},{13,15},{10,14},{15,... | collective-permute-start | bytes 565256 | tf_op jit(solution)/shard_map/ppermute | solution.py:322
  15.3 9.5 %collective-permute-start.9 = (bf16[736,128]{1,0:T(8,128)(2,1)S(1)}, bf16[736,128]{1,0:T(8,128)(2,1)S(1)}, u32[]{:S(2)}, u32[]{:S(2)}) collective-permute-start(bf16[736,128]{1,0:T(8,128)(2,1)S(1)} %collective-permute-done.5.a_ref), channel_id=1, source_target_pairs={{0,4},{5,1},{4,8},{9,5},{8,12},{13,9},{12,14},{15,13},{14,10},{11,... | collective-permute-start | bytes 565256 | tf_op jit(solution)/shard_map/ppermute | solution.py:322
  18.1 8.8 %collective-permute-start.8 = (bf16[144,768]{1,0:T(8,128)(2,1)S(1)}, bf16[144,768]{1,0:T(8,128)(2,1)S(1)}, u32[]{:S(2)}, u32[]{:S(2)}) collective-permute-start(bf16[144,768]{1,0:T(8,128)(2,1)S(1)} %collective-permute-done.4.b_ref), channel_id=1, source_target_pairs={{4,0},{1,5},{8,4},{5,9},{12,8},{9,13},{14,12},{13,15},{10,14},{15,... | collective-permute-start | bytes 663560 | tf_op jit(solution)/shard_map/ppermute | solution.py:322
  20.0 8.8 %collective-permute-start.7 = (bf16[144,768]{1,0:T(8,128)(2,1)S(1)}, bf16[144,768]{1,0:T(8,128)(2,1)S(1)}, u32[]{:S(2)}, u32[]{:S(2)}) collective-permute-start(bf16[144,768]{1,0:T(8,128)(2,1)S(1)} %collective-permute-done.3.b_ref), channel_id=1, source_target_pairs={{0,4},{5,1},{4,8},{9,5},{8,12},{13,9},{12,14},{15,13},{14,10},{11,... | collective-permute-start | bytes 663560 | tf_op jit(solution)/shard_map/ppermute | solution.py:322
  22.1 8.8 %collective-permute-start.6 = (bf16[736,128]{1,0:T(8,128)(2,1)S(1)}, bf16[736,128]{1,0:T(8,128)(2,1)S(1)}, u32[]{:S(2)}, u32[]{:S(2)}) collective-permute-start(bf16[736,128]{1,0:T(8,128)(2,1)S(1)} %collective-permute-done.2.a_ref), channel_id=1, source_target_pairs={{4,0},{1,5},{8,4},{5,9},{12,8},{9,13},{14,12},{13,15},{10,14},{15,... | collective-permute-start | bytes 565256 | tf_op jit(solution)/shard_map/ppermute | solution.py:322
  24.8 10.2 %collective-permute-start.14 = (bf16[736,128]{1,0:T(8,128)(2,1)S(1)}, bf16[736,128]{1,0:T(8,128)(2,1)S(1)}, u32[]{:S(2)}, u32[]{:S(2)}) collective-permute-start(bf16[736,128]{1,0:T(8,128)(2,1)S(1)} %collective-permute-done.9.a_ref), channel_id=1, source_target_pairs={{0,4},{5,1},{4,8},{9,5},{8,12},{13,9},{12,14},{15,13},{14,10},{11,... | collective-permute-start | bytes 565256 | tf_op jit(solution)/shard_map/ppermute | solution.py:322
  26.9 9.1 %collective-permute-start.13 = (bf16[144,768]{1,0:T(8,128)(2,1)S(1)}, bf16[144,768]{1,0:T(8,128)(2,1)S(1)}, u32[]{:S(2)}, u32[]{:S(2)}) collective-permute-start(bf16[144,768]{1,0:T(8,128)(2,1)S(1)} %collective-permute-done.8.b_ref), channel_id=1, source_target_pairs={{4,0},{1,5},{8,4},{5,9},{12,8},{9,13},{14,12},{13,15},{10,14},{15,... | collective-permute-start | bytes 663560 | tf_op jit(solution)/shard_map/ppermute | solution.py:322
  30.9 7.1 %collective-permute-start.12 = (bf16[144,768]{1,0:T(8,128)(2,1)S(1)}, bf16[144,768]{1,0:T(8,128)(2,1)S(1)}, u32[]{:S(2)}, u32[]{:S(2)}) collective-permute-start(bf16[144,768]{1,0:T(8,128)(2,1)S(1)} %collective-permute-done.7.b_ref), channel_id=1, source_target_pairs={{0,4},{5,1},{4,8},{9,5},{8,12},{13,9},{12,14},{15,13},{14,10},{11,... | collective-permute-start | bytes 663560 | tf_op jit(solution)/shard_map/ppermute | solution.py:322
  32.5 6.0 %collective-permute-start.11 = (bf16[736,128]{1,0:T(8,128)(2,1)S(1)}, bf16[736,128]{1,0:T(8,128)(2,1)S(1)}, u32[]{:S(2)}, u32[]{:S(2)}) collective-permute-start(bf16[736,128]{1,0:T(8,128)(2,1)S(1)} %collective-permute-done.6.a_ref), channel_id=1, source_target_pairs={{4,0},{1,5},{8,4},{5,9},{12,8},{9,13},{14,12},{13,15},{10,14},{15,... | collective-permute-start | bytes 565256 | tf_op jit(solution)/shard_map/ppermute | solution.py:322
  37.1 3.2 %collective-permute-start.17 = (f32[256,768]{1,0:T(8,128)S(1)}, f32[256,768]{1,0:T(8,128)S(1)}, u32[]{:S(2)}, u32[]{:S(2)}) collective-permute-start(f32[256,768]{1,0:T(8,128)S(1)} %get-tuple-element.176), channel_id=1, source_target_pairs={{0,1},{1,0},{2,3},{3,2},{4,5},{5,4},{6,7},{7,6},{8,9},{9,8},{10,11... | collective-permute-start | bytes 2359304 | tf_op jit(solution)/shard_map/ppermute | solution.py:322
  38.0 2.2 %copy-start.1 = (f32[256,768]{1,0:T(8,128)S(1)}, f32[256,768]{1,0:T(8,128)}, u32[]{:S(2)}) copy-start(f32[256,768]{1,0:T(8,128)} %weights_ref.3) | copy-start | bytes 2359300
  38.0 2.2 %copy-start.2 = (f32[256,768]{1,0:T(8,128)S(1)}, f32[256,768]{1,0:T(8,128)}, u32[]{:S(2)}) copy-start(f32[256,768]{1,0:T(8,128)} %first_ref.1) | copy-start | bytes 2359300
  38.0 2.2 %copy-start.3 = (f32[256,768]{1,0:T(8,128)S(1)}, f32[256,768]{1,0:T(8,128)}, u32[]{:S(2)}) copy-start(f32[256,768]{1,0:T(8,128)} %second_ref.1) | copy-start | bytes 2359300
  38.5 1.8 %collective-permute-start.16 = (bf16[144,768]{1,0:T(8,128)(2,1)S(1)}, bf16[144,768]{1,0:T(8,128)(2,1)S(1)}, u32[]{:S(2)}, u32[]{:S(2)}) collective-permute-start(bf16[144,768]{1,0:T(8,128)(2,1)S(1)} %collective-permute-done.12.b_ref), channel_id=1, source_target_pairs={{0,1},{1,0},{2,3},{3,2},{4,5},{5,4},{6,7},{7,6},{8,9},{9,8},{10,11... | collective-permute-start | bytes 663560 | tf_op jit(solution)/shard_map/ppermute | solution.py:322
  38.5 1.7 %collective-permute-start.15 = (bf16[736,128]{1,0:T(8,128)(2,1)S(1)}, bf16[736,128]{1,0:T(8,128)(2,1)S(1)}, u32[]{:S(2)}, u32[]{:S(2)}) collective-permute-start(bf16[736,128]{1,0:T(8,128)(2,1)S(1)} %collective-permute-done.11.a_ref), channel_id=1, source_target_pairs={{0,1},{1,0},{2,3},{3,2},{4,5},{5,4},{6,7},{7,6},{8,9},{9,8},{10,11... | collective-permute-start | bytes 565256 | tf_op jit(solution)/shard_map/ppermute | solution.py:322

commit v20 on v18

--- a/solution.py
+++ b/solution.py
@@ -21,7 +21,7 @@
 PIECES = 2
 VMEM_LIMIT = 32 * 1024 * 1024
 FLOPS = 2 * 10**8
-LATE_FLOPS = 10 * 10**8
+LATE_FLOPS = 5 * 10**8
 END_FLOPS = 100 * 10**8
 
 
@@ -343,19 +343,21 @@
                 side = message.split("_")[0]
                 waiting.append((came[side + "_a"], came[side + "_b"]))
             if last:
-                number = 2 if message == "down_a" else 1
+                number = {"down_a": 2, "down_b": 0}.get(message, 1)
             else:
                 number = 1 if step > 1 and message in ("down_a", "up_a") else 0
             for _ in range(min(number, len(waiting))):
                 sums = work(LATE_FLOPS if last else FLOPS)
-    while waiting:
+    while len(waiting) > 1:
         sums = work(LATE_FLOPS)
-    mine_sum, other_sum = sums
+    docs = waiting.pop()
+    (other_sum,) = add_gradient(bits, (1,), *docs, cast[1:], sums[1:], LATE_FLOPS)
     got = send(other_sum, swap)
+    (mine_sum,) = add_gradient(bits, (0,), *docs, cast[:1], sums[:1], LATE_FLOPS)
+    last_a, mine_sum = together((coming["down_a"], mine_sum))
+    beside_a = send(last_a, swap)
     last_b, mine_sum = together((coming["up_b"], mine_sum))
     beside_b = send(last_b, swap)
-    last_a, mine_sum = together((coming["down_a"], mine_sum))
-    beside_a = send(last_a, swap)
     (mine_sum,) = add_gradient(bits, (0,), last_a, last_b, [mine], [mine_sum], END_FLOPS)
     state = (weights, first_moment, second_moment)
     return finish(bits, beside_a, beside_b, mine, mine_sum, got, *state)

time: 40.7 us -> 41.8 us (1.027)
  waiting for transfers between devices: 6.14 us -> 8.84 us
  starting transfers between devices: 21.9 us -> 20 us
    ppermute x18, waiting for transfers between devices: 6.14 us -> 8.84 us  [send(): return lax.ppermute(value, 'blk', pairs)]
    ppermute x18, starting transfers between devices: 21.9 us -> 20 us  [send(): return lax.ppermute(value, 'blk', pairs)]
    pallas_call x8 -> x9, Pallas kernels: 7.7 us -> 8 us  [add_gradient(): pl.pallas_call(functools.partial(gradient_kernel, bits, owners, not sums)...]
  transfers between devices with their start and end apart: 18 -> 18, of which waited for: 10 -> 8; matrix products, arithmetic and copies ran while one was open for 0% -> 0% of each run, Pallas kernels for 20% -> 19%
where the time goes in v20:
time: 41.8 us; the launch traced here: 41.7 us
  starting transfers between devices  20 us (48%)
  Pallas kernels  12 us (29%)
  waiting for transfers between devices  8.84 us (21%)
  between operations  0.81 us (2%)
    ppermute x18, starting transfers between devices, send(): return lax.ppermute(value, 'blk', pairs)  20 us
    ppermute x18, waiting for transfers between devices, send(): return lax.ppermute(value, 'blk', pairs)  8.84 us
    pallas_call x9, Pallas kernels, add_gradient(): pl.pallas_call(functools.partial(gradient_kernel, bits, owners, not sums)...  8 us
    pallas_call x1, Pallas kernels, finish(): pl.pallas_call(functools.partial(finish_kernel, bits), in_specs=[pl.Block...  2.35 us
    pallas_call x1, Pallas kernels, fetch(): pl.pallas_call(fetch_kernel, in_specs=[pl.BlockSpec(memory_space=pltpu.HB...  1.14 us
  transfers between devices with their start and end apart: 18, of which 8 were waited for; matrix products, arithmetic and copies ran while one was open for 0% of the time, Pallas kernels for 19%

profile of v20, /device:TPU:0, one launch (start us, length us, event | category | flops | bytes accessed | tf_op | source)
XLA Modules:
  0.0 41.7 jit_solution(15700476708388523525)
XLA Ops:
  0.6 1.1 %fetch.1 = (bf16[128,768]{1,0:T(8,128)(2,1)S(1)}, bf16[128,768]{1,0:T(8,128)(2,1)S(1)}, s32[32,256]{1,0:T(8,128)S(1)}, s32[1,256]{1,0:T(1,128)S(1)}, s32[32,128]{1,0:T(8,128)S(1)}) custom-call(s32[32,256]{1,0:T(8,128)} %bitcast.3, s32[1,256]{1,0:T(1,128)} %bitcast.5, s32[32,128]{1,0:T(8,128)} %bitcast.4, bf16[256,768]{1,0:T(8,128)(2,1)} %docs_hbm.1), custom_call_target="tpu_custom_call" | custom-call | tf_op jit(solution)/shard_map/fetch/pallas_call | solution.py:70
  1.8 0.4 %prepare.1.a_ref = bf16[832,128]{1,0:T(8,128)(2,1)S(1)} custom-call(bf16[128,768]{1,0:T(8,128)(2,1)S(1)} %get-tuple-element.88.top_ref, s32[32,256]{1,0:T(8,128)S(1)} %get-tuple-element.89.ids_ref, s32[1,256]{1,0:T(1,128)S(1)} %get-tuple-element.90.count_ref, s32[32,128]{1,0:T(8,128)S(1)} %get-tuple-element.91.table_ref), custom_call_target="tpu_custom_call" | custom-call | tf_op jit(solution)/shard_map/prepare/pallas_call | solution.py:126
  2.2 3.0 %collective-permute-start = (bf16[832,128]{1,0:T(8,128)(2,1)S(1)}, bf16[832,128]{1,0:T(8,128)(2,1)S(1)}, u32[]{:S(2)}, u32[]{:S(2)}) collective-permute-start(bf16[832,128]{1,0:T(8,128)(2,1)S(1)} %prepare.1.a_ref), channel_id=1, source_target_pairs={{4,0},{1,5},{8,4},{5,9},{12,8},{9,13},{14,12},{13,15},{10,14},{15,... | collective-permute-start | bytes 638984 | tf_op jit(solution)/shard_map/ppermute | solution.py:320
  5.4 2.0 %collective-permute-start.5 = (bf16[832,128]{1,0:T(8,128)(2,1)S(1)}, bf16[832,128]{1,0:T(8,128)(2,1)S(1)}, u32[]{:S(2)}, u32[]{:S(2)}) collective-permute-start(bf16[832,128]{1,0:T(8,128)(2,1)S(1)} %prepare.1.a_ref), channel_id=1, source_target_pairs={{0,4},{5,1},{4,8},{9,5},{8,12},{13,9},{12,14},{15,13},{14,10},{11,... | collective-permute-start | bytes 638984 | tf_op jit(solution)/shard_map/ppermute | solution.py:320
  7.5 0.5 %collective-permute-start.4 = (bf16[128,768]{1,0:T(8,128)(2,1)S(1)}, bf16[128,768]{1,0:T(8,128)(2,1)S(1)}, u32[]{:S(2)}, u32[]{:S(2)}) collective-permute-start(bf16[128,768]{1,0:T(8,128)(2,1)S(1)} %get-tuple-element.120.b_ref), channel_id=1, source_target_pairs={{4,0},{1,5},{8,4},{5,9},{12,8},{9,13},{14,12},{13,15},{10,14},{15,... | collective-permute-start | bytes 589832 | tf_op jit(solution)/shard_map/ppermute | solution.py:320
  8.0 3.2 %collective-permute-done.1.b_ref = bf16[128,768]{1,0:T(8,128)(2,1)S(1)} collective-permute-done((bf16[128,768]{1,0:T(8,128)(2,1)S(1)}, bf16[128,768]{1,0:T(8,128)(2,1)S(1)}, u32[]{:S(2)}, u32[]{:S(2)}) %collective-permute-start.1) | collective-permute-done | bytes 196640 | tf_op jit(solution)/shard_map/ppermute | solution.py:320
  11.2 0.9 %collective-permute-start.3 = (bf16[128,768]{1,0:T(8,128)(2,1)S(1)}, bf16[128,768]{1,0:T(8,128)(2,1)S(1)}, u32[]{:S(2)}, u32[]{:S(2)}) collective-permute-start(bf16[128,768]{1,0:T(8,128)(2,1)S(1)} %collective-permute-done.1.b_ref), channel_id=1, source_target_pairs={{0,4},{5,1},{4,8},{9,5},{8,12},{13,9},{12,14},{15,13},{14,10},{11,... | collective-permute-start | bytes 589832 | tf_op jit(solution)/shard_map/ppermute | solution.py:320
  12.1 2.2 %collective-permute-start.2 = (bf16[832,128]{1,0:T(8,128)(2,1)S(1)}, bf16[832,128]{1,0:T(8,128)(2,1)S(1)}, u32[]{:S(2)}, u32[]{:S(2)}) collective-permute-start(bf16[832,128]{1,0:T(8,128)(2,1)S(1)} %collective-permute-done.a_ref), channel_id=1, source_target_pairs={{4,0},{1,5},{8,4},{5,9},{12,8},{9,13},{14,12},{13,15},{10,14},{15,... | collective-permute-start | bytes 638984 | tf_op jit(solution)/shard_map/ppermute | solution.py:320
  14.3 1.5 %collective-permute-done.5.a_ref = bf16[832,128]{1,0:T(8,128)(2,1)S(1)} collective-permute-done((bf16[832,128]{1,0:T(8,128)(2,1)S(1)}, bf16[832,128]{1,0:T(8,128)(2,1)S(1)}, u32[]{:S(2)}, u32[]{:S(2)}) %collective-permute-start.5) | collective-permute-done | bytes 213024 | tf_op jit(solution)/shard_map/ppermute | solution.py:320
  15.8 0.8 %collective-permute-start.9 = (bf16[832,128]{1,0:T(8,128)(2,1)S(1)}, bf16[832,128]{1,0:T(8,128)(2,1)S(1)}, u32[]{:S(2)}, u32[]{:S(2)}) collective-permute-start(bf16[832,128]{1,0:T(8,128)(2,1)S(1)} %collective-permute-done.5.a_ref), channel_id=1, source_target_pairs={{0,4},{5,1},{4,8},{9,5},{8,12},{13,9},{12,14},{15,13},{14,10},{11,... | collective-permute-start | bytes 638984 | tf_op jit(solution)/shard_map/ppermute | solution.py:320
  16.6 2.0 %collective-permute-start.8 = (bf16[128,768]{1,0:T(8,128)(2,1)S(1)}, bf16[128,768]{1,0:T(8,128)(2,1)S(1)}, u32[]{:S(2)}, u32[]{:S(2)}) collective-permute-start(bf16[128,768]{1,0:T(8,128)(2,1)S(1)} %collective-permute-done.4.b_ref), channel_id=1, source_target_pairs={{4,0},{1,5},{8,4},{5,9},{12,8},{9,13},{14,12},{13,15},{10,14},{15,... | collective-permute-start | bytes 589832 | tf_op jit(solution)/shard_map/ppermute | solution.py:320
  18.6 1.5 %collective-permute-done.3.b_ref = bf16[128,768]{1,0:T(8,128)(2,1)S(1)} collective-permute-done((bf16[128,768]{1,0:T(8,128)(2,1)S(1)}, bf16[128,768]{1,0:T(8,128)(2,1)S(1)}, u32[]{:S(2)}, u32[]{:S(2)}) %collective-permute-start.3) | collective-permute-done | bytes 196640 | tf_op jit(solution)/shard_map/ppermute | solution.py:320
  20.1 0.7 %collective-permute-start.7 = (bf16[128,768]{1,0:T(8,128)(2,1)S(1)}, bf16[128,768]{1,0:T(8,128)(2,1)S(1)}, u32[]{:S(2)}, u32[]{:S(2)}) collective-permute-start(bf16[128,768]{1,0:T(8,128)(2,1)S(1)} %collective-permute-done.3.b_ref), channel_id=1, source_target_pairs={{0,4},{5,1},{4,8},{9,5},{8,12},{13,9},{12,14},{15,13},{14,10},{11,... | collective-permute-start | bytes 589832 | tf_op jit(solution)/shard_map/ppermute | solution.py:320
  20.8 2.0 %collective-permute-start.6 = (bf16[832,128]{1,0:T(8,128)(2,1)S(1)}, bf16[832,128]{1,0:T(8,128)(2,1)S(1)}, u32[]{:S(2)}, u32[]{:S(2)}) collective-permute-start(bf16[832,128]{1,0:T(8,128)(2,1)S(1)} %collective-permute-done.2.a_ref), channel_id=1, source_target_pairs={{4,0},{1,5},{8,4},{5,9},{12,8},{9,13},{14,12},{13,15},{10,14},{15,... | collective-permute-start | bytes 638984 | tf_op jit(solution)/shard_map/ppermute | solution.py:320
  22.8 1.0 %gradient.9 = (f32[256,768]{1,0:T(8,128)S(1)}, f32[256,768]{1,0:T(8,128)S(1)}) custom-call(bf16[832,128]{1,0:T(8,128)(2,1)S(1)} %prepare.1.a_ref, bf16[128,768]{1,0:T(8,128)(2,1)S(1)} %get-tuple-element.120.b_ref, bf16[256,768]{1,0:T(8,128)(2,1)S(1)} %cast.1.refs_0_.cast_ref, bf16[256,768]{1,0:T(8,128)(2,1)S(1)} %collective-permute-done.10.refs_1_.refs_0_), custom_call_target="tpu_custom_call" | custom-call | flops 200000000 | bytes 1000000 | tf_op jit(solution)/shard_map/gradient/pallas_call | solution.py:209
  23.8 1.0 %collective-permute-done.9.a_ref = bf16[832,128]{1,0:T(8,128)(2,1)S(1)} collective-permute-done((bf16[832,128]{1,0:T(8,128)(2,1)S(1)}, bf16[832,128]{1,0:T(8,128)(2,1)S(1)}, u32[]{:S(2)}, u32[]{:S(2)}) %collective-permute-start.9) | collective-permute-done | bytes 213024 | tf_op jit(solution)/shard_map/ppermute | solution.py:320
  24.8 0.6 %collective-permute-start.13 = (bf16[832,128]{1,0:T(8,128)(2,1)S(1)}, bf16[832,128]{1,0:T(8,128)(2,1)S(1)}, u32[]{:S(2)}, u32[]{:S(2)}) collective-permute-start(bf16[832,128]{1,0:T(8,128)(2,1)S(1)} %collective-permute-done.9.a_ref), channel_id=1, source_target_pairs={{0,4},{5,1},{4,8},{9,5},{8,12},{13,9},{12,14},{15,13},{14,10},{11,... | collective-permute-start | bytes 638984 | tf_op jit(solution)/shard_map/ppermute | solution.py:320
  25.4 1.0 %gradient.10 = (f32[256,768]{1,0:T(8,128)S(1)}, f32[256,768]{1,0:T(8,128)S(1)}) custom-call(bf16[832,128]{1,0:T(8,128)(2,1)S(1)} %collective-permute-done.5.a_ref, bf16[128,768]{1,0:T(8,128)(2,1)S(1)} %collective-permute-done.1.b_ref, bf16[256,768]{1,0:T(8,128)(2,1)S(1)} %cast.1.refs_0_.cast_ref, ...), custom_call_target="tpu_custom_call", output_to_operand_aliasing={{0}: (4, {}), {1}: (5, {})} | custom-call | flops 200000000 | bytes 1000000 | tf_op jit(solution)/shard_map/gradient/pallas_call | solution.py:209
  26.4 2.0 %collective-permute-start.12 = (bf16[128,768]{1,0:T(8,128)(2,1)S(1)}, bf16[128,768]{1,0:T(8,128)(2,1)S(1)}, u32[]{:S(2)}, u32[]{:S(2)}) collective-permute-start(bf16[128,768]{1,0:T(8,128)(2,1)S(1)} %collective-permute-done.8.b_ref), channel_id=1, source_target_pairs={{4,0},{1,5},{8,4},{5,9},{12,8},{9,13},{14,12},{13,15},{10,14},{15,... | collective-permute-start | bytes 589832 | tf_op jit(solution)/shard_map/ppermute | solution.py:320
  28.5 0.4 collective-permute-done.7.b_ref
  28.8 0.8 %collective-permute-start.15 = (bf16[128,768]{1,0:T(8,128)(2,1)S(1)}, bf16[128,768]{1,0:T(8,128)(2,1)S(1)}, u32[]{:S(2)}, u32[]{:S(2)}) collective-permute-start(bf16[128,768]{1,0:T(8,128)(2,1)S(1)} %collective-permute-done.7.b_ref), channel_id=1, source_target_pairs={{0,4},{5,1},{4,8},{9,5},{8,12},{13,9},{12,14},{15,13},{14,10},{11,... | collective-permute-start | bytes 589832 | tf_op jit(solution)/shard_map/ppermute | solution.py:320
  29.6 1.0 %gradient.11 = (f32[256,768]{1,0:T(8,128)S(1)}, f32[256,768]{1,0:T(8,128)S(1)}) custom-call(bf16[832,128]{1,0:T(8,128)(2,1)S(1)} %collective-permute-done.a_ref, bf16[128,768]{1,0:T(8,128)(2,1)S(1)} %collective-permute-done.4.b_ref, bf16[256,768]{1,0:T(8,128)(2,1)S(1)} %cast.1.refs_0_.cast_ref, ...), custom_call_target="tpu_custom_call", output_to_operand_aliasing={{0}: (4, {}), {1}: (5, {})} | custom-call | flops 500000000 | bytes 1000000 | tf_op jit(solution)/shard_map/gradient/pallas_call | solution.py:209
  30.6 1.7 %collective-permute-start.11 = (bf16[832,128]{1,0:T(8,128)(2,1)S(1)}, bf16[832,128]{1,0:T(8,128)(2,1)S(1)}, u32[]{:S(2)}, u32[]{:S(2)}) collective-permute-start(bf16[832,128]{1,0:T(8,128)(2,1)S(1)} %collective-permute-done.6.a_ref), channel_id=1, source_target_pairs={{4,0},{1,5},{8,4},{5,9},{12,8},{9,13},{14,12},{13,15},{10,14},{15,... | collective-permute-start | bytes 638984 | tf_op jit(solution)/shard_map/ppermute | solution.py:320
  32.4 1.0 %gradient.12 = (f32[256,768]{1,0:T(8,128)S(1)}, f32[256,768]{1,0:T(8,128)S(1)}) custom-call(bf16[832,128]{1,0:T(8,128)(2,1)S(1)} %collective-permute-done.9.a_ref, bf16[128,768]{1,0:T(8,128)(2,1)S(1)} %collective-permute-done.3.b_ref, bf16[256,768]{1,0:T(8,128)(2,1)S(1)} %cast.1.refs_0_.cast_ref, ...), custom_call_target="tpu_custom_call", output_to_operand_aliasing={{0}: (4, {}), {1}: (5, {})} | custom-call | flops 500000000 | bytes 1000000 | tf_op jit(solution)/shard_map/gradient/pallas_call | solution.py:209
  33.4 1.0 %gradient.13 = (f32[256,768]{1,0:T(8,128)S(1)}, f32[256,768]{1,0:T(8,128)S(1)}) custom-call(bf16[832,128]{1,0:T(8,128)(2,1)S(1)} %collective-permute-done.2.a_ref, bf16[128,768]{1,0:T(8,128)(2,1)S(1)} %collective-permute-done.8.b_ref, bf16[256,768]{1,0:T(8,128)(2,1)S(1)} %cast.1.refs_0_.cast_ref, ...), custom_call_target="tpu_custom_call", output_to_operand_aliasing={{0}: (4, {}), {1}: (5, {})} | custom-call | flops 500000000 | bytes 1000000 | tf_op jit(solution)/shard_map/gradient/pallas_call | solution.py:209
  34.4 1.0 %gradient.14 = (f32[256,768]{1,0:T(8,128)S(1)}, f32[256,768]{1,0:T(8,128)S(1)}) custom-call(bf16[832,128]{1,0:T(8,128)(2,1)S(1)} %collective-permute-done.13.a_ref, bf16[128,768]{1,0:T(8,128)(2,1)S(1)} %collective-permute-done.7.b_ref, bf16[256,768]{1,0:T(8,128)(2,1)S(1)} %cast.1.refs_0_.cast_ref, ...), custom_call_target="tpu_custom_call", output_to_operand_aliasing={{0}: (4, {}), {1}: (5, {})} | custom-call | flops 500000000 | bytes 1000000 | tf_op jit(solution)/shard_map/gradient/pallas_call | solution.py:209
  35.4 0.7 %gradient.17 = f32[256,768]{1,0:T(8,128)S(1)} custom-call(bf16[832,128]{1,0:T(8,128)(2,1)S(1)} %collective-permute-done.6.a_ref, bf16[128,768]{1,0:T(8,128)(2,1)S(1)} %collective-permute-done.12.b_ref, bf16[256,768]{1,0:T(8,128)(2,1)S(1)} %collective-permute-done.10.refs_1_.refs_0_, ...), custom_call_target="tpu_custom_call", output_to_operand_aliasing={{}: (3, {})} | custom-call | flops 500000000 | bytes 1000000 | tf_op jit(solution)/shard_map/gradient/pallas_call | solution.py:209
  36.2 0.7 %gradient.15.refs_1_ = f32[256,768]{1,0:T(8,128)S(1)} custom-call(bf16[832,128]{1,0:T(8,128)(2,1)S(1)} %collective-permute-done.6.a_ref, bf16[128,768]{1,0:T(8,128)(2,1)S(1)} %collective-permute-done.12.b_ref, bf16[256,768]{1,0:T(8,128)(2,1)S(1)} %cast.1.refs_0_.cast_ref, f32[256,768]{1,0:T(8,128)S(1)} %get-tuple-element.167.refs_1_), custom_call_target="tpu_custom_call", output_to_operand_aliasing={{}: (3, {})} | custom-call | flops 500000000 | bytes 1000000 | tf_op jit(solution)/shard_map/gradient/pallas_call | solution.py:209
  36.9 0.7 %collective-permute-done.11.a_ref = bf16[832,128]{1,0:T(8,128)(2,1)S(1)} collective-permute-done((bf16[832,128]{1,0:T(8,128)(2,1)S(1)}, bf16[832,128]{1,0:T(8,128)(2,1)S(1)}, u32[]{:S(2)}, u32[]{:S(2)}) %collective-permute-start.11) | collective-permute-done | bytes 213024 | tf_op jit(solution)/shard_map/ppermute | solution.py:320
  37.6 0.5 %collective-permute-start.14 = (bf16[832,128]{1,0:T(8,128)(2,1)S(1)}, bf16[832,128]{1,0:T(8,128)(2,1)S(1)}, u32[]{:S(2)}, u32[]{:S(2)}) collective-permute-start(bf16[832,128]{1,0:T(8,128)(2,1)S(1)} %collective-permute-done.11.a_ref), channel_id=1, source_target_pairs={{0,1},{1,0},{2,3},{3,2},{4,5},{5,4},{6,7},{7,6},{8,9},{9,8},{10,11... | collective-permute-start | bytes 638984 | tf_op jit(solution)/shard_map/ppermute | solution.py:320
  38.1 0.7 %gradient.16.sum_ref = f32[256,768]{1,0:T(8,128)S(1)} custom-call(bf16[832,128]{1,0:T(8,128)(2,1)S(1)} %collective-permute-done.11.a_ref, bf16[128,768]{1,0:T(8,128)(2,1)S(1)} %collective-permute-done.15.b_ref, bf16[256,768]{1,0:T(8,128)(2,1)S(1)} %cast.1.refs_0_.cast_ref, f32[256,768]{1,0:T(8,128)S(1)} %gradient.15.refs_1_), custom_call_target="tpu_custom_call", output_to_operand_aliasing={{}: (3, {})} | custom-call | flops 10000000000 | bytes 1000000 | tf_op jit(solution)/shard_map/gradient/pallas_call | solution.py:209
  39.3 2.3 %finish.1 = (f32[256,768]{1,0:T(8,128)}, f32[256,768]{1,0:T(8,128)}, f32[256,768]{1,0:T(8,128)}) custom-call(bf16[832,128]{1,0:T(8,128)(2,1)S(1)} %collective-permute-done.14.a_ref, bf16[128,768]{1,0:T(8,128)(2,1)S(1)} %collective-permute-done.16.b_ref, bf16[256,768]{1,0:T(8,128)(2,1)S(1)} %cast.1.refs_0_.cast_ref, f32[256,768]{1,0:T(8,128)S(1)} %gradient.16.sum_ref, ...), custom_call_target="tpu_custom_call" | custom-call | flops 10000000000 | bytes 1000000 | tf_op jit(solution)/shard_map/finish/pallas_call | solution.py:266
  (23 shorter events, 0.9 us)
Async XLA Ops:
  0.6 6.7 %copy-start = (f32[256,768]{1,0:T(8,128)S(1)}, f32[256,768]{1,0:T(8,128)}, u32[]{:S(2)}) copy-start(f32[256,768]{1,0:T(8,128)} %weights_ref.3) | copy-start | bytes 2359300
  2.2 9.9 %collective-permute-start = (bf16[832,128]{1,0:T(8,128)(2,1)S(1)}, bf16[832,128]{1,0:T(8,128)(2,1)S(1)}, u32[]{:S(2)}, u32[]{:S(2)}) collective-permute-start(bf16[832,128]{1,0:T(8,128)(2,1)S(1)} %prepare.1.a_ref), channel_id=1, source_target_pairs={{4,0},{1,5},{8,4},{5,9},{12,8},{9,13},{14,12},{13,15},{10,14},{15,... | collective-permute-start | bytes 638984 | tf_op jit(solution)/shard_map/ppermute | solution.py:320
  5.3 6.0 %collective-permute-start.1 = (bf16[128,768]{1,0:T(8,128)(2,1)S(1)}, bf16[128,768]{1,0:T(8,128)(2,1)S(1)}, u32[]{:S(2)}, u32[]{:S(2)}) collective-permute-start(bf16[128,768]{1,0:T(8,128)(2,1)S(1)} %get-tuple-element.120.b_ref), channel_id=1, source_target_pairs={{0,4},{5,1},{4,8},{9,5},{8,12},{13,9},{12,14},{15,13},{14,10},{11,... | collective-permute-start | bytes 589832 | tf_op jit(solution)/shard_map/ppermute | solution.py:320
  5.4 10.4 %collective-permute-start.5 = (bf16[832,128]{1,0:T(8,128)(2,1)S(1)}, bf16[832,128]{1,0:T(8,128)(2,1)S(1)}, u32[]{:S(2)}, u32[]{:S(2)}) collective-permute-start(bf16[832,128]{1,0:T(8,128)(2,1)S(1)} %prepare.1.a_ref), channel_id=1, source_target_pairs={{0,4},{5,1},{4,8},{9,5},{8,12},{13,9},{12,14},{15,13},{14,10},{11,... | collective-permute-start | bytes 638984 | tf_op jit(solution)/shard_map/ppermute | solution.py:320
  7.4 15.4 %collective-permute-start.10 = (bf16[256,768]{1,0:T(8,128)(2,1)S(1)}, bf16[256,768]{1,0:T(8,128)(2,1)S(1)}, u32[]{:S(2)}, u32[]{:S(2)}) collective-permute-start(bf16[256,768]{1,0:T(8,128)(2,1)S(1)} %cast.1.refs_0_.cast_ref), channel_id=1, source_target_pairs={{0,1},{1,0},{2,3},{3,2},{4,5},{5,4},{6,7},{7,6},{8,9},{9,8},{10,11... | collective-permute-start | bytes 1179656 | tf_op jit(solution)/shard_map/ppermute | solution.py:320
  7.5 9.1 %collective-permute-start.4 = (bf16[128,768]{1,0:T(8,128)(2,1)S(1)}, bf16[128,768]{1,0:T(8,128)(2,1)S(1)}, u32[]{:S(2)}, u32[]{:S(2)}) collective-permute-start(bf16[128,768]{1,0:T(8,128)(2,1)S(1)} %get-tuple-element.120.b_ref), channel_id=1, source_target_pairs={{4,0},{1,5},{8,4},{5,9},{12,8},{9,13},{14,12},{13,15},{10,14},{15,... | collective-permute-start | bytes 589832 | tf_op jit(solution)/shard_map/ppermute | solution.py:320
  11.2 8.9 %collective-permute-start.3 = (bf16[128,768]{1,0:T(8,128)(2,1)S(1)}, bf16[128,768]{1,0:T(8,128)(2,1)S(1)}, u32[]{:S(2)}, u32[]{:S(2)}) collective-permute-start(bf16[128,768]{1,0:T(8,128)(2,1)S(1)} %collective-permute-done.1.b_ref), channel_id=1, source_target_pairs={{0,4},{5,1},{4,8},{9,5},{8,12},{13,9},{12,14},{15,13},{14,10},{11,... | collective-permute-start | bytes 589832 | tf_op jit(solution)/shard_map/ppermute | solution.py:320
  12.1 8.7 %collective-permute-start.2 = (bf16[832,128]{1,0:T(8,128)(2,1)S(1)}, bf16[832,128]{1,0:T(8,128)(2,1)S(1)}, u32[]{:S(2)}, u32[]{:S(2)}) collective-permute-start(bf16[832,128]{1,0:T(8,128)(2,1)S(1)} %collective-permute-done.a_ref), channel_id=1, source_target_pairs={{4,0},{1,5},{8,4},{5,9},{12,8},{9,13},{14,12},{13,15},{10,14},{15,... | collective-permute-start | bytes 638984 | tf_op jit(solution)/shard_map/ppermute | solution.py:320
  15.8 9.0 %collective-permute-start.9 = (bf16[832,128]{1,0:T(8,128)(2,1)S(1)}, bf16[832,128]{1,0:T(8,128)(2,1)S(1)}, u32[]{:S(2)}, u32[]{:S(2)}) collective-permute-start(bf16[832,128]{1,0:T(8,128)(2,1)S(1)} %collective-permute-done.5.a_ref), channel_id=1, source_target_pairs={{0,4},{5,1},{4,8},{9,5},{8,12},{13,9},{12,14},{15,13},{14,10},{11,... | collective-permute-start | bytes 638984 | tf_op jit(solution)/shard_map/ppermute | solution.py:320
  16.6 9.8 %collective-permute-start.8 = (bf16[128,768]{1,0:T(8,128)(2,1)S(1)}, bf16[128,768]{1,0:T(8,128)(2,1)S(1)}, u32[]{:S(2)}, u32[]{:S(2)}) collective-permute-start(bf16[128,768]{1,0:T(8,128)(2,1)S(1)} %collective-permute-done.4.b_ref), channel_id=1, source_target_pairs={{4,0},{1,5},{8,4},{5,9},{12,8},{9,13},{14,12},{13,15},{10,14},{15,... | collective-permute-start | bytes 589832 | tf_op jit(solution)/shard_map/ppermute | solution.py:320
  20.1 8.7 %collective-permute-start.7 = (bf16[128,768]{1,0:T(8,128)(2,1)S(1)}, bf16[128,768]{1,0:T(8,128)(2,1)S(1)}, u32[]{:S(2)}, u32[]{:S(2)}) collective-permute-start(bf16[128,768]{1,0:T(8,128)(2,1)S(1)} %collective-permute-done.3.b_ref), channel_id=1, source_target_pairs={{0,4},{5,1},{4,8},{9,5},{8,12},{13,9},{12,14},{15,13},{14,10},{11,... | collective-permute-start | bytes 589832 | tf_op jit(solution)/shard_map/ppermute | solution.py:320
  20.8 9.8 %collective-permute-start.6 = (bf16[832,128]{1,0:T(8,128)(2,1)S(1)}, bf16[832,128]{1,0:T(8,128)(2,1)S(1)}, u32[]{:S(2)}, u32[]{:S(2)}) collective-permute-start(bf16[832,128]{1,0:T(8,128)(2,1)S(1)} %collective-permute-done.2.a_ref), channel_id=1, source_target_pairs={{4,0},{1,5},{8,4},{5,9},{12,8},{9,13},{14,12},{13,15},{10,14},{15,... | collective-permute-start | bytes 638984 | tf_op jit(solution)/shard_map/ppermute | solution.py:320
  24.8 9.6 %collective-permute-start.13 = (bf16[832,128]{1,0:T(8,128)(2,1)S(1)}, bf16[832,128]{1,0:T(8,128)(2,1)S(1)}, u32[]{:S(2)}, u32[]{:S(2)}) collective-permute-start(bf16[832,128]{1,0:T(8,128)(2,1)S(1)} %collective-permute-done.9.a_ref), channel_id=1, source_target_pairs={{0,4},{5,1},{4,8},{9,5},{8,12},{13,9},{12,14},{15,13},{14,10},{11,... | collective-permute-start | bytes 638984 | tf_op jit(solution)/shard_map/ppermute | solution.py:320
  26.4 9.0 %collective-permute-start.12 = (bf16[128,768]{1,0:T(8,128)(2,1)S(1)}, bf16[128,768]{1,0:T(8,128)(2,1)S(1)}, u32[]{:S(2)}, u32[]{:S(2)}) collective-permute-start(bf16[128,768]{1,0:T(8,128)(2,1)S(1)} %collective-permute-done.8.b_ref), channel_id=1, source_target_pairs={{4,0},{1,5},{8,4},{5,9},{12,8},{9,13},{14,12},{13,15},{10,14},{15,... | collective-permute-start | bytes 589832 | tf_op jit(solution)/shard_map/ppermute | solution.py:320
  28.8 8.8 %collective-permute-start.15 = (bf16[128,768]{1,0:T(8,128)(2,1)S(1)}, bf16[128,768]{1,0:T(8,128)(2,1)S(1)}, u32[]{:S(2)}, u32[]{:S(2)}) collective-permute-start(bf16[128,768]{1,0:T(8,128)(2,1)S(1)} %collective-permute-done.7.b_ref), channel_id=1, source_target_pairs={{0,4},{5,1},{4,8},{9,5},{8,12},{13,9},{12,14},{15,13},{14,10},{11,... | collective-permute-start | bytes 589832 | tf_op jit(solution)/shard_map/ppermute | solution.py:320
  30.6 6.9 %collective-permute-start.11 = (bf16[832,128]{1,0:T(8,128)(2,1)S(1)}, bf16[832,128]{1,0:T(8,128)(2,1)S(1)}, u32[]{:S(2)}, u32[]{:S(2)}) collective-permute-start(bf16[832,128]{1,0:T(8,128)(2,1)S(1)} %collective-permute-done.6.a_ref), channel_id=1, source_target_pairs={{4,0},{1,5},{8,4},{5,9},{12,8},{9,13},{14,12},{13,15},{10,14},{15,... | collective-permute-start | bytes 638984 | tf_op jit(solution)/shard_map/ppermute | solution.py:320
  36.1 3.2 %collective-permute-start.17 = (f32[256,768]{1,0:T(8,128)S(1)}, f32[256,768]{1,0:T(8,128)S(1)}, u32[]{:S(2)}, u32[]{:S(2)}) collective-permute-start(f32[256,768]{1,0:T(8,128)S(1)} %gradient.17), channel_id=1, source_target_pairs={{0,1},{1,0},{2,3},{3,2},{4,5},{5,4},{6,7},{7,6},{8,9},{9,8},{10,11... | collective-permute-start | bytes 2359304 | tf_op jit(solution)/shard_map/ppermute | solution.py:320
  36.9 2.5 %copy-start.1 = (f32[256,768]{1,0:T(8,128)S(1)}, f32[256,768]{1,0:T(8,128)}, u32[]{:S(2)}) copy-start(f32[256,768]{1,0:T(8,128)} %first_ref.1) | copy-start | bytes 2359300
  36.9 2.5 %copy-start.2 = (f32[256,768]{1,0:T(8,128)S(1)}, f32[256,768]{1,0:T(8,128)}, u32[]{:S(2)}) copy-start(f32[256,768]{1,0:T(8,128)} %second_ref.1) | copy-start | bytes 2359300
  37.6 1.4 %collective-permute-start.16 = (bf16[128,768]{1,0:T(8,128)(2,1)S(1)}, bf16[128,768]{1,0:T(8,128)(2,1)S(1)}, u32[]{:S(2)}, u32[]{:S(2)}) collective-permute-start(bf16[128,768]{1,0:T(8,128)(2,1)S(1)} %collective-permute-done.15.b_ref), channel_id=1, source_target_pairs={{0,1},{1,0},{2,3},{3,2},{4,5},{5,4},{6,7},{7,6},{8,9},{9,8},{10,11... | collective-permute-start | bytes 589832 | tf_op jit(solution)/shard_map/ppermute | solution.py:320
  37.6 1.7 %collective-permute-start.14 = (bf16[832,128]{1,0:T(8,128)(2,1)S(1)}, bf16[832,128]{1,0:T(8,128)(2,1)S(1)}, u32[]{:S(2)}, u32[]{:S(2)}) collective-permute-start(bf16[832,128]{1,0:T(8,128)(2,1)S(1)} %collective-permute-done.11.a_ref), channel_id=1, source_target_pairs={{0,1},{1,0},{2,3},{3,2},{4,5},{5,4},{6,7},{7,6},{8,9},{9,8},{10,11... | collective-permute-start | bytes 638984 | tf_op jit(solution)/shard_map/ppermute | solution.py:320
